TPU v7x, 32 devices: a whole 2x2x4 slice. The times are simulated.
32 devices in a mesh: space: 8 (over y, x, core), mode: 4 (over z).
Axes of the slice: x: 2, y: 2, z: 4, core: 2. Of those that a mesh axis runs over, the one named last changes fastest.
Arguments:
- state: float32 [128, 8, 64, 256], P('mode', 'space'), may hold values from -6 to 6
- control: float32 [128, 8, 64, 256], P('mode', 'space'), may hold values from -6 to 6
- adjoint: float32 [128, 8, 64, 256], P('mode', 'space'), may hold values from -6 to 6
- coefficient: float32 [7, 8, 64, 256], P(None, 'space'), may hold values from 0.1 to 1
- pattern: int32 [7, 128, 4], replicated, may hold values from 0 to 127
- weights: float32 [7, 128, 4], replicated, may hold values from -3 to 3
Outputs:
- state_residual: float32 [128, 8, 64, 256], P('mode', 'space')
- control_residual: float32 [128, 8, 64, 256], P('mode', 'space')
- adjoint_residual: float32 [128, 8, 64, 256], P('mode', 'space')
Inputs may be any that keep to these rules, and one draw needn't show every extreme that they name: `pattern`: each entry names a chaos mode.
All inputs are finite; a program needn't handle non-finite values.
Results may differ from a plain program's by a relative error of at most 0.0001.
Values sent between devices are 32-bit elements; how exact they have to be, the bound alone decides.
No kernel may reach another device: no remote copies, remote signals or barrier semaphores. Data moves between devices by JAX's collectives and lax.ppermute only.
A program may use at most 384 MiB of HBM per device.

v0:
```python
import jax
import jax.numpy as jnp
from jax import lax
from jax.sharding import PartitionSpec as P


def padded(block, sides, width):
    for axis, dim in sides:
        count = lax.axis_size(axis)
        forward = [(i, i + 1) for i in range(count - 1)]
        backward = [(target, source) for source, target in forward]
        low = lax.ppermute(
            lax.slice_in_dim(block, block.shape[dim] - width, None, axis=dim), axis, forward
        )
        high = lax.ppermute(lax.slice_in_dim(block, 0, width, axis=dim), axis, backward)
        block = jnp.concatenate([low, block, high], axis=dim)
    return block


def coupling_matrices(pattern, weights):
    count = pattern.shape[1]
    modes = jnp.arange(count, dtype=jnp.int32)
    onehot = (pattern[..., None] == modes).astype(jnp.float32)
    dense = jnp.einsum("kis,kisj->kij", weights, onehot, precision=lax.Precision.HIGHEST)
    return 0.5 * (dense + jnp.swapaxes(dense, 1, 2))


def diffuse_slab(coef_ext, field_ext):
    centre_coef = coef_ext[1]
    centre_field = field_ext[:, 1]
    total = 0.5 * (centre_coef + coef_ext[0]) * (centre_field - field_ext[:, 0])
    total = total + 0.5 * (centre_coef + coef_ext[2]) * (centre_field - field_ext[:, 2])
    width_y, width_z = centre_coef.shape
    coef_pad = jnp.pad(centre_coef, 1)
    field_pad = jnp.pad(centre_field, ((0, 0), (1, 1), (1, 1)))
    for shift in ((1, 0), (-1, 0), (0, 1), (0, -1)):
        oy, oz = (1 + shift[0], 1 + shift[1])
        coef_next = coef_pad[oy : oy + width_y, oz : oz + width_z]
        field_next = field_pad[:, oy : oy + width_y, oz : oz + width_z]
        total = total + 0.5 * (centre_coef + coef_next) * (centre_field - field_next)
    return total


def shards(state, control, adjoint, coefficient, pattern, weights):
    modes_here = state.shape[0]
    width_y, width_z = (state.shape[2], state.shape[3])
    cells = width_y * width_z
    terms = coefficient.shape[0]
    coupling = coupling_matrices(pattern, weights)
    first = lax.axis_index("mode") * modes_here
    paired = jnp.stack([state, adjoint], 1).reshape(2 * modes_here, 1, width_y, width_z)
    local = paired.reshape(modes_here, 2 * cells)
    own_rows = lax.dynamic_slice_in_dim(coupling, first, modes_here, 1)
    mixed_terms = jnp.einsum(
        "kmj,jc->kmc",
        own_rows,
        lax.all_gather(local, "mode", axis=0, tiled=True),
        precision=lax.Precision.HIGHEST,
    )
    slabs = mixed_terms.reshape(terms * 2 * modes_here, 1, width_y, width_z)
    stacked = jnp.concatenate([slabs, coefficient], 0)
    extended = padded(stacked, (("space", 1),), 1)
    coef_ext = extended[terms * 2 * modes_here :]
    result = jnp.zeros((2 * modes_here, width_y, width_z), jnp.float32)
    for term in range(terms):
        block = extended[term * 2 * modes_here : (term + 1) * 2 * modes_here]
        result = result + diffuse_slab(coef_ext[term], block)
    mixed = result.reshape(modes_here, 2 * cells)
    applied = mixed.reshape(modes_here, 2, 1, width_y, width_z)
    state_residual = state + applied[:, 1]
    control_residual = 0.5 * control - adjoint
    adjoint_residual = applied[:, 0] - control
    return (state_residual, control_residual, adjoint_residual)


def solution(mesh):
    in_specs = (
        P("mode", "space", None, None),
        P("mode", "space", None, None),
        P("mode", "space", None, None),
        P(None, "space", None, None),
        P(),
        P(),
    )
    out_specs = (
        P("mode", "space", None, None),
        P("mode", "space", None, None),
        P("mode", "space", None, None),
    )
    return jax.shard_map(shards, mesh=mesh, in_specs=in_specs, out_specs=out_specs, check_vma=False)
```

profile of v0, /device:TPU:4, one launch (start us, length us, event | category | flops | bytes accessed | tf_op | source)
XLA Modules:
  0.0 1134.7 jit_solution(13708698842081231265)
XLA Ops:
  7.2 2.5 pad_maximum_fusion.1
  9.7 2.3 copy.24
  12.0 5.0 reshape_reshape.6
  17.0 0.7 copy-done.3
  17.7 0.2 copy.47
  17.9 0.2 copy.22
  18.1 5.0 select_reduce_fusion
  23.1 0.2 copy.46
  23.3 281.8 %all-gather.2.cloned.1.call-done = f32[128,32768]{1,0:T(8,128)} async-done(((f32[32,32768]{1,0:T(8,128)}), f32[128,32768]{1,0:T(8,128)}) %all-gather.2.cloned.1.call-update) | async-done | bytes 16777232 | tf_op jit(solution)/shard_map/all_gather | solution.py:57
  305.1 28.9 %fusion = f32[7,32,32768]{2,1,0:T(8,128)} fusion(f32[128,32768]{1,0:T(8,128)} %all-gather.2.cloned.1.call-done, f32[7,128,128]{2,1,0:T(8,128)S(1)} %bitcast.301, s32[]{:T(128)S(6)} %select_n.3, f32[7,128,128]{2,1,0:T(8,128)S(1)} %select_reduce_fusion), kind=kOutput, calls=%fused_computation.1 | convolution fusion | flops 11274346496 | bytes 46366724 | tf_op jit(solution)/shard_map/kmj,jc->kmc/dot_general | solution.py:54
  334.1 31.2 %reshape.234 = f32[448,1,64,256]{3,2,0,1:T(8,128)} reshape(f32[7,32,32768]{2,1,0:T(8,128)} %fusion) | data formatting | bytes 58720256 | tf_op jit(solution)/shard_map/reshape | solution.py:60
  365.2 30.3 %pad_maximum_fusion = (f32[455,1,64,256]{3,2,1,0:T(8,128)}, f32[455,1,64,256]{3,2,0,1:T(8,128)}) fusion(f32[7,1,64,256]{3,2,1,0:T(8,128)S(1)} %copy-done.2, f32[448,1,64,256]{3,2,1,0:T(8,128)} %bitcast.297), kind=kLoop, calls=%fused_computation | loop fusion | flops 7454720 | bytes 89456640 | tf_op jit(solution)/shard_map/concatenate | solution.py:61
  395.5 3.1 collective-permute-start.1
  398.7 2.1 collective-permute-start
  400.9 0.1 fusion.167
  401.1 0.8 fusion.151
  401.9 0.9 fusion.135
  402.8 1.7 multiply_subtract_fusion
  404.4 19.7 %fusion.222 = (f32[1,32,32768]{2,1,0:T(8,128)}, f32[1,32,32768]{2,1,0:T(8,128)}, f32[1,32,32768]{2,1,0:T(8,128)}, f32[1,32,32768]{2,1,0:T(8,128)}, f32[1,32,3276...) fusion(f32[7,32,32768]{2,1,0:T(8,128)} %fusion), kind=kLoop, calls=%fused_computation.320 | loop fusion | bytes 58720256 | tf_op jit(solution)/shard_map/slice | solution.py:30
  424.2 4.9 squeeze.141
  429.1 4.9 squeeze.147
  434.0 4.9 squeeze.153
  438.9 4.9 squeeze.159
  443.8 4.9 squeeze.165
  448.7 4.9 squeeze.171
  453.6 4.9 squeeze.177
  458.5 578.5 %collective-permute-done.1 = f32[455,1,64,256]{3,2,0,1:T(8,128)} collective-permute-done((f32[455,1,64,256]{3,2,0,1:T(8,128)}, f32[455,1,64,256]{3,2,0,1:T(8,128)}, u32[]{:S(2)}, u32[]{:S(2)}) %collective-permute-start.1) | collective-permute-done | bytes 29818912 | tf_op jit(solution)/shard_map/ppermute | solution.py:15
  1037.1 1.8 fusion.215
  1038.9 1.2 collective-permute-done
  1040.1 1.8 fusion.217
  1041.9 80.2 %fusion.13 = f32[64,64,256]{2,1,0:T(8,128)} fusion(f32[64,64,256]{2,1,0:T(8,128)} %squeeze.141, f32[64,64,256]{2,1,0:T(8,128)} %squeeze.147, f32[64,64,256]{2,1,0:T(8,128)} %squeeze.153, f32[64,64,256]{2,1,0:T(8,128)} %squeeze.159, f32[64,64,256]{2,1,0:T(8,128)} %squeeze.165, f32[64,64,256]{2,1,0:T(8,128)} %squeeze.171, f32[64,64,256]{2,1,0:T(8,128)} %squeeze.177, ...), kind=kLoop, calls=%fused_computation.42 | loop fusion | flops 131072000 | bytes 95027200 | tf_op jit(solution)/shard_map/add | solution.py:67
  1122.1 5.8 fusion.128
  (13 shorter events, 0.2 us)
Async XLA Ops:
  7.2 298.0 %all-gather.2.cloned.1.call-start = ((), (), s32[]{:S(2)}) async-start(), calls=%async_computation | async-start | bytes 20971520 | tf_op jit(solution)/shard_map/all_gather | solution.py:57
  17.0 0.7 copy-start.3
  17.0 0.9 copy-start.4
  334.1 31.2 %copy-start.2 = (f32[7,1,64,256]{3,2,1,0:T(8,128)S(1)}, f32[7,1,64,256]{3,2,1,0:T(8,128)}, u32[]{:S(2)}) copy-start(f32[7,1,64,256]{3,2,1,0:T(8,128)} %param.9) | copy-start | bytes 1376260
  365.2 37.5 %copy-start.1 = (f32[32,1,64,256]{3,2,1,0:T(8,128)S(1)}, f32[32,1,64,256]{3,2,1,0:T(8,128)}, u32[]{:S(2)}) copy-start(f32[32,1,64,256]{3,2,1,0:T(8,128)} %param.7) | copy-start | bytes 6291460
  395.5 7.2 copy-start
  395.5 641.6 %collective-permute-start.1 = (f32[455,1,64,256]{3,2,0,1:T(8,128)}, f32[455,1,64,256]{3,2,0,1:T(8,128)}, u32[]{:S(2)}, u32[]{:S(2)}) collective-permute-start(f32[455,1,64,256]{3,2,0,1:T(8,128)} %get-tuple-element.23), channel_id=1, source_target_pairs={{4,0},{8,4},{12,8},{16,12},{20,16},{24,20},{28,24},{5,1},{9,5},{13... | collective-permute-start | bytes 89456648 | tf_op jit(solution)/shard_map/ppermute | solution.py:15
  398.7 641.4 %collective-permute-start = (f32[455,1,64,256]{3,2,1,0:T(8,128)}, f32[455,1,64,256]{3,2,1,0:T(8,128)}, u32[]{:S(2)}, u32[]{:S(2)}) collective-permute-start(f32[455,1,64,256]{3,2,1,0:T(8,128)} %get-tuple-element.22), channel_id=1, source_target_pairs={{0,4},{4,8},{8,12},{12,16},{16,20},{20,24},{24,28},{1,5},{5,9},{9,... | collective-permute-start | bytes 89456648 | tf_op jit(solution)/shard_map/ppermute | solution.py:12
Sparse Core Ops, SparseCore 0:
  17.1 287.9 all-gather.1
where the time goes:
time: 1140 us; the launch traced here: 1130 us
  waiting for transfers between devices  862 us (76%)
  other arithmetic  131 us (11%)
  local copies, waits for them, and re-layouts  93.9 us (8%)
  matrix products  28.9 us (3%)
  between operations  14.1 us (1%)
    ppermute x1, waiting for transfers between devices, padded(): lax.ppermute(lax.slice_in_dim(block, 0, width, axis=dim), axis, backward)  579 us
    all_gather x1, waiting for transfers between devices, shards(): lax.all_gather(local, 'mode', axis=0, tiled=True)  282 us
    add x1, other arithmetic, shards(): result = result + diffuse_slab(coef_ext[term], block)  80.2 us
    squeeze x7, local copies, waits for them, and re-layouts, diffuse_slab(): centre_field = field_ext[:, 1]  34.4 us
    reshape x1, local copies, waits for them, and re-layouts, shards(): slabs = mixed_terms.reshape(terms * 2 * modes_here, 1, width_y, width_z)  31.2 us
    concatenate x1, other arithmetic, shards(): stacked = jnp.concatenate([slabs, coefficient], 0)  30.3 us
    dot_general x1, matrix products, shards(): jnp.einsum('kmj,jc->kmc', own_rows, lax.all_gather(local, 'mode', axis=0,...  28.9 us
  transfers between devices with their start and end apart: 3, of which 3 were waited for; matrix products, arithmetic and copies ran while one was open for 6% of the time, Pallas kernels for 0%

commit v1 on v0

v1 whole, which is shorter than its diff:
```python
import functools

import jax
import jax.numpy as jnp
from jax import lax
from jax.experimental import pallas as pl
from jax.experimental.pallas import tpu as pltpu
from jax.sharding import PartitionSpec as P

CHUNK_ROWS = 8
VMEM_LIMIT = 48 * 1024 * 1024


def params():
    return pltpu.CompilerParams(vmem_limit_bytes=VMEM_LIMIT)


def coupling_matrices(pattern, weights):
    count = pattern.shape[1]
    modes = jnp.arange(count, dtype=jnp.int32)
    hits = pattern[..., None] == modes
    dense = jnp.sum(jnp.where(hits, weights[..., None], 0.0), axis=2)
    coupling = 0.5 * (dense + jnp.swapaxes(dense, 1, 2))
    wide = jnp.swapaxes(coupling, 0, 1).reshape(count, -1)
    high = lax.reduce_precision(wide, 8, 7)
    return jnp.concatenate([high, wide - high], 0).astype(jnp.bfloat16)


def face_coefficients(own, below, above, first, rows):
    centre = lax.dynamic_slice_in_dim(own, first, rows, 1)
    tall = jnp.pad(own, ((0, 0), (1, 1), (0, 0)))
    near = lax.dynamic_slice_in_dim(tall, first, rows + 2, 1)
    wide = jnp.pad(centre, ((0, 0), (0, 0), (1, 1)))
    others = [below, above, near[:, :-2], near[:, 2:], wide[:, :, :-2], wide[:, :, 2:]]
    faces = jnp.stack([0.5 * (centre + other) for other in others], 1)
    terms, _, _, width = faces.shape
    return jnp.transpose(faces.reshape(terms * 6, rows, width), (1, 0, 2))


def pack_kernel(edge_rows, state_ref, adjoint_ref, *refs):
    out_ref = refs[-1]
    rows = state_ref.shape[1]
    out_ref[0, 0, :rows] = jnp.swapaxes(state_ref[...], 0, 1)
    out_ref[1, 0, :rows] = jnp.swapaxes(adjoint_ref[...], 0, 1)
    if edge_rows:
        out_ref[:, 0, rows:] = refs[0][:, 0]


def pack(state, adjoint, edges, chunk, rows, halves):
    modes, height, width = state.shape
    per_half = height // halves // rows
    block = pl.BlockSpec((modes, rows, width), lambda h: (0, h * per_half + chunk, 0))
    edge_rows = 0 if edges is None else edges.shape[2]
    in_specs = [block, block]
    operands = [state, adjoint]
    if edge_rows:
        in_specs.append(pl.BlockSpec((2, 1, edge_rows, modes, width), lambda h: (0, h, 0, 0, 0)))
        operands.append(edges)
    total = rows + edge_rows
    return pl.pallas_call(
        functools.partial(pack_kernel, edge_rows),
        grid=(halves,),
        in_specs=in_specs,
        out_specs=pl.BlockSpec((2, 1, total, modes, width), lambda h: (0, h, 0, 0, 0)),
        out_shape=jax.ShapeDtypeStruct((2, halves, total, modes, width), jnp.float32),
        compiler_params=params(),
        name="pack",
    )(*operands)


def edge_rows_of(state, adjoint, halves):
    height = state.shape[1]
    rows = height // halves
    fields = jnp.stack([state, adjoint])
    if halves == 1:
        return None
    if halves == 2:
        picked = jnp.stack([fields[:, :, rows], fields[:, :, rows - 1]], 1)
        return picked[:, :, None]
    tall = jnp.pad(fields, ((0, 0), (0, 0), (1, 1), (0, 0)))
    pairs = [jnp.stack([tall[:, :, h * rows], tall[:, :, (h + 1) * rows + 1]], 1) for h in range(halves)]
    return jnp.stack(pairs, 1)


def operator_kernel(rows, terms, modes, own_ref, before_ref, after_ref, below_ref, above_ref, face_ref, matrix_ref, out_ref, high, low):
    sources, _, part, width = own_ref.shape
    lanes = lax.broadcasted_iota(jnp.int32, (part, width), 1)
    step = 16

    def shifted(block):
        left = jnp.where(lanes[:step] == 0, 0.0, pltpu.roll(block, 1, 1))
        right = jnp.where(lanes[:step] == width - 1, 0.0, pltpu.roll(block, width - 1, 1))
        return left, right

    for row in range(rows):
        for source in range(sources):
            for start in range(0, part, step):
                here = pl.ds(start, step)
                centre = own_ref[source, row, here, :]
                up = own_ref[source, row - 1, here, :] if row else before_ref[source, 0, here, :]
                down = own_ref[source, row + 1, here, :] if row < rows - 1 else after_ref[source, 0, here, :]
                left, right = shifted(centre)
                others = (below_ref[source, row, here, :], above_ref[source, row, here, :], up, down, left, right)
                slopes = [centre - other for other in others]
                for term in range(terms):
                    total = face_ref[row, 6 * term : 6 * term + 1, :] * slopes[0]
                    for side in range(1, 6):
                        total = total + face_ref[row, 6 * term + side : 6 * term + side + 1, :] * slopes[side]
                    rounded = total.astype(jnp.bfloat16)
                    place = pl.ds(term * modes + source * part + start, step)
                    high[place, :] = rounded
                    low[place, :] = (total - rounded.astype(jnp.float32)).astype(jnp.bfloat16)
        both = jnp.dot(matrix_ref[...], high[...], preferred_element_type=jnp.float32)
        rest = jnp.dot(matrix_ref[:modes, :], low[...], preferred_element_type=jnp.float32)
        mixed = both[:modes] + both[modes:] + rest
        for source in range(sources):
            out_ref[source, row] = mixed[source * part : (source + 1) * part]


def apply_operator(own, before, after, below, above, faces, matrix, chunk, rows):
    sources, _, part, width = own.shape
    modes = sources * part
    terms = matrix.shape[1] // modes

    def whole(array):
        return pl.BlockSpec(array.shape, lambda i: (0,) * array.ndim)

    block = pl.BlockSpec((sources, rows, part, width), lambda i: (0, 0, 0, 0))
    edge = pl.BlockSpec((sources, 1, part, width), lambda i: (0, 0, 0, 0))
    return pl.pallas_call(
        functools.partial(operator_kernel, rows, terms, modes),
        grid=(1,),
        in_specs=[
            block,
            edge,
            edge,
            block,
            block,
            pl.BlockSpec((rows, 6 * terms, width), lambda i: (chunk, 0, 0)),
            whole(matrix),
        ],
        out_specs=block,
        out_shape=jax.ShapeDtypeStruct((sources, rows, part, width), jnp.float32),
        scratch_shapes=[
            pltpu.VMEM((terms * modes, width), jnp.bfloat16),
            pltpu.VMEM((terms * modes, width), jnp.bfloat16),
        ],
        compiler_params=params(),
        name="operator",
    )(own, before, after, below, above, faces, matrix)


def finish_kernel(mixed_ref, state_ref, control_ref, adjoint_ref, *refs):
    state_out, control_out, adjoint_out = refs[-3:]
    control = control_ref[...]
    state_out[...] = state_ref[...] + jnp.swapaxes(mixed_ref[1, 0], 0, 1)
    control_out[...] = 0.5 * control - adjoint_ref[...]
    adjoint_out[...] = jnp.swapaxes(mixed_ref[0, 0], 0, 1) - control


def finish(mixed, state, control, adjoint, outputs, chunk, rows, halves):
    modes, height, width = state.shape
    per_half = height // halves // rows
    block = pl.BlockSpec((modes, rows, width), lambda h: (0, h * per_half + chunk, 0))
    mixed = mixed.reshape(2, halves, rows, modes, width)
    in_specs = [pl.BlockSpec((2, 1, rows, modes, width), lambda h: (0, h, 0, 0, 0)), block, block, block]
    operands = [mixed, state, control, adjoint]
    aliases = {}
    if outputs is not None:
        in_specs += [pl.BlockSpec(memory_space=pl.ANY)] * 3
        operands += list(outputs)
        aliases = {4: 0, 5: 1, 6: 2}
    return pl.pallas_call(
        finish_kernel,
        grid=(halves,),
        in_specs=in_specs,
        out_specs=[block] * 3,
        out_shape=[jax.ShapeDtypeStruct(state.shape, jnp.float32)] * 3,
        input_output_aliases=aliases,
        compiler_params=params(),
        name="finish",
    )(*operands)


def shards(state, control, adjoint, coefficient, pattern, weights):
    shape = state.shape
    modes, _, height, width = shape
    state, control, adjoint = (a.reshape(modes, height, width) for a in (state, control, adjoint))
    owners = lax.axis_size("mode")
    halves = owners // 2
    half_rows = height // halves
    rows = min(CHUNK_ROWS, half_rows)
    chunks = half_rows // rows
    planes = lax.axis_size("space")
    forward = [(i, i + 1) for i in range(planes - 1)]
    backward = [(i + 1, i) for i in range(planes - 1)]
    half = lax.rem(lax.axis_index("mode"), halves)

    edges = edge_rows_of(state, adjoint, halves)
    fields = []
    for chunk in range(chunks):
        packed = pack(state, adjoint, edges if chunk == 0 else None, chunk, rows, halves)
        packed = packed.reshape((owners,) + packed.shape[2:])
        fields.append(lax.all_to_all(packed, "mode", 0, 0, tiled=True))

    matrix = coupling_matrices(pattern, weights)
    own = coefficient[:, 0]
    mine = lax.dynamic_slice_in_dim(own, half * half_rows, half_rows, 1)
    faces = face_coefficients(
        own,
        lax.ppermute(mine, "space", forward),
        lax.ppermute(mine, "space", backward),
        half * half_rows,
        half_rows,
    )

    nothing = jnp.zeros((owners, 1, modes, width), jnp.float32)
    first = last = nothing
    if halves == 2:
        edge = fields[0][:, rows : rows + 1]
        first = jnp.where(half == 1, edge, 0.0)
        last = jnp.where(half == 0, edge, 0.0)
    elif halves > 2:
        first = fields[0][:, rows : rows + 1]
        last = fields[0][:, rows + 1 : rows + 2]

    outputs = None
    for chunk in range(chunks):
        block = fields[chunk]
        body = block[:, :rows]
        below = lax.ppermute(body, "space", forward)
        above = lax.ppermute(body, "space", backward)
        before = fields[chunk - 1][:, rows - 1 : rows] if chunk else first
        after = fields[chunk + 1][:, :1] if chunk < chunks - 1 else last
        mixed = apply_operator(block, before, after, below, above, faces, matrix, chunk, rows)
        mixed = lax.all_to_all(mixed, "mode", 0, 0, tiled=True)
        outputs = finish(mixed, state, control, adjoint, outputs, chunk, rows, halves)
    return tuple(out.reshape(shape) for out in outputs)


def solution(mesh):
    split = P("mode", "space", None, None)
    in_specs = (split, split, split, P(None, "space", None, None), P(), P())
    return jax.shard_map(shards, mesh=mesh, in_specs=in_specs, out_specs=(split, split, split), check_vma=False)
```

time: 1140 us -> 283 us (0.25)
  waiting for transfers between devices: 862 us -> 137 us
  other arithmetic: 131 us -> 10.6 us
  local copies, waits for them, and re-layouts: 93.9 us -> 35.4 us
  starting transfers between devices: 5.29 us -> 62.5 us
  Pallas kernels: 0 us -> 33.2 us
  matrix products: 28.9 us -> 0 us
  between operations: 14.1 us -> 1.05 us
    ppermute x2 -> x10, waiting for transfers between devices: 580 us -> 69.6 us  [the longest x4 64.4 us: shards(): above = lax.ppermute(body, 'space', backward)]
    all_gather x1 -> x0, waiting for transfers between devices: 282 us -> none  [shards(): lax.all_gather(local, 'mode', axis=0, tiled=True)]
    add x1 -> x0, other arithmetic: 80.2 us -> none  [shards(): result = result + diffuse_slab(coef_ext[term], block)]
    all_to_all x0 -> x8, waiting for transfers between devices: none -> 67.1 us  [the longest x4 49.8 us: shards(): fields.append(lax.all_to_all(packed, 'mode', 0, 0, tiled=True))]
    all_to_all x0 -> x8, starting transfers between devices: none -> 35.9 us  [the longest x4 18.9 us: shards(): mixed = lax.all_to_all(mixed, 'mode', 0, 0, tiled=True)]
    squeeze x8 -> x0, local copies, waits for them, and re-layouts: 34.4 us -> none  [the longest x7 34.4 us: diffuse_slab(): centre_field = field_ext[:, 1]]
    pallas_call x0 -> x12, Pallas kernels: none -> 33.2 us  [the longest x4 22.5 us: apply_operator(): pl.pallas_call(functools.partial(operator_kernel, rows, terms, modes), gr...]
    concatenate x1, other arithmetic: 30.3 us -> 1.14 us  [coupling_matrices(): return jnp.concatenate([high, wide - high], 0).astype(jnp.bfloat16)]
  transfers between devices with their start and end apart: 3 -> 18, of which waited for: 3 -> 10; matrix products, arithmetic and copies ran while one was open for 6% -> 9% of each run, Pallas kernels for 0% -> 11%
where the time goes in v1:
time: 283 us; the launch traced here: 279 us
  waiting for transfers between devices  137 us (48%)
  starting transfers between devices  62.5 us (22%)
  local copies, waits for them, and re-layouts  35.4 us (13%)
  Pallas kernels  33.2 us (12%)
  other arithmetic  10.6 us (4%)
    ppermute x4, waiting for transfers between devices, shards(): above = lax.ppermute(body, 'space', backward)  64.4 us
    all_to_all x4, waiting for transfers between devices, shards(): fields.append(lax.all_to_all(packed, 'mode', 0, 0, tiled=True))  49.8 us
    pallas_call x4, Pallas kernels, apply_operator(): pl.pallas_call(functools.partial(operator_kernel, rows, terms, modes), gr...  22.5 us
    unnamed x46, local copies, waits for them, and re-layouts  20.2 us
    all_to_all x4, starting transfers between devices, shards(): mixed = lax.all_to_all(mixed, 'mode', 0, 0, tiled=True)  18.9 us
    all_to_all x4, waiting for transfers between devices, shards(): mixed = lax.all_to_all(mixed, 'mode', 0, 0, tiled=True)  17.2 us
    all_to_all x4, starting transfers between devices, shards(): fields.append(lax.all_to_all(packed, 'mode', 0, 0, tiled=True))  17 us
    ppermute x4, starting transfers between devices, shards(): above = lax.ppermute(body, 'space', backward)  12.3 us
  transfers between devices with their start and end apart: 18, of which 10 were waited for; matrix products, arithmetic and copies ran while one was open for 9% of the time, Pallas kernels for 11%

profile of v1, /device:TPU:4, one launch (start us, length us, event | category | flops | bytes accessed | tf_op | source)
XLA Modules:
  0.0 279.5 jit_solution(8334631228176234523)
XLA Ops:
  5.2 5.0 %all-to-all-start.4 = ((f32[4,8,32,256]{3,2,1,0:T(8,128)}), f32[4,8,32,256]{3,2,1,0:T(8,128)S(1)}, u32[]{:S(2)}, u32[]{:S(2)}) async-start(f32[4,8,32,256]{3,2,1,0:T(8,128)} %bitcast.107), calls=%async_computation.4 | async-start | bytes 2097152 | tf_op jit(solution)/shard_map/all_to_all | solution.py:204
  13.2 22.7 %all-to-all-done.4.own_ref = f32[4,8,32,256]{3,2,1,0:T(8,128)S(1)} async-done(((f32[4,8,32,256]{3,2,1,0:T(8,128)}), f32[4,8,32,256]{3,2,1,0:T(8,128)S(1)}, u32[]{:S(2)}, u32[]{:S(2)}) %all-to-all-start.4) | async-done | bytes 1048608 | tf_op jit(solution)/shard_map/all_to_all | solution.py:204
  35.9 4.2 %all-to-all-start.1 = ((f32[4,8,32,256]{3,2,1,0:T(8,128)}), f32[4,8,32,256]{3,2,1,0:T(8,128)}, u32[]{:S(2)}, u32[]{:S(2)}) async-start(f32[4,8,32,256]{3,2,1,0:T(8,128)} %bitcast.106), calls=%async_computation.1 | async-start | bytes 2097152 | tf_op jit(solution)/shard_map/all_to_all | solution.py:204
  43.2 22.3 %all-to-all-done.1.own_ref = f32[4,8,32,256]{3,2,1,0:T(8,128)} async-done(((f32[4,8,32,256]{3,2,1,0:T(8,128)}), f32[4,8,32,256]{3,2,1,0:T(8,128)}, u32[]{:S(2)}, u32[]{:S(2)}) %all-to-all-start.1) | async-done | bytes 1048608 | tf_op jit(solution)/shard_map/all_to_all | solution.py:204
  65.5 3.5 %all-to-all-start = ((f32[4,8,32,256]{3,2,1,0:T(8,128)}), f32[4,8,32,256]{3,2,1,0:T(8,128)S(1)}, u32[]{:S(2)}, u32[]{:S(2)}) async-start(f32[4,8,32,256]{3,2,1,0:T(8,128)} %bitcast.105), calls=%async_computation | async-start | bytes 2097152 | tf_op jit(solution)/shard_map/all_to_all | solution.py:204
  72.0 2.3 collective-permute-start.2
  82.3 4.0 %copy_bitcast_fusion = (f32[1,32,64,256]{3,1,0,2:T(8,128)S(1)}, f32[1,32,64,256]{3,1,0,2:T(8,128)S(1)}) fusion(f32[32,1,64,256]{3,2,1,0:T(8,128)} %param.8, f32[32,1,64,256]{3,2,1,0:T(8,128)S(1)} %copy-done.1), kind=kLoop, calls=%fused_computation | loop fusion | bytes 8388608 | tf_op jit(solution)/shard_map/stack;reshape | solution.py:74
  89.4 4.8 %all-to-all-done.own_ref = f32[4,8,32,256]{3,2,1,0:T(8,128)S(1)} async-done(((f32[4,8,32,256]{3,2,1,0:T(8,128)}), f32[4,8,32,256]{3,2,1,0:T(8,128)S(1)}, u32[]{:S(2)}, u32[]{:S(2)}) %all-to-all-start) | async-done | bytes 1048608 | tf_op jit(solution)/shard_map/all_to_all | solution.py:204
  94.2 4.3 %all-to-all-start.2 = ((f32[4,9,32,256]{3,2,1,0:T(8,128)}), f32[4,9,32,256]{3,2,1,0:T(8,128)}, u32[]{:S(2)}, u32[]{:S(2)}) async-start(f32[4,9,32,256]{3,2,1,0:T(8,128)} %bitcast.104), calls=%async_computation.2 | async-start | bytes 2359296 | tf_op jit(solution)/shard_map/all_to_all | solution.py:204
  104.6 2.3 collective-permute-start.4
  112.3 13.3 %collective-permute-done.5.above_ref = f32[4,8,32,256]{3,2,1,0:T(8,128)S(1)} collective-permute-done((f32[4,8,32,256]{3,2,1,0:T(8,128)}, f32[4,8,32,256]{3,2,1,0:T(8,128)S(1)}, u32[]{:S(2)}, u32[]{:S(2)}) %collective-permute-start.5) | collective-permute-done | bytes 1048608 | tf_op jit(solution)/shard_map/ppermute | solution.py:232
  125.6 4.5 %collective-permute-done.4.below_ref = f32[4,8,32,256]{3,2,1,0:T(8,128)S(1)} collective-permute-done((f32[4,8,32,256]{3,2,1,0:T(8,128)}, f32[4,8,32,256]{3,2,1,0:T(8,128)S(1)}, u32[]{:S(2)}, u32[]{:S(2)}) %collective-permute-start.4) | collective-permute-done | bytes 1048608 | tf_op jit(solution)/shard_map/ppermute | solution.py:231
  130.1 5.6 %operator.5 = f32[4,8,32,256]{3,2,1,0:T(8,128)S(1)} custom-call(f32[4,8,32,256]{3,2,1,0:T(8,128)} %all-to-all-done.1.own_ref, f32[4,1,32,256]{3,2,1,0:T(8,128)S(1)} %get-tuple-element.42.before_ref, f32[4,1,32,256]{3,2,1,0:T(8,128)S(1)} %slice.59.after_ref, f32[4,8,32,256]{3,2,1,0:T(8,128)S(1)} %collective-permute-done.4.below_ref, ...), custom_call_target="tpu_custom_call" | custom-call | tf_op jit(solution)/shard_map/operator/pallas_call | solution.py:130
  136.7 5.0 %all-to-all-start.5 = ((f32[4,8,32,256]{3,2,1,0:T(8,128)}), f32[4,8,32,256]{3,2,1,0:T(8,128)}, u32[]{:S(2)}, u32[]{:S(2)}) async-start(f32[4,8,32,256]{3,2,1,0:T(8,128)} %copy-done.14), calls=%async_computation.5 | async-start | bytes 2097152 | tf_op jit(solution)/shard_map/all_to_all | solution.py:236
  143.7 2.6 collective-permute-start.6
  148.4 17.1 %collective-permute-done.7.above_ref = f32[4,8,32,256]{3,2,1,0:T(8,128)} collective-permute-done((f32[4,8,32,256]{3,2,1,0:T(8,128)}, f32[4,8,32,256]{3,2,1,0:T(8,128)}, u32[]{:S(2)}, u32[]{:S(2)}) %collective-permute-start.7) | collective-permute-done | bytes 1048608 | tf_op jit(solution)/shard_map/ppermute | solution.py:232
  166.3 5.9 %operator.6 = f32[4,8,32,256]{3,2,1,0:T(8,128)S(1)} custom-call(f32[4,8,32,256]{3,2,1,0:T(8,128)S(1)} %copy-done.9, f32[4,1,32,256]{3,2,1,0:T(8,128)S(1)} %get-tuple-element.39.before_ref, f32[4,1,32,256]{3,2,1,0:T(8,128)S(1)} %get-tuple-element.43.after_ref, f32[4,8,32,256]{3,2,1,0:T(8,128)} %collective-permute-done.6.below_ref, ...), custom_call_target="tpu_custom_call" | custom-call | tf_op jit(solution)/shard_map/operator/pallas_call | solution.py:130
  173.2 4.8 %all-to-all-start.6 = ((f32[4,8,32,256]{3,2,1,0:T(8,128)}), f32[4,8,32,256]{3,2,1,0:T(8,128)}, u32[]{:S(2)}, u32[]{:S(2)}) async-start(f32[4,8,32,256]{3,2,1,0:T(8,128)} %copy-done.17), calls=%async_computation.6 | async-start | bytes 2097152 | tf_op jit(solution)/shard_map/all_to_all | solution.py:236
  179.3 4.0 %collective-permute-start.9 = (f32[4,8,32,256]{3,2,1,0:T(8,128)S(1)}, f32[4,8,32,256]{3,2,1,0:T(8,128)S(1)}, u32[]{:S(2)}, u32[]{:S(2)}) collective-permute-start(f32[4,8,32,256]{3,2,1,0:T(8,128)S(1)} %slice.63), channel_id=1, source_target_pairs={{4,0},{8,4},{12,8},{16,12},{20,16},{24,20},{28,24},{5,1},{9,5},{13... | collective-permute-start | bytes 3145736 | tf_op jit(solution)/shard_map/ppermute | solution.py:232
  185.3 18.2 %collective-permute-done.9.above_ref = f32[4,8,32,256]{3,2,1,0:T(8,128)S(1)} collective-permute-done((f32[4,8,32,256]{3,2,1,0:T(8,128)S(1)}, f32[4,8,32,256]{3,2,1,0:T(8,128)S(1)}, u32[]{:S(2)}, u32[]{:S(2)}) %collective-permute-start.9) | collective-permute-done | bytes 1048608 | tf_op jit(solution)/shard_map/ppermute | solution.py:232
  203.5 5.6 %operator.7 = f32[4,8,32,256]{3,2,1,0:T(8,128)S(1)} custom-call(f32[4,9,32,256]{3,2,1,0:T(8,128)} %all-to-all-done.2.own_ref, f32[4,1,32,256]{3,2,1,0:T(8,128)S(1)} %get-tuple-element.38.before_ref, f32[4,1,32,256]{3,2,1,0:T(8,128)S(1)} %get-tuple-element.41.after_ref, f32[4,8,32,256]{3,2,1,0:T(8,128)S(1)} %collective-permute-done.8.below_ref, ...), custom_call_target="tpu_custom_call" | custom-call | tf_op jit(solution)/shard_map/operator/pallas_call | solution.py:130
  210.1 4.5 %all-to-all-start.7 = ((f32[4,8,32,256]{3,2,1,0:T(8,128)}), f32[4,8,32,256]{3,2,1,0:T(8,128)}, u32[]{:S(2)}, u32[]{:S(2)}) async-start(f32[4,8,32,256]{3,2,1,0:T(8,128)} %copy-done.16), calls=%async_computation.7 | async-start | bytes 2097152 | tf_op jit(solution)/shard_map/all_to_all | solution.py:236
  214.7 4.4 %collective-permute-start.1 = (f32[4,8,32,256]{3,2,1,0:T(8,128)}, f32[4,8,32,256]{3,2,1,0:T(8,128)S(1)}, u32[]{:S(2)}, u32[]{:S(2)}) collective-permute-start(f32[4,8,32,256]{3,2,1,0:T(8,128)} %copy-done.10), channel_id=1, source_target_pairs={{4,0},{8,4},{12,8},{16,12},{20,16},{24,20},{28,24},{5,1},{9,5},{13... | collective-permute-start | bytes 3145736 | tf_op jit(solution)/shard_map/ppermute | solution.py:232
  219.1 3.1 %collective-permute-start = (f32[4,8,32,256]{3,2,1,0:T(8,128)}, f32[4,8,32,256]{3,2,1,0:T(8,128)S(1)}, u32[]{:S(2)}, u32[]{:S(2)}) collective-permute-start(f32[4,8,32,256]{3,2,1,0:T(8,128)} %copy-done.10), channel_id=1, source_target_pairs={{0,4},{4,8},{8,12},{12,16},{16,20},{20,24},{24,28},{1,5},{5,9},{9,... | collective-permute-start | bytes 3145736 | tf_op jit(solution)/shard_map/ppermute | solution.py:231
  222.2 15.7 %collective-permute-done.1.above_ref = f32[4,8,32,256]{3,2,1,0:T(8,128)S(1)} collective-permute-done((f32[4,8,32,256]{3,2,1,0:T(8,128)}, f32[4,8,32,256]{3,2,1,0:T(8,128)S(1)}, u32[]{:S(2)}, u32[]{:S(2)}) %collective-permute-start.1) | collective-permute-done | bytes 1048608 | tf_op jit(solution)/shard_map/ppermute | solution.py:232
  239.1 5.3 %operator.4 = f32[4,8,32,256]{3,2,1,0:T(8,128)S(1)} custom-call(f32[4,8,32,256]{3,2,1,0:T(8,128)S(1)} %copy-done.11, f32[4,1,32,256]{3,2,1,0:T(8,128)S(1)} %get-tuple-element.44.before_ref, f32[4,1,32,256]{3,2,1,0:T(8,128)S(1)} %get-tuple-element.40.after_ref, f32[4,8,32,256]{3,2,1,0:T(8,128)S(1)} %collective-permute-done.below_ref, ...), custom_call_target="tpu_custom_call" | custom-call | tf_op jit(solution)/shard_map/operator/pallas_call | solution.py:130
  245.5 4.5 %all-to-all-start.3 = ((f32[4,8,32,256]{3,2,1,0:T(8,128)}), f32[4,8,32,256]{3,2,1,0:T(8,128)S(1)}, u32[]{:S(2)}, u32[]{:S(2)}) async-start(f32[4,8,32,256]{3,2,1,0:T(8,128)} %copy-done.15), calls=%async_computation.3 | async-start | bytes 2097152 | tf_op jit(solution)/shard_map/all_to_all | solution.py:236
  251.6 2.3 finish.4
  253.9 2.3 finish.5
  256.2 2.3 finish.6
  258.5 17.2 %all-to-all-done.3 = f32[4,8,32,256]{3,2,1,0:T(8,128)S(1)} async-done(((f32[4,8,32,256]{3,2,1,0:T(8,128)}), f32[4,8,32,256]{3,2,1,0:T(8,128)S(1)}, u32[]{:S(2)}, u32[]{:S(2)}) %all-to-all-start.3) | async-done | bytes 1048608 | tf_op jit(solution)/shard_map/all_to_all | solution.py:236
  277.3 2.2 finish.7
  (84 shorter events, 52.2 us)
Async XLA Ops:
  0.6 1.6 copy-start
  2.2 1.6 copy-start.2
  5.2 5.0 %copy-start.1 = (f32[32,1,64,256]{3,2,1,0:T(8,128)S(1)}, f32[32,1,64,256]{3,2,1,0:T(8,128)}, u32[]{:S(2)}) copy-start(f32[32,1,64,256]{3,2,1,0:T(8,128)} %param.6) | copy-start | bytes 6291460
  5.2 30.7 %all-to-all-start.4 = ((f32[4,8,32,256]{3,2,1,0:T(8,128)}), f32[4,8,32,256]{3,2,1,0:T(8,128)S(1)}, u32[]{:S(2)}, u32[]{:S(2)}) async-start(f32[4,8,32,256]{3,2,1,0:T(8,128)} %bitcast.107), calls=%async_computation.4 | async-start | bytes 2097152 | tf_op jit(solution)/shard_map/all_to_all | solution.py:204
  10.2 1.6 copy-start.3
  35.9 6.3 %copy-start.8 = (f32[4,8,32,256]{3,2,1,0:T(8,128)}, f32[4,8,32,256]{3,2,1,0:T(8,128)S(1)}, u32[]{:S(2)}) copy-start(f32[4,8,32,256]{3,2,1,0:T(8,128)S(1)} %all-to-all-done.4.own_ref) | copy-start | bytes 3145732
  35.9 29.5 %all-to-all-start.1 = ((f32[4,8,32,256]{3,2,1,0:T(8,128)}), f32[4,8,32,256]{3,2,1,0:T(8,128)}, u32[]{:S(2)}, u32[]{:S(2)}) async-start(f32[4,8,32,256]{3,2,1,0:T(8,128)} %bitcast.106), calls=%async_computation.1 | async-start | bytes 2097152 | tf_op jit(solution)/shard_map/all_to_all | solution.py:204
  40.2 1.6 copy-start.4
  43.2 31.2 %copy-start.21 = (f32[7,128,4]{1,2,0:T(4,128)S(1)}, f32[7,128,4]{1,2,0:T(4,128)}, u32[]{:S(2)}) copy-start(f32[7,128,4]{1,2,0:T(4,128)} %param.11) | copy-start | bytes 43012
  43.2 31.2 %copy-start.22 = (s32[7,128,4]{1,2,0:T(4,128)S(1)}, s32[7,128,4]{1,2,0:T(4,128)}, u32[]{:S(2)}) copy-start(s32[7,128,4]{1,2,0:T(4,128)} %param.10) | copy-start | bytes 43012
  65.5 28.7 %all-to-all-start = ((f32[4,8,32,256]{3,2,1,0:T(8,128)}), f32[4,8,32,256]{3,2,1,0:T(8,128)S(1)}, u32[]{:S(2)}, u32[]{:S(2)}) async-start(f32[4,8,32,256]{3,2,1,0:T(8,128)} %bitcast.105), calls=%async_computation | async-start | bytes 2097152 | tf_op jit(solution)/shard_map/all_to_all | solution.py:204
  70.0 36.9 %collective-permute-start.3 = (f32[7,32,256]{2,1,0:T(8,128)S(1)}, f32[7,32,256]{2,1,0:T(8,128)}, u32[]{:S(2)}, u32[]{:S(2)}) collective-permute-start(f32[7,32,256]{2,1,0:T(8,128)S(1)} %dynamic-slice_bitcast_fusion), channel_id=1, source_target_pairs={{4,0},{8,4},{12,8},{16,12},{20,16},{24,20},{28,24},{5,1},{9,5},{13... | collective-permute-start | bytes 688136 | tf_op jit(solution)/shard_map/ppermute | solution.py:212
  72.0 29.5 %collective-permute-start.2 = (f32[7,32,256]{2,1,0:T(8,128)S(1)}, f32[7,32,256]{2,1,0:T(8,128)}, u32[]{:S(2)}, u32[]{:S(2)}) collective-permute-start(f32[7,32,256]{2,1,0:T(8,128)S(1)} %dynamic-slice_bitcast_fusion), channel_id=1, source_target_pairs={{0,4},{4,8},{8,12},{12,16},{16,20},{20,24},{24,28},{1,5},{5,9},{9,... | collective-permute-start | bytes 688136 | tf_op jit(solution)/shard_map/ppermute | solution.py:211
  86.3 1.6 copy-start.5
  94.2 6.1 %copy-start.10 = (f32[4,8,32,256]{3,2,1,0:T(8,128)}, f32[4,8,32,256]{3,2,1,0:T(8,128)S(1)}, u32[]{:S(2)}) copy-start(f32[4,8,32,256]{3,2,1,0:T(8,128)S(1)} %all-to-all-done.own_ref) | copy-start | bytes 3145732
  94.2 42.6 %all-to-all-start.2 = ((f32[4,9,32,256]{3,2,1,0:T(8,128)}), f32[4,9,32,256]{3,2,1,0:T(8,128)}, u32[]{:S(2)}, u32[]{:S(2)}) async-start(f32[4,9,32,256]{3,2,1,0:T(8,128)} %bitcast.104), calls=%async_computation.2 | async-start | bytes 2359296 | tf_op jit(solution)/shard_map/all_to_all | solution.py:204
  100.3 7.7 %copy-start.20 = (f32[7,1,64,256]{3,2,1,0:T(8,128)S(1)}, f32[7,1,64,256]{3,2,1,0:T(8,128)}, u32[]{:S(2)}) copy-start(f32[7,1,64,256]{3,2,1,0:T(8,128)} %param.9) | copy-start | bytes 1376260
  102.6 23.0 %collective-permute-start.5 = (f32[4,8,32,256]{3,2,1,0:T(8,128)}, f32[4,8,32,256]{3,2,1,0:T(8,128)S(1)}, u32[]{:S(2)}, u32[]{:S(2)}) collective-permute-start(f32[4,8,32,256]{3,2,1,0:T(8,128)} %all-to-all-done.1.own_ref), channel_id=1, source_target_pairs={{4,0},{8,4},{12,8},{16,12},{20,16},{24,20},{28,24},{5,1},{9,5},{13... | collective-permute-start | bytes 3145736 | tf_op jit(solution)/shard_map/ppermute | solution.py:232
  104.6 25.6 %collective-permute-start.4 = (f32[4,8,32,256]{3,2,1,0:T(8,128)}, f32[4,8,32,256]{3,2,1,0:T(8,128)S(1)}, u32[]{:S(2)}, u32[]{:S(2)}) collective-permute-start(f32[4,8,32,256]{3,2,1,0:T(8,128)} %all-to-all-done.1.own_ref), channel_id=1, source_target_pairs={{0,4},{4,8},{8,12},{12,16},{16,20},{20,24},{24,28},{1,5},{5,9},{9,... | collective-permute-start | bytes 3145736 | tf_op jit(solution)/shard_map/ppermute | solution.py:231
  136.7 36.4 %all-to-all-start.5 = ((f32[4,8,32,256]{3,2,1,0:T(8,128)}), f32[4,8,32,256]{3,2,1,0:T(8,128)}, u32[]{:S(2)}, u32[]{:S(2)}) async-start(f32[4,8,32,256]{3,2,1,0:T(8,128)} %copy-done.14), calls=%async_computation.5 | async-start | bytes 2097152 | tf_op jit(solution)/shard_map/all_to_all | solution.py:236
  141.8 23.8 %collective-permute-start.7 = (f32[4,8,32,256]{3,2,1,0:T(8,128)}, f32[4,8,32,256]{3,2,1,0:T(8,128)}, u32[]{:S(2)}, u32[]{:S(2)}) collective-permute-start(f32[4,8,32,256]{3,2,1,0:T(8,128)} %copy-done.8), channel_id=1, source_target_pairs={{4,0},{8,4},{12,8},{16,12},{20,16},{24,20},{28,24},{5,1},{9,5},{13... | collective-permute-start | bytes 3145736 | tf_op jit(solution)/shard_map/ppermute | solution.py:232
  143.7 22.6 %collective-permute-start.6 = (f32[4,8,32,256]{3,2,1,0:T(8,128)}, f32[4,8,32,256]{3,2,1,0:T(8,128)}, u32[]{:S(2)}, u32[]{:S(2)}) collective-permute-start(f32[4,8,32,256]{3,2,1,0:T(8,128)} %copy-done.8), channel_id=1, source_target_pairs={{0,4},{4,8},{8,12},{12,16},{16,20},{20,24},{24,28},{1,5},{5,9},{9,... | collective-permute-start | bytes 3145736 | tf_op jit(solution)/shard_map/ppermute | solution.py:231
  146.3 20.0 %copy-start.9 = (f32[4,8,32,256]{3,2,1,0:T(8,128)S(1)}, f32[4,8,32,256]{3,2,1,0:T(8,128)}, u32[]{:S(2)}) copy-start(f32[4,8,32,256]{3,2,1,0:T(8,128)} %copy-done.8) | copy-start | bytes 3145732
  173.2 36.9 %all-to-all-start.6 = ((f32[4,8,32,256]{3,2,1,0:T(8,128)}), f32[4,8,32,256]{3,2,1,0:T(8,128)}, u32[]{:S(2)}, u32[]{:S(2)}) async-start(f32[4,8,32,256]{3,2,1,0:T(8,128)} %copy-done.17), calls=%async_computation.6 | async-start | bytes 2097152 | tf_op jit(solution)/shard_map/all_to_all | solution.py:236
  179.3 24.2 %collective-permute-start.9 = (f32[4,8,32,256]{3,2,1,0:T(8,128)S(1)}, f32[4,8,32,256]{3,2,1,0:T(8,128)S(1)}, u32[]{:S(2)}, u32[]{:S(2)}) collective-permute-start(f32[4,8,32,256]{3,2,1,0:T(8,128)S(1)} %slice.63), channel_id=1, source_target_pairs={{4,0},{8,4},{12,8},{16,12},{20,16},{24,20},{28,24},{5,1},{9,5},{13... | collective-permute-start | bytes 3145736 | tf_op jit(solution)/shard_map/ppermute | solution.py:232
  183.3 20.2 %collective-permute-start.8 = (f32[4,8,32,256]{3,2,1,0:T(8,128)S(1)}, f32[4,8,32,256]{3,2,1,0:T(8,128)S(1)}, u32[]{:S(2)}, u32[]{:S(2)}) collective-permute-start(f32[4,8,32,256]{3,2,1,0:T(8,128)S(1)} %slice.63), channel_id=1, source_target_pairs={{0,4},{4,8},{8,12},{12,16},{16,20},{20,24},{24,28},{1,5},{5,9},{9,... | collective-permute-start | bytes 3145736 | tf_op jit(solution)/shard_map/ppermute | solution.py:231
  210.1 35.3 %all-to-all-start.7 = ((f32[4,8,32,256]{3,2,1,0:T(8,128)}), f32[4,8,32,256]{3,2,1,0:T(8,128)}, u32[]{:S(2)}, u32[]{:S(2)}) async-start(f32[4,8,32,256]{3,2,1,0:T(8,128)} %copy-done.16), calls=%async_computation.7 | async-start | bytes 2097152 | tf_op jit(solution)/shard_map/all_to_all | solution.py:236
  214.7 23.2 %collective-permute-start.1 = (f32[4,8,32,256]{3,2,1,0:T(8,128)}, f32[4,8,32,256]{3,2,1,0:T(8,128)S(1)}, u32[]{:S(2)}, u32[]{:S(2)}) collective-permute-start(f32[4,8,32,256]{3,2,1,0:T(8,128)} %copy-done.10), channel_id=1, source_target_pairs={{4,0},{8,4},{12,8},{16,12},{20,16},{24,20},{28,24},{5,1},{9,5},{13... | collective-permute-start | bytes 3145736 | tf_op jit(solution)/shard_map/ppermute | solution.py:232
  219.1 18.8 %collective-permute-start = (f32[4,8,32,256]{3,2,1,0:T(8,128)}, f32[4,8,32,256]{3,2,1,0:T(8,128)S(1)}, u32[]{:S(2)}, u32[]{:S(2)}) collective-permute-start(f32[4,8,32,256]{3,2,1,0:T(8,128)} %copy-done.10), channel_id=1, source_target_pairs={{0,4},{4,8},{8,12},{12,16},{16,20},{20,24},{24,28},{1,5},{5,9},{9,... | collective-permute-start | bytes 3145736 | tf_op jit(solution)/shard_map/ppermute | solution.py:231
  245.5 30.2 %all-to-all-start.3 = ((f32[4,8,32,256]{3,2,1,0:T(8,128)}), f32[4,8,32,256]{3,2,1,0:T(8,128)S(1)}, u32[]{:S(2)}, u32[]{:S(2)}) async-start(f32[4,8,32,256]{3,2,1,0:T(8,128)} %copy-done.15), calls=%async_computation.3 | async-start | bytes 2097152 | tf_op jit(solution)/shard_map/all_to_all | solution.py:236
  250.0 1.6 copy-start.6
  275.7 1.6 copy-start.7
  (9 other events, 9.2 us)

commit v2 on v1

--- a/solution.py
+++ b/solution.py
@@ -9,6 +9,7 @@
 
 CHUNK_ROWS = 8
 VMEM_LIMIT = 48 * 1024 * 1024
+ANYWHERE = pl.BlockSpec(memory_space=pl.ANY)
 
 
 def params():
@@ -46,7 +47,7 @@
         out_ref[:, 0, rows:] = refs[0][:, 0]
 
 
-def pack(state, adjoint, edges, chunk, rows, halves):
+def pack(state, adjoint, edges, chunk, rows, halves, earlier):
     modes, height, width = state.shape
     per_half = height // halves // rows
     block = pl.BlockSpec((modes, rows, width), lambda h: (0, h * per_half + chunk, 0))
@@ -56,6 +57,8 @@
     if edge_rows:
         in_specs.append(pl.BlockSpec((2, 1, edge_rows, modes, width), lambda h: (0, h, 0, 0, 0)))
         operands.append(edges)
+    in_specs += [ANYWHERE] * len(earlier)
+    operands += earlier
     total = rows + edge_rows
     return pl.pallas_call(
         functools.partial(pack_kernel, edge_rows),
@@ -82,7 +85,8 @@
     return jnp.stack(pairs, 1)
 
 
-def operator_kernel(rows, terms, modes, own_ref, before_ref, after_ref, below_ref, above_ref, face_ref, matrix_ref, out_ref, high, low):
+def operator_kernel(rows, terms, modes, own_ref, before_ref, after_ref, below_ref, above_ref, face_ref, matrix_ref, *refs):
+    out_ref, high, low = refs[-3:]
     sources, _, part, width = own_ref.shape
     lanes = lax.broadcasted_iota(jnp.int32, (part, width), 1)
     step = 16
@@ -117,7 +121,7 @@
             out_ref[source, row] = mixed[source * part : (source + 1) * part]
 
 
-def apply_operator(own, before, after, below, above, faces, matrix, chunk, rows):
+def apply_operator(own, before, after, below, above, faces, matrix, chunk, rows, earlier):
     sources, _, part, width = own.shape
     modes = sources * part
     terms = matrix.shape[1] // modes
@@ -138,7 +142,8 @@
             block,
             pl.BlockSpec((rows, 6 * terms, width), lambda i: (chunk, 0, 0)),
             whole(matrix),
-        ],
+        ]
+        + [ANYWHERE] * len(earlier),
         out_specs=block,
         out_shape=jax.ShapeDtypeStruct((sources, rows, part, width), jnp.float32),
         scratch_shapes=[
@@ -147,7 +152,7 @@
         ],
         compiler_params=params(),
         name="operator",
-    )(own, before, after, below, above, faces, matrix)
+    )(own, before, after, below, above, faces, matrix, *earlier)
 
 
 def finish_kernel(mixed_ref, state_ref, control_ref, adjoint_ref, *refs):
@@ -196,13 +201,6 @@
     backward = [(i + 1, i) for i in range(planes - 1)]
     half = lax.rem(lax.axis_index("mode"), halves)
 
-    edges = edge_rows_of(state, adjoint, halves)
-    fields = []
-    for chunk in range(chunks):
-        packed = pack(state, adjoint, edges if chunk == 0 else None, chunk, rows, halves)
-        packed = packed.reshape((owners,) + packed.shape[2:])
-        fields.append(lax.all_to_all(packed, "mode", 0, 0, tiled=True))
-
     matrix = coupling_matrices(pattern, weights)
     own = coefficient[:, 0]
     mine = lax.dynamic_slice_in_dim(own, half * half_rows, half_rows, 1)
@@ -214,6 +212,16 @@
         half_rows,
     )
 
+    edges = edge_rows_of(state, adjoint, halves)
+    fields, halos = [], []
+    for chunk in range(chunks):
+        earlier = list(halos[chunk - 2]) if chunk >= 2 else []
+        packed = pack(state, adjoint, edges if chunk == 0 else None, chunk, rows, halves, earlier)
+        packed = packed.reshape((owners,) + packed.shape[2:])
+        fields.append(lax.all_to_all(packed, "mode", 0, 0, tiled=True))
+        body = fields[chunk][:, :rows]
+        halos.append((lax.ppermute(body, "space", forward), lax.ppermute(body, "space", backward)))
+
     nothing = jnp.zeros((owners, 1, modes, width), jnp.float32)
     first = last = nothing
     if halves == 2:
@@ -227,12 +235,11 @@
     outputs = None
     for chunk in range(chunks):
         block = fields[chunk]
-        body = block[:, :rows]
-        below = lax.ppermute(body, "space", forward)
-        above = lax.ppermute(body, "space", backward)
+        below, above = halos[chunk]
         before = fields[chunk - 1][:, rows - 1 : rows] if chunk else first
         after = fields[chunk + 1][:, :1] if chunk < chunks - 1 else last
-        mixed = apply_operator(block, before, after, below, above, faces, matrix, chunk, rows)
+        earlier = list(halos[chunk + 2]) if chunk + 2 < chunks else []
+        mixed = apply_operator(block, before, after, below, above, faces, matrix, chunk, rows, earlier)
         mixed = lax.all_to_all(mixed, "mode", 0, 0, tiled=True)
         outputs = finish(mixed, state, control, adjoint, outputs, chunk, rows, halves)
     return tuple(out.reshape(shape) for out in outputs)

time: 283 us -> 281 us (level)
  waiting for transfers between devices: 137 us -> 128 us
  local copies, waits for them, and re-layouts: 35.4 us -> 43.3 us
    all_to_all x4, waiting for transfers between devices: 17.2 us -> 51.4 us  [shards(): mixed = lax.all_to_all(mixed, 'mode', 0, 0, tiled=True)]
    ppermute x8, waiting for transfers between devices: 69.6 us -> 43.1 us  [the longest x4 34.9 us: shards(): lax.ppermute(body, 'space', backward)]
    all_to_all x4, waiting for transfers between devices: 49.8 us -> 33.8 us  [shards(): fields.append(lax.all_to_all(packed, 'mode', 0, 0, tiled=True))]
    unnamed x46 -> x60, local copies, waits for them, and re-layouts: 20.2 us -> 27.2 us
    ppermute x8, starting transfers between devices: 22.3 us -> 19.4 us  [the longest x4 11 us: shards(): lax.ppermute(body, 'space', forward)]
  transfers between devices with their start and end apart: 18 -> 18, of which waited for: 10 -> 10; matrix products, arithmetic and copies ran while one was open for 9% -> 9% of each run, Pallas kernels for 11% -> 10%
where the time goes in v2:
time: 281 us; the launch traced here: 279 us
  waiting for transfers between devices  128 us (46%)
  starting transfers between devices  61.6 us (22%)
  local copies, waits for them, and re-layouts  43.3 us (15%)
  Pallas kernels  35.6 us (13%)
  other arithmetic  9.26 us (3%)
    all_to_all x4, waiting for transfers between devices, shards(): mixed = lax.all_to_all(mixed, 'mode', 0, 0, tiled=True)  51.4 us
    ppermute x4, waiting for transfers between devices, shards(): lax.ppermute(body, 'space', backward)  34.9 us
    all_to_all x4, waiting for transfers between devices, shards(): fields.append(lax.all_to_all(packed, 'mode', 0, 0, tiled=True))  33.8 us
    unnamed x60, local copies, waits for them, and re-layouts  27.2 us
    pallas_call x4, Pallas kernels, apply_operator(): pl.pallas_call(functools.partial(operator_kernel, rows, terms, modes), gr...  23.1 us
    all_to_all x4, starting transfers between devices, shards(): fields.append(lax.all_to_all(packed, 'mode', 0, 0, tiled=True))  19.4 us
    all_to_all x4, starting transfers between devices, shards(): mixed = lax.all_to_all(mixed, 'mode', 0, 0, tiled=True)  16.8 us
    ppermute x4, starting transfers between devices, shards(): lax.ppermute(body, 'space', forward)  11 us
  transfers between devices with their start and end apart: 18, of which 10 were waited for; matrix products, arithmetic and copies ran while one was open for 9% of the time, Pallas kernels for 10%

profile of v2, /device:TPU:4, one launch (start us, length us, event | category | flops | bytes accessed | tf_op | source)
XLA Modules:
  0.0 279.2 jit_solution(3175658543867663224)
XLA Ops:
  5.2 5.0 %all-to-all-start = ((f32[4,8,32,256]{3,2,1,0:T(8,128)}), f32[4,8,32,256]{3,2,1,0:T(8,128)S(1)}, u32[]{:S(2)}, u32[]{:S(2)}) async-start(f32[4,8,32,256]{3,2,1,0:T(8,128)} %bitcast.107), calls=%async_computation | async-start | bytes 2097152 | tf_op jit(solution)/shard_map/all_to_all | solution.py:221
  10.2 4.0 %copy_bitcast_fusion = (f32[1,32,64,256]{3,1,0,2:T(8,128)S(1)}, f32[1,32,64,256]{3,1,0,2:T(8,128)S(1)}) fusion(f32[32,1,64,256]{3,2,1,0:T(8,128)} %param.8, f32[32,1,64,256]{3,2,1,0:T(8,128)S(1)} %copy-done.1), kind=kLoop, calls=%fused_computation | loop fusion | bytes 8388608 | tf_op jit(solution)/shard_map/stack;reshape | solution.py:77
  17.3 18.7 %all-to-all-done.own_ref = f32[4,8,32,256]{3,2,1,0:T(8,128)S(1)} async-done(((f32[4,8,32,256]{3,2,1,0:T(8,128)}), f32[4,8,32,256]{3,2,1,0:T(8,128)S(1)}, u32[]{:S(2)}, u32[]{:S(2)}) %all-to-all-start) | async-done | bytes 1048608 | tf_op jit(solution)/shard_map/all_to_all | solution.py:221
  35.9 4.3 %all-to-all-start.2 = ((f32[4,9,32,256]{3,2,1,0:T(8,128)}), f32[4,9,32,256]{3,2,1,0:T(8,128)}, u32[]{:S(2)}, u32[]{:S(2)}) async-start(f32[4,9,32,256]{3,2,1,0:T(8,128)} %bitcast.104), calls=%async_computation.2 | async-start | bytes 2359296 | tf_op jit(solution)/shard_map/all_to_all | solution.py:221
  42.3 2.3 collective-permute-start
  44.6 18.4 %collective-permute-done.1.refs_1_.above_ref = f32[4,8,32,256]{3,2,1,0:T(8,128)S(1)} collective-permute-done((f32[4,8,32,256]{3,2,1,0:T(8,128)S(1)}, f32[4,8,32,256]{3,2,1,0:T(8,128)S(1)}, u32[]{:S(2)}, u32[]{:S(2)}) %collective-permute-start.1) | collective-permute-done | bytes 1048608 | tf_op jit(solution)/shard_map/ppermute | solution.py:223
  63.0 4.6 %collective-permute-done.refs_0_.below_ref = f32[4,8,32,256]{3,2,1,0:T(8,128)S(1)} collective-permute-done((f32[4,8,32,256]{3,2,1,0:T(8,128)S(1)}, f32[4,8,32,256]{3,2,1,0:T(8,128)S(1)}, u32[]{:S(2)}, u32[]{:S(2)}) %collective-permute-start) | collective-permute-done | bytes 1048608 | tf_op jit(solution)/shard_map/ppermute | solution.py:223
  71.9 5.2 %all-to-all-start.1 = ((f32[4,8,32,256]{3,2,1,0:T(8,128)}), f32[4,8,32,256]{3,2,1,0:T(8,128)}, u32[]{:S(2)}, u32[]{:S(2)}) async-start(f32[4,8,32,256]{3,2,1,0:T(8,128)} %bitcast.106), calls=%async_computation.1 | async-start | bytes 2097152 | tf_op jit(solution)/shard_map/all_to_all | solution.py:221
  77.1 2.3 slice.56
  81.3 2.4 collective-permute-start.2
  84.7 4.1 %collective-permute-start.7 = (f32[7,32,256]{2,1,0:T(8,128)S(1)}, f32[7,32,256]{2,1,0:T(8,128)}, u32[]{:S(2)}, u32[]{:S(2)}) collective-permute-start(f32[7,32,256]{2,1,0:T(8,128)S(1)} %dynamic-slice_bitcast_fusion), channel_id=1, source_target_pairs={{4,0},{8,4},{12,8},{16,12},{20,16},{24,20},{28,24},{5,1},{9,5},{13... | collective-permute-start | bytes 688136 | tf_op jit(solution)/shard_map/ppermute | solution.py:210
  98.7 4.4 %collective-permute-done.3.refs_1_.above_ref = f32[4,8,32,256]{3,2,1,0:T(8,128)S(1)} collective-permute-done((f32[4,8,32,256]{3,2,1,0:T(8,128)}, f32[4,8,32,256]{3,2,1,0:T(8,128)S(1)}, u32[]{:S(2)}, u32[]{:S(2)}) %collective-permute-start.3) | collective-permute-done | bytes 1048608 | tf_op jit(solution)/shard_map/ppermute | solution.py:223
  103.2 3.6 %collective-permute-done.2.refs_0_.below_ref = f32[4,8,32,256]{3,2,1,0:T(8,128)} collective-permute-done((f32[4,8,32,256]{3,2,1,0:T(8,128)}, f32[4,8,32,256]{3,2,1,0:T(8,128)}, u32[]{:S(2)}, u32[]{:S(2)}) %collective-permute-start.2) | collective-permute-done | bytes 1048608 | tf_op jit(solution)/shard_map/ppermute | solution.py:223
  109.0 4.9 %all-to-all-start.3 = ((f32[4,8,32,256]{3,2,1,0:T(8,128)}), f32[4,8,32,256]{3,2,1,0:T(8,128)}, u32[]{:S(2)}, u32[]{:S(2)}) async-start(f32[4,8,32,256]{3,2,1,0:T(8,128)} %bitcast.105), calls=%async_computation.3 | async-start | bytes 2097152 | tf_op jit(solution)/shard_map/all_to_all | solution.py:221
  119.8 2.4 collective-permute-start.4
  125.6 15.2 %all-to-all-done.3.own_ref = f32[4,8,32,256]{3,2,1,0:T(8,128)} async-done(((f32[4,8,32,256]{3,2,1,0:T(8,128)}), f32[4,8,32,256]{3,2,1,0:T(8,128)}, u32[]{:S(2)}, u32[]{:S(2)}) %all-to-all-start.3) | async-done | bytes 1048608 | tf_op jit(solution)/shard_map/all_to_all | solution.py:221
  145.5 5.3 %operator.6 = f32[4,8,32,256]{3,2,1,0:T(8,128)S(1)} custom-call(f32[4,8,32,256]{3,2,1,0:T(8,128)S(1)} %copy-done.7, f32[4,1,32,256]{3,2,1,0:T(8,128)S(1)} %get-tuple-element.39.before_ref, f32[4,1,32,256]{3,2,1,0:T(8,128)S(1)} %get-tuple-element.43.after_ref, f32[4,8,32,256]{3,2,1,0:T(8,128)S(1)} %copy-done.24, f32[4,8,32,256]{3,2,1,0:T(8,128)S(1)} %copy-done.22, ...), custom_call_target="tpu_custom_call" | custom-call | tf_op jit(solution)/shard_map/operator/pallas_call | solution.py:134
  151.8 4.2 %all-to-all-start.6 = ((f32[4,8,32,256]{3,2,1,0:T(8,128)}), f32[4,8,32,256]{3,2,1,0:T(8,128)}, u32[]{:S(2)}, u32[]{:S(2)}) async-start(f32[4,8,32,256]{3,2,1,0:T(8,128)} %copy-done.25), calls=%async_computation.6 | async-start | bytes 2097152 | tf_op jit(solution)/shard_map/all_to_all | solution.py:243
  156.0 2.6 collective-permute-start.9
  158.6 3.8 %collective-permute-start.8 = (f32[4,8,32,256]{3,2,1,0:T(8,128)}, f32[4,8,32,256]{3,2,1,0:T(8,128)S(1)}, u32[]{:S(2)}, u32[]{:S(2)}) collective-permute-start(f32[4,8,32,256]{3,2,1,0:T(8,128)} %all-to-all-done.3.own_ref), channel_id=1, source_target_pairs={{0,4},{4,8},{8,12},{12,16},{16,20},{20,24},{24,28},{1,5},{5,9},{9,... | collective-permute-start | bytes 3145736 | tf_op jit(solution)/shard_map/ppermute | solution.py:223
  164.3 12.1 %collective-permute-done.9.above_ref.refs_1_ = f32[4,8,32,256]{3,2,1,0:T(8,128)S(1)} collective-permute-done((f32[4,8,32,256]{3,2,1,0:T(8,128)}, f32[4,8,32,256]{3,2,1,0:T(8,128)S(1)}, u32[]{:S(2)}, u32[]{:S(2)}) %collective-permute-start.9) | collective-permute-done | bytes 1048608 | tf_op jit(solution)/shard_map/ppermute | solution.py:223
  176.5 5.6 %operator.5 = f32[4,8,32,256]{3,2,1,0:T(8,128)S(1)} custom-call(f32[4,8,32,256]{3,2,1,0:T(8,128)} %all-to-all-done.3.own_ref, f32[4,1,32,256]{3,2,1,0:T(8,128)S(1)} %get-tuple-element.42.before_ref, f32[4,1,32,256]{3,2,1,0:T(8,128)S(1)} %slice.60.after_ref, f32[4,8,32,256]{3,2,1,0:T(8,128)S(1)} %collective-permute-done.8.below_ref.refs_0_, ...), custom_call_target="tpu_custom_call" | custom-call | tf_op jit(solution)/shard_map/operator/pallas_call | solution.py:134
  185.1 4.5 %all-to-all-start.5 = ((f32[4,8,32,256]{3,2,1,0:T(8,128)}), f32[4,8,32,256]{3,2,1,0:T(8,128)}, u32[]{:S(2)}, u32[]{:S(2)}) async-start(f32[4,8,32,256]{3,2,1,0:T(8,128)} %copy-done.19), calls=%async_computation.5 | async-start | bytes 2097152 | tf_op jit(solution)/shard_map/all_to_all | solution.py:243
  193.3 5.9 %operator.7 = f32[4,8,32,256]{3,2,1,0:T(8,128)S(1)} custom-call(f32[4,9,32,256]{3,2,1,0:T(8,128)} %all-to-all-done.2.own_ref, f32[4,1,32,256]{3,2,1,0:T(8,128)S(1)} %get-tuple-element.38.before_ref, f32[4,1,32,256]{3,2,1,0:T(8,128)S(1)} %get-tuple-element.41.after_ref, f32[4,8,32,256]{3,2,1,0:T(8,128)} %collective-permute-done.2.refs_0_.below_ref, ...), custom_call_target="tpu_custom_call" | custom-call | tf_op jit(solution)/shard_map/operator/pallas_call | solution.py:134
  200.2 14.3 %all-to-all-done.5 = f32[4,8,32,256]{3,2,1,0:T(8,128)} async-done(((f32[4,8,32,256]{3,2,1,0:T(8,128)}), f32[4,8,32,256]{3,2,1,0:T(8,128)}, u32[]{:S(2)}, u32[]{:S(2)}) %all-to-all-start.5) | async-done | bytes 1048608 | tf_op jit(solution)/shard_map/all_to_all | solution.py:243
  214.5 4.5 %all-to-all-start.7 = ((f32[4,8,32,256]{3,2,1,0:T(8,128)}), f32[4,8,32,256]{3,2,1,0:T(8,128)}, u32[]{:S(2)}, u32[]{:S(2)}) async-start(f32[4,8,32,256]{3,2,1,0:T(8,128)} %copy-done.18), calls=%async_computation.7 | async-start | bytes 2097152 | tf_op jit(solution)/shard_map/all_to_all | solution.py:243
  219.0 6.3 %operator.4 = f32[4,8,32,256]{3,2,1,0:T(8,128)S(1)} custom-call(f32[4,8,32,256]{3,2,1,0:T(8,128)} %all-to-all-done.1.own_ref, f32[4,1,32,256]{3,2,1,0:T(8,128)S(1)} %get-tuple-element.44.before_ref, f32[4,1,32,256]{3,2,1,0:T(8,128)S(1)} %get-tuple-element.40.after_ref, f32[4,8,32,256]{3,2,1,0:T(8,128)} %collective-permute-done.4.below_ref.refs_0_, ...), custom_call_target="tpu_custom_call" | custom-call | tf_op jit(solution)/shard_map/operator/pallas_call | solution.py:134
  226.3 18.7 %all-to-all-done.7 = f32[4,8,32,256]{3,2,1,0:T(8,128)} async-done(((f32[4,8,32,256]{3,2,1,0:T(8,128)}), f32[4,8,32,256]{3,2,1,0:T(8,128)}, u32[]{:S(2)}, u32[]{:S(2)}) %all-to-all-start.7) | async-done | bytes 1048608 | tf_op jit(solution)/shard_map/all_to_all | solution.py:243
  244.9 3.5 %all-to-all-start.4 = ((f32[4,8,32,256]{3,2,1,0:T(8,128)}), f32[4,8,32,256]{3,2,1,0:T(8,128)S(1)}, u32[]{:S(2)}, u32[]{:S(2)}) async-start(f32[4,8,32,256]{3,2,1,0:T(8,128)} %copy-done.17), calls=%async_computation.4 | async-start | bytes 2097152 | tf_op jit(solution)/shard_map/all_to_all | solution.py:243
  252.3 2.3 finish.5
  254.6 2.3 finish.6
  256.9 18.5 %all-to-all-done.4 = f32[4,8,32,256]{3,2,1,0:T(8,128)S(1)} async-done(((f32[4,8,32,256]{3,2,1,0:T(8,128)}), f32[4,8,32,256]{3,2,1,0:T(8,128)S(1)}, u32[]{:S(2)}, u32[]{:S(2)}) %all-to-all-start.4) | async-done | bytes 1048608 | tf_op jit(solution)/shard_map/all_to_all | solution.py:243
  (98 shorter events, 61.9 us)
Async XLA Ops:
  0.6 1.6 copy-start
  2.2 1.6 copy-start.2
  5.2 5.0 %copy-start.1 = (f32[32,1,64,256]{3,2,1,0:T(8,128)S(1)}, f32[32,1,64,256]{3,2,1,0:T(8,128)}, u32[]{:S(2)}) copy-start(f32[32,1,64,256]{3,2,1,0:T(8,128)} %param.6) | copy-start | bytes 6291460
  5.2 30.7 %all-to-all-start = ((f32[4,8,32,256]{3,2,1,0:T(8,128)}), f32[4,8,32,256]{3,2,1,0:T(8,128)S(1)}, u32[]{:S(2)}, u32[]{:S(2)}) async-start(f32[4,8,32,256]{3,2,1,0:T(8,128)} %bitcast.107), calls=%async_computation | async-start | bytes 2097152 | tf_op jit(solution)/shard_map/all_to_all | solution.py:221
  14.2 1.6 copy-start.3
  35.9 32.9 %copy-start.6 = (f32[4,8,32,256]{3,2,1,0:T(8,128)}, f32[4,8,32,256]{3,2,1,0:T(8,128)S(1)}, u32[]{:S(2)}) copy-start(f32[4,8,32,256]{3,2,1,0:T(8,128)S(1)} %all-to-all-done.own_ref) | copy-start | bytes 3145732
  35.9 36.0 %all-to-all-start.2 = ((f32[4,9,32,256]{3,2,1,0:T(8,128)}), f32[4,9,32,256]{3,2,1,0:T(8,128)}, u32[]{:S(2)}, u32[]{:S(2)}) async-start(f32[4,9,32,256]{3,2,1,0:T(8,128)} %bitcast.104), calls=%async_computation.2 | async-start | bytes 2359296 | tf_op jit(solution)/shard_map/all_to_all | solution.py:221
  40.2 22.7 %collective-permute-start.1 = (f32[4,8,32,256]{3,2,1,0:T(8,128)S(1)}, f32[4,8,32,256]{3,2,1,0:T(8,128)S(1)}, u32[]{:S(2)}, u32[]{:S(2)}) collective-permute-start(f32[4,8,32,256]{3,2,1,0:T(8,128)S(1)} %all-to-all-done.own_ref), channel_id=1, source_target_pairs={{4,0},{8,4},{12,8},{16,12},{20,16},{24,20},{28,24},{5,1},{9,5},{13... | collective-permute-start | bytes 3145736 | tf_op jit(solution)/shard_map/ppermute | solution.py:223
  42.3 25.3 %collective-permute-start = (f32[4,8,32,256]{3,2,1,0:T(8,128)S(1)}, f32[4,8,32,256]{3,2,1,0:T(8,128)S(1)}, u32[]{:S(2)}, u32[]{:S(2)}) collective-permute-start(f32[4,8,32,256]{3,2,1,0:T(8,128)S(1)} %all-to-all-done.own_ref), channel_id=1, source_target_pairs={{0,4},{4,8},{8,12},{12,16},{16,20},{20,24},{24,28},{1,5},{5,9},{9,... | collective-permute-start | bytes 3145736 | tf_op jit(solution)/shard_map/ppermute | solution.py:223
  71.9 18.8 %copy-start.28 = (f32[7,128,4]{1,2,0:T(4,128)S(1)}, f32[7,128,4]{1,2,0:T(4,128)}, u32[]{:S(2)}) copy-start(f32[7,128,4]{1,2,0:T(4,128)} %param.11) | copy-start | bytes 43012
  71.9 18.8 %copy-start.29 = (s32[7,128,4]{1,2,0:T(4,128)S(1)}, s32[7,128,4]{1,2,0:T(4,128)}, u32[]{:S(2)}) copy-start(s32[7,128,4]{1,2,0:T(4,128)} %param.10) | copy-start | bytes 43012
  71.9 37.1 %all-to-all-start.1 = ((f32[4,8,32,256]{3,2,1,0:T(8,128)}), f32[4,8,32,256]{3,2,1,0:T(8,128)}, u32[]{:S(2)}, u32[]{:S(2)}) async-start(f32[4,8,32,256]{3,2,1,0:T(8,128)} %bitcast.106), calls=%async_computation.1 | async-start | bytes 2097152 | tf_op jit(solution)/shard_map/all_to_all | solution.py:221
  79.4 23.8 %collective-permute-start.3 = (f32[4,8,32,256]{3,2,1,0:T(8,128)}, f32[4,8,32,256]{3,2,1,0:T(8,128)S(1)}, u32[]{:S(2)}, u32[]{:S(2)}) collective-permute-start(f32[4,8,32,256]{3,2,1,0:T(8,128)} %slice.56), channel_id=1, source_target_pairs={{4,0},{8,4},{12,8},{16,12},{20,16},{24,20},{28,24},{5,1},{9,5},{13... | collective-permute-start | bytes 3145736 | tf_op jit(solution)/shard_map/ppermute | solution.py:223
  81.3 25.4 %collective-permute-start.2 = (f32[4,8,32,256]{3,2,1,0:T(8,128)}, f32[4,8,32,256]{3,2,1,0:T(8,128)}, u32[]{:S(2)}, u32[]{:S(2)}) collective-permute-start(f32[4,8,32,256]{3,2,1,0:T(8,128)} %slice.56), channel_id=1, source_target_pairs={{0,4},{4,8},{8,12},{12,16},{16,20},{20,24},{24,28},{1,5},{5,9},{9,... | collective-permute-start | bytes 3145736 | tf_op jit(solution)/shard_map/ppermute | solution.py:223
  84.7 32.2 %collective-permute-start.7 = (f32[7,32,256]{2,1,0:T(8,128)S(1)}, f32[7,32,256]{2,1,0:T(8,128)}, u32[]{:S(2)}, u32[]{:S(2)}) collective-permute-start(f32[7,32,256]{2,1,0:T(8,128)S(1)} %dynamic-slice_bitcast_fusion), channel_id=1, source_target_pairs={{4,0},{8,4},{12,8},{16,12},{20,16},{24,20},{28,24},{5,1},{9,5},{13... | collective-permute-start | bytes 688136 | tf_op jit(solution)/shard_map/ppermute | solution.py:210
  88.8 27.1 %collective-permute-start.6 = (f32[7,32,256]{2,1,0:T(8,128)S(1)}, f32[7,32,256]{2,1,0:T(8,128)}, u32[]{:S(2)}, u32[]{:S(2)}) collective-permute-start(f32[7,32,256]{2,1,0:T(8,128)S(1)} %dynamic-slice_bitcast_fusion), channel_id=1, source_target_pairs={{0,4},{4,8},{8,12},{12,16},{16,20},{20,24},{24,28},{1,5},{5,9},{9,... | collective-permute-start | bytes 688136 | tf_op jit(solution)/shard_map/ppermute | solution.py:209
  103.2 4.9 %copy-start.9 = (f32[4,8,32,256]{3,2,1,0:T(8,128)}, f32[4,8,32,256]{3,2,1,0:T(8,128)S(1)}, u32[]{:S(2)}) copy-start(f32[4,8,32,256]{3,2,1,0:T(8,128)S(1)} %collective-permute-done.3.refs_1_.above_ref) | copy-start | bytes 3145732
  109.0 5.0 %copy-start.27 = (f32[128,896]{1,0:T(8,128)S(1)}, f32[128,896]{1,0:T(8,128)}, u32[]{:S(2)}) copy-start(f32[128,896]{1,0:T(8,128)} %copy.55) | copy-start | bytes 1376260
  109.0 6.9 %copy-start.26 = (f32[7,1,64,256]{3,2,1,0:T(8,128)S(1)}, f32[7,1,64,256]{3,2,1,0:T(8,128)}, u32[]{:S(2)}) copy-start(f32[7,1,64,256]{3,2,1,0:T(8,128)} %param.9) | copy-start | bytes 1376260
  109.0 31.8 %all-to-all-start.3 = ((f32[4,8,32,256]{3,2,1,0:T(8,128)}), f32[4,8,32,256]{3,2,1,0:T(8,128)}, u32[]{:S(2)}, u32[]{:S(2)}) async-start(f32[4,8,32,256]{3,2,1,0:T(8,128)} %bitcast.105), calls=%async_computation.3 | async-start | bytes 2097152 | tf_op jit(solution)/shard_map/all_to_all | solution.py:221
  117.9 23.8 %collective-permute-start.5 = (f32[4,8,32,256]{3,2,1,0:T(8,128)}, f32[4,8,32,256]{3,2,1,0:T(8,128)}, u32[]{:S(2)}, u32[]{:S(2)}) collective-permute-start(f32[4,8,32,256]{3,2,1,0:T(8,128)} %all-to-all-done.1.own_ref), channel_id=1, source_target_pairs={{4,0},{8,4},{12,8},{16,12},{20,16},{24,20},{28,24},{5,1},{9,5},{13... | collective-permute-start | bytes 3145736 | tf_op jit(solution)/shard_map/ppermute | solution.py:223
  119.8 21.9 %collective-permute-start.4 = (f32[4,8,32,256]{3,2,1,0:T(8,128)}, f32[4,8,32,256]{3,2,1,0:T(8,128)}, u32[]{:S(2)}, u32[]{:S(2)}) collective-permute-start(f32[4,8,32,256]{3,2,1,0:T(8,128)} %all-to-all-done.1.own_ref), channel_id=1, source_target_pairs={{0,4},{4,8},{8,12},{12,16},{16,20},{20,24},{24,28},{1,5},{5,9},{9,... | collective-permute-start | bytes 3145736 | tf_op jit(solution)/shard_map/ppermute | solution.py:223
  141.8 1.2 copy-start.7
  143.0 1.2 copy-start.22
  151.8 33.3 %all-to-all-start.6 = ((f32[4,8,32,256]{3,2,1,0:T(8,128)}), f32[4,8,32,256]{3,2,1,0:T(8,128)}, u32[]{:S(2)}, u32[]{:S(2)}) async-start(f32[4,8,32,256]{3,2,1,0:T(8,128)} %copy-done.25), calls=%async_computation.6 | async-start | bytes 2097152 | tf_op jit(solution)/shard_map/all_to_all | solution.py:243
  156.0 20.5 %collective-permute-start.9 = (f32[4,8,32,256]{3,2,1,0:T(8,128)}, f32[4,8,32,256]{3,2,1,0:T(8,128)S(1)}, u32[]{:S(2)}, u32[]{:S(2)}) collective-permute-start(f32[4,8,32,256]{3,2,1,0:T(8,128)} %all-to-all-done.3.own_ref), channel_id=1, source_target_pairs={{4,0},{8,4},{12,8},{16,12},{20,16},{24,20},{28,24},{5,1},{9,5},{13... | collective-permute-start | bytes 3145736 | tf_op jit(solution)/shard_map/ppermute | solution.py:223
  158.6 17.9 %collective-permute-start.8 = (f32[4,8,32,256]{3,2,1,0:T(8,128)}, f32[4,8,32,256]{3,2,1,0:T(8,128)S(1)}, u32[]{:S(2)}, u32[]{:S(2)}) collective-permute-start(f32[4,8,32,256]{3,2,1,0:T(8,128)} %all-to-all-done.3.own_ref), channel_id=1, source_target_pairs={{0,4},{4,8},{8,12},{12,16},{16,20},{20,24},{24,28},{1,5},{5,9},{9,... | collective-permute-start | bytes 3145736 | tf_op jit(solution)/shard_map/ppermute | solution.py:223
  185.1 29.4 %all-to-all-start.5 = ((f32[4,8,32,256]{3,2,1,0:T(8,128)}), f32[4,8,32,256]{3,2,1,0:T(8,128)}, u32[]{:S(2)}, u32[]{:S(2)}) async-start(f32[4,8,32,256]{3,2,1,0:T(8,128)} %copy-done.19), calls=%async_computation.5 | async-start | bytes 2097152 | tf_op jit(solution)/shard_map/all_to_all | solution.py:243
  214.5 30.4 %all-to-all-start.7 = ((f32[4,8,32,256]{3,2,1,0:T(8,128)}), f32[4,8,32,256]{3,2,1,0:T(8,128)}, u32[]{:S(2)}, u32[]{:S(2)}) async-start(f32[4,8,32,256]{3,2,1,0:T(8,128)} %copy-done.18), calls=%async_computation.7 | async-start | bytes 2097152 | tf_op jit(solution)/shard_map/all_to_all | solution.py:243
  244.9 30.5 %all-to-all-start.4 = ((f32[4,8,32,256]{3,2,1,0:T(8,128)}), f32[4,8,32,256]{3,2,1,0:T(8,128)S(1)}, u32[]{:S(2)}, u32[]{:S(2)}) async-start(f32[4,8,32,256]{3,2,1,0:T(8,128)} %copy-done.17), calls=%async_computation.4 | async-start | bytes 2097152 | tf_op jit(solution)/shard_map/all_to_all | solution.py:243
  248.4 1.6 copy-start.4
  275.4 1.6 copy-start.5
  (16 other events, 16.9 us)

commit v3 on v1

v3 whole, which is shorter than its diff:
```python
import functools

import jax
import jax.numpy as jnp
from jax import lax
from jax.experimental import pallas as pl
from jax.experimental.pallas import tpu as pltpu
from jax.sharding import PartitionSpec as P

PARTS = 2
VMEM_LIMIT = 48 * 1024 * 1024
ANYWHERE = pl.BlockSpec(memory_space=pl.ANY)
SCALARS = pl.BlockSpec(memory_space=pltpu.SMEM)


def whole(array):
    return pl.BlockSpec(array.shape, lambda *_: (0,) * array.ndim)


def params():
    return pltpu.CompilerParams(vmem_limit_bytes=VMEM_LIMIT)


def coupling_matrices(pattern, weights):
    count = pattern.shape[1]
    modes = jnp.arange(count, dtype=jnp.int32)
    hits = pattern[..., None] == modes
    dense = jnp.sum(jnp.where(hits, weights[..., None], 0.0), axis=2)
    coupling = 0.5 * (dense + jnp.swapaxes(dense, 1, 2))
    wide = jnp.swapaxes(coupling, 0, 1).reshape(count, -1)
    high = lax.reduce_precision(wide, 8, 7)
    return jnp.concatenate([high, wide - high], 0).astype(jnp.bfloat16)


def face_coefficients(own, below, above, first, rows):
    centre = lax.dynamic_slice_in_dim(own, first, rows, 1)
    tall = jnp.pad(own, ((0, 0), (1, 1), (0, 0)))
    near = lax.dynamic_slice_in_dim(tall, first, rows + 2, 1)
    wide = jnp.pad(centre, ((0, 0), (0, 0), (1, 1)))
    others = [below, above, near[:, :-2], near[:, 2:], wide[:, :, :-2], wide[:, :, 2:]]
    faces = jnp.stack([0.5 * (centre + other) for other in others], 1)
    terms, _, _, width = faces.shape
    return jnp.transpose(faces.reshape(terms * 6, rows, width), (1, 0, 2))


def pack_kernel(shift, owners, me_ref, state_ref, adjoint_ref, *refs):
    out_ref = refs[-1]
    field = lax.rem(me_ref[0] + shift, owners) // (owners // 2)

    @pl.when(field == 0)
    def _():
        out_ref[...] = jnp.swapaxes(state_ref[...], 0, 1)

    @pl.when(field == 1)
    def _():
        out_ref[...] = jnp.swapaxes(adjoint_ref[...], 0, 1)


def pack(me, state, adjoint, shift, part, rows, owners, earlier):
    modes, _, width = state.shape
    halves = owners // 2

    def place(i, me_ref):
        half = lax.rem(lax.rem(me_ref[0] + shift, owners), halves)
        return 0, half * PARTS + part, 0

    block = pl.BlockSpec((modes, rows, width), place)
    return pl.pallas_call(
        functools.partial(pack_kernel, shift, owners),
        grid_spec=pltpu.PrefetchScalarGridSpec(
            num_scalar_prefetch=1,
            grid=(1,),
            in_specs=[block, block] + [ANYWHERE] * len(earlier),
            out_specs=pl.BlockSpec((rows, modes, width), lambda i, me_ref: (0, 0, 0)),
        ),
        out_shape=jax.ShapeDtypeStruct((rows, modes, width), jnp.float32),
        compiler_params=params(),
        name="pack",
    )(me, state, adjoint, *earlier)


def extra_kernel(rows, halves, state_ref, adjoint_ref, out_ref):
    height = state_ref.shape[1]

    def row_of(ref, row):
        if row < 0 or row >= height:
            return jnp.zeros((ref.shape[0], ref.shape[2]), jnp.float32)
        tile = row // 8 * 8
        return jnp.swapaxes(ref[:, tile : tile + 8, :], 0, 1)[row - tile]

    for field, ref in enumerate((state_ref, adjoint_ref)):
        for half in range(halves):
            first = half * rows * PARTS
            places = [first + rows, first - 1, first + rows * PARTS]
            if halves == 2:
                places.pop(1 + half if half == 1 else 1)
            for index, row in enumerate(places):
                out_ref[field * halves + half, index] = row_of(ref, row)


def extra_rows(state, adjoint, rows, halves):
    modes, _, width = state.shape
    count = 2 if halves == 2 else 3
    shape = (2 * halves, count, modes, width)
    return pl.pallas_call(
        functools.partial(extra_kernel, rows, halves),
        grid=(1,),
        in_specs=[whole(state), whole(adjoint)],
        out_specs=pl.BlockSpec(shape, lambda i: (0,) * 4),
        out_shape=jax.ShapeDtypeStruct(shape, jnp.float32),
        compiler_params=params(),
        name="extra_rows",
    )(state, adjoint)


def operator_kernel(rows, terms, owners, part, me_ref, extra_ref, face_ref, matrix_ref, *refs):
    own, below, above, before = (refs[i * owners : (i + 1) * owners] for i in range(4))
    outs = refs[-owners - 3 : -3]
    high, low, mixed = refs[-3:]
    _, block, width = own[0].shape
    modes = owners * block
    halves = owners // 2
    me = me_ref[0]
    half = lax.rem(me, halves)
    step = 16
    lanes = lax.broadcasted_iota(jnp.int32, (step, width), 1)
    last = rows - 1

    def edge(source, which, here):
        if halves == 2:
            return jnp.where(half == 1 - which, extra_ref[source, 1, here, :], 0.0)
        return extra_ref[source, 1 + which, here, :]

    def one_row(row, place):
        for shift in range(owners):
            source = lax.rem(me + owners - shift, owners)
            for start in range(0, block, step):
                here = pl.ds(start, step)
                centre = own[shift][row, here, :]
                if place != "first":
                    up = own[shift][row - 1, here, :]
                elif part == 0:
                    up = edge(source, 0, here)
                else:
                    up = before[shift][0, here, :]
                if place != "last":
                    down = own[shift][row + 1, here, :]
                elif part == 0:
                    down = extra_ref[source, 0, here, :]
                else:
                    down = edge(source, 1, here)
                left = jnp.where(lanes == 0, 0.0, pltpu.roll(centre, 1, 1))
                right = jnp.where(lanes == width - 1, 0.0, pltpu.roll(centre, width - 1, 1))
                others = (below[shift][row, here, :], above[shift][row, here, :], up, down, left, right)
                slopes = [centre - other for other in others]
                for term in range(terms):
                    total = face_ref[row, 6 * term : 6 * term + 1, :] * slopes[0]
                    for side in range(1, 6):
                        total = total + face_ref[row, 6 * term + side : 6 * term + side + 1, :] * slopes[side]
                    rounded = total.astype(jnp.bfloat16)
                    at = pl.ds(pl.multiple_of(source * block + (term * modes + start), step), step)
                    high[at, :] = rounded
                    low[at, :] = (total - rounded.astype(jnp.float32)).astype(jnp.bfloat16)
        both = jnp.dot(matrix_ref[...], high[...], preferred_element_type=jnp.float32)
        rest = jnp.dot(matrix_ref[:modes, :], low[...], preferred_element_type=jnp.float32)
        mixed[...] = both[:modes] + both[modes:] + rest
        for shift in range(owners):
            owner = lax.rem(me + shift, owners)
            outs[shift][row] = mixed[pl.ds(pl.multiple_of(owner * block, block), block), :]

    def middle(row, carry):
        one_row(row, "middle")
        return carry

    one_row(0, "first")
    lax.fori_loop(1, last, middle, 0)
    one_row(last, "last")


def apply_operator(me, extra, faces, matrix, own, below, above, before, part, earlier):
    rows, block, width = own[0].shape
    owners = len(own)
    modes = owners * block
    terms = matrix.shape[1] // modes
    edge = pl.BlockSpec((1, block, width), lambda i: (rows - 1, 0, 0))
    out = whole(own[0])
    return pl.pallas_call(
        functools.partial(operator_kernel, rows, terms, owners, part),
        grid=(1,),
        in_specs=[
            SCALARS,
            whole(extra),
            pl.BlockSpec((rows, 6 * terms, width), lambda i: (part, 0, 0)),
            whole(matrix),
        ]
        + [out] * (3 * owners)
        + [edge] * owners
        + [ANYWHERE] * len(earlier),
        out_specs=[out] * owners,
        out_shape=[jax.ShapeDtypeStruct((rows, block, width), jnp.float32)] * owners,
        scratch_shapes=[
            pltpu.VMEM((terms * modes, width), jnp.bfloat16),
            pltpu.VMEM((terms * modes, width), jnp.bfloat16),
            pltpu.VMEM((modes, width), jnp.float32),
        ],
        compiler_params=params(),
        name="operator",
    )(me, extra, faces, matrix, *own, *below, *above, *before, *earlier)


def finish_kernel(owners, me_ref, *refs):
    mixed = refs[:owners]
    state_ref, control_ref, adjoint_ref = refs[owners : owners + 3]
    state_out, control_out, adjoint_out = refs[-3:]
    halves = owners // 2
    half = pl.program_id(0)
    control_out[...] = 0.5 * control_ref[...] - adjoint_ref[...]
    for shift in range(owners):
        source = lax.rem(me_ref[0] + owners - shift, owners)

        @pl.when(source == half)
        def _(shift=shift):
            adjoint_out[...] = jnp.swapaxes(mixed[shift][...], 0, 1) - control_ref[...]

        @pl.when(source == halves + half)
        def _(shift=shift):
            state_out[...] = state_ref[...] + jnp.swapaxes(mixed[shift][...], 0, 1)


def finish(me, mixed, state, control, adjoint, outputs, part):
    modes, _, width = state.shape
    owners = len(mixed)
    rows = mixed[0].shape[0]
    block = pl.BlockSpec((modes, rows, width), lambda h: (0, h * PARTS + part, 0))
    in_specs = [SCALARS] + [whole(m) for m in mixed] + [block] * 3
    operands = [me, *mixed, state, control, adjoint]
    aliases = {}
    if outputs is not None:
        aliases = {len(operands) + i: i for i in range(3)}
        in_specs += [ANYWHERE] * 3
        operands += list(outputs)
    return pl.pallas_call(
        functools.partial(finish_kernel, owners),
        grid=(owners // 2,),
        in_specs=in_specs,
        out_specs=[block] * 3,
        out_shape=[jax.ShapeDtypeStruct(state.shape, jnp.float32)] * 3,
        input_output_aliases=aliases,
        compiler_params=params(),
        name="finish",
    )(*operands)


def shards(state, control, adjoint, coefficient, pattern, weights):
    shape = state.shape
    modes, _, height, width = shape
    state, control, adjoint = (a.reshape(modes, height, width) for a in (state, control, adjoint))
    owners = lax.axis_size("mode")
    halves = owners // 2
    half_rows = height // halves
    rows = half_rows // PARTS
    planes = lax.axis_size("space")
    forward = [(i, i + 1) for i in range(planes - 1)]
    backward = [(i + 1, i) for i in range(planes - 1)]
    position = lax.axis_index("mode")
    me = position.astype(jnp.int32).reshape(1)
    first = lax.rem(position, halves) * half_rows
    shifts = sorted(range(1, owners), key=lambda s: min(s, owners - s))

    def move(array, shift):
        return lax.ppermute(array, "mode", [(i, (i + shift) % owners) for i in range(owners)])

    def beside(array):
        return lax.ppermute(array, "space", forward), lax.ppermute(array, "space", backward)

    own = coefficient[:, 0]
    below, above = beside(lax.dynamic_slice_in_dim(own, first, half_rows, 1))
    faces = face_coefficients(own, below, above, first, half_rows)
    matrix = coupling_matrices(pattern, weights)

    pieces = [[None] * owners for _ in range(PARTS)]
    halos = [[None] * owners for _ in range(PARTS)]
    order = []
    for part in range(PARTS):
        for shift in [0] + shifts:
            sent = len(order) - part - 1
            earlier = list(order[sent - 2]) if shift and sent >= 2 else []
            piece = pack(me, state, adjoint, shift, part, rows, owners, earlier)
            if shift:
                piece = move(piece, shift)
            pieces[part][shift] = piece
            halos[part][shift] = beside(piece)
            order.append(halos[part][shift])
    extra = lax.all_to_all(extra_rows(state, adjoint, rows, halves), "mode", 0, 0, tiled=True)

    outputs = None
    for part in range(PARTS):
        below, above = zip(*halos[part])
        before = pieces[0]
        earlier = [] if part else list(halos[1][0]) + list(halos[1][shifts[0]])
        mixed = apply_operator(me, extra, faces, matrix, pieces[part], below, above, before, part, earlier)
        mixed = [move(m, shift) if shift else m for shift, m in enumerate(mixed)]
        outputs = finish(me, mixed, state, control, adjoint, outputs, part)
    return tuple(out.reshape(shape) for out in outputs)


def solution(mesh):
    split = P("mode", "space", None, None)
    in_specs = (split, split, split, P(None, "space", None, None), P(), P())
    return jax.shard_map(shards, mesh=mesh, in_specs=in_specs, out_specs=(split, split, split), check_vma=False)
```

time: 283 us -> 255 us (0.901)
  the two profiles are of different devices: /device:TPU:4 before, /device:TPU:11 now
where the time goes in v3:
time: 255 us; the launch traced here: 254 us
  starting transfers between devices  89.4 us (35%)
  waiting for transfers between devices  86.9 us (34%)
  Pallas kernels  44.7 us (18%)
  local copies, waits for them, and re-layouts  21.1 us (8%)
  other arithmetic  11.1 us (4%)
    ppermute x12, waiting for transfers between devices, move(): lax.ppermute(array, 'mode', [(i, (i + shift) % owners) for i in range(own...  82.9 us
    ppermute x9, starting transfers between devices, beside(): lax.ppermute(array, 'space', forward)  41.5 us
    pallas_call x2, Pallas kernels, apply_operator(): pl.pallas_call(functools.partial(operator_kernel, rows, terms, owners, pa...  34.3 us
    ppermute x9, starting transfers between devices, beside(): lax.ppermute(array, 'space', backward)  20.8 us
    all_to_all x1, starting transfers between devices, shards(): lax.all_to_all(extra_rows(state, adjoint, rows, halves), 'mode', 0, 0, ti...  14.8 us
    unnamed x54, local copies, waits for them, and re-layouts  13.5 us
    ppermute x12, starting transfers between devices, move(): lax.ppermute(array, 'mode', [(i, (i + shift) % owners) for i in range(own...  12.3 us
    pallas_call x2, Pallas kernels, finish(): pl.pallas_call(functools.partial(finish_kernel, owners), grid=(owners //...  6.46 us
  transfers between devices with their start and end apart: 31, of which 10 were waited for; matrix products, arithmetic and copies ran while one was open for 7% of the time, Pallas kernels for 16%

profile of v3, /device:TPU:11, one launch (start us, length us, event | category | flops | bytes accessed | tf_op | source)
XLA Modules:
  0.0 254.2 jit_solution(8305669266070114796)
XLA Ops:
  6.3 2.9 %collective-permute-start.7 = (f32[16,32,256]{2,1,0:T(8,128)S(1)}, f32[16,32,256]{2,1,0:T(8,128)}, u32[]{:S(2)}, u32[]{:S(2)}) collective-permute-start(f32[16,32,256]{2,1,0:T(8,128)S(1)} %pack.11.refs_12_.refs_0_), channel_id=1, source_target_pairs={{4,0},{8,4},{12,8},{16,12},{20,16},{24,20},{28,24},{5,1},{9,5},{13... | collective-permute-start | bytes 1572872 | tf_op jit(solution)/shard_map/ppermute | solution.py:274
  9.1 3.6 %collective-permute-start.6 = (f32[16,32,256]{2,1,0:T(8,128)S(1)}, f32[16,32,256]{2,1,0:T(8,128)}, u32[]{:S(2)}, u32[]{:S(2)}) collective-permute-start(f32[16,32,256]{2,1,0:T(8,128)S(1)} %pack.11.refs_12_.refs_0_), channel_id=1, source_target_pairs={{0,4},{4,8},{8,12},{12,16},{16,20},{20,24},{24,28},{1,5},{5,9},{9,... | collective-permute-start | bytes 1572872 | tf_op jit(solution)/shard_map/ppermute | solution.py:274
  13.9 4.0 %collective-permute-done.2.refs_13_.refs_1_ = f32[16,32,256]{2,1,0:T(8,128)S(1)} collective-permute-done((f32[16,32,256]{2,1,0:T(8,128)}, f32[16,32,256]{2,1,0:T(8,128)S(1)}, u32[]{:S(2)}, u32[]{:S(2)}) %collective-permute-start.2) | collective-permute-done | bytes 524320 | tf_op jit(solution)/shard_map/ppermute | solution.py:271
  17.9 4.5 %collective-permute-start.4 = (f32[16,32,256]{2,1,0:T(8,128)S(1)}, f32[16,32,256]{2,1,0:T(8,128)}, u32[]{:S(2)}, u32[]{:S(2)}) collective-permute-start(f32[16,32,256]{2,1,0:T(8,128)S(1)} %collective-permute-done.2.refs_13_.refs_1_), channel_id=1, source_target_pairs={{4,0},{8,4},{12,8},{16,12},{20,16},{24,20},{28,24},{5,1},{9,5},{13... | collective-permute-start | bytes 1572872 | tf_op jit(solution)/shard_map/ppermute | solution.py:274
  28.4 14.8 %all-to-all-start = ((f32[4,2,32,256]{3,2,1,0:T(8,128)}), f32[4,2,32,256]{3,2,1,0:T(8,128)S(1)}, u32[]{:S(2)}, u32[]{:S(2)}) async-start(f32[4,2,32,256]{3,2,1,0:T(8,128)} %copy-done.19), calls=%async_computation | async-start | bytes 524288 | tf_op jit(solution)/shard_map/all_to_all | solution.py:294
  43.3 2.0 select_reduce_fusion
  45.3 2.0 copy.39
  49.9 2.1 collective-permute-start.8
  52.0 5.4 %collective-permute-start.3 = (f32[16,32,256]{2,1,0:T(8,128)S(1)}, f32[16,32,256]{2,1,0:T(8,128)}, u32[]{:S(2)}, u32[]{:S(2)}) collective-permute-start(f32[16,32,256]{2,1,0:T(8,128)S(1)} %collective-permute-done.2.refs_13_.refs_1_), channel_id=1, source_target_pairs={{0,4},{4,8},{8,12},{12,16},{16,20},{20,24},{24,28},{1,5},{5,9},{9,... | collective-permute-start | bytes 1572872 | tf_op jit(solution)/shard_map/ppermute | solution.py:274
  60.1 2.0 copy.40
  62.1 4.5 %collective-permute-start = (f32[7,32,256]{2,1,0:T(8,128)}, f32[7,32,256]{2,1,0:T(8,128)}, u32[]{:S(2)}, u32[]{:S(2)}) collective-permute-start(f32[7,32,256]{2,1,0:T(8,128)} %dynamic-slice_bitcast_fusion), channel_id=1, source_target_pairs={{0,4},{4,8},{8,12},{12,16},{16,20},{20,24},{24,28},{1,5},{5,9},{9,... | collective-permute-start | bytes 688136 | tf_op jit(solution)/shard_map/ppermute | solution.py:274
  76.7 4.7 %collective-permute-start.13 = (f32[16,32,256]{2,1,0:T(8,128)}, f32[16,32,256]{2,1,0:T(8,128)S(1)}, u32[]{:S(2)}, u32[]{:S(2)}) collective-permute-start(f32[16,32,256]{2,1,0:T(8,128)} %collective-permute-done.12.refs_15_.refs_3_), channel_id=1, source_target_pairs={{0,4},{4,8},{8,12},{12,16},{16,20},{20,24},{24,28},{1,5},{5,9},{9,... | collective-permute-start | bytes 1572872 | tf_op jit(solution)/shard_map/ppermute | solution.py:274
  83.4 4.5 %collective-permute-start.9 = (f32[16,32,256]{2,1,0:T(8,128)}, f32[16,32,256]{2,1,0:T(8,128)S(1)}, u32[]{:S(2)}, u32[]{:S(2)}) collective-permute-start(f32[16,32,256]{2,1,0:T(8,128)} %collective-permute-done.8.refs_14_.refs_2_), channel_id=1, source_target_pairs={{0,4},{4,8},{8,12},{12,16},{16,20},{20,24},{24,28},{1,5},{5,9},{9,... | collective-permute-start | bytes 1572872 | tf_op jit(solution)/shard_map/ppermute | solution.py:274
  90.0 3.3 %collective-permute-done.13.refs_0_.refs_7_ = f32[16,32,256]{2,1,0:T(8,128)S(1)} collective-permute-done((f32[16,32,256]{2,1,0:T(8,128)}, f32[16,32,256]{2,1,0:T(8,128)S(1)}, u32[]{:S(2)}, u32[]{:S(2)}) %collective-permute-start.13) | collective-permute-done | bytes 524320 | tf_op jit(solution)/shard_map/ppermute | solution.py:274
  93.3 5.2 %collective-permute-start.16 = (f32[16,32,256]{2,1,0:T(8,128)S(1)}, f32[16,32,256]{2,1,0:T(8,128)S(1)}, u32[]{:S(2)}, u32[]{:S(2)}) collective-permute-start(f32[16,32,256]{2,1,0:T(8,128)S(1)} %copy-done.15), channel_id=1, source_target_pairs={{0,4},{4,8},{8,12},{12,16},{16,20},{20,24},{24,28},{1,5},{5,9},{9,... | collective-permute-start | bytes 1572872 | tf_op jit(solution)/shard_map/ppermute | solution.py:274
  104.0 4.5 %collective-permute-start.17 = (f32[16,32,256]{2,1,0:T(8,128)}, f32[16,32,256]{2,1,0:T(8,128)}, u32[]{:S(2)}, u32[]{:S(2)}) collective-permute-start(f32[16,32,256]{2,1,0:T(8,128)} %collective-permute-done.5.refs_1_), channel_id=1, source_target_pairs={{0,4},{4,8},{8,12},{12,16},{16,20},{20,24},{24,28},{1,5},{5,9},{9,... | collective-permute-start | bytes 1572872 | tf_op jit(solution)/shard_map/ppermute | solution.py:274
  111.0 13.4 %collective-permute-done.15.refs_3_ = f32[16,32,256]{2,1,0:T(8,128)} collective-permute-done((f32[16,32,256]{2,1,0:T(8,128)S(1)}, f32[16,32,256]{2,1,0:T(8,128)}, u32[]{:S(2)}, u32[]{:S(2)}) %collective-permute-start.15) | collective-permute-done | bytes 524320 | tf_op jit(solution)/shard_map/ppermute | solution.py:271
  126.3 1.9 copy.46
  128.3 4.5 %collective-permute-start.19 = (f32[16,32,256]{2,1,0:T(8,128)}, f32[16,32,256]{2,1,0:T(8,128)}, u32[]{:S(2)}, u32[]{:S(2)}) collective-permute-start(f32[16,32,256]{2,1,0:T(8,128)} %collective-permute-done.15.refs_3_), channel_id=1, source_target_pairs={{0,4},{4,8},{8,12},{12,16},{16,20},{20,24},{24,28},{1,5},{5,9},{9,... | collective-permute-start | bytes 1572872 | tf_op jit(solution)/shard_map/ppermute | solution.py:274
  135.6 4.5 %collective-permute-start.18 = (f32[16,32,256]{2,1,0:T(8,128)}, f32[16,32,256]{2,1,0:T(8,128)}, u32[]{:S(2)}, u32[]{:S(2)}) collective-permute-start(f32[16,32,256]{2,1,0:T(8,128)} %collective-permute-done.11.refs_2_), channel_id=1, source_target_pairs={{0,4},{4,8},{8,12},{12,16},{16,20},{20,24},{24,28},{1,5},{5,9},{9,... | collective-permute-start | bytes 1572872 | tf_op jit(solution)/shard_map/ppermute | solution.py:274
  141.2 17.2 %operator.3 = (f32[16,32,256]{2,1,0:T(8,128)S(1)}, f32[16,32,256]{2,1,0:T(8,128)S(1)}, f32[16,32,256]{2,1,0:T(8,128)S(1)}, f32[16,32,256]{2,1,0:T(8,128)S(1)}) custom-call(s32[1]{0:T(128)} %bitcast.me_ref, f32[4,2,32,256]{3,2,1,0:T(8,128)S(1)} %all-to-all-done.extra_ref, f32[32,42,256]{2,1,0:T(8,128)} %bitcast.87, bf16[256,896]{1,0:T(8,128)(2,1)S(1)} %copy-done.9, ...), custom_call_target="tpu_custom_call" | custom-call | tf_op jit(solution)/shard_map/operator/pallas_call | solution.py:187
  158.5 3.1 %collective-permute-start.28 = (f32[16,32,256]{2,1,0:T(8,128)S(1)}, f32[16,32,256]{2,1,0:T(8,128)S(1)}, u32[]{:S(2)}, u32[]{:S(2)}) collective-permute-start(f32[16,32,256]{2,1,0:T(8,128)S(1)} %get-tuple-element.23), channel_id=1, source_target_pairs={{0,2},{1,3},{2,0},{3,1},{4,6},{5,7},{6,4},{7,5},{8,10},{9,11},{10,... | collective-permute-start | bytes 1572872 | tf_op jit(solution)/shard_map/ppermute | solution.py:271
  162.4 17.1 %operator.2 = (f32[16,32,256]{2,1,0:T(8,128)S(1)}, f32[16,32,256]{2,1,0:T(8,128)S(1)}, f32[16,32,256]{2,1,0:T(8,128)S(1)}, f32[16,32,256]{2,1,0:T(8,128)S(1)}) custom-call(s32[1]{0:T(128)} %bitcast.me_ref, f32[4,2,32,256]{3,2,1,0:T(8,128)S(1)} %all-to-all-done.extra_ref, f32[32,42,256]{2,1,0:T(8,128)} %bitcast.88, bf16[256,896]{1,0:T(8,128)(2,1)S(1)} %copy-done.10, ...), custom_call_target="tpu_custom_call" | custom-call | tf_op jit(solution)/shard_map/operator/pallas_call | solution.py:187
  180.2 2.0 collective-permute-start.25
  182.3 8.8 %collective-permute-done.27.refs_1_ = f32[16,32,256]{2,1,0:T(8,128)S(1)} collective-permute-done((f32[16,32,256]{2,1,0:T(8,128)S(1)}, f32[16,32,256]{2,1,0:T(8,128)S(1)}, u32[]{:S(2)}, u32[]{:S(2)}) %collective-permute-start.27) | collective-permute-done | bytes 524320 | tf_op jit(solution)/shard_map/ppermute | solution.py:271
  191.1 35.3 %collective-permute-done.28.refs_2_ = f32[16,32,256]{2,1,0:T(8,128)S(1)} collective-permute-done((f32[16,32,256]{2,1,0:T(8,128)S(1)}, f32[16,32,256]{2,1,0:T(8,128)S(1)}, u32[]{:S(2)}, u32[]{:S(2)}) %collective-permute-start.28) | collective-permute-done | bytes 524320 | tf_op jit(solution)/shard_map/ppermute | solution.py:271
  226.3 2.2 collective-permute-done.29.refs_3_
  228.5 3.2 %finish.2 = (f32[32,64,256]{2,1,0:T(8,128)}, f32[32,64,256]{2,1,0:T(8,128)}, f32[32,64,256]{2,1,0:T(8,128)}) custom-call(s32[1]{0:T(128)} %bitcast.me_ref, f32[16,32,256]{2,1,0:T(8,128)S(1)} %get-tuple-element.21.refs_0_, f32[16,32,256]{2,1,0:T(8,128)S(1)} %collective-permute-done.27.refs_1_, f32[16,32,256]{2,1,0:T(8,128)S(1)} %collective-permute-done.28.refs_2_, ...), custom_call_target="tpu_custom_call" | custom-call | tf_op jit(solution)/shard_map/finish/pallas_call | solution.py:242
  231.8 6.0 %collective-permute-done.24.refs_1_ = f32[16,32,256]{2,1,0:T(8,128)S(1)} collective-permute-done((f32[16,32,256]{2,1,0:T(8,128)S(1)}, f32[16,32,256]{2,1,0:T(8,128)S(1)}, u32[]{:S(2)}, u32[]{:S(2)}) %collective-permute-start.24) | collective-permute-done | bytes 524320 | tf_op jit(solution)/shard_map/ppermute | solution.py:271
  237.7 9.2 %collective-permute-done.25.refs_2_ = f32[16,32,256]{2,1,0:T(8,128)S(1)} collective-permute-done((f32[16,32,256]{2,1,0:T(8,128)S(1)}, f32[16,32,256]{2,1,0:T(8,128)S(1)}, u32[]{:S(2)}, u32[]{:S(2)}) %collective-permute-start.25) | collective-permute-done | bytes 524320 | tf_op jit(solution)/shard_map/ppermute | solution.py:271
  247.0 4.1 %collective-permute-done.26.refs_3_ = f32[16,32,256]{2,1,0:T(8,128)S(1)} collective-permute-done((f32[16,32,256]{2,1,0:T(8,128)S(1)}, f32[16,32,256]{2,1,0:T(8,128)S(1)}, u32[]{:S(2)}, u32[]{:S(2)}) %collective-permute-start.26) | collective-permute-done | bytes 524320 | tf_op jit(solution)/shard_map/ppermute | solution.py:271
  251.0 3.2 %finish.3 = (f32[32,64,256]{2,1,0:T(8,128)}, f32[32,64,256]{2,1,0:T(8,128)}, f32[32,64,256]{2,1,0:T(8,128)}) custom-call(s32[1]{0:T(128)} %bitcast.me_ref, f32[16,32,256]{2,1,0:T(8,128)S(1)} %get-tuple-element.17.refs_0_, f32[16,32,256]{2,1,0:T(8,128)S(1)} %collective-permute-done.24.refs_1_, ...), custom_call_target="tpu_custom_call", output_to_operand_aliasing={{0}: (8, {}), {1}: (9, {}), {2}: (10, {})} | custom-call | tf_op jit(solution)/shard_map/finish/pallas_call | solution.py:242
  (111 shorter events, 47.3 us)
Async XLA Ops:
  4.8 13.1 %collective-permute-start.2 = (f32[16,32,256]{2,1,0:T(8,128)}, f32[16,32,256]{2,1,0:T(8,128)S(1)}, u32[]{:S(2)}, u32[]{:S(2)}) collective-permute-start(f32[16,32,256]{2,1,0:T(8,128)} %pack.9), channel_id=1, source_target_pairs={{0,1},{1,2},{2,3},{3,0},{4,5},{5,6},{6,7},{7,4},{8,9},{9,10},{10,1... | collective-permute-start | bytes 1572872 | tf_op jit(solution)/shard_map/ppermute | solution.py:271
  6.3 133.9 %copy-start.7 = (f32[16,32,256]{2,1,0:T(8,128)}, f32[16,32,256]{2,1,0:T(8,128)S(1)}, u32[]{:S(2)}) copy-start(f32[16,32,256]{2,1,0:T(8,128)S(1)} %pack.11.refs_12_.refs_0_) | copy-start | bytes 1572868
  6.3 41.1 %collective-permute-start.7 = (f32[16,32,256]{2,1,0:T(8,128)S(1)}, f32[16,32,256]{2,1,0:T(8,128)}, u32[]{:S(2)}, u32[]{:S(2)}) collective-permute-start(f32[16,32,256]{2,1,0:T(8,128)S(1)} %pack.11.refs_12_.refs_0_), channel_id=1, source_target_pairs={{4,0},{8,4},{12,8},{16,12},{20,16},{24,20},{28,24},{5,1},{9,5},{13... | collective-permute-start | bytes 1572872 | tf_op jit(solution)/shard_map/ppermute | solution.py:274
  9.1 38.2 %collective-permute-start.6 = (f32[16,32,256]{2,1,0:T(8,128)S(1)}, f32[16,32,256]{2,1,0:T(8,128)}, u32[]{:S(2)}, u32[]{:S(2)}) collective-permute-start(f32[16,32,256]{2,1,0:T(8,128)S(1)} %pack.11.refs_12_.refs_0_), channel_id=1, source_target_pairs={{0,4},{4,8},{8,12},{12,16},{16,20},{20,24},{24,28},{1,5},{5,9},{9,... | collective-permute-start | bytes 1572872 | tf_op jit(solution)/shard_map/ppermute | solution.py:274
  13.7 43.6 %collective-permute-start.12 = (f32[16,32,256]{2,1,0:T(8,128)}, f32[16,32,256]{2,1,0:T(8,128)}, u32[]{:S(2)}, u32[]{:S(2)}) collective-permute-start(f32[16,32,256]{2,1,0:T(8,128)} %pack.14), channel_id=1, source_target_pairs={{0,3},{1,0},{2,1},{3,2},{4,7},{5,4},{6,5},{7,6},{8,11},{9,8},{10,9... | collective-permute-start | bytes 1572872 | tf_op jit(solution)/shard_map/ppermute | solution.py:271
  17.9 44.2 %collective-permute-start.4 = (f32[16,32,256]{2,1,0:T(8,128)S(1)}, f32[16,32,256]{2,1,0:T(8,128)}, u32[]{:S(2)}, u32[]{:S(2)}) collective-permute-start(f32[16,32,256]{2,1,0:T(8,128)S(1)} %collective-permute-done.2.refs_13_.refs_1_), channel_id=1, source_target_pairs={{4,0},{8,4},{12,8},{16,12},{20,16},{24,20},{28,24},{5,1},{9,5},{13... | collective-permute-start | bytes 1572872 | tf_op jit(solution)/shard_map/ppermute | solution.py:274
  24.1 52.7 %collective-permute-start.1 = (f32[7,32,256]{2,1,0:T(8,128)}, f32[7,32,256]{2,1,0:T(8,128)}, u32[]{:S(2)}, u32[]{:S(2)}) collective-permute-start(f32[7,32,256]{2,1,0:T(8,128)} %dynamic-slice_bitcast_fusion), channel_id=1, source_target_pairs={{4,0},{8,4},{12,8},{16,12},{20,16},{24,20},{28,24},{5,1},{9,5},{13... | collective-permute-start | bytes 688136 | tf_op jit(solution)/shard_map/ppermute | solution.py:274
  28.4 111.7 %all-to-all-start = ((f32[4,2,32,256]{3,2,1,0:T(8,128)}), f32[4,2,32,256]{3,2,1,0:T(8,128)S(1)}, u32[]{:S(2)}, u32[]{:S(2)}) async-start(f32[4,2,32,256]{3,2,1,0:T(8,128)} %copy-done.19), calls=%async_computation | async-start | bytes 524288 | tf_op jit(solution)/shard_map/all_to_all | solution.py:294
  49.9 31.6 %collective-permute-start.8 = (f32[16,32,256]{2,1,0:T(8,128)}, f32[16,32,256]{2,1,0:T(8,128)}, u32[]{:S(2)}, u32[]{:S(2)}) collective-permute-start(f32[16,32,256]{2,1,0:T(8,128)} %pack.12), channel_id=1, source_target_pairs={{0,2},{1,3},{2,0},{3,1},{4,6},{5,7},{6,4},{7,5},{8,10},{9,11},{10,... | collective-permute-start | bytes 1572872 | tf_op jit(solution)/shard_map/ppermute | solution.py:271
  52.0 21.0 %collective-permute-start.3 = (f32[16,32,256]{2,1,0:T(8,128)S(1)}, f32[16,32,256]{2,1,0:T(8,128)}, u32[]{:S(2)}, u32[]{:S(2)}) collective-permute-start(f32[16,32,256]{2,1,0:T(8,128)S(1)} %collective-permute-done.2.refs_13_.refs_1_), channel_id=1, source_target_pairs={{0,4},{4,8},{8,12},{12,16},{16,20},{20,24},{24,28},{1,5},{5,9},{9,... | collective-permute-start | bytes 1572872 | tf_op jit(solution)/shard_map/ppermute | solution.py:274
  57.4 26.1 %collective-permute-start.14 = (f32[16,32,256]{2,1,0:T(8,128)}, f32[16,32,256]{2,1,0:T(8,128)}, u32[]{:S(2)}, u32[]{:S(2)}) collective-permute-start(f32[16,32,256]{2,1,0:T(8,128)} %collective-permute-done.12.refs_15_.refs_3_), channel_id=1, source_target_pairs={{4,0},{8,4},{12,8},{16,12},{20,16},{24,20},{28,24},{5,1},{9,5},{13... | collective-permute-start | bytes 1572872 | tf_op jit(solution)/shard_map/ppermute | solution.py:274
  62.1 19.3 %collective-permute-start = (f32[7,32,256]{2,1,0:T(8,128)}, f32[7,32,256]{2,1,0:T(8,128)}, u32[]{:S(2)}, u32[]{:S(2)}) collective-permute-start(f32[7,32,256]{2,1,0:T(8,128)} %dynamic-slice_bitcast_fusion), channel_id=1, source_target_pairs={{0,4},{4,8},{8,12},{12,16},{16,20},{20,24},{24,28},{1,5},{5,9},{9,... | collective-permute-start | bytes 688136 | tf_op jit(solution)/shard_map/ppermute | solution.py:274
  73.0 31.0 %collective-permute-start.20 = (f32[16,32,256]{2,1,0:T(8,128)}, f32[16,32,256]{2,1,0:T(8,128)S(1)}, u32[]{:S(2)}, u32[]{:S(2)}) collective-permute-start(f32[16,32,256]{2,1,0:T(8,128)} %copy-done.14), channel_id=1, source_target_pairs={{4,0},{8,4},{12,8},{16,12},{20,16},{24,20},{28,24},{5,1},{9,5},{13... | collective-permute-start | bytes 1572872 | tf_op jit(solution)/shard_map/ppermute | solution.py:274
  76.7 16.6 %collective-permute-start.13 = (f32[16,32,256]{2,1,0:T(8,128)}, f32[16,32,256]{2,1,0:T(8,128)S(1)}, u32[]{:S(2)}, u32[]{:S(2)}) collective-permute-start(f32[16,32,256]{2,1,0:T(8,128)} %collective-permute-done.12.refs_15_.refs_3_), channel_id=1, source_target_pairs={{0,4},{4,8},{8,12},{12,16},{16,20},{20,24},{24,28},{1,5},{5,9},{9,... | collective-permute-start | bytes 1572872 | tf_op jit(solution)/shard_map/ppermute | solution.py:274
  81.4 20.7 %collective-permute-start.5 = (f32[16,32,256]{2,1,0:T(8,128)S(1)}, f32[16,32,256]{2,1,0:T(8,128)}, u32[]{:S(2)}, u32[]{:S(2)}) collective-permute-start(f32[16,32,256]{2,1,0:T(8,128)S(1)} %pack.10), channel_id=1, source_target_pairs={{0,1},{1,2},{2,3},{3,0},{4,5},{5,6},{6,7},{7,4},{8,9},{9,10},{10,1... | collective-permute-start | bytes 1572872 | tf_op jit(solution)/shard_map/ppermute | solution.py:271
  81.5 17.8 %collective-permute-start.10 = (f32[16,32,256]{2,1,0:T(8,128)}, f32[16,32,256]{2,1,0:T(8,128)S(1)}, u32[]{:S(2)}, u32[]{:S(2)}) collective-permute-start(f32[16,32,256]{2,1,0:T(8,128)} %collective-permute-done.8.refs_14_.refs_2_), channel_id=1, source_target_pairs={{4,0},{8,4},{12,8},{16,12},{20,16},{24,20},{28,24},{5,1},{9,5},{13... | collective-permute-start | bytes 1572872 | tf_op jit(solution)/shard_map/ppermute | solution.py:274
  83.4 16.8 %collective-permute-start.9 = (f32[16,32,256]{2,1,0:T(8,128)}, f32[16,32,256]{2,1,0:T(8,128)S(1)}, u32[]{:S(2)}, u32[]{:S(2)}) collective-permute-start(f32[16,32,256]{2,1,0:T(8,128)} %collective-permute-done.8.refs_14_.refs_2_), channel_id=1, source_target_pairs={{0,4},{4,8},{8,12},{12,16},{16,20},{20,24},{24,28},{1,5},{5,9},{9,... | collective-permute-start | bytes 1572872 | tf_op jit(solution)/shard_map/ppermute | solution.py:274
  93.3 35.0 %collective-permute-start.16 = (f32[16,32,256]{2,1,0:T(8,128)S(1)}, f32[16,32,256]{2,1,0:T(8,128)S(1)}, u32[]{:S(2)}, u32[]{:S(2)}) collective-permute-start(f32[16,32,256]{2,1,0:T(8,128)S(1)} %copy-done.15), channel_id=1, source_target_pairs={{0,4},{4,8},{8,12},{12,16},{16,20},{20,24},{24,28},{1,5},{5,9},{9,... | collective-permute-start | bytes 1572872 | tf_op jit(solution)/shard_map/ppermute | solution.py:274
  99.3 25.1 %collective-permute-start.15 = (f32[16,32,256]{2,1,0:T(8,128)S(1)}, f32[16,32,256]{2,1,0:T(8,128)}, u32[]{:S(2)}, u32[]{:S(2)}) collective-permute-start(f32[16,32,256]{2,1,0:T(8,128)S(1)} %pack.15), channel_id=1, source_target_pairs={{0,3},{1,0},{2,1},{3,2},{4,7},{5,4},{6,5},{7,6},{8,11},{9,8},{10,9... | collective-permute-start | bytes 1572872 | tf_op jit(solution)/shard_map/ppermute | solution.py:271
  101.0 31.8 %collective-permute-start.11 = (f32[16,32,256]{2,1,0:T(8,128)S(1)}, f32[16,32,256]{2,1,0:T(8,128)}, u32[]{:S(2)}, u32[]{:S(2)}) collective-permute-start(f32[16,32,256]{2,1,0:T(8,128)S(1)} %pack.13), channel_id=1, source_target_pairs={{0,2},{1,3},{2,0},{3,1},{4,6},{5,7},{6,4},{7,5},{8,10},{9,11},{10,... | collective-permute-start | bytes 1572872 | tf_op jit(solution)/shard_map/ppermute | solution.py:271
  102.1 32.7 %collective-permute-start.21 = (f32[16,32,256]{2,1,0:T(8,128)}, f32[16,32,256]{2,1,0:T(8,128)S(1)}, u32[]{:S(2)}, u32[]{:S(2)}) collective-permute-start(f32[16,32,256]{2,1,0:T(8,128)} %collective-permute-done.5.refs_1_), channel_id=1, source_target_pairs={{4,0},{8,4},{12,8},{16,12},{20,16},{24,20},{28,24},{5,1},{9,5},{13... | collective-permute-start | bytes 1572872 | tf_op jit(solution)/shard_map/ppermute | solution.py:274
  104.0 36.1 %collective-permute-start.17 = (f32[16,32,256]{2,1,0:T(8,128)}, f32[16,32,256]{2,1,0:T(8,128)}, u32[]{:S(2)}, u32[]{:S(2)}) collective-permute-start(f32[16,32,256]{2,1,0:T(8,128)} %collective-permute-done.5.refs_1_), channel_id=1, source_target_pairs={{0,4},{4,8},{8,12},{12,16},{16,20},{20,24},{24,28},{1,5},{5,9},{9,... | collective-permute-start | bytes 1572872 | tf_op jit(solution)/shard_map/ppermute | solution.py:274
  124.4 34.1 %collective-permute-start.23 = (f32[16,32,256]{2,1,0:T(8,128)}, f32[16,32,256]{2,1,0:T(8,128)}, u32[]{:S(2)}, u32[]{:S(2)}) collective-permute-start(f32[16,32,256]{2,1,0:T(8,128)} %collective-permute-done.15.refs_3_), channel_id=1, source_target_pairs={{4,0},{8,4},{12,8},{16,12},{20,16},{24,20},{28,24},{5,1},{9,5},{13... | collective-permute-start | bytes 1572872 | tf_op jit(solution)/shard_map/ppermute | solution.py:274
  128.3 33.3 %collective-permute-start.19 = (f32[16,32,256]{2,1,0:T(8,128)}, f32[16,32,256]{2,1,0:T(8,128)}, u32[]{:S(2)}, u32[]{:S(2)}) collective-permute-start(f32[16,32,256]{2,1,0:T(8,128)} %collective-permute-done.15.refs_3_), channel_id=1, source_target_pairs={{0,4},{4,8},{8,12},{12,16},{16,20},{20,24},{24,28},{1,5},{5,9},{9,... | collective-permute-start | bytes 1572872 | tf_op jit(solution)/shard_map/ppermute | solution.py:274
  132.8 29.6 %collective-permute-start.22 = (f32[16,32,256]{2,1,0:T(8,128)}, f32[16,32,256]{2,1,0:T(8,128)}, u32[]{:S(2)}, u32[]{:S(2)}) collective-permute-start(f32[16,32,256]{2,1,0:T(8,128)} %collective-permute-done.11.refs_2_), channel_id=1, source_target_pairs={{4,0},{8,4},{12,8},{16,12},{20,16},{24,20},{28,24},{5,1},{9,5},{13... | collective-permute-start | bytes 1572872 | tf_op jit(solution)/shard_map/ppermute | solution.py:274
  135.6 26.8 %collective-permute-start.18 = (f32[16,32,256]{2,1,0:T(8,128)}, f32[16,32,256]{2,1,0:T(8,128)}, u32[]{:S(2)}, u32[]{:S(2)}) collective-permute-start(f32[16,32,256]{2,1,0:T(8,128)} %collective-permute-done.11.refs_2_), channel_id=1, source_target_pairs={{0,4},{4,8},{8,12},{12,16},{16,20},{20,24},{24,28},{1,5},{5,9},{9,... | collective-permute-start | bytes 1572872 | tf_op jit(solution)/shard_map/ppermute | solution.py:274
  158.4 32.7 %collective-permute-start.27 = (f32[16,32,256]{2,1,0:T(8,128)S(1)}, f32[16,32,256]{2,1,0:T(8,128)S(1)}, u32[]{:S(2)}, u32[]{:S(2)}) collective-permute-start(f32[16,32,256]{2,1,0:T(8,128)S(1)} %get-tuple-element.22), channel_id=1, source_target_pairs={{0,1},{1,2},{2,3},{3,0},{4,5},{5,6},{6,7},{7,4},{8,9},{9,10},{10,1... | collective-permute-start | bytes 1572872 | tf_op jit(solution)/shard_map/ppermute | solution.py:271
  158.5 67.9 %collective-permute-start.28 = (f32[16,32,256]{2,1,0:T(8,128)S(1)}, f32[16,32,256]{2,1,0:T(8,128)S(1)}, u32[]{:S(2)}, u32[]{:S(2)}) collective-permute-start(f32[16,32,256]{2,1,0:T(8,128)S(1)} %get-tuple-element.23), channel_id=1, source_target_pairs={{0,2},{1,3},{2,0},{3,1},{4,6},{5,7},{6,4},{7,5},{8,10},{9,11},{10,... | collective-permute-start | bytes 1572872 | tf_op jit(solution)/shard_map/ppermute | solution.py:271
  161.6 67.0 %collective-permute-start.29 = (f32[16,32,256]{2,1,0:T(8,128)S(1)}, f32[16,32,256]{2,1,0:T(8,128)S(1)}, u32[]{:S(2)}, u32[]{:S(2)}) collective-permute-start(f32[16,32,256]{2,1,0:T(8,128)S(1)} %get-tuple-element.24), channel_id=1, source_target_pairs={{0,3},{1,0},{2,1},{3,2},{4,7},{5,4},{6,5},{7,6},{8,11},{9,8},{10,9... | collective-permute-start | bytes 1572872 | tf_op jit(solution)/shard_map/ppermute | solution.py:271
  179.5 58.2 %collective-permute-start.24 = (f32[16,32,256]{2,1,0:T(8,128)S(1)}, f32[16,32,256]{2,1,0:T(8,128)S(1)}, u32[]{:S(2)}, u32[]{:S(2)}) collective-permute-start(f32[16,32,256]{2,1,0:T(8,128)S(1)} %get-tuple-element.18), channel_id=1, source_target_pairs={{0,1},{1,2},{2,3},{3,0},{4,5},{5,6},{6,7},{7,4},{8,9},{9,10},{10,1... | collective-permute-start | bytes 1572872 | tf_op jit(solution)/shard_map/ppermute | solution.py:271
  180.2 66.7 %collective-permute-start.25 = (f32[16,32,256]{2,1,0:T(8,128)S(1)}, f32[16,32,256]{2,1,0:T(8,128)S(1)}, u32[]{:S(2)}, u32[]{:S(2)}) collective-permute-start(f32[16,32,256]{2,1,0:T(8,128)S(1)} %get-tuple-element.19), channel_id=1, source_target_pairs={{0,2},{1,3},{2,0},{3,1},{4,6},{5,7},{6,4},{7,5},{8,10},{9,11},{10,... | collective-permute-start | bytes 1572872 | tf_op jit(solution)/shard_map/ppermute | solution.py:271
  191.1 59.9 %collective-permute-start.26 = (f32[16,32,256]{2,1,0:T(8,128)S(1)}, f32[16,32,256]{2,1,0:T(8,128)S(1)}, u32[]{:S(2)}, u32[]{:S(2)}) collective-permute-start(f32[16,32,256]{2,1,0:T(8,128)S(1)} %get-tuple-element.20), channel_id=1, source_target_pairs={{0,3},{1,0},{2,1},{3,2},{4,7},{5,4},{6,5},{7,6},{8,11},{9,8},{10,9... | collective-permute-start | bytes 1572872 | tf_op jit(solution)/shard_map/ppermute | solution.py:271
  (26 other events, 335.7 us)

commit v4 on v0

v4 whole, which is shorter than its diff:
```python
import functools

import jax
import jax.numpy as jnp
from jax import lax
from jax.experimental import pallas as pl
from jax.experimental.pallas import tpu as pltpu
from jax.sharding import PartitionSpec as P

PARTS = 2
TILE = 8
ANYWHERE = pl.BlockSpec(memory_space=pl.ANY)
SCALARS = pl.BlockSpec(memory_space=pltpu.SMEM)


def whole(array):
    return pl.BlockSpec(array.shape, lambda *_: (0,) * array.ndim)


def params(mib=48):
    return pltpu.CompilerParams(vmem_limit_bytes=mib * 1024 * 1024)


def matrix_kernel(pattern_ref, weights_ref, out_ref):
    terms, entries, modes = pattern_ref.shape
    rows = lax.broadcasted_iota(jnp.int32, (modes, modes), 0)
    for term in range(terms):
        flipped = jnp.zeros((modes, modes), jnp.float32)
        for entry in range(entries):
            hits = pattern_ref[term, entry : entry + 1, :] == rows
            flipped = flipped + jnp.where(hits, weights_ref[term, entry : entry + 1, :], 0.0)
        coupling = 0.5 * (flipped + flipped.T)
        high = coupling.astype(jnp.bfloat16)
        at = slice(term * modes, (term + 1) * modes)
        out_ref[:modes, at] = high
        out_ref[modes:, at] = (coupling - high.astype(jnp.float32)).astype(jnp.bfloat16)


def coupling_matrices(pattern, weights):
    terms, modes, _ = pattern.shape
    pattern, weights = jnp.swapaxes(pattern, 1, 2), jnp.swapaxes(weights, 1, 2)
    shape = (2 * modes, terms * modes)
    return pl.pallas_call(
        matrix_kernel,
        grid=(1,),
        in_specs=[whole(pattern), whole(weights)],
        out_specs=pl.BlockSpec(shape, lambda i: (0, 0)),
        out_shape=jax.ShapeDtypeStruct(shape, jnp.bfloat16),
        compiler_params=params(),
        name="coupling",
    )(pattern, weights)


def target(me_ref, shift, owners):
    block = lax.rem(me_ref[0] + shift, owners)
    return block // (owners // 2), lax.rem(block, owners // 2)


def edge_count(halves):
    return 1 if halves == 2 else 2


def tile_specs(modes, height, width, shift, owners, part_rows):
    halves = owners // 2
    half_tiles = height // halves // TILE

    def spec(index):
        def place(i, me_ref):
            _, half = target(me_ref, shift, owners)
            return 0, jnp.clip(half * half_tiles + index, 0, height // TILE - 1), 0

        return pl.BlockSpec((modes, TILE, width), place)

    return [spec(part_rows // TILE), spec(-1), spec(half_tiles)]


def write_edges(out_ref, at, half, halves, before_ref, after_ref):
    before = jnp.swapaxes(before_ref[...], 0, 1)[TILE - 1]
    after = jnp.swapaxes(after_ref[...], 0, 1)[0]
    if halves == 2:
        out_ref[at] = jnp.where(half == 1, before, after)
    else:
        out_ref[at] = jnp.where(half > 0, before, 0.0)
        out_ref[at + 1] = jnp.where(half < halves - 1, after, 0.0)


def pack_kernel(shifts, owners, extras, me_ref, *refs):
    halves = owners // 2
    per_field = 4 if extras else 1
    outs = refs[-len(shifts) :]
    for index, shift in enumerate(shifts):
        field, half = target(me_ref, shift, owners)
        out_ref = outs[index]
        for which in range(2):
            mine = refs[(2 * index + which) * per_field : (2 * index + which + 1) * per_field]

            @pl.when(field == which)
            def _(mine=mine, out_ref=out_ref, half=half):
                rows = mine[0].shape[1]
                out_ref[:rows] = jnp.swapaxes(mine[0][...], 0, 1)
                if extras:
                    out_ref[rows] = jnp.swapaxes(mine[1][...], 0, 1)[0]
                    write_edges(out_ref, rows + 1, half, halves, mine[2], mine[3])


def pack(me, state, adjoint, shifts, part, rows, owners, earlier):
    modes, height, width = state.shape
    extras = part == 0
    count = rows + (1 + edge_count(owners // 2) if extras else 0)
    in_specs, operands = [], []
    for shift in shifts:

        def place(i, me_ref, shift=shift):
            return 0, target(me_ref, shift, owners)[1] * PARTS + part, 0

        specs = [pl.BlockSpec((modes, rows, width), place)]
        if extras:
            specs += tile_specs(modes, height, width, shift, owners, rows)
        for array in (state, adjoint):
            in_specs += specs
            operands += [array] * len(specs)
    return pl.pallas_call(
        functools.partial(pack_kernel, shifts, owners, extras),
        grid_spec=pltpu.PrefetchScalarGridSpec(
            num_scalar_prefetch=1,
            grid=(1,),
            in_specs=in_specs + [ANYWHERE] * len(earlier),
            out_specs=[pl.BlockSpec((count, modes, width), lambda i, me_ref: (0, 0, 0))] * len(shifts),
        ),
        out_shape=[jax.ShapeDtypeStruct((count, modes, width), jnp.float32)] * len(shifts),
        compiler_params=params(60),
        name="pack",
    )(me, *operands, *earlier)


def pack_own_kernel(owners, me_ref, *refs):
    coef_ref, out_ref = refs[-2:]
    halves = owners // 2
    field, half = target(me_ref, 0, owners)
    for which in range(2):
        mine = refs[which * 3 : which * 3 + 3]

        @pl.when(field == which)
        def _(mine=mine):
            rows = mine[0].shape[1]
            out_ref[:rows] = jnp.swapaxes(mine[0][...], 0, 1)
            write_edges(out_ref, rows, half, halves, mine[1], mine[2])

    terms = coef_ref.shape[0]
    out_ref[out_ref.shape[0] - terms :] = coef_ref[...]


def pack_own(me, state, adjoint, coef, owners):
    modes, height, width = state.shape
    halves = owners // 2
    half_rows = height // halves
    terms = coef.shape[0]
    count = half_rows + edge_count(halves) + terms

    def place(i, me_ref):
        return 0, target(me_ref, 0, owners)[1], 0

    specs = [pl.BlockSpec((modes, half_rows, width), place)]
    specs += tile_specs(modes, height, width, 0, owners, half_rows // PARTS)[1:]
    return pl.pallas_call(
        functools.partial(pack_own_kernel, owners),
        grid_spec=pltpu.PrefetchScalarGridSpec(
            num_scalar_prefetch=1,
            grid=(1,),
            in_specs=specs + specs + [pl.BlockSpec((terms, half_rows, width), place)],
            out_specs=pl.BlockSpec((count, modes, width), lambda i, me_ref: (0, 0, 0)),
        ),
        out_shape=jax.ShapeDtypeStruct((count, modes, width), jnp.float32),
        compiler_params=params(60),
        name="pack_own",
    )(me, *([state] * 3 + [adjoint] * 3), coef)


def operator_kernel(shifts, rows, terms, part, me_ref, coef_ref, matrix_ref, *refs):
    owners = len(shifts) + 1
    own, own_below, own_above, below, above = refs[:5]
    head = refs[5 : 5 + len(shifts)]
    pieces = refs[5 + part * len(shifts) : 5 + (part + 1) * len(shifts)]
    outs = refs[-owners - 6 : -6]
    slots, mixed, faces = ((refs[-6], refs[-5]), (refs[-4], refs[-3])), refs[-2], refs[-1]
    _, block, width = own.shape
    modes = owners * block
    halves = owners // 2
    half_rows = rows * PARTS
    edges = edge_count(halves)
    me = me_ref[0]
    half = lax.rem(me, halves)
    step = 16
    lanes = lax.broadcasted_iota(jnp.int32, (step, width), 1)
    last = rows - 1

    def with_sides(values, lane):
        left = jnp.where(lane == 0, 0.0, pltpu.roll(values, 1, 1))
        right = jnp.where(lane == width - 1, 0.0, pltpu.roll(values, width - 1, 1))
        return left, right

    first_row = half * half_rows + part * rows
    height = coef_ref.shape[1]
    face_lanes = lax.broadcasted_iota(jnp.int32, (rows, width), 1)
    face_rows = lax.broadcasted_iota(jnp.int32, (rows, width), 0)
    for term in range(terms):
        centre = coef_ref[term, pl.ds(pl.multiple_of(first_row, TILE), rows), :]
        row_before = coef_ref[term, pl.ds(jnp.maximum(first_row - 1, 0), 1), :]
        row_after = coef_ref[term, pl.ds(jnp.minimum(first_row + rows, height - 1), 1), :]
        row_before = jnp.where(first_row > 0, row_before, 0.0)
        row_after = jnp.where(first_row + rows < height, row_after, 0.0)
        up = jnp.where(face_rows == 0, row_before, pltpu.roll(centre, 1, 0))
        down = jnp.where(face_rows == last, row_after, pltpu.roll(centre, last, 0))
        left, right = with_sides(centre, face_lanes)
        at = half_rows + edges + term
        here = slice(part * rows, (part + 1) * rows)
        others = (own_below[at, here, :], own_above[at, here, :], up, down, left, right)
        for side, other in enumerate(others):
            faces[6 * term + side] = 0.5 * (centre + other)

    def edge(index, which, here):
        ref, at = (head[index - 1], rows + 1) if index else (own, half_rows)
        if halves == 2:
            return jnp.where(half == 1 - which, ref[at, here, :], 0.0)
        return ref[at + which, here, :]

    def stencil(row, place, slot):
        high, low = slots[slot]
        for index, shift in enumerate([0] + shifts):
            source = lax.rem(me + owners - shift, owners)
            if index:
                base, near, ref, below_ref, above_ref = 0, (index - 1) * rows, pieces[index - 1], below, above
            else:
                base, near, ref, below_ref, above_ref = part * rows, part * rows, own, own_below, own_above
            for start in range(0, block, step):
                here = pl.ds(start, step)
                centre = ref[base + row, here, :]
                if place != "first":
                    up = ref[base + row - 1, here, :]
                elif part == 0:
                    up = edge(index, 0, here)
                else:
                    up = head[index - 1][last, here, :] if index else own[base - 1, here, :]
                if place != "last":
                    down = ref[base + row + 1, here, :]
                elif part == 0:
                    down = ref[base + rows, here, :]
                else:
                    down = edge(index, 1, here)
                left, right = with_sides(centre, lanes)
                others = (below_ref[near + row, here, :], above_ref[near + row, here, :], up, down, left, right)
                slopes = [centre - other for other in others]
                for term in range(terms):
                    total = faces[6 * term, pl.ds(row, 1), :] * slopes[0]
                    for side in range(1, 6):
                        total = total + faces[6 * term + side, pl.ds(row, 1), :] * slopes[side]
                    rounded = total.astype(jnp.bfloat16)
                    at = pl.ds(pl.multiple_of(source * block + (term * modes + start), step), step)
                    high[at, :] = rounded
                    low[at, :] = (total - rounded.astype(jnp.float32)).astype(jnp.bfloat16)

    def mix(row, slot):
        high, low = slots[slot]
        both = jnp.dot(matrix_ref[...], high[...], preferred_element_type=jnp.float32)
        rest = jnp.dot(matrix_ref[:modes, :], low[...], preferred_element_type=jnp.float32)
        mixed[...] = both[:modes] + both[modes:] + rest
        for index, shift in enumerate([0] + shifts):
            owner = lax.rem(me + shift, owners)
            outs[index][row] = mixed[pl.ds(pl.multiple_of(owner * block, block), block), :]

    def two_rows(pair, carry):
        row = 2 * pair
        stencil(row + 1, "middle", 1)
        mix(row, 0)
        stencil(row + 2, "middle", 0)
        mix(row + 1, 1)
        return carry

    stencil(0, "first", 0)
    lax.fori_loop(0, rows // 2 - 1, two_rows, 0)
    stencil(last, "last", 1)
    mix(last - 1, 0)
    mix(last, 1)


def apply_operator(me, coef, matrix, own, own_near, pieces, near, part, rows, shifts):
    _, block, width = own.shape
    owners = len(shifts) + 1
    modes = owners * block
    terms = coef.shape[0]
    operands = [coef, matrix, own, *own_near, *near]
    for piece in pieces[: part + 1]:
        operands += piece
    shape = (rows, block, width)
    return pl.pallas_call(
        functools.partial(operator_kernel, shifts, rows, terms, part),
        grid=(1,),
        in_specs=[SCALARS] + [whole(array) for array in operands],
        out_specs=[pl.BlockSpec(shape, lambda i: (0, 0, 0))] * owners,
        out_shape=[jax.ShapeDtypeStruct(shape, jnp.float32)] * owners,
        scratch_shapes=[pltpu.VMEM((terms * modes, width), jnp.bfloat16)] * 4
        + [pltpu.VMEM((modes, width), jnp.float32), pltpu.VMEM((6 * terms, rows, width), jnp.float32)],
        compiler_params=params(),
        name="operator",
    )(me, *operands)


def finish_kernel(shifts, me_ref, *refs):
    owners = len(shifts) + 1
    halves = owners // 2
    mixed = refs[:owners]
    state_ref, control_ref = refs[owners : owners + 2]
    state_out, adjoint_out = refs[-2:]
    half = pl.program_id(0)
    for index, shift in enumerate([0] + shifts):
        source = lax.rem(me_ref[0] + owners - shift, owners)

        @pl.when(source == half)
        def _(index=index):
            adjoint_out[...] = jnp.swapaxes(mixed[index][...], 0, 1) - control_ref[...]

        @pl.when(source == halves + half)
        def _(index=index):
            state_out[...] = state_ref[...] + jnp.swapaxes(mixed[index][...], 0, 1)


def finish(me, mixed, state, control, outputs, part, shifts):
    modes, _, width = state.shape
    owners = len(mixed)
    rows = mixed[0].shape[0]
    block = pl.BlockSpec((modes, rows, width), lambda h: (0, h * PARTS + part, 0))
    in_specs = [SCALARS] + [whole(m) for m in mixed] + [block] * 2
    operands = [me, *mixed, state, control]
    aliases = {}
    if outputs is not None:
        aliases = {len(operands) + i: i for i in range(2)}
        in_specs += [ANYWHERE] * 2
        operands += list(outputs)
    return pl.pallas_call(
        functools.partial(finish_kernel, shifts),
        grid=(owners // 2,),
        in_specs=in_specs,
        out_specs=[block] * 2,
        out_shape=[jax.ShapeDtypeStruct(state.shape, jnp.float32)] * 2,
        input_output_aliases=aliases,
        compiler_params=params(60),
        name="finish",
    )(*operands)


def shards(state, control, adjoint, coefficient, pattern, weights):
    shape = state.shape
    modes, _, height, width = shape
    control_residual = 0.5 * control - adjoint
    state, control, adjoint = (a.reshape(modes, height, width) for a in (state, control, adjoint))
    coef = coefficient[:, 0]
    owners = lax.axis_size("mode")
    rows = height // (owners // 2) // PARTS
    planes = lax.axis_size("space")
    forward = [(i, i + 1) for i in range(planes - 1)]
    backward = [(i + 1, i) for i in range(planes - 1)]
    me = lax.axis_index("mode").astype(jnp.int32).reshape(1)
    shifts = sorted(range(1, owners), key=lambda s: min(s, owners - s))

    def move(array, shift):
        return lax.ppermute(array, "mode", [(i, (i + shift) % owners) for i in range(owners)])

    def beside(array):
        return lax.ppermute(array, "space", forward), lax.ppermute(array, "space", backward)

    matrix = coupling_matrices(pattern, weights)
    pieces, near = [], []
    for part in range(PARTS):
        if part:
            own = pack_own(me, state, adjoint, coef, owners)
            own_near = beside(own)
        packed = pack(me, state, adjoint, shifts, part, rows, owners, list(own_near) if part else [])
        arrived = [move(piece, shift) for piece, shift in zip(packed, shifts)]
        pieces.append(arrived)
        near.append(beside(jnp.concatenate([piece[:rows] for piece in arrived])))

    outputs = None
    for part in range(PARTS):
        mixed = apply_operator(me, coef, matrix, own, own_near, pieces, near[part], part, rows, shifts)
        mixed = [mixed[0]] + [move(m, shift) for m, shift in zip(mixed[1:], shifts)]
        outputs = finish(me, mixed, state, control, outputs, part, shifts)
    return outputs[0].reshape(shape), control_residual, outputs[1].reshape(shape)


def solution(mesh):
    split = P("mode", "space", None, None)
    in_specs = (split, split, split, P(None, "space", None, None), P(), P())
    return jax.shard_map(shards, mesh=mesh, in_specs=in_specs, out_specs=(split, split, split), check_vma=False)
```

time: 1140 us -> 238 us (0.21)
  waiting for transfers between devices: 862 us -> 125 us
  other arithmetic: 131 us -> 1.89 us
  local copies, waits for them, and re-layouts: 93.9 us -> 6.63 us
  Pallas kernels: 0 us -> 48.9 us
  starting transfers between devices: 5.29 us -> 52.6 us
  matrix products: 28.9 us -> 0 us
  between operations: 14.1 us -> 0.91 us
    ppermute x2 -> x18, waiting for transfers between devices: 580 us -> 125 us  [the longest x12 95.8 us: move(): lax.ppermute(array, 'mode', [(i, (i + shift) % owners) for i in range(own...]
    all_gather x1 -> x0, waiting for transfers between devices: 282 us -> none  [shards(): lax.all_gather(local, 'mode', axis=0, tiled=True)]
    add x1 -> x0, other arithmetic: 80.2 us -> none  [shards(): result = result + diffuse_slab(coef_ext[term], block)]
    pallas_call x0 -> x8, Pallas kernels: none -> 48.9 us  [the longest x2 30.1 us: apply_operator(): pl.pallas_call(functools.partial(operator_kernel, shifts, rows, terms, pa...]
    ppermute x2 -> x18, starting transfers between devices: 5.25 us -> 52.6 us  [the longest x12 33.2 us: move(): lax.ppermute(array, 'mode', [(i, (i + shift) % owners) for i in range(own...]
    squeeze x8 -> x0, local copies, waits for them, and re-layouts: 34.4 us -> none  [the longest x7 34.4 us: diffuse_slab(): centre_field = field_ext[:, 1]]
    reshape x1 -> x0, local copies, waits for them, and re-layouts: 31.2 us -> none  [shards(): slabs = mixed_terms.reshape(terms * 2 * modes_here, 1, width_y, width_z)]
    concatenate x1, other arithmetic: 30.3 us -> 0.16 us  [shards(): near.append(beside(jnp.concatenate([piece[:rows] for piece in arrived])))]
  transfers between devices with their start and end apart: 3 -> 18, of which waited for: 3 -> 9; matrix products, arithmetic and copies ran while one was open for 6% -> 2% of each run, Pallas kernels for 0% -> 18%
where the time goes in v4:
time: 238 us; the launch traced here: 236 us
  waiting for transfers between devices  125 us (53%)
  starting transfers between devices  52.6 us (22%)
  Pallas kernels  48.9 us (21%)
  local copies, waits for them, and re-layouts  6.63 us (3%)
    ppermute x12, waiting for transfers between devices, move(): lax.ppermute(array, 'mode', [(i, (i + shift) % owners) for i in range(own...  95.8 us
    ppermute x12, starting transfers between devices, move(): lax.ppermute(array, 'mode', [(i, (i + shift) % owners) for i in range(own...  33.2 us
    pallas_call x2, Pallas kernels, apply_operator(): pl.pallas_call(functools.partial(operator_kernel, shifts, rows, terms, pa...  30.1 us
    ppermute x3, waiting for transfers between devices, beside(): lax.ppermute(array, 'space', forward)  26.8 us
    ppermute x3, starting transfers between devices, beside(): lax.ppermute(array, 'space', backward)  13.6 us
    pallas_call x2, Pallas kernels, pack(): pl.pallas_call(functools.partial(pack_kernel, shifts, owners, extras), gr...  8.35 us
    pallas_call x2, Pallas kernels, finish(): pl.pallas_call(functools.partial(finish_kernel, shifts), grid=(owners //...  6.86 us
    ppermute x3, starting transfers between devices, beside(): lax.ppermute(array, 'space', forward)  5.87 us
  transfers between devices with their start and end apart: 18, of which 9 were waited for; matrix products, arithmetic and copies ran while one was open for 2% of the time, Pallas kernels for 18%

profile of v4, /device:TPU:4, one launch (start us, length us, event | category | flops | bytes accessed | tf_op | source)
XLA Modules:
  0.0 235.9 jit_solution(2111995577623413699)
XLA Ops:
  0.6 3.2 %pack_own.1.refs_0_ = f32[40,32,256]{2,1,0:T(8,128)} custom-call(s32[1]{0:T(128)} %bitcast.me_ref, f32[32,64,256]{2,1,0:T(8,128)} %bitcast.18, f32[32,64,256]{2,1,0:T(8,128)} %bitcast.19, f32[32,64,256]{2,1,0:T(8,128)} %bitcast.20, f32[32,64,256]{2,1,0:T(8,128)} %bitcast.38, f32[32,64,256]{2,1,0:T(8,128)} %bitcast.39, f32[32,64,256]{2,1,0:T(8,128)} %bitcast.40, ...), custom_call_target="tpu_custom_call" | custom-call | tf_op jit(solution)/shard_map/pack_own/pallas_call | solution.py:165
  3.9 1.9 collective-permute-start
  5.8 4.5 %collective-permute-start.1 = (f32[40,32,256]{2,1,0:T(8,128)}, f32[40,32,256]{2,1,0:T(8,128)}, u32[]{:S(2)}, u32[]{:S(2)}) collective-permute-start(f32[40,32,256]{2,1,0:T(8,128)} %pack_own.1.refs_0_), channel_id=1, source_target_pairs={{4,0},{8,4},{12,8},{16,12},{20,16},{24,20},{28,24},{5,1},{9,5},{13... | collective-permute-start | bytes 3932168 | tf_op jit(solution)/shard_map/ppermute | solution.py:369
  10.3 5.0 %pack.3 = (f32[18,32,256]{2,1,0:T(8,128)}, f32[18,32,256]{2,1,0:T(8,128)}, f32[18,32,256]{2,1,0:T(8,128)}) custom-call(s32[1]{0:T(128)} %bitcast.me_ref, f32[32,64,256]{2,1,0:T(8,128)} %bitcast.21, f32[32,64,256]{2,1,0:T(8,128)} %bitcast.22, f32[32,64,256]{2,1,0:T(8,128)} %bitcast.23, f32[32,64,256]{2,1,0:T(8,128)} %bitcast.24, f32[32,64,256]{2,1,0:T(8,128)} %bitcast.41, ...), custom_call_target="tpu_custom_call" | custom-call | tf_op jit(solution)/shard_map/pack/pallas_call | solution.py:122
  15.3 2.6 %collective-permute-start.9 = (f32[18,32,256]{2,1,0:T(8,128)}, f32[18,32,256]{2,1,0:T(8,128)S(1)}, u32[]{:S(2)}, u32[]{:S(2)}) collective-permute-start(f32[18,32,256]{2,1,0:T(8,128)} %get-tuple-element.26), channel_id=1, source_target_pairs={{0,2},{1,3},{2,0},{3,1},{4,6},{5,7},{6,4},{7,5},{8,10},{9,11},{10,... | collective-permute-start | bytes 1769480 | tf_op jit(solution)/shard_map/ppermute | solution.py:366
  17.9 1.5 collective-permute-start.8
  20.0 15.2 %collective-permute-done.refs_6_.refs_1_ = f32[40,32,256]{2,1,0:T(8,128)S(1)} collective-permute-done((f32[40,32,256]{2,1,0:T(8,128)}, f32[40,32,256]{2,1,0:T(8,128)S(1)}, u32[]{:S(2)}, u32[]{:S(2)}) %collective-permute-start) | collective-permute-done | bytes 1310752 | tf_op jit(solution)/shard_map/ppermute | solution.py:369
  35.1 1.0 collective-permute-done.1.refs_7_.refs_2_
  36.2 3.3 %pack.2 = (f32[16,32,256]{2,1,0:T(8,128)}, f32[16,32,256]{2,1,0:T(8,128)}, f32[16,32,256]{2,1,0:T(8,128)}) custom-call(s32[1]{0:T(128)} %bitcast.me_ref, f32[32,64,256]{2,1,0:T(8,128)} %bitcast.33, f32[32,64,256]{2,1,0:T(8,128)} %bitcast.53, f32[32,64,256]{2,1,0:T(8,128)} %bitcast.34, f32[32,64,256]{2,1,0:T(8,128)} %bitcast.54, f32[32,64,256]{2,1,0:T(8,128)} %bitcast.35, ...), custom_call_target="tpu_custom_call" | custom-call | tf_op jit(solution)/shard_map/pack/pallas_call | solution.py:122
  39.5 1.6 collective-permute-start.2
  41.1 2.3 collective-permute-start.3
  43.4 23.3 %collective-permute-done.9.refs_7_ = f32[18,32,256]{2,1,0:T(8,128)S(1)} collective-permute-done((f32[18,32,256]{2,1,0:T(8,128)}, f32[18,32,256]{2,1,0:T(8,128)S(1)}, u32[]{:S(2)}, u32[]{:S(2)}) %collective-permute-start.9) | collective-permute-done | bytes 589856 | tf_op jit(solution)/shard_map/ppermute | solution.py:366
  66.8 15.8 %collective-permute-start.4 = (f32[16,32,256]{2,1,0:T(8,128)S(1)}, f32[16,32,256]{2,1,0:T(8,128)S(1)}, u32[]{:S(2)}, u32[]{:S(2)}) collective-permute-start(f32[16,32,256]{2,1,0:T(8,128)S(1)} %copy-done.19), channel_id=1, source_target_pairs={{0,2},{1,3},{2,0},{3,1},{4,6},{5,7},{6,4},{7,5},{8,10},{9,11},{10,... | collective-permute-start | bytes 1572872 | tf_op jit(solution)/shard_map/ppermute | solution.py:366
  82.9 2.1 collective-permute-start.13
  85.0 4.5 %collective-permute-start.14 = (f32[48,32,256]{2,1,0:T(8,128)S(1)}, f32[48,32,256]{2,1,0:T(8,128)S(1)}, u32[]{:S(2)}, u32[]{:S(2)}) collective-permute-start(f32[48,32,256]{2,1,0:T(8,128)S(1)} %pad_maximum_fusion), channel_id=1, source_target_pairs={{4,0},{8,4},{12,8},{16,12},{20,16},{24,20},{28,24},{5,1},{9,5},{13... | collective-permute-start | bytes 4718600 | tf_op jit(solution)/shard_map/ppermute | solution.py:369
  91.2 22.4 %collective-permute-done.4.refs_10_ = f32[16,32,256]{2,1,0:T(8,128)S(1)} collective-permute-done((f32[16,32,256]{2,1,0:T(8,128)S(1)}, f32[16,32,256]{2,1,0:T(8,128)S(1)}, u32[]{:S(2)}, u32[]{:S(2)}) %collective-permute-start.4) | collective-permute-done | bytes 524320 | tf_op jit(solution)/shard_map/ppermute | solution.py:366
  114.4 1.9 collective-permute-start.5
  116.3 4.5 %collective-permute-start.6 = (f32[48,32,256]{2,1,0:T(8,128)}, f32[48,32,256]{2,1,0:T(8,128)}, u32[]{:S(2)}, u32[]{:S(2)}) collective-permute-start(f32[48,32,256]{2,1,0:T(8,128)} %constant_dynamic-update-slice_fusion), channel_id=1, source_target_pairs={{4,0},{8,4},{12,8},{16,12},{20,16},{24,20},{28,24},{5,1},{9,5},{13... | collective-permute-start | bytes 4718600 | tf_op jit(solution)/shard_map/ppermute | solution.py:369
  121.3 1.3 collective-permute-done.14.refs_4_
  122.6 1.1 copy-done.11
  123.8 14.8 %operator.3 = (f32[16,32,256]{2,1,0:T(8,128)S(1)}, f32[16,32,256]{2,1,0:T(8,128)S(1)}, f32[16,32,256]{2,1,0:T(8,128)S(1)}, f32[16,32,256]{2,1,0:T(8,128)S(1)}) custom-call(s32[1]{0:T(128)} %bitcast.me_ref, f32[7,64,256]{2,1,0:T(8,128)S(1)} %bitcast.14, bf16[256,896]{1,0:T(8,128)(2,1)S(1)} %coupling.1.matrix_ref, f32[40,32,256]{2,1,0:T(8,128)S(1)} %copy-done, ...), custom_call_target="tpu_custom_call" | custom-call | tf_op jit(solution)/shard_map/operator/pallas_call | solution.py:295
  139.1 3.4 %collective-permute-start.16 = (f32[16,32,256]{2,1,0:T(8,128)S(1)}, f32[16,32,256]{2,1,0:T(8,128)S(1)}, u32[]{:S(2)}, u32[]{:S(2)}) collective-permute-start(f32[16,32,256]{2,1,0:T(8,128)S(1)} %get-tuple-element.33), channel_id=1, source_target_pairs={{0,3},{1,0},{2,1},{3,2},{4,7},{5,4},{6,5},{7,6},{8,11},{9,8},{10,9... | collective-permute-start | bytes 1572872 | tf_op jit(solution)/shard_map/ppermute | solution.py:366
  142.5 11.7 %collective-permute-done.5.refs_3_ = f32[48,32,256]{2,1,0:T(8,128)S(1)} collective-permute-done((f32[48,32,256]{2,1,0:T(8,128)}, f32[48,32,256]{2,1,0:T(8,128)S(1)}, u32[]{:S(2)}, u32[]{:S(2)}) %collective-permute-start.5) | collective-permute-done | bytes 1572896 | tf_op jit(solution)/shard_map/ppermute | solution.py:369
  154.2 1.1 copy-done.12
  155.3 15.3 %operator.2 = (f32[16,32,256]{2,1,0:T(8,128)S(1)}, f32[16,32,256]{2,1,0:T(8,128)S(1)}, f32[16,32,256]{2,1,0:T(8,128)S(1)}, f32[16,32,256]{2,1,0:T(8,128)S(1)}) custom-call(s32[1]{0:T(128)} %bitcast.me_ref, f32[7,64,256]{2,1,0:T(8,128)S(1)} %bitcast.15, bf16[256,896]{1,0:T(8,128)(2,1)S(1)} %coupling.1.matrix_ref, f32[40,32,256]{2,1,0:T(8,128)} %pack_own.1.refs_0_, ...), custom_call_target="tpu_custom_call" | custom-call | tf_op jit(solution)/shard_map/operator/pallas_call | solution.py:295
  170.7 3.8 %collective-permute-start.11 = (f32[16,32,256]{2,1,0:T(8,128)S(1)}, f32[16,32,256]{2,1,0:T(8,128)S(1)}, u32[]{:S(2)}, u32[]{:S(2)}) collective-permute-start(f32[16,32,256]{2,1,0:T(8,128)S(1)} %get-tuple-element.29), channel_id=1, source_target_pairs={{0,3},{1,0},{2,1},{3,2},{4,7},{5,4},{6,5},{7,6},{8,11},{9,8},{10,9... | collective-permute-start | bytes 1572872 | tf_op jit(solution)/shard_map/ppermute | solution.py:366
  174.5 1.1 collective-permute-start.12
  175.6 1.7 multiply_subtract_fusion
  177.4 22.9 %collective-permute-done.17.refs_3_ = f32[16,32,256]{2,1,0:T(8,128)S(1)} collective-permute-done((f32[16,32,256]{2,1,0:T(8,128)S(1)}, f32[16,32,256]{2,1,0:T(8,128)S(1)}, u32[]{:S(2)}, u32[]{:S(2)}) %collective-permute-start.17) | collective-permute-done | bytes 524320 | tf_op jit(solution)/shard_map/ppermute | solution.py:366
  201.1 3.4 %finish.2 = (f32[32,64,256]{2,1,0:T(8,128)}, f32[32,64,256]{2,1,0:T(8,128)}) custom-call(s32[1]{0:T(128)} %bitcast.me_ref, f32[16,32,256]{2,1,0:T(8,128)} %copy-done.3, f32[16,32,256]{2,1,0:T(8,128)} %copy-done.13, f32[16,32,256]{2,1,0:T(8,128)} %copy-done.14, f32[16,32,256]{2,1,0:T(8,128)} %copy-done.15, f32[32,64,256]{2,1,0:T(8,128)} %bitcast.36, ...), custom_call_target="tpu_custom_call" | custom-call | tf_op jit(solution)/shard_map/finish/pallas_call | solution.py:339
  205.3 26.4 %collective-permute-done.12.refs_3_ = f32[16,32,256]{2,1,0:T(8,128)S(1)} collective-permute-done((f32[16,32,256]{2,1,0:T(8,128)S(1)}, f32[16,32,256]{2,1,0:T(8,128)S(1)}, u32[]{:S(2)}, u32[]{:S(2)}) %collective-permute-start.12) | collective-permute-done | bytes 524320 | tf_op jit(solution)/shard_map/ppermute | solution.py:366
  232.5 3.4 %finish.3 = (f32[32,64,256]{2,1,0:T(8,128)}, f32[32,64,256]{2,1,0:T(8,128)}) custom-call(s32[1]{0:T(128)} %bitcast.me_ref, f32[16,32,256]{2,1,0:T(8,128)} %copy-done.4, f32[16,32,256]{2,1,0:T(8,128)} %copy-done.16, f32[16,32,256]{2,1,0:T(8,128)} %copy-done.17, f32[16,32,256]{2,1,0:T(8,128)} %copy-done.18, ...), custom_call_target="tpu_custom_call", output_to_operand_aliasing={{0}: (7, {}), {1}: (8, {})} | custom-call | tf_op jit(solution)/shard_map/finish/pallas_call | solution.py:339
  (60 shorter events, 6.8 us)
Async XLA Ops:
  3.9 31.3 %collective-permute-start = (f32[40,32,256]{2,1,0:T(8,128)}, f32[40,32,256]{2,1,0:T(8,128)S(1)}, u32[]{:S(2)}, u32[]{:S(2)}) collective-permute-start(f32[40,32,256]{2,1,0:T(8,128)} %pack_own.1.refs_0_), channel_id=1, source_target_pairs={{0,4},{4,8},{8,12},{12,16},{16,20},{20,24},{24,28},{1,5},{5,9},{9,... | collective-permute-start | bytes 3932168 | tf_op jit(solution)/shard_map/ppermute | solution.py:369
  5.8 30.4 %collective-permute-start.1 = (f32[40,32,256]{2,1,0:T(8,128)}, f32[40,32,256]{2,1,0:T(8,128)}, u32[]{:S(2)}, u32[]{:S(2)}) collective-permute-start(f32[40,32,256]{2,1,0:T(8,128)} %pack_own.1.refs_0_), channel_id=1, source_target_pairs={{4,0},{8,4},{12,8},{16,12},{20,16},{24,20},{28,24},{5,1},{9,5},{13... | collective-permute-start | bytes 3932168 | tf_op jit(solution)/shard_map/ppermute | solution.py:369
  15.3 51.3 %collective-permute-start.9 = (f32[18,32,256]{2,1,0:T(8,128)}, f32[18,32,256]{2,1,0:T(8,128)S(1)}, u32[]{:S(2)}, u32[]{:S(2)}) collective-permute-start(f32[18,32,256]{2,1,0:T(8,128)} %get-tuple-element.26), channel_id=1, source_target_pairs={{0,2},{1,3},{2,0},{3,1},{4,6},{5,7},{6,4},{7,5},{8,10},{9,11},{10,... | collective-permute-start | bytes 1769480 | tf_op jit(solution)/shard_map/ppermute | solution.py:366
  17.9 48.8 %collective-permute-start.8 = (f32[18,32,256]{2,1,0:T(8,128)}, f32[18,32,256]{2,1,0:T(8,128)S(1)}, u32[]{:S(2)}, u32[]{:S(2)}) collective-permute-start(f32[18,32,256]{2,1,0:T(8,128)} %get-tuple-element.25), channel_id=1, source_target_pairs={{0,3},{1,0},{2,1},{3,2},{4,7},{5,4},{6,5},{7,6},{8,11},{9,8},{10,9... | collective-permute-start | bytes 1769480 | tf_op jit(solution)/shard_map/ppermute | solution.py:366
  19.4 47.3 %collective-permute-start.7 = (f32[18,32,256]{2,1,0:T(8,128)}, f32[18,32,256]{2,1,0:T(8,128)S(1)}, u32[]{:S(2)}, u32[]{:S(2)}) collective-permute-start(f32[18,32,256]{2,1,0:T(8,128)} %get-tuple-element.24), channel_id=1, source_target_pairs={{0,1},{1,2},{2,3},{3,0},{4,5},{5,6},{6,7},{7,4},{8,9},{9,10},{10,1... | collective-permute-start | bytes 1769480 | tf_op jit(solution)/shard_map/ppermute | solution.py:366
  39.5 50.0 %collective-permute-start.2 = (f32[16,32,256]{2,1,0:T(8,128)}, f32[16,32,256]{2,1,0:T(8,128)S(1)}, u32[]{:S(2)}, u32[]{:S(2)}) collective-permute-start(f32[16,32,256]{2,1,0:T(8,128)} %get-tuple-element.21), channel_id=1, source_target_pairs={{0,1},{1,2},{2,3},{3,0},{4,5},{5,6},{6,7},{7,4},{8,9},{9,10},{10,1... | collective-permute-start | bytes 1572872 | tf_op jit(solution)/shard_map/ppermute | solution.py:366
  41.1 25.7 %copy-start.19 = (f32[16,32,256]{2,1,0:T(8,128)S(1)}, f32[16,32,256]{2,1,0:T(8,128)}, u32[]{:S(2)}) copy-start(f32[16,32,256]{2,1,0:T(8,128)} %get-tuple-element.23) | copy-start | bytes 1572868
  41.1 49.2 %collective-permute-start.3 = (f32[16,32,256]{2,1,0:T(8,128)}, f32[16,32,256]{2,1,0:T(8,128)S(1)}, u32[]{:S(2)}, u32[]{:S(2)}) collective-permute-start(f32[16,32,256]{2,1,0:T(8,128)} %get-tuple-element.22), channel_id=1, source_target_pairs={{0,3},{1,0},{2,1},{3,2},{4,7},{5,4},{6,5},{7,6},{8,11},{9,8},{10,9... | collective-permute-start | bytes 1572872 | tf_op jit(solution)/shard_map/ppermute | solution.py:366
  66.7 56.0 %copy-start.1 = (f32[18,32,256]{2,1,0:T(8,128)}, f32[18,32,256]{2,1,0:T(8,128)S(1)}, u32[]{:S(2)}) copy-start(f32[18,32,256]{2,1,0:T(8,128)S(1)} %collective-permute-done.9.refs_7_) | copy-start | bytes 1769476
  66.8 46.7 %collective-permute-start.4 = (f32[16,32,256]{2,1,0:T(8,128)S(1)}, f32[16,32,256]{2,1,0:T(8,128)S(1)}, u32[]{:S(2)}, u32[]{:S(2)}) collective-permute-start(f32[16,32,256]{2,1,0:T(8,128)S(1)} %copy-done.19), channel_id=1, source_target_pairs={{0,2},{1,3},{2,0},{3,1},{4,6},{5,7},{6,4},{7,5},{8,10},{9,11},{10,... | collective-permute-start | bytes 1572872 | tf_op jit(solution)/shard_map/ppermute | solution.py:366
  82.8 38.0 %copy-start.5 = (s32[7,128,4]{1,2,0:T(4,128)S(1)}, s32[7,128,4]{1,2,0:T(4,128)}, u32[]{:S(2)}) copy-start(s32[7,128,4]{1,2,0:T(4,128)} %param.10) | copy-start | bytes 43012
  82.9 38.0 %copy-start.6 = (f32[7,128,4]{1,2,0:T(4,128)S(1)}, f32[7,128,4]{1,2,0:T(4,128)}, u32[]{:S(2)}) copy-start(f32[7,128,4]{1,2,0:T(4,128)} %param.11) | copy-start | bytes 43012
  82.9 40.9 %copy-start = (f32[40,32,256]{2,1,0:T(8,128)S(1)}, f32[40,32,256]{2,1,0:T(8,128)}, u32[]{:S(2)}) copy-start(f32[40,32,256]{2,1,0:T(8,128)} %pack_own.1.refs_0_) | copy-start | bytes 3932164
  82.9 40.9 %copy-start.2 = (f32[7,1,64,256]{3,2,1,0:T(8,128)S(1)}, f32[7,1,64,256]{3,2,1,0:T(8,128)}, u32[]{:S(2)}) copy-start(f32[7,1,64,256]{3,2,1,0:T(8,128)} %param.9) | copy-start | bytes 1376260
  82.9 38.4 %collective-permute-start.13 = (f32[48,32,256]{2,1,0:T(8,128)S(1)}, f32[48,32,256]{2,1,0:T(8,128)S(1)}, u32[]{:S(2)}, u32[]{:S(2)}) collective-permute-start(f32[48,32,256]{2,1,0:T(8,128)S(1)} %pad_maximum_fusion), channel_id=1, source_target_pairs={{0,4},{4,8},{8,12},{12,16},{16,20},{20,24},{24,28},{1,5},{5,9},{9,... | collective-permute-start | bytes 4718600 | tf_op jit(solution)/shard_map/ppermute | solution.py:369
  85.0 37.7 %collective-permute-start.14 = (f32[48,32,256]{2,1,0:T(8,128)S(1)}, f32[48,32,256]{2,1,0:T(8,128)S(1)}, u32[]{:S(2)}, u32[]{:S(2)}) collective-permute-start(f32[48,32,256]{2,1,0:T(8,128)S(1)} %pad_maximum_fusion), channel_id=1, source_target_pairs={{4,0},{8,4},{12,8},{16,12},{20,16},{24,20},{28,24},{5,1},{9,5},{13... | collective-permute-start | bytes 4718600 | tf_op jit(solution)/shard_map/ppermute | solution.py:369
  114.4 39.7 %collective-permute-start.5 = (f32[48,32,256]{2,1,0:T(8,128)}, f32[48,32,256]{2,1,0:T(8,128)S(1)}, u32[]{:S(2)}, u32[]{:S(2)}) collective-permute-start(f32[48,32,256]{2,1,0:T(8,128)} %constant_dynamic-update-slice_fusion), channel_id=1, source_target_pairs={{0,4},{4,8},{8,12},{12,16},{16,20},{20,24},{24,28},{1,5},{5,9},{9,... | collective-permute-start | bytes 4718600 | tf_op jit(solution)/shard_map/ppermute | solution.py:369
  116.3 39.0 %collective-permute-start.6 = (f32[48,32,256]{2,1,0:T(8,128)}, f32[48,32,256]{2,1,0:T(8,128)}, u32[]{:S(2)}, u32[]{:S(2)}) collective-permute-start(f32[48,32,256]{2,1,0:T(8,128)} %constant_dynamic-update-slice_fusion), channel_id=1, source_target_pairs={{4,0},{8,4},{12,8},{16,12},{20,16},{24,20},{28,24},{5,1},{9,5},{13... | collective-permute-start | bytes 4718600 | tf_op jit(solution)/shard_map/ppermute | solution.py:369
  138.6 32.0 %copy-start.3 = (f32[16,32,256]{2,1,0:T(8,128)}, f32[16,32,256]{2,1,0:T(8,128)S(1)}, u32[]{:S(2)}) copy-start(f32[16,32,256]{2,1,0:T(8,128)S(1)} %get-tuple-element.31.refs_0_) | copy-start | bytes 1572868
  138.6 35.9 %collective-permute-start.15 = (f32[16,32,256]{2,1,0:T(8,128)S(1)}, f32[16,32,256]{2,1,0:T(8,128)S(1)}, u32[]{:S(2)}, u32[]{:S(2)}) collective-permute-start(f32[16,32,256]{2,1,0:T(8,128)S(1)} %get-tuple-element.32), channel_id=1, source_target_pairs={{0,1},{1,2},{2,3},{3,0},{4,5},{5,6},{6,7},{7,4},{8,9},{9,10},{10,1... | collective-permute-start | bytes 1572872 | tf_op jit(solution)/shard_map/ppermute | solution.py:366
  139.1 38.2 %collective-permute-start.16 = (f32[16,32,256]{2,1,0:T(8,128)S(1)}, f32[16,32,256]{2,1,0:T(8,128)S(1)}, u32[]{:S(2)}, u32[]{:S(2)}) collective-permute-start(f32[16,32,256]{2,1,0:T(8,128)S(1)} %get-tuple-element.33), channel_id=1, source_target_pairs={{0,3},{1,0},{2,1},{3,2},{4,7},{5,4},{6,5},{7,6},{8,11},{9,8},{10,9... | collective-permute-start | bytes 1572872 | tf_op jit(solution)/shard_map/ppermute | solution.py:366
  142.5 33.1 %copy-start.7 = (f32[32,1,64,256]{3,2,1,0:T(8,128)S(1)}, f32[32,1,64,256]{3,2,1,0:T(8,128)}, u32[]{:S(2)}) copy-start(f32[32,1,64,256]{3,2,1,0:T(8,128)} %param.8) | copy-start | bytes 6291460
  142.5 33.1 %copy-start.8 = (f32[32,1,64,256]{3,2,1,0:T(8,128)S(1)}, f32[32,1,64,256]{3,2,1,0:T(8,128)}, u32[]{:S(2)}) copy-start(f32[32,1,64,256]{3,2,1,0:T(8,128)} %param.7) | copy-start | bytes 6291460
  142.5 57.8 %collective-permute-start.17 = (f32[16,32,256]{2,1,0:T(8,128)S(1)}, f32[16,32,256]{2,1,0:T(8,128)S(1)}, u32[]{:S(2)}, u32[]{:S(2)}) collective-permute-start(f32[16,32,256]{2,1,0:T(8,128)S(1)} %get-tuple-element.34), channel_id=1, source_target_pairs={{0,2},{1,3},{2,0},{3,1},{4,6},{5,7},{6,4},{7,5},{8,10},{9,11},{10,... | collective-permute-start | bytes 1572872 | tf_op jit(solution)/shard_map/ppermute | solution.py:366
  170.6 6.7 %copy-start.4 = (f32[16,32,256]{2,1,0:T(8,128)}, f32[16,32,256]{2,1,0:T(8,128)S(1)}, u32[]{:S(2)}) copy-start(f32[16,32,256]{2,1,0:T(8,128)S(1)} %get-tuple-element.27.refs_0_) | copy-start | bytes 1572868
  170.6 33.9 %collective-permute-start.10 = (f32[16,32,256]{2,1,0:T(8,128)S(1)}, f32[16,32,256]{2,1,0:T(8,128)S(1)}, u32[]{:S(2)}, u32[]{:S(2)}) collective-permute-start(f32[16,32,256]{2,1,0:T(8,128)S(1)} %get-tuple-element.28), channel_id=1, source_target_pairs={{0,1},{1,2},{2,3},{3,0},{4,5},{5,6},{6,7},{7,4},{8,9},{9,10},{10,1... | collective-permute-start | bytes 1572872 | tf_op jit(solution)/shard_map/ppermute | solution.py:366
  170.7 34.7 %collective-permute-start.11 = (f32[16,32,256]{2,1,0:T(8,128)S(1)}, f32[16,32,256]{2,1,0:T(8,128)S(1)}, u32[]{:S(2)}, u32[]{:S(2)}) collective-permute-start(f32[16,32,256]{2,1,0:T(8,128)S(1)} %get-tuple-element.29), channel_id=1, source_target_pairs={{0,3},{1,0},{2,1},{3,2},{4,7},{5,4},{6,5},{7,6},{8,11},{9,8},{10,9... | collective-permute-start | bytes 1572872 | tf_op jit(solution)/shard_map/ppermute | solution.py:366
  174.5 2.9 %copy-start.13 = (f32[16,32,256]{2,1,0:T(8,128)}, f32[16,32,256]{2,1,0:T(8,128)S(1)}, u32[]{:S(2)}) copy-start(f32[16,32,256]{2,1,0:T(8,128)S(1)} %collective-permute-done.15.refs_1_) | copy-start | bytes 1572868
  174.5 57.2 %collective-permute-start.12 = (f32[16,32,256]{2,1,0:T(8,128)S(1)}, f32[16,32,256]{2,1,0:T(8,128)S(1)}, u32[]{:S(2)}, u32[]{:S(2)}) collective-permute-start(f32[16,32,256]{2,1,0:T(8,128)S(1)} %get-tuple-element.30), channel_id=1, source_target_pairs={{0,2},{1,3},{2,0},{3,1},{4,6},{5,7},{6,4},{7,5},{8,10},{9,11},{10,... | collective-permute-start | bytes 1572872 | tf_op jit(solution)/shard_map/ppermute | solution.py:366
  177.4 22.9 %copy-start.14 = (f32[16,32,256]{2,1,0:T(8,128)}, f32[16,32,256]{2,1,0:T(8,128)S(1)}, u32[]{:S(2)}) copy-start(f32[16,32,256]{2,1,0:T(8,128)S(1)} %collective-permute-done.16.refs_2_) | copy-start | bytes 1572868
  204.5 27.2 %copy-start.16 = (f32[16,32,256]{2,1,0:T(8,128)}, f32[16,32,256]{2,1,0:T(8,128)S(1)}, u32[]{:S(2)}) copy-start(f32[16,32,256]{2,1,0:T(8,128)S(1)} %collective-permute-done.10.refs_1_) | copy-start | bytes 1572868
  205.3 26.4 %copy-start.17 = (f32[16,32,256]{2,1,0:T(8,128)}, f32[16,32,256]{2,1,0:T(8,128)S(1)}, u32[]{:S(2)}) copy-start(f32[16,32,256]{2,1,0:T(8,128)S(1)} %collective-permute-done.11.refs_2_) | copy-start | bytes 1572868
  (6 other events, 6.3 us)

commit v5 on v4

--- a/solution.py
+++ b/solution.py
@@ -7,7 +7,6 @@
 from jax.experimental.pallas import tpu as pltpu
 from jax.sharding import PartitionSpec as P
 
-PARTS = 2
 TILE = 8
 ANYWHERE = pl.BlockSpec(memory_space=pl.ANY)
 SCALARS = pl.BlockSpec(memory_space=pltpu.SMEM)
@@ -60,7 +59,7 @@
     return 1 if halves == 2 else 2
 
 
-def tile_specs(modes, height, width, shift, owners, part_rows):
+def tile_specs(modes, height, width, shift, owners):
     halves = owners // 2
     half_tiles = height // halves // TILE
 
@@ -71,7 +70,7 @@
 
         return pl.BlockSpec((modes, TILE, width), place)
 
-    return [spec(part_rows // TILE), spec(-1), spec(half_tiles)]
+    return [spec(-1), spec(half_tiles)]
 
 
 def write_edges(out_ref, at, half, halves, before_ref, after_ref):
@@ -86,7 +85,7 @@
 
 def pack_kernel(shifts, owners, extras, me_ref, *refs):
     halves = owners // 2
-    per_field = 4 if extras else 1
+    per_field = 3 if extras else 1
     outs = refs[-len(shifts) :]
     for index, shift in enumerate(shifts):
         field, half = target(me_ref, shift, owners)
@@ -99,23 +98,23 @@
                 rows = mine[0].shape[1]
                 out_ref[:rows] = jnp.swapaxes(mine[0][...], 0, 1)
                 if extras:
-                    out_ref[rows] = jnp.swapaxes(mine[1][...], 0, 1)[0]
-                    write_edges(out_ref, rows + 1, half, halves, mine[2], mine[3])
+                    write_edges(out_ref, rows, half, halves, mine[1], mine[2])
 
 
 def pack(me, state, adjoint, shifts, part, rows, owners, earlier):
     modes, height, width = state.shape
     extras = part == 0
-    count = rows + (1 + edge_count(owners // 2) if extras else 0)
+    count = rows + (edge_count(owners // 2) if extras else 0)
+    parts = height // (owners // 2) // rows
     in_specs, operands = [], []
     for shift in shifts:
 
         def place(i, me_ref, shift=shift):
-            return 0, target(me_ref, shift, owners)[1] * PARTS + part, 0
+            return 0, target(me_ref, shift, owners)[1] * parts + part, 0
 
         specs = [pl.BlockSpec((modes, rows, width), place)]
         if extras:
-            specs += tile_specs(modes, height, width, shift, owners, rows)
+            specs += tile_specs(modes, height, width, shift, owners)
         for array in (state, adjoint):
             in_specs += specs
             operands += [array] * len(specs)
@@ -134,7 +133,7 @@
 
 
 def pack_own_kernel(owners, me_ref, *refs):
-    coef_ref, out_ref = refs[-2:]
+    coef_ref, out_ref = refs[6], refs[-1]
     halves = owners // 2
     field, half = target(me_ref, 0, owners)
     for which in range(2):
@@ -150,7 +149,7 @@
     out_ref[out_ref.shape[0] - terms :] = coef_ref[...]
 
 
-def pack_own(me, state, adjoint, coef, owners):
+def pack_own(me, state, adjoint, coef, owners, earlier):
     modes, height, width = state.shape
     halves = owners // 2
     half_rows = height // halves
@@ -161,32 +160,31 @@
         return 0, target(me_ref, 0, owners)[1], 0
 
     specs = [pl.BlockSpec((modes, half_rows, width), place)]
-    specs += tile_specs(modes, height, width, 0, owners, half_rows // PARTS)[1:]
+    specs += tile_specs(modes, height, width, 0, owners)
     return pl.pallas_call(
         functools.partial(pack_own_kernel, owners),
         grid_spec=pltpu.PrefetchScalarGridSpec(
             num_scalar_prefetch=1,
             grid=(1,),
-            in_specs=specs + specs + [pl.BlockSpec((terms, half_rows, width), place)],
+            in_specs=specs + specs + [pl.BlockSpec((terms, half_rows, width), place)] + [ANYWHERE] * len(earlier),
             out_specs=pl.BlockSpec((count, modes, width), lambda i, me_ref: (0, 0, 0)),
         ),
         out_shape=jax.ShapeDtypeStruct((count, modes, width), jnp.float32),
         compiler_params=params(60),
         name="pack_own",
-    )(me, *([state] * 3 + [adjoint] * 3), coef)
-
-
-def operator_kernel(shifts, rows, terms, part, me_ref, coef_ref, matrix_ref, *refs):
+    )(me, *([state] * 3 + [adjoint] * 3), coef, *earlier)
+
+
+def operator_kernel(shifts, rows, terms, part, parts, me_ref, coef_ref, matrix_ref, *refs):
     owners = len(shifts) + 1
     own, own_below, own_above, below, above = refs[:5]
-    head = refs[5 : 5 + len(shifts)]
-    pieces = refs[5 + part * len(shifts) : 5 + (part + 1) * len(shifts)]
+    pieces, before, after = (refs[5 + i * len(shifts) : 5 + (i + 1) * len(shifts)] for i in range(3))
     outs = refs[-owners - 6 : -6]
     slots, mixed, faces = ((refs[-6], refs[-5]), (refs[-4], refs[-3])), refs[-2], refs[-1]
     _, block, width = own.shape
     modes = owners * block
     halves = owners // 2
-    half_rows = rows * PARTS
+    half_rows = rows * parts
     edges = edge_count(halves)
     me = me_ref[0]
     half = lax.rem(me, halves)
@@ -219,7 +217,7 @@
             faces[6 * term + side] = 0.5 * (centre + other)
 
     def edge(index, which, here):
-        ref, at = (head[index - 1], rows + 1) if index else (own, half_rows)
+        ref, at = ((before, after)[which][index - 1], 0) if index else (own, half_rows)
         if halves == 2:
             return jnp.where(half == 1 - which, ref[at, here, :], 0.0)
         return ref[at + which, here, :]
@@ -240,13 +238,13 @@
                 elif part == 0:
                     up = edge(index, 0, here)
                 else:
-                    up = head[index - 1][last, here, :] if index else own[base - 1, here, :]
+                    up = before[index - 1][0, here, :] if index else own[base - 1, here, :]
                 if place != "last":
                     down = ref[base + row + 1, here, :]
-                elif part == 0:
-                    down = ref[base + rows, here, :]
+                elif part == parts - 1:
+                    down = edge(index, 1, here)
                 else:
-                    down = edge(index, 1, here)
+                    down = after[index - 1][0, here, :] if index else own[base + rows, here, :]
                 left, right = with_sides(centre, lanes)
                 others = (below_ref[near + row, here, :], above_ref[near + row, here, :], up, down, left, right)
                 slopes = [centre - other for other in others]
@@ -288,14 +286,24 @@
     owners = len(shifts) + 1
     modes = owners * block
     terms = coef.shape[0]
-    operands = [coef, matrix, own, *own_near, *near]
-    for piece in pieces[: part + 1]:
-        operands += piece
+    parts = len(pieces)
+    edges = edge_count(owners // 2)
+    operands = [coef, matrix, own, *own_near, *near[part], *pieces[part]]
+    in_specs = [SCALARS] + [whole(array) for array in operands]
+    edge_block = pl.BlockSpec((edges, block, width), lambda i: (rows // edges, 0, 0))
+    for other, row in ((part - 1, rows - 1), (part + 1, 0)):
+        inside = 0 <= other < parts
+        row_block = pl.BlockSpec((1, block, width), lambda i, row=row: (row, 0, 0))
+        operands += pieces[other if inside else 0]
+        in_specs += [row_block if inside else edge_block] * len(shifts)
+    earlier = near[part + 1] if part + 1 < parts else []
+    operands += earlier
+    in_specs += [ANYWHERE] * len(earlier)
     shape = (rows, block, width)
     return pl.pallas_call(
-        functools.partial(operator_kernel, shifts, rows, terms, part),
+        functools.partial(operator_kernel, shifts, rows, terms, part, parts),
         grid=(1,),
-        in_specs=[SCALARS] + [whole(array) for array in operands],
+        in_specs=in_specs,
         out_specs=[pl.BlockSpec(shape, lambda i: (0, 0, 0))] * owners,
         out_shape=[jax.ShapeDtypeStruct(shape, jnp.float32)] * owners,
         scratch_shapes=[pltpu.VMEM((terms * modes, width), jnp.bfloat16)] * 4
@@ -328,7 +336,8 @@
     modes, _, width = state.shape
     owners = len(mixed)
     rows = mixed[0].shape[0]
-    block = pl.BlockSpec((modes, rows, width), lambda h: (0, h * PARTS + part, 0))
+    parts = state.shape[1] // (owners // 2) // rows
+    block = pl.BlockSpec((modes, rows, width), lambda h: (0, h * parts + part, 0))
     in_specs = [SCALARS] + [whole(m) for m in mixed] + [block] * 2
     operands = [me, *mixed, state, control]
     aliases = {}
@@ -355,7 +364,8 @@
     state, control, adjoint = (a.reshape(modes, height, width) for a in (state, control, adjoint))
     coef = coefficient[:, 0]
     owners = lax.axis_size("mode")
-    rows = height // (owners // 2) // PARTS
+    rows = TILE
+    parts = height // (owners // 2) // rows
     planes = lax.axis_size("space")
     forward = [(i, i + 1) for i in range(planes - 1)]
     backward = [(i + 1, i) for i in range(planes - 1)]
@@ -370,18 +380,24 @@
 
     matrix = coupling_matrices(pattern, weights)
     pieces, near = [], []
-    for part in range(PARTS):
-        if part:
-            own = pack_own(me, state, adjoint, coef, owners)
-            own_near = beside(own)
-        packed = pack(me, state, adjoint, shifts, part, rows, owners, list(own_near) if part else [])
+    for part in range(parts):
+        if part == 0:
+            earlier = []
+        elif part == 1:
+            earlier = [own]
+        else:
+            earlier = near[part - 3] if part > 2 else own_near
+        packed = pack(me, state, adjoint, shifts, part, rows, owners, earlier)
+        if part == 0:
+            own = pack_own(me, state, adjoint, coef, owners, packed)
+            own_near = list(beside(own))
         arrived = [move(piece, shift) for piece, shift in zip(packed, shifts)]
         pieces.append(arrived)
-        near.append(beside(jnp.concatenate([piece[:rows] for piece in arrived])))
+        near.append(list(beside(jnp.concatenate([piece[:rows] for piece in arrived]))))
 
     outputs = None
-    for part in range(PARTS):
-        mixed = apply_operator(me, coef, matrix, own, own_near, pieces, near[part], part, rows, shifts)
+    for part in range(parts):
+        mixed = apply_operator(me, coef, matrix, own, own_near, pieces, near, part, rows, shifts)
         mixed = [mixed[0]] + [move(m, shift) for m, shift in zip(mixed[1:], shifts)]
         outputs = finish(me, mixed, state, control, outputs, part, shifts)
     return outputs[0].reshape(shape), control_residual, outputs[1].reshape(shape)

time: 238 us -> 235 us (0.987)
  waiting for transfers between devices: 125 us -> 101 us
  Pallas kernels: 48.9 us -> 57.5 us
  starting transfers between devices: 52.6 us -> 59.8 us
  local copies, waits for them, and re-layouts: 6.63 us -> 11.4 us
    ppermute x3 -> x5, waiting for transfers between devices: 26.8 us -> 0.01 us  [beside(): lax.ppermute(array, 'space', forward)]
    ppermute x12 -> x24, waiting for transfers between devices: 95.8 us -> 101 us  [move(): lax.ppermute(array, 'mode', [(i, (i + shift) % owners) for i in range(own...]
    unnamed x42 -> x80, local copies, waits for them, and re-layouts: 5.66 us -> 10.6 us
    ppermute x3 -> x5, starting transfers between devices: 5.87 us -> 10.1 us  [beside(): lax.ppermute(array, 'space', forward)]
    pallas_call x2 -> x4, Pallas kernels: 6.86 us -> 10.1 us  [finish(): pl.pallas_call(functools.partial(finish_kernel, shifts), grid=(owners //...]
    pallas_call x2 -> x4, Pallas kernels: 8.35 us -> 11.1 us  [pack(): pl.pallas_call(functools.partial(pack_kernel, shifts, owners, extras), gr...]
    ppermute x12 -> x24, starting transfers between devices: 33.2 us -> 35.7 us  [move(): lax.ppermute(array, 'mode', [(i, (i + shift) % owners) for i in range(own...]
    pallas_call x2 -> x4, Pallas kernels: 30.1 us -> 32.6 us  [apply_operator(): pl.pallas_call(functools.partial(operator_kernel, shifts, rows, terms, pa...]
  transfers between devices with their start and end apart: 18 -> 34, of which waited for: 9 -> 11; matrix products, arithmetic and copies ran while one was open for 2% -> 2% of each run, Pallas kernels for 18% -> 21%
where the time goes in v5:
time: 235 us; the launch traced here: 233 us
  waiting for transfers between devices  101 us (43%)
  starting transfers between devices  59.8 us (25%)
  Pallas kernels  57.5 us (24%)
  local copies, waits for them, and re-layouts  11.4 us (5%)
  other arithmetic  2.69 us (1%)
    ppermute x24, waiting for transfers between devices, move(): lax.ppermute(array, 'mode', [(i, (i + shift) % owners) for i in range(own...  101 us
    ppermute x24, starting transfers between devices, move(): lax.ppermute(array, 'mode', [(i, (i + shift) % owners) for i in range(own...  35.7 us
    pallas_call x4, Pallas kernels, apply_operator(): pl.pallas_call(functools.partial(operator_kernel, shifts, rows, terms, pa...  32.6 us
    ppermute x5, starting transfers between devices, beside(): lax.ppermute(array, 'space', backward)  14.1 us
    pallas_call x4, Pallas kernels, pack(): pl.pallas_call(functools.partial(pack_kernel, shifts, owners, extras), gr...  11.1 us
    unnamed x80, local copies, waits for them, and re-layouts  10.6 us
    pallas_call x4, Pallas kernels, finish(): pl.pallas_call(functools.partial(finish_kernel, shifts), grid=(owners //...  10.1 us
    ppermute x5, starting transfers between devices, beside(): lax.ppermute(array, 'space', forward)  10.1 us
  transfers between devices with their start and end apart: 34, of which 11 were waited for; matrix products, arithmetic and copies ran while one was open for 2% of the time, Pallas kernels for 21%

profile of v5, /device:TPU:4, one launch (start us, length us, event | category | flops | bytes accessed | tf_op | source)
XLA Modules:
  0.0 233.4 jit_solution(1770605774035180790)
XLA Ops:
  0.6 3.8 %pack.4 = (f32[9,32,256]{2,1,0:T(8,128)}, f32[9,32,256]{2,1,0:T(8,128)}, f32[9,32,256]{2,1,0:T(8,128)}) custom-call(s32[1]{0:T(128)} %bitcast.me_ref, f32[32,64,256]{2,1,0:T(8,128)} %bitcast.20, f32[32,64,256]{2,1,0:T(8,128)} %bitcast.21, f32[32,64,256]{2,1,0:T(8,128)} %bitcast.22, f32[32,64,256]{2,1,0:T(8,128)} %bitcast.45, f32[32,64,256]{2,1,0:T(8,128)} %bitcast.46, ...), custom_call_target="tpu_custom_call" | custom-call | tf_op jit(solution)/shard_map/pack/pallas_call | solution.py:121
  4.4 3.3 %pack_own.1.refs_0_.refs_6_ = f32[40,32,256]{2,1,0:T(8,128)} custom-call(s32[1]{0:T(128)} %bitcast.me_ref, f32[32,64,256]{2,1,0:T(8,128)} %bitcast.29, f32[32,64,256]{2,1,0:T(8,128)} %bitcast.30, f32[32,64,256]{2,1,0:T(8,128)} %bitcast.31, f32[32,64,256]{2,1,0:T(8,128)} %bitcast.54, f32[32,64,256]{2,1,0:T(8,128)} %bitcast.55, f32[32,64,256]{2,1,0:T(8,128)} %bitcast.56, ...), custom_call_target="tpu_custom_call" | custom-call | tf_op jit(solution)/shard_map/pack_own/pallas_call | solution.py:164
  7.7 2.8 %collective-permute-start.1 = (f32[40,32,256]{2,1,0:T(8,128)}, f32[40,32,256]{2,1,0:T(8,128)}, u32[]{:S(2)}, u32[]{:S(2)}) collective-permute-start(f32[40,32,256]{2,1,0:T(8,128)} %pack_own.1.refs_0_.refs_6_), channel_id=1, source_target_pairs={{4,0},{8,4},{12,8},{16,12},{20,16},{24,20},{28,24},{5,1},{9,5},{13... | collective-permute-start | bytes 3932168 | tf_op jit(solution)/shard_map/ppermute | solution.py:379
  19.5 4.7 %collective-permute-done.2.refs_11_.refs_8_.refs_5_ = f32[9,32,256]{2,1,0:T(8,128)S(1)} collective-permute-done((f32[9,32,256]{2,1,0:T(8,128)S(1)}, f32[9,32,256]{2,1,0:T(8,128)S(1)}, u32[]{:S(2)}, u32[]{:S(2)}) %collective-permute-start.2) | collective-permute-done | bytes 294944 | tf_op jit(solution)/shard_map/ppermute | solution.py:376
  24.2 5.5 %collective-permute-done.3.refs_12_.refs_9_.refs_6_ = f32[9,32,256]{2,1,0:T(8,128)S(1)} collective-permute-done((f32[9,32,256]{2,1,0:T(8,128)S(1)}, f32[9,32,256]{2,1,0:T(8,128)S(1)}, u32[]{:S(2)}, u32[]{:S(2)}) %collective-permute-start.3) | collective-permute-done | bytes 294944 | tf_op jit(solution)/shard_map/ppermute | solution.py:376
  29.8 18.8 %collective-permute-done.4.refs_13_.refs_10_.refs_7_ = f32[9,32,256]{2,1,0:T(8,128)S(1)} collective-permute-done((f32[9,32,256]{2,1,0:T(8,128)S(1)}, f32[9,32,256]{2,1,0:T(8,128)S(1)}, u32[]{:S(2)}, u32[]{:S(2)}) %collective-permute-start.4) | collective-permute-done | bytes 294944 | tf_op jit(solution)/shard_map/ppermute | solution.py:376
  49.6 2.7 %collective-permute-start.6 = (f32[24,32,256]{2,1,0:T(8,128)}, f32[24,32,256]{2,1,0:T(8,128)S(1)}, u32[]{:S(2)}, u32[]{:S(2)}) collective-permute-start(f32[24,32,256]{2,1,0:T(8,128)} %pad_maximum_fusion), channel_id=1, source_target_pairs={{4,0},{8,4},{12,8},{16,12},{20,16},{24,20},{28,24},{5,1},{9,5},{13... | collective-permute-start | bytes 2359304 | tf_op jit(solution)/shard_map/ppermute | solution.py:379
  55.2 2.5 %pack.6 = (f32[8,32,256]{2,1,0:T(8,128)}, f32[8,32,256]{2,1,0:T(8,128)}, f32[8,32,256]{2,1,0:T(8,128)}) custom-call(s32[1]{0:T(128)} %bitcast.me_ref, f32[32,64,256]{2,1,0:T(8,128)} %bitcast.35, f32[32,64,256]{2,1,0:T(8,128)} %bitcast.60, f32[32,64,256]{2,1,0:T(8,128)} %bitcast.36, f32[32,64,256]{2,1,0:T(8,128)} %bitcast.61, f32[32,64,256]{2,1,0:T(8,128)} %bitcast.37, ...), custom_call_target="tpu_custom_call" | custom-call | tf_op jit(solution)/shard_map/pack/pallas_call | solution.py:121
  59.6 5.3 %collective-permute-done.21.refs_9_.refs_6_.refs_12_ = f32[8,32,256]{2,1,0:T(8,128)S(1)} collective-permute-done((f32[8,32,256]{2,1,0:T(8,128)}, f32[8,32,256]{2,1,0:T(8,128)S(1)}, u32[]{:S(2)}, u32[]{:S(2)}) %collective-permute-start.21) | collective-permute-done | bytes 262176 | tf_op jit(solution)/shard_map/ppermute | solution.py:376
  66.0 12.3 %collective-permute-done.22.refs_10_.refs_7_.refs_13_ = f32[8,32,256]{2,1,0:T(8,128)S(1)} collective-permute-done((f32[8,32,256]{2,1,0:T(8,128)S(1)}, f32[8,32,256]{2,1,0:T(8,128)S(1)}, u32[]{:S(2)}, u32[]{:S(2)}) %collective-permute-start.22) | collective-permute-done | bytes 262176 | tf_op jit(solution)/shard_map/ppermute | solution.py:376
  79.0 3.7 %collective-permute-start.27 = (f32[24,32,256]{2,1,0:T(8,128)}, f32[24,32,256]{2,1,0:T(8,128)}, u32[]{:S(2)}, u32[]{:S(2)}) collective-permute-start(f32[24,32,256]{2,1,0:T(8,128)} %constant_dynamic-update-slice_fusion.6), channel_id=1, source_target_pairs={{4,0},{8,4},{12,8},{16,12},{20,16},{24,20},{28,24},{5,1},{9,5},{13... | collective-permute-start | bytes 2359304 | tf_op jit(solution)/shard_map/ppermute | solution.py:379
  84.8 2.5 %pack.5 = (f32[8,32,256]{2,1,0:T(8,128)}, f32[8,32,256]{2,1,0:T(8,128)}, f32[8,32,256]{2,1,0:T(8,128)}) custom-call(s32[1]{0:T(128)} %bitcast.me_ref, f32[32,64,256]{2,1,0:T(8,128)} %bitcast.38, f32[32,64,256]{2,1,0:T(8,128)} %bitcast.63, f32[32,64,256]{2,1,0:T(8,128)} %bitcast.39, f32[32,64,256]{2,1,0:T(8,128)} %bitcast.64, f32[32,64,256]{2,1,0:T(8,128)} %bitcast.40, ...), custom_call_target="tpu_custom_call" | custom-call | tf_op jit(solution)/shard_map/pack/pallas_call | solution.py:121
  87.4 3.5 %collective-permute-start.7 = (f32[8,32,256]{2,1,0:T(8,128)}, f32[8,32,256]{2,1,0:T(8,128)S(1)}, u32[]{:S(2)}, u32[]{:S(2)}) collective-permute-start(f32[8,32,256]{2,1,0:T(8,128)} %get-tuple-element.42), channel_id=1, source_target_pairs={{0,1},{1,2},{2,3},{3,0},{4,5},{5,6},{6,7},{7,4},{8,9},{9,10},{10,1... | collective-permute-start | bytes 786440 | tf_op jit(solution)/shard_map/ppermute | solution.py:376
  91.3 9.5 %collective-permute-done.14.refs_10_.refs_7_.refs_13_ = f32[8,32,256]{2,1,0:T(8,128)S(1)} collective-permute-done((f32[8,32,256]{2,1,0:T(8,128)}, f32[8,32,256]{2,1,0:T(8,128)S(1)}, u32[]{:S(2)}, u32[]{:S(2)}) %collective-permute-start.14) | collective-permute-done | bytes 262176 | tf_op jit(solution)/shard_map/ppermute | solution.py:376
  100.8 2.9 %collective-permute-start.19 = (f32[24,32,256]{2,1,0:T(8,128)S(1)}, f32[24,32,256]{2,1,0:T(8,128)S(1)}, u32[]{:S(2)}, u32[]{:S(2)}) collective-permute-start(f32[24,32,256]{2,1,0:T(8,128)S(1)} %constant_dynamic-update-slice_fusion.3), channel_id=1, source_target_pairs={{4,0},{8,4},{12,8},{16,12},{20,16},{24,20},{28,24},{5,1},{9,5},{13... | collective-permute-start | bytes 2359304 | tf_op jit(solution)/shard_map/ppermute | solution.py:379
  103.8 2.6 %collective-permute-done.8.refs_6_.refs_12_ = f32[8,32,256]{2,1,0:T(8,128)S(1)} collective-permute-done((f32[8,32,256]{2,1,0:T(8,128)}, f32[8,32,256]{2,1,0:T(8,128)S(1)}, u32[]{:S(2)}, u32[]{:S(2)}) %collective-permute-start.8) | collective-permute-done | bytes 262176 | tf_op jit(solution)/shard_map/ppermute | solution.py:376
  108.4 9.2 %collective-permute-done.9.refs_7_.refs_13_ = f32[8,32,256]{2,1,0:T(8,128)S(1)} collective-permute-done((f32[8,32,256]{2,1,0:T(8,128)}, f32[8,32,256]{2,1,0:T(8,128)S(1)}, u32[]{:S(2)}, u32[]{:S(2)}) %collective-permute-start.9) | collective-permute-done | bytes 262176 | tf_op jit(solution)/shard_map/ppermute | solution.py:376
  122.4 8.0 %operator.7 = (f32[8,32,256]{2,1,0:T(8,128)S(1)}, f32[8,32,256]{2,1,0:T(8,128)S(1)}, f32[8,32,256]{2,1,0:T(8,128)S(1)}, f32[8,32,256]{2,1,0:T(8,128)S(1)}) custom-call(s32[1]{0:T(128)} %bitcast.me_ref, f32[7,64,256]{2,1,0:T(8,128)S(1)} %bitcast.14, bf16[256,896]{1,0:T(8,128)(2,1)S(1)} %coupling.1.matrix_ref, f32[40,32,256]{2,1,0:T(8,128)} %pack_own.1.refs_0_.refs_6_, ...), custom_call_target="tpu_custom_call" | custom-call | tf_op jit(solution)/shard_map/operator/pallas_call | solution.py:303
  131.1 2.5 %collective-permute-start.31 = (f32[8,32,256]{2,1,0:T(8,128)S(1)}, f32[8,32,256]{2,1,0:T(8,128)S(1)}, u32[]{:S(2)}, u32[]{:S(2)}) collective-permute-start(f32[8,32,256]{2,1,0:T(8,128)S(1)} %get-tuple-element.64), channel_id=1, source_target_pairs={{0,1},{1,2},{2,3},{3,0},{4,5},{5,6},{6,7},{7,4},{8,9},{9,10},{10,1... | collective-permute-start | bytes 786440 | tf_op jit(solution)/shard_map/ppermute | solution.py:376
  135.3 5.0 %collective-permute-start.33 = (f32[8,32,256]{2,1,0:T(8,128)S(1)}, f32[8,32,256]{2,1,0:T(8,128)S(1)}, u32[]{:S(2)}, u32[]{:S(2)}) collective-permute-start(f32[8,32,256]{2,1,0:T(8,128)S(1)} %get-tuple-element.66), channel_id=1, source_target_pairs={{0,2},{1,3},{2,0},{3,1},{4,6},{5,7},{6,4},{7,5},{8,10},{9,11},{10,... | collective-permute-start | bytes 786440 | tf_op jit(solution)/shard_map/ppermute | solution.py:376
  140.3 8.4 %operator.6 = (f32[8,32,256]{2,1,0:T(8,128)S(1)}, f32[8,32,256]{2,1,0:T(8,128)S(1)}, f32[8,32,256]{2,1,0:T(8,128)S(1)}, f32[8,32,256]{2,1,0:T(8,128)S(1)}) custom-call(s32[1]{0:T(128)} %bitcast.me_ref, f32[7,64,256]{2,1,0:T(8,128)S(1)} %bitcast.15, bf16[256,896]{1,0:T(8,128)(2,1)S(1)} %coupling.1.matrix_ref, f32[40,32,256]{2,1,0:T(8,128)} %pack_own.1.refs_0_.refs_6_, ...), custom_call_target="tpu_custom_call" | custom-call | tf_op jit(solution)/shard_map/operator/pallas_call | solution.py:303
  149.5 3.8 %collective-permute-start.29 = (f32[8,32,256]{2,1,0:T(8,128)S(1)}, f32[8,32,256]{2,1,0:T(8,128)S(1)}, u32[]{:S(2)}, u32[]{:S(2)}) collective-permute-start(f32[8,32,256]{2,1,0:T(8,128)S(1)} %get-tuple-element.61), channel_id=1, source_target_pairs={{0,3},{1,0},{2,1},{3,2},{4,7},{5,4},{6,5},{7,6},{8,11},{9,8},{10,9... | collective-permute-start | bytes 786440 | tf_op jit(solution)/shard_map/ppermute | solution.py:376
  155.6 8.0 %operator.5 = (f32[8,32,256]{2,1,0:T(8,128)S(1)}, f32[8,32,256]{2,1,0:T(8,128)S(1)}, f32[8,32,256]{2,1,0:T(8,128)S(1)}, f32[8,32,256]{2,1,0:T(8,128)S(1)}) custom-call(s32[1]{0:T(128)} %bitcast.me_ref, f32[7,64,256]{2,1,0:T(8,128)S(1)} %bitcast.16, bf16[256,896]{1,0:T(8,128)(2,1)S(1)} %coupling.1.matrix_ref, f32[40,32,256]{2,1,0:T(8,128)} %pack_own.1.refs_0_.refs_6_, ...), custom_call_target="tpu_custom_call" | custom-call | tf_op jit(solution)/shard_map/operator/pallas_call | solution.py:303
  169.8 8.1 %operator.4 = (f32[8,32,256]{2,1,0:T(8,128)S(1)}, f32[8,32,256]{2,1,0:T(8,128)S(1)}, f32[8,32,256]{2,1,0:T(8,128)S(1)}, f32[8,32,256]{2,1,0:T(8,128)S(1)}) custom-call(s32[1]{0:T(128)} %bitcast.me_ref, f32[7,64,256]{2,1,0:T(8,128)S(1)} %bitcast.17, bf16[256,896]{1,0:T(8,128)(2,1)S(1)} %coupling.1.matrix_ref, f32[40,32,256]{2,1,0:T(8,128)} %pack_own.1.refs_0_.refs_6_, ...), custom_call_target="tpu_custom_call" | custom-call | tf_op jit(solution)/shard_map/operator/pallas_call | solution.py:303
  179.0 2.8 %collective-permute-start.16 = (f32[8,32,256]{2,1,0:T(8,128)S(1)}, f32[8,32,256]{2,1,0:T(8,128)S(1)}, u32[]{:S(2)}, u32[]{:S(2)}) collective-permute-start(f32[8,32,256]{2,1,0:T(8,128)S(1)} %get-tuple-element.50), channel_id=1, source_target_pairs={{0,3},{1,0},{2,1},{3,2},{4,7},{5,4},{6,5},{7,6},{8,11},{9,8},{10,9... | collective-permute-start | bytes 786440 | tf_op jit(solution)/shard_map/ppermute | solution.py:376
  181.8 3.3 %collective-permute-start.17 = (f32[8,32,256]{2,1,0:T(8,128)S(1)}, f32[8,32,256]{2,1,0:T(8,128)S(1)}, u32[]{:S(2)}, u32[]{:S(2)}) collective-permute-start(f32[8,32,256]{2,1,0:T(8,128)S(1)} %get-tuple-element.51), channel_id=1, source_target_pairs={{0,2},{1,3},{2,0},{3,1},{4,6},{5,7},{6,4},{7,5},{8,10},{9,11},{10,... | collective-permute-start | bytes 786440 | tf_op jit(solution)/shard_map/ppermute | solution.py:376
  185.1 13.6 %collective-permute-done.30.refs_3_ = f32[8,32,256]{2,1,0:T(8,128)S(1)} collective-permute-done((f32[8,32,256]{2,1,0:T(8,128)S(1)}, f32[8,32,256]{2,1,0:T(8,128)S(1)}, u32[]{:S(2)}, u32[]{:S(2)}) %collective-permute-start.30) | collective-permute-done | bytes 262176 | tf_op jit(solution)/shard_map/ppermute | solution.py:376
  202.3 2.6 %finish.4 = (f32[32,64,256]{2,1,0:T(8,128)}, f32[32,64,256]{2,1,0:T(8,128)}) custom-call(s32[1]{0:T(128)} %bitcast.me_ref, f32[8,32,256]{2,1,0:T(8,128)} %copy-done.16, f32[8,32,256]{2,1,0:T(8,128)} %copy-done.33, f32[8,32,256]{2,1,0:T(8,128)} %copy-done.34, f32[8,32,256]{2,1,0:T(8,128)} %copy-done.35, f32[32,64,256]{2,1,0:T(8,128)} %bitcast.41, ...), custom_call_target="tpu_custom_call" | custom-call | tf_op jit(solution)/shard_map/finish/pallas_call | solution.py:348
  204.9 2.5 %finish.5 = (f32[32,64,256]{2,1,0:T(8,128)}, f32[32,64,256]{2,1,0:T(8,128)}) custom-call(s32[1]{0:T(128)} %bitcast.me_ref, f32[8,32,256]{2,1,0:T(8,128)} %copy-done.13, f32[8,32,256]{2,1,0:T(8,128)} %copy-done.24, f32[8,32,256]{2,1,0:T(8,128)} %copy-done.25, f32[8,32,256]{2,1,0:T(8,128)} %copy-done.28, ...), custom_call_target="tpu_custom_call", output_to_operand_aliasing={{0}: (7, {}), {1}: (8, {})} | custom-call | tf_op jit(solution)/shard_map/finish/pallas_call | solution.py:348
  208.6 18.1 %collective-permute-done.25.refs_3_ = f32[8,32,256]{2,1,0:T(8,128)S(1)} collective-permute-done((f32[8,32,256]{2,1,0:T(8,128)S(1)}, f32[8,32,256]{2,1,0:T(8,128)S(1)}, u32[]{:S(2)}, u32[]{:S(2)}) %collective-permute-start.25) | collective-permute-done | bytes 262176 | tf_op jit(solution)/shard_map/ppermute | solution.py:376
  227.4 2.5 %finish.6 = (f32[32,64,256]{2,1,0:T(8,128)}, f32[32,64,256]{2,1,0:T(8,128)}) custom-call(s32[1]{0:T(128)} %bitcast.me_ref, f32[8,32,256]{2,1,0:T(8,128)} %copy-done.14, f32[8,32,256]{2,1,0:T(8,128)} %copy-done.26, f32[8,32,256]{2,1,0:T(8,128)} %copy-done.31, f32[8,32,256]{2,1,0:T(8,128)} %copy-done.32, ...), custom_call_target="tpu_custom_call", output_to_operand_aliasing={{0}: (7, {}), {1}: (8, {})} | custom-call | tf_op jit(solution)/shard_map/finish/pallas_call | solution.py:348
  230.8 2.5 %finish.7 = (f32[32,64,256]{2,1,0:T(8,128)}, f32[32,64,256]{2,1,0:T(8,128)}) custom-call(s32[1]{0:T(128)} %bitcast.me_ref, f32[8,32,256]{2,1,0:T(8,128)} %copy-done.15, f32[8,32,256]{2,1,0:T(8,128)} %copy-done.27, f32[8,32,256]{2,1,0:T(8,128)} %copy-done.29, f32[8,32,256]{2,1,0:T(8,128)} %copy-done.30, ...), custom_call_target="tpu_custom_call", output_to_operand_aliasing={{0}: (7, {}), {1}: (8, {})} | custom-call | tf_op jit(solution)/shard_map/finish/pallas_call | solution.py:348
  (138 shorter events, 44.8 us)
Async XLA Ops:
  7.7 46.6 %collective-permute-start.1 = (f32[40,32,256]{2,1,0:T(8,128)}, f32[40,32,256]{2,1,0:T(8,128)}, u32[]{:S(2)}, u32[]{:S(2)}) collective-permute-start(f32[40,32,256]{2,1,0:T(8,128)} %pack_own.1.refs_0_.refs_6_), channel_id=1, source_target_pairs={{4,0},{8,4},{12,8},{16,12},{20,16},{24,20},{28,24},{5,1},{9,5},{13... | collective-permute-start | bytes 3932168 | tf_op jit(solution)/shard_map/ppermute | solution.py:379
  10.5 44.7 %collective-permute-start = (f32[40,32,256]{2,1,0:T(8,128)}, f32[40,32,256]{2,1,0:T(8,128)}, u32[]{:S(2)}, u32[]{:S(2)}) collective-permute-start(f32[40,32,256]{2,1,0:T(8,128)} %pack_own.1.refs_0_.refs_6_), channel_id=1, source_target_pairs={{0,4},{4,8},{8,12},{12,16},{16,20},{20,24},{24,28},{1,5},{5,9},{9,... | collective-permute-start | bytes 3932168 | tf_op jit(solution)/shard_map/ppermute | solution.py:379
  12.4 11.8 %collective-permute-start.2 = (f32[9,32,256]{2,1,0:T(8,128)S(1)}, f32[9,32,256]{2,1,0:T(8,128)S(1)}, u32[]{:S(2)}, u32[]{:S(2)}) collective-permute-start(f32[9,32,256]{2,1,0:T(8,128)S(1)} %copy-done.23), channel_id=1, source_target_pairs={{0,1},{1,2},{2,3},{3,0},{4,5},{5,6},{6,7},{7,4},{8,9},{9,10},{10,1... | collective-permute-start | bytes 884744 | tf_op jit(solution)/shard_map/ppermute | solution.py:376
  14.1 15.7 %collective-permute-start.3 = (f32[9,32,256]{2,1,0:T(8,128)S(1)}, f32[9,32,256]{2,1,0:T(8,128)S(1)}, u32[]{:S(2)}, u32[]{:S(2)}) collective-permute-start(f32[9,32,256]{2,1,0:T(8,128)S(1)} %copy-done.22), channel_id=1, source_target_pairs={{0,3},{1,0},{2,1},{3,2},{4,7},{5,4},{6,5},{7,6},{8,11},{9,8},{10,9... | collective-permute-start | bytes 884744 | tf_op jit(solution)/shard_map/ppermute | solution.py:376
  16.3 32.3 %collective-permute-start.4 = (f32[9,32,256]{2,1,0:T(8,128)S(1)}, f32[9,32,256]{2,1,0:T(8,128)S(1)}, u32[]{:S(2)}, u32[]{:S(2)}) collective-permute-start(f32[9,32,256]{2,1,0:T(8,128)S(1)} %copy-done.21), channel_id=1, source_target_pairs={{0,2},{1,3},{2,0},{3,1},{4,6},{5,7},{6,4},{7,5},{8,10},{9,11},{10,... | collective-permute-start | bytes 884744 | tf_op jit(solution)/shard_map/ppermute | solution.py:376
  24.2 30.0 %collective-permute-start.20 = (f32[8,32,256]{2,1,0:T(8,128)}, f32[8,32,256]{2,1,0:T(8,128)S(1)}, u32[]{:S(2)}, u32[]{:S(2)}) collective-permute-start(f32[8,32,256]{2,1,0:T(8,128)} %get-tuple-element.52), channel_id=1, source_target_pairs={{0,1},{1,2},{2,3},{3,0},{4,5},{5,6},{6,7},{7,4},{8,9},{9,10},{10,1... | collective-permute-start | bytes 786440 | tf_op jit(solution)/shard_map/ppermute | solution.py:376
  49.6 33.2 %collective-permute-start.6 = (f32[24,32,256]{2,1,0:T(8,128)}, f32[24,32,256]{2,1,0:T(8,128)S(1)}, u32[]{:S(2)}, u32[]{:S(2)}) collective-permute-start(f32[24,32,256]{2,1,0:T(8,128)} %pad_maximum_fusion), channel_id=1, source_target_pairs={{4,0},{8,4},{12,8},{16,12},{20,16},{24,20},{28,24},{5,1},{9,5},{13... | collective-permute-start | bytes 2359304 | tf_op jit(solution)/shard_map/ppermute | solution.py:379
  52.3 30.6 %collective-permute-start.5 = (f32[24,32,256]{2,1,0:T(8,128)}, f32[24,32,256]{2,1,0:T(8,128)S(1)}, u32[]{:S(2)}, u32[]{:S(2)}) collective-permute-start(f32[24,32,256]{2,1,0:T(8,128)} %pad_maximum_fusion), channel_id=1, source_target_pairs={{0,4},{4,8},{8,12},{12,16},{16,20},{20,24},{24,28},{1,5},{5,9},{9,... | collective-permute-start | bytes 2359304 | tf_op jit(solution)/shard_map/ppermute | solution.py:379
  54.3 24.0 %collective-permute-start.22 = (f32[8,32,256]{2,1,0:T(8,128)S(1)}, f32[8,32,256]{2,1,0:T(8,128)S(1)}, u32[]{:S(2)}, u32[]{:S(2)}) collective-permute-start(f32[8,32,256]{2,1,0:T(8,128)S(1)} %copy-done.36), channel_id=1, source_target_pairs={{0,2},{1,3},{2,0},{3,1},{4,6},{5,7},{6,4},{7,5},{8,10},{9,11},{10,... | collective-permute-start | bytes 786440 | tf_op jit(solution)/shard_map/ppermute | solution.py:376
  57.6 29.7 %collective-permute-start.12 = (f32[8,32,256]{2,1,0:T(8,128)}, f32[8,32,256]{2,1,0:T(8,128)S(1)}, u32[]{:S(2)}, u32[]{:S(2)}) collective-permute-start(f32[8,32,256]{2,1,0:T(8,128)} %get-tuple-element.45), channel_id=1, source_target_pairs={{0,1},{1,2},{2,3},{3,0},{4,5},{5,6},{6,7},{7,4},{8,9},{9,10},{10,1... | collective-permute-start | bytes 786440 | tf_op jit(solution)/shard_map/ppermute | solution.py:376
  65.6 25.2 %collective-permute-start.13 = (f32[8,32,256]{2,1,0:T(8,128)}, f32[8,32,256]{2,1,0:T(8,128)S(1)}, u32[]{:S(2)}, u32[]{:S(2)}) collective-permute-start(f32[8,32,256]{2,1,0:T(8,128)} %get-tuple-element.46), channel_id=1, source_target_pairs={{0,3},{1,0},{2,1},{3,2},{4,7},{5,4},{6,5},{7,6},{8,11},{9,8},{10,9... | collective-permute-start | bytes 786440 | tf_op jit(solution)/shard_map/ppermute | solution.py:376
  79.0 40.6 %collective-permute-start.27 = (f32[24,32,256]{2,1,0:T(8,128)}, f32[24,32,256]{2,1,0:T(8,128)}, u32[]{:S(2)}, u32[]{:S(2)}) collective-permute-start(f32[24,32,256]{2,1,0:T(8,128)} %constant_dynamic-update-slice_fusion.6), channel_id=1, source_target_pairs={{4,0},{8,4},{12,8},{16,12},{20,16},{24,20},{28,24},{5,1},{9,5},{13... | collective-permute-start | bytes 2359304 | tf_op jit(solution)/shard_map/ppermute | solution.py:379
  82.8 18.0 %collective-permute-start.14 = (f32[8,32,256]{2,1,0:T(8,128)}, f32[8,32,256]{2,1,0:T(8,128)S(1)}, u32[]{:S(2)}, u32[]{:S(2)}) collective-permute-start(f32[8,32,256]{2,1,0:T(8,128)} %get-tuple-element.47), channel_id=1, source_target_pairs={{0,2},{1,3},{2,0},{3,1},{4,6},{5,7},{6,4},{7,5},{8,10},{9,11},{10,... | collective-permute-start | bytes 786440 | tf_op jit(solution)/shard_map/ppermute | solution.py:376
  82.9 39.5 %collective-permute-start.26 = (f32[24,32,256]{2,1,0:T(8,128)}, f32[24,32,256]{2,1,0:T(8,128)}, u32[]{:S(2)}, u32[]{:S(2)}) collective-permute-start(f32[24,32,256]{2,1,0:T(8,128)} %constant_dynamic-update-slice_fusion.6), channel_id=1, source_target_pairs={{0,4},{4,8},{8,12},{12,16},{16,20},{20,24},{24,28},{1,5},{5,9},{9,... | collective-permute-start | bytes 2359304 | tf_op jit(solution)/shard_map/ppermute | solution.py:379
  87.4 13.5 %collective-permute-start.7 = (f32[8,32,256]{2,1,0:T(8,128)}, f32[8,32,256]{2,1,0:T(8,128)S(1)}, u32[]{:S(2)}, u32[]{:S(2)}) collective-permute-start(f32[8,32,256]{2,1,0:T(8,128)} %get-tuple-element.42), channel_id=1, source_target_pairs={{0,1},{1,2},{2,3},{3,0},{4,5},{5,6},{6,7},{7,4},{8,9},{9,10},{10,1... | collective-permute-start | bytes 786440 | tf_op jit(solution)/shard_map/ppermute | solution.py:376
  90.9 15.5 %collective-permute-start.8 = (f32[8,32,256]{2,1,0:T(8,128)}, f32[8,32,256]{2,1,0:T(8,128)S(1)}, u32[]{:S(2)}, u32[]{:S(2)}) collective-permute-start(f32[8,32,256]{2,1,0:T(8,128)} %get-tuple-element.43), channel_id=1, source_target_pairs={{0,3},{1,0},{2,1},{3,2},{4,7},{5,4},{6,5},{7,6},{8,11},{9,8},{10,9... | collective-permute-start | bytes 786440 | tf_op jit(solution)/shard_map/ppermute | solution.py:376
  100.8 16.8 %collective-permute-start.9 = (f32[8,32,256]{2,1,0:T(8,128)}, f32[8,32,256]{2,1,0:T(8,128)S(1)}, u32[]{:S(2)}, u32[]{:S(2)}) collective-permute-start(f32[8,32,256]{2,1,0:T(8,128)} %get-tuple-element.44), channel_id=1, source_target_pairs={{0,2},{1,3},{2,0},{3,1},{4,6},{5,7},{6,4},{7,5},{8,10},{9,11},{10,... | collective-permute-start | bytes 786440 | tf_op jit(solution)/shard_map/ppermute | solution.py:376
  100.8 32.7 %collective-permute-start.19 = (f32[24,32,256]{2,1,0:T(8,128)S(1)}, f32[24,32,256]{2,1,0:T(8,128)S(1)}, u32[]{:S(2)}, u32[]{:S(2)}) collective-permute-start(f32[24,32,256]{2,1,0:T(8,128)S(1)} %constant_dynamic-update-slice_fusion.3), channel_id=1, source_target_pairs={{4,0},{8,4},{12,8},{16,12},{20,16},{24,20},{28,24},{5,1},{9,5},{13... | collective-permute-start | bytes 2359304 | tf_op jit(solution)/shard_map/ppermute | solution.py:379
  106.5 28.8 %collective-permute-start.18 = (f32[24,32,256]{2,1,0:T(8,128)S(1)}, f32[24,32,256]{2,1,0:T(8,128)S(1)}, u32[]{:S(2)}, u32[]{:S(2)}) collective-permute-start(f32[24,32,256]{2,1,0:T(8,128)S(1)} %constant_dynamic-update-slice_fusion.3), channel_id=1, source_target_pairs={{0,4},{4,8},{8,12},{12,16},{16,20},{20,24},{24,28},{1,5},{5,9},{9,... | collective-permute-start | bytes 2359304 | tf_op jit(solution)/shard_map/ppermute | solution.py:379
  117.6 31.8 %collective-permute-start.11 = (f32[24,32,256]{2,1,0:T(8,128)S(1)}, f32[24,32,256]{2,1,0:T(8,128)S(1)}, u32[]{:S(2)}, u32[]{:S(2)}) collective-permute-start(f32[24,32,256]{2,1,0:T(8,128)S(1)} %constant_dynamic-update-slice_fusion), channel_id=1, source_target_pairs={{4,0},{8,4},{12,8},{16,12},{20,16},{24,20},{28,24},{5,1},{9,5},{13... | collective-permute-start | bytes 2359304 | tf_op jit(solution)/shard_map/ppermute | solution.py:379
  119.6 29.8 %collective-permute-start.10 = (f32[24,32,256]{2,1,0:T(8,128)S(1)}, f32[24,32,256]{2,1,0:T(8,128)S(1)}, u32[]{:S(2)}, u32[]{:S(2)}) collective-permute-start(f32[24,32,256]{2,1,0:T(8,128)S(1)} %constant_dynamic-update-slice_fusion), channel_id=1, source_target_pairs={{0,4},{4,8},{8,12},{12,16},{16,20},{20,24},{24,28},{1,5},{5,9},{9,... | collective-permute-start | bytes 2359304 | tf_op jit(solution)/shard_map/ppermute | solution.py:379
  131.1 33.1 %collective-permute-start.31 = (f32[8,32,256]{2,1,0:T(8,128)S(1)}, f32[8,32,256]{2,1,0:T(8,128)S(1)}, u32[]{:S(2)}, u32[]{:S(2)}) collective-permute-start(f32[8,32,256]{2,1,0:T(8,128)S(1)} %get-tuple-element.64), channel_id=1, source_target_pairs={{0,1},{1,2},{2,3},{3,0},{4,5},{5,6},{6,7},{7,4},{8,9},{9,10},{10,1... | collective-permute-start | bytes 786440 | tf_op jit(solution)/shard_map/ppermute | solution.py:376
  133.6 32.0 %collective-permute-start.32 = (f32[8,32,256]{2,1,0:T(8,128)S(1)}, f32[8,32,256]{2,1,0:T(8,128)S(1)}, u32[]{:S(2)}, u32[]{:S(2)}) collective-permute-start(f32[8,32,256]{2,1,0:T(8,128)S(1)} %get-tuple-element.65), channel_id=1, source_target_pairs={{0,3},{1,0},{2,1},{3,2},{4,7},{5,4},{6,5},{7,6},{8,11},{9,8},{10,9... | collective-permute-start | bytes 786440 | tf_op jit(solution)/shard_map/ppermute | solution.py:376
  135.3 42.6 %collective-permute-start.33 = (f32[8,32,256]{2,1,0:T(8,128)S(1)}, f32[8,32,256]{2,1,0:T(8,128)S(1)}, u32[]{:S(2)}, u32[]{:S(2)}) collective-permute-start(f32[8,32,256]{2,1,0:T(8,128)S(1)} %get-tuple-element.66), channel_id=1, source_target_pairs={{0,2},{1,3},{2,0},{3,1},{4,6},{5,7},{6,4},{7,5},{8,10},{9,11},{10,... | collective-permute-start | bytes 786440 | tf_op jit(solution)/shard_map/ppermute | solution.py:376
  149.5 29.5 %collective-permute-start.28 = (f32[8,32,256]{2,1,0:T(8,128)S(1)}, f32[8,32,256]{2,1,0:T(8,128)S(1)}, u32[]{:S(2)}, u32[]{:S(2)}) collective-permute-start(f32[8,32,256]{2,1,0:T(8,128)S(1)} %get-tuple-element.60), channel_id=1, source_target_pairs={{0,1},{1,2},{2,3},{3,0},{4,5},{5,6},{6,7},{7,4},{8,9},{9,10},{10,1... | collective-permute-start | bytes 786440 | tf_op jit(solution)/shard_map/ppermute | solution.py:376
  149.5 32.3 %collective-permute-start.29 = (f32[8,32,256]{2,1,0:T(8,128)S(1)}, f32[8,32,256]{2,1,0:T(8,128)S(1)}, u32[]{:S(2)}, u32[]{:S(2)}) collective-permute-start(f32[8,32,256]{2,1,0:T(8,128)S(1)} %get-tuple-element.61), channel_id=1, source_target_pairs={{0,3},{1,0},{2,1},{3,2},{4,7},{5,4},{6,5},{7,6},{8,11},{9,8},{10,9... | collective-permute-start | bytes 786440 | tf_op jit(solution)/shard_map/ppermute | solution.py:376
  164.3 34.4 %collective-permute-start.30 = (f32[8,32,256]{2,1,0:T(8,128)S(1)}, f32[8,32,256]{2,1,0:T(8,128)S(1)}, u32[]{:S(2)}, u32[]{:S(2)}) collective-permute-start(f32[8,32,256]{2,1,0:T(8,128)S(1)} %get-tuple-element.62), channel_id=1, source_target_pairs={{0,2},{1,3},{2,0},{3,1},{4,6},{5,7},{6,4},{7,5},{8,10},{9,11},{10,... | collective-permute-start | bytes 786440 | tf_op jit(solution)/shard_map/ppermute | solution.py:376
  166.3 32.3 %collective-permute-start.23 = (f32[8,32,256]{2,1,0:T(8,128)S(1)}, f32[8,32,256]{2,1,0:T(8,128)S(1)}, u32[]{:S(2)}, u32[]{:S(2)}) collective-permute-start(f32[8,32,256]{2,1,0:T(8,128)S(1)} %get-tuple-element.56), channel_id=1, source_target_pairs={{0,1},{1,2},{2,3},{3,0},{4,5},{5,6},{6,7},{7,4},{8,9},{9,10},{10,1... | collective-permute-start | bytes 786440 | tf_op jit(solution)/shard_map/ppermute | solution.py:376
  177.9 52.0 %collective-permute-start.15 = (f32[8,32,256]{2,1,0:T(8,128)S(1)}, f32[8,32,256]{2,1,0:T(8,128)S(1)}, u32[]{:S(2)}, u32[]{:S(2)}) collective-permute-start(f32[8,32,256]{2,1,0:T(8,128)S(1)} %get-tuple-element.49), channel_id=1, source_target_pairs={{0,1},{1,2},{2,3},{3,0},{4,5},{5,6},{6,7},{7,4},{8,9},{9,10},{10,1... | collective-permute-start | bytes 786440 | tf_op jit(solution)/shard_map/ppermute | solution.py:376
  179.0 51.0 %collective-permute-start.16 = (f32[8,32,256]{2,1,0:T(8,128)S(1)}, f32[8,32,256]{2,1,0:T(8,128)S(1)}, u32[]{:S(2)}, u32[]{:S(2)}) collective-permute-start(f32[8,32,256]{2,1,0:T(8,128)S(1)} %get-tuple-element.50), channel_id=1, source_target_pairs={{0,3},{1,0},{2,1},{3,2},{4,7},{5,4},{6,5},{7,6},{8,11},{9,8},{10,9... | collective-permute-start | bytes 786440 | tf_op jit(solution)/shard_map/ppermute | solution.py:376
  181.8 48.2 %collective-permute-start.17 = (f32[8,32,256]{2,1,0:T(8,128)S(1)}, f32[8,32,256]{2,1,0:T(8,128)S(1)}, u32[]{:S(2)}, u32[]{:S(2)}) collective-permute-start(f32[8,32,256]{2,1,0:T(8,128)S(1)} %get-tuple-element.51), channel_id=1, source_target_pairs={{0,2},{1,3},{2,0},{3,1},{4,6},{5,7},{6,4},{7,5},{8,10},{9,11},{10,... | collective-permute-start | bytes 786440 | tf_op jit(solution)/shard_map/ppermute | solution.py:376
  198.7 28.0 %collective-permute-start.25 = (f32[8,32,256]{2,1,0:T(8,128)S(1)}, f32[8,32,256]{2,1,0:T(8,128)S(1)}, u32[]{:S(2)}, u32[]{:S(2)}) collective-permute-start(f32[8,32,256]{2,1,0:T(8,128)S(1)} %get-tuple-element.58), channel_id=1, source_target_pairs={{0,2},{1,3},{2,0},{3,1},{4,6},{5,7},{6,4},{7,5},{8,10},{9,11},{10,... | collective-permute-start | bytes 786440 | tf_op jit(solution)/shard_map/ppermute | solution.py:376
  (39 other events, 475.1 us)

commit v6 on v4

v6 whole, which is shorter than its diff:
```python
import functools

import jax
import jax.numpy as jnp
from jax import lax
from jax.experimental import pallas as pl
from jax.experimental.pallas import tpu as pltpu
from jax.sharding import PartitionSpec as P

TILE = 8
ANYWHERE = pl.BlockSpec(memory_space=pl.ANY)
SCALARS = pl.BlockSpec(memory_space=pltpu.SMEM)


def whole(array):
    return pl.BlockSpec(array.shape, lambda *_: (0,) * array.ndim)


def params(mib=48):
    return pltpu.CompilerParams(vmem_limit_bytes=mib * 1024 * 1024)


def matrix_kernel(pattern_ref, weights_ref, out_ref):
    terms, entries, modes = pattern_ref.shape
    rows = lax.broadcasted_iota(jnp.int32, (modes, modes), 0)
    for term in range(terms):
        flipped = jnp.zeros((modes, modes), jnp.float32)
        for entry in range(entries):
            hits = pattern_ref[term, entry : entry + 1, :] == rows
            flipped = flipped + jnp.where(hits, weights_ref[term, entry : entry + 1, :], 0.0)
        coupling = 0.5 * (flipped + flipped.T)
        high = coupling.astype(jnp.bfloat16)
        at = slice(term * modes, (term + 1) * modes)
        out_ref[:modes, at] = high
        out_ref[modes:, at] = (coupling - high.astype(jnp.float32)).astype(jnp.bfloat16)


def coupling_matrices(pattern, weights):
    terms, modes, _ = pattern.shape
    pattern, weights = jnp.swapaxes(pattern, 1, 2), jnp.swapaxes(weights, 1, 2)
    shape = (2 * modes, terms * modes)
    return pl.pallas_call(
        matrix_kernel,
        grid=(1,),
        in_specs=[whole(pattern), whole(weights)],
        out_specs=pl.BlockSpec(shape, lambda i: (0, 0)),
        out_shape=jax.ShapeDtypeStruct(shape, jnp.bfloat16),
        compiler_params=params(),
        name="coupling",
    )(pattern, weights)


def edge_count(halves):
    return 1 if halves == 2 else 2


def pack_kernel(extras, halves, *refs):
    out_ref = refs[-1]
    half = pl.program_id(0)
    per_field = 3 if extras else 1
    for field in range(2):
        rows_ref, *tiles = refs[field * per_field : (field + 1) * per_field]
        rows = rows_ref.shape[1]
        out_ref[field, 0, :rows] = jnp.swapaxes(rows_ref[...], 0, 1)
        if extras:
            before = jnp.swapaxes(tiles[0][...], 0, 1)[TILE - 1]
            after = jnp.swapaxes(tiles[1][...], 0, 1)[0]
            if halves == 2:
                out_ref[field, 0, rows] = jnp.where(half == 1, before, after)
            else:
                out_ref[field, 0, rows] = jnp.where(half > 0, before, 0.0)
                out_ref[field, 0, rows + 1] = jnp.where(half < halves - 1, after, 0.0)


def pack(state, adjoint, group, rows, halves):
    modes, height, width = state.shape
    extras = group == 0
    half_tiles = height // halves // TILE
    groups = height // halves // rows
    total = rows + (edge_count(halves) if extras else 0)

    def tile(index):
        return pl.BlockSpec(
            (modes, TILE, width),
            lambda h: (0, jnp.clip(h * half_tiles + index, 0, height // TILE - 1), 0),
        )

    specs = [pl.BlockSpec((modes, rows, width), lambda h: (0, h * groups + group, 0))]
    if extras:
        specs += [tile(-1), tile(half_tiles)]
    return pl.pallas_call(
        functools.partial(pack_kernel, extras, halves),
        grid=(halves,),
        in_specs=specs * 2,
        out_specs=pl.BlockSpec((2, 1, total, modes, width), lambda h: (0, h, 0, 0, 0)),
        out_shape=jax.ShapeDtypeStruct((2, halves, total, modes, width), jnp.float32),
        compiler_params=params(60),
        name="pack",
    )(*([state] * len(specs) + [adjoint] * len(specs)))


def gather_kernel(part_ref, *refs):
    refs[-1][...] = part_ref[...]


def gather(pieces, rows, index, earlier):
    owners, _, modes, width = pieces.shape
    shape = (owners, rows, modes, width)
    return pl.pallas_call(
        gather_kernel,
        grid=(1,),
        in_specs=[pl.BlockSpec(shape, lambda i: (0, index, 0, 0))] + [ANYWHERE] * len(earlier),
        out_specs=pl.BlockSpec(shape, lambda i: (0, 0, 0, 0)),
        out_shape=jax.ShapeDtypeStruct(shape, jnp.float32),
        compiler_params=params(),
        name="gather",
    )(pieces, *earlier)


def operator_kernel(shifts, terms, part, parts, me_ref, coef_ref, coef_below, coef_above, matrix_ref, *refs):
    below, above, pieces, before, after = refs[:5]
    owners, rows, block, width = pieces.shape
    outs = refs[-owners - 6 : -6]
    slots, mixed, faces = ((refs[-6], refs[-5]), (refs[-4], refs[-3])), refs[-2], refs[-1]
    modes = owners * block
    halves = owners // 2
    me = me_ref[0]
    half = lax.rem(me, halves)
    step = 16
    lanes = lax.broadcasted_iota(jnp.int32, (step, width), 1)
    last = rows - 1

    def with_sides(values, lane):
        left = jnp.where(lane == 0, 0.0, pltpu.roll(values, 1, 1))
        right = jnp.where(lane == width - 1, 0.0, pltpu.roll(values, width - 1, 1))
        return left, right

    first_row = (half * parts + part) * rows
    height = coef_ref.shape[1]
    face_lanes = lax.broadcasted_iota(jnp.int32, (rows, width), 1)
    face_rows = lax.broadcasted_iota(jnp.int32, (rows, width), 0)
    for term in range(terms):
        centre = coef_ref[term, pl.ds(pl.multiple_of(first_row, TILE), rows), :]
        row_before = coef_ref[term, pl.ds(jnp.maximum(first_row - 1, 0), 1), :]
        row_after = coef_ref[term, pl.ds(jnp.minimum(first_row + rows, height - 1), 1), :]
        row_before = jnp.where(first_row > 0, row_before, 0.0)
        row_after = jnp.where(first_row + rows < height, row_after, 0.0)
        up = jnp.where(face_rows == 0, row_before, pltpu.roll(centre, 1, 0))
        down = jnp.where(face_rows == last, row_after, pltpu.roll(centre, last, 0))
        left, right = with_sides(centre, face_lanes)
        others = (coef_below[term], coef_above[term], up, down, left, right)
        for side, other in enumerate(others):
            faces[6 * term + side] = 0.5 * (centre + other)

    def beyond(source, which, here):
        ref = (before, after)[which]
        if part != (0, parts - 1)[which]:
            return ref[source, 0, here, :]
        if halves == 2:
            return jnp.where(half == 1 - which, ref[source, 0, here, :], 0.0)
        return ref[source, which, here, :]

    def stencil(row, slot):
        high, low = slots[slot]
        for source in range(owners):
            for start in range(0, block, step):
                here = pl.ds(start, step)
                centre = pieces[source, row, here, :]
                up = pieces[source, row - 1, here, :] if row > 0 else beyond(source, 0, here)
                down = pieces[source, row + 1, here, :] if row < last else beyond(source, 1, here)
                left, right = with_sides(centre, lanes)
                others = (below[source, row, here, :], above[source, row, here, :], up, down, left, right)
                slopes = [centre - other for other in others]
                for term in range(terms):
                    total = faces[6 * term, row : row + 1, :] * slopes[0]
                    for side in range(1, 6):
                        total = total + faces[6 * term + side, row : row + 1, :] * slopes[side]
                    rounded = total.astype(jnp.bfloat16)
                    at = pl.ds(term * modes + source * block + start, step)
                    high[at, :] = rounded
                    low[at, :] = (total - rounded.astype(jnp.float32)).astype(jnp.bfloat16)

    def mix(row, slot):
        high, low = slots[slot]
        both = jnp.dot(matrix_ref[...], high[...], preferred_element_type=jnp.float32)
        rest = jnp.dot(matrix_ref[:modes, :], low[...], preferred_element_type=jnp.float32)
        mixed[...] = both[:modes] + both[modes:] + rest
        for index, shift in enumerate([0] + shifts):
            owner = lax.rem(me + shift, owners)
            outs[index][row] = mixed[pl.ds(pl.multiple_of(owner * block, block), block), :]

    stencil(0, 0)
    for row in range(rows):
        if row < last:
            stencil(row + 1, (row + 1) % 2)
        mix(row, row % 2)


def apply_operator(me, coef, coef_near, matrix, groups, near, part, rows, shifts):
    owners, _, block, width = near[0].shape
    modes = owners * block
    terms, height, _ = coef.shape
    parts = height // (owners // 2) // rows
    edges = edge_count(owners // 2)
    group_rows = rows * parts // len(groups)

    def at(count, first):
        return pl.BlockSpec((owners, count, block, width), lambda i: (0, first // count, 0, 0))

    operands = [coef, *coef_near, matrix, *near]
    in_specs = [SCALARS, whole(coef)]
    in_specs += [pl.BlockSpec((terms, rows, width), lambda i: (0, part, 0))] * 2 + [whole(matrix), *map(whole, near)]
    for first, count in ((part * rows, rows), (part * rows - 1, 1), ((part + 1) * rows, 1)):
        if 0 <= first < parts * rows:
            operands.append(groups[first // group_rows])
            in_specs.append(at(count, first % group_rows))
        else:
            operands.append(groups[0])
            in_specs.append(at(edges, group_rows))
    shape = (rows, block, width)
    return pl.pallas_call(
        functools.partial(operator_kernel, shifts, terms, part, parts),
        grid=(1,),
        in_specs=in_specs,
        out_specs=[pl.BlockSpec(shape, lambda i: (0, 0, 0))] * owners,
        out_shape=[jax.ShapeDtypeStruct(shape, jnp.float32)] * owners,
        scratch_shapes=[pltpu.VMEM((terms * modes, width), jnp.bfloat16)] * 4
        + [pltpu.VMEM((modes, width), jnp.float32), pltpu.VMEM((6 * terms, rows, width), jnp.float32)],
        compiler_params=params(),
        name="operator",
    )(me, *operands)


def finish_kernel(shifts, me_ref, *refs):
    owners = len(shifts) + 1
    halves = owners // 2
    mixed = refs[:owners]
    state_ref, control_ref = refs[owners : owners + 2]
    state_out, adjoint_out = refs[-2:]
    half = pl.program_id(0)
    for index, shift in enumerate([0] + shifts):
        source = lax.rem(me_ref[0] + owners - shift, owners)

        @pl.when(source == half)
        def _(index=index):
            adjoint_out[...] = jnp.swapaxes(mixed[index][...], 0, 1) - control_ref[...]

        @pl.when(source == halves + half)
        def _(index=index):
            state_out[...] = state_ref[...] + jnp.swapaxes(mixed[index][...], 0, 1)


def finish(me, mixed, state, control, outputs, part, shifts):
    modes, _, width = state.shape
    owners = len(mixed)
    rows = mixed[0].shape[0]
    parts = state.shape[1] // (owners // 2) // rows
    block = pl.BlockSpec((modes, rows, width), lambda h: (0, h * parts + part, 0))
    in_specs = [SCALARS] + [whole(m) for m in mixed] + [block] * 2
    operands = [me, *mixed, state, control]
    aliases = {}
    if outputs is not None:
        aliases = {len(operands) + i: i for i in range(2)}
        in_specs += [ANYWHERE] * 2
        operands += list(outputs)
    return pl.pallas_call(
        functools.partial(finish_kernel, shifts),
        grid=(owners // 2,),
        in_specs=in_specs,
        out_specs=[block] * 2,
        out_shape=[jax.ShapeDtypeStruct(state.shape, jnp.float32)] * 2,
        input_output_aliases=aliases,
        compiler_params=params(60),
        name="finish",
    )(*operands)


def shards(state, control, adjoint, coefficient, pattern, weights):
    shape = state.shape
    modes, _, height, width = shape
    control_residual = 0.5 * control - adjoint
    state, control, adjoint = (a.reshape(modes, height, width) for a in (state, control, adjoint))
    coef = coefficient[:, 0]
    owners = lax.axis_size("mode")
    rows = TILE
    parts = height // (owners // 2) // rows
    planes = lax.axis_size("space")
    forward = [(i, i + 1) for i in range(planes - 1)]
    backward = [(i + 1, i) for i in range(planes - 1)]
    me = lax.axis_index("mode").astype(jnp.int32).reshape(1)
    shifts = sorted(range(1, owners), key=lambda s: min(s, owners - s))

    def move(array, shift):
        return lax.ppermute(array, "mode", [(i, (i + shift) % owners) for i in range(owners)])

    def beside(array):
        return lax.ppermute(array, "space", forward), lax.ppermute(array, "space", backward)

    matrix = coupling_matrices(pattern, weights)
    half_rows = parts * rows
    first = lax.rem(me[0], owners // 2) * half_rows
    coef_near = beside(lax.dynamic_slice_in_dim(coef, first, half_rows, 1))
    per_group = max(parts // 2, 1)
    groups = []
    for group in range(parts // per_group):
        packed = pack(state, adjoint, group, per_group * rows, owners // 2)
        packed = packed.reshape((owners,) + packed.shape[2:])
        groups.append(lax.all_to_all(packed, "mode", 0, 0, tiled=True))

    outputs, mixed, earlier = None, [], list(coef_near)
    for part in range(parts):
        if part >= per_group:
            earlier = earlier + [mixed[part - per_group][0]]
        body = gather(groups[part // per_group], rows, part % per_group, earlier)
        near, earlier = beside(body), [body]
        mixed.append(apply_operator(me, coef, coef_near, matrix, groups, near, part, rows, shifts))
        returned = [mixed[part][0]] + [move(m, shift) for m, shift in zip(mixed[part][1:], shifts)]
        outputs = finish(me, returned, state, control, outputs, part, shifts)
    return outputs[0].reshape(shape), control_residual, outputs[1].reshape(shape)


def solution(mesh):
    split = P("mode", "space", None, None)
    in_specs = (split, split, split, P(None, "space", None, None), P(), P())
    return jax.shard_map(shards, mesh=mesh, in_specs=in_specs, out_specs=(split, split, split), check_vma=False)
```

time: 238 us -> 245 us (1.029)
  starting transfers between devices: 52.6 us -> 76.1 us
  waiting for transfers between devices: 125 us -> 115 us
  local copies, waits for them, and re-layouts: 6.63 us -> 2.4 us
  Pallas kernels: 48.9 us -> 45.8 us
    ppermute x12, waiting for transfers between devices: 95.8 us -> 32.4 us  [move(): lax.ppermute(array, 'mode', [(i, (i + shift) % owners) for i in range(own...]
    all_to_all x0 -> x2, waiting for transfers between devices: none -> 48.4 us  [shards(): groups.append(lax.all_to_all(packed, 'mode', 0, 0, tiled=True))]
    ppermute x3 -> x5, waiting for transfers between devices: 2.37 us -> 11.9 us  [beside(): lax.ppermute(array, 'space', backward)]
    all_to_all x0 -> x2, starting transfers between devices: none -> 9.44 us  [shards(): groups.append(lax.all_to_all(packed, 'mode', 0, 0, tiled=True))]
    ppermute x3 -> x5, starting transfers between devices: 13.6 us -> 22.9 us  [beside(): lax.ppermute(array, 'space', backward)]
    pallas_call x5 -> x10, Pallas kernels: 41.7 us -> 35.3 us  [the longest x4 25.2 us: apply_operator(): pl.pallas_call(functools.partial(operator_kernel, shifts, terms, part, pa...]
    ppermute x3 -> x5, starting transfers between devices: 5.87 us -> 10.8 us  [beside(): lax.ppermute(array, 'space', forward)]
    ppermute x3 -> x5, waiting for transfers between devices: 26.8 us -> 21.9 us  [beside(): lax.ppermute(array, 'space', forward)]
  transfers between devices with their start and end apart: 18 -> 24, of which waited for: 9 -> 14; matrix products, arithmetic and copies ran while one was open for 2% -> 1% of each run, Pallas kernels for 18% -> 16%
where the time goes in v6:
time: 245 us; the launch traced here: 242 us
  waiting for transfers between devices  115 us (47%)
  starting transfers between devices  76.1 us (31%)
  Pallas kernels  45.8 us (19%)
    all_to_all x2, waiting for transfers between devices, shards(): groups.append(lax.all_to_all(packed, 'mode', 0, 0, tiled=True))  48.4 us
    ppermute x12, starting transfers between devices, move(): lax.ppermute(array, 'mode', [(i, (i + shift) % owners) for i in range(own...  32.9 us
    ppermute x12, waiting for transfers between devices, move(): lax.ppermute(array, 'mode', [(i, (i + shift) % owners) for i in range(own...  32.4 us
    pallas_call x4, Pallas kernels, apply_operator(): pl.pallas_call(functools.partial(operator_kernel, shifts, terms, part, pa...  25.2 us
    ppermute x5, starting transfers between devices, beside(): lax.ppermute(array, 'space', backward)  22.9 us
    ppermute x5, waiting for transfers between devices, beside(): lax.ppermute(array, 'space', forward)  21.9 us
    ppermute x5, waiting for transfers between devices, beside(): lax.ppermute(array, 'space', backward)  11.9 us
    ppermute x5, starting transfers between devices, beside(): lax.ppermute(array, 'space', forward)  10.8 us
  transfers between devices with their start and end apart: 24, of which 14 were waited for; matrix products, arithmetic and copies ran while one was open for 1% of the time, Pallas kernels for 16%

profile of v6, /device:TPU:4, one launch (start us, length us, event | category | flops | bytes accessed | tf_op | source)
XLA Modules:
  0.0 241.6 jit_solution(5749931978188141368)
XLA Ops:
  0.6 3.5 %pack.3 = f32[2,2,17,32,256]{4,3,2,1,0:T(8,128)} custom-call(f32[32,64,256]{2,1,0:T(8,128)} %bitcast.23, f32[32,64,256]{2,1,0:T(8,128)} %bitcast.24, f32[32,64,256]{2,1,0:T(8,128)} %bitcast.25, f32[32,64,256]{2,1,0:T(8,128)} %bitcast.31, f32[32,64,256]{2,1,0:T(8,128)} %bitcast.32, f32[32,64,256]{2,1,0:T(8,128)} %bitcast.33), custom_call_target="tpu_custom_call" | custom-call | tf_op jit(solution)/shard_map/pack/pallas_call | solution.py:91
  4.2 4.9 %all-to-all-start.1 = ((f32[4,17,32,256]{3,2,1,0:T(8,128)}), f32[4,17,32,256]{3,2,1,0:T(8,128)S(1)}, u32[]{:S(2)}, u32[]{:S(2)}) async-start(f32[4,17,32,256]{3,2,1,0:T(8,128)} %bitcast.41), calls=%async_computation.1 | async-start | bytes 4456448 | tf_op jit(solution)/shard_map/all_to_all | solution.py:308
  9.0 2.7 %pack.2 = f32[2,2,16,32,256]{4,3,2,1,0:T(8,128)} custom-call(f32[32,64,256]{2,1,0:T(8,128)} %bitcast.26, f32[32,64,256]{2,1,0:T(8,128)} %bitcast.34), custom_call_target="tpu_custom_call" | custom-call | tf_op jit(solution)/shard_map/pack/pallas_call | solution.py:91
  11.8 48.3 %all-to-all-done.1.part_ref.refs_2_.refs_3_.refs_4_ = f32[4,17,32,256]{3,2,1,0:T(8,128)S(1)} async-done(((f32[4,17,32,256]{3,2,1,0:T(8,128)}), f32[4,17,32,256]{3,2,1,0:T(8,128)S(1)}, u32[]{:S(2)}, u32[]{:S(2)}) %all-to-all-start.1) | async-done | bytes 2228256 | tf_op jit(solution)/shard_map/all_to_all | solution.py:308
  60.0 4.6 %all-to-all-start = ((f32[4,16,32,256]{3,2,1,0:T(8,128)}), f32[4,16,32,256]{3,2,1,0:T(8,128)}, u32[]{:S(2)}, u32[]{:S(2)}) async-start(f32[4,16,32,256]{3,2,1,0:T(8,128)} %bitcast.42), calls=%async_computation | async-start | bytes 4194304 | tf_op jit(solution)/shard_map/all_to_all | solution.py:308
  66.6 4.5 %collective-permute-start.1 = (f32[7,32,256]{2,1,0:T(8,128)S(1)}, f32[7,32,256]{2,1,0:T(8,128)S(1)}, u32[]{:S(2)}, u32[]{:S(2)}) collective-permute-start(f32[7,32,256]{2,1,0:T(8,128)S(1)} %dynamic-slice_bitcast_fusion), channel_id=1, source_target_pairs={{4,0},{8,4},{12,8},{16,12},{20,16},{24,20},{28,24},{5,1},{9,5},{13... | collective-permute-start | bytes 688136 | tf_op jit(solution)/shard_map/ppermute | solution.py:297
  74.8 3.2 %collective-permute-start.2 = (f32[4,8,32,256]{3,2,1,0:T(8,128)S(1)}, f32[4,8,32,256]{3,2,1,0:T(8,128)S(1)}, u32[]{:S(2)}, u32[]{:S(2)}) collective-permute-start(f32[4,8,32,256]{3,2,1,0:T(8,128)S(1)} %gather.4.refs_0_), channel_id=1, source_target_pairs={{0,4},{4,8},{8,12},{12,16},{16,20},{20,24},{24,28},{1,5},{5,9},{9,... | collective-permute-start | bytes 3145736 | tf_op jit(solution)/shard_map/ppermute | solution.py:297
  78.0 3.9 %collective-permute-start.3 = (f32[4,8,32,256]{3,2,1,0:T(8,128)S(1)}, f32[4,8,32,256]{3,2,1,0:T(8,128)S(1)}, u32[]{:S(2)}, u32[]{:S(2)}) collective-permute-start(f32[4,8,32,256]{3,2,1,0:T(8,128)S(1)} %gather.4.refs_0_), channel_id=1, source_target_pairs={{4,0},{8,4},{12,8},{16,12},{20,16},{24,20},{28,24},{5,1},{9,5},{13... | collective-permute-start | bytes 3145736 | tf_op jit(solution)/shard_map/ppermute | solution.py:297
  84.8 4.5 %collective-permute-start.5 = (f32[4,8,32,256]{3,2,1,0:T(8,128)}, f32[4,8,32,256]{3,2,1,0:T(8,128)}, u32[]{:S(2)}, u32[]{:S(2)}) collective-permute-start(f32[4,8,32,256]{3,2,1,0:T(8,128)} %gather.5.refs_0_), channel_id=1, source_target_pairs={{4,0},{8,4},{12,8},{16,12},{20,16},{24,20},{28,24},{5,1},{9,5},{13... | collective-permute-start | bytes 3145736 | tf_op jit(solution)/shard_map/ppermute | solution.py:297
  89.7 11.2 %collective-permute-done.2.refs_0_ = f32[4,8,32,256]{3,2,1,0:T(8,128)S(1)} collective-permute-done((f32[4,8,32,256]{3,2,1,0:T(8,128)S(1)}, f32[4,8,32,256]{3,2,1,0:T(8,128)S(1)}, u32[]{:S(2)}, u32[]{:S(2)}) %collective-permute-start.2) | collective-permute-done | bytes 1048608 | tf_op jit(solution)/shard_map/ppermute | solution.py:297
  100.9 4.5 %collective-permute-done.3.refs_1_ = f32[4,8,32,256]{3,2,1,0:T(8,128)S(1)} collective-permute-done((f32[4,8,32,256]{3,2,1,0:T(8,128)S(1)}, f32[4,8,32,256]{3,2,1,0:T(8,128)S(1)}, u32[]{:S(2)}, u32[]{:S(2)}) %collective-permute-start.3) | collective-permute-done | bytes 1048608 | tf_op jit(solution)/shard_map/ppermute | solution.py:297
  105.4 6.1 %operator.4 = (f32[8,32,256]{2,1,0:T(8,128)S(1)}, f32[8,32,256]{2,1,0:T(8,128)S(1)}, f32[8,32,256]{2,1,0:T(8,128)S(1)}, f32[8,32,256]{2,1,0:T(8,128)S(1)}) custom-call(s32[1]{0:T(128)} %bitcast.me_ref, f32[7,64,256]{2,1,0:T(8,128)S(1)} %bitcast.17, f32[7,32,256]{2,1,0:T(8,128)S(1)} %collective-permute-done.refs_0_.coef_below, ...), custom_call_target="tpu_custom_call" | custom-call | tf_op jit(solution)/shard_map/operator/pallas_call | solution.py:221
  115.6 5.3 %collective-permute-start.12 = (f32[4,8,32,256]{3,2,1,0:T(8,128)S(1)}, f32[4,8,32,256]{3,2,1,0:T(8,128)S(1)}, u32[]{:S(2)}, u32[]{:S(2)}) collective-permute-start(f32[4,8,32,256]{3,2,1,0:T(8,128)S(1)} %gather.6.refs_0_), channel_id=1, source_target_pairs={{4,0},{8,4},{12,8},{16,12},{20,16},{24,20},{28,24},{5,1},{9,5},{13... | collective-permute-start | bytes 3145736 | tf_op jit(solution)/shard_map/ppermute | solution.py:297
  120.9 2.6 %collective-permute-done.4.refs_0_ = f32[4,8,32,256]{3,2,1,0:T(8,128)} collective-permute-done((f32[4,8,32,256]{3,2,1,0:T(8,128)}, f32[4,8,32,256]{3,2,1,0:T(8,128)}, u32[]{:S(2)}, u32[]{:S(2)}) %collective-permute-start.4) | collective-permute-done | bytes 1048608 | tf_op jit(solution)/shard_map/ppermute | solution.py:297
  123.5 4.5 %collective-permute-done.5.refs_1_ = f32[4,8,32,256]{3,2,1,0:T(8,128)} collective-permute-done((f32[4,8,32,256]{3,2,1,0:T(8,128)}, f32[4,8,32,256]{3,2,1,0:T(8,128)}, u32[]{:S(2)}, u32[]{:S(2)}) %collective-permute-start.5) | collective-permute-done | bytes 1048608 | tf_op jit(solution)/shard_map/ppermute | solution.py:297
  128.0 6.8 %operator.5 = (f32[8,32,256]{2,1,0:T(8,128)S(1)}, f32[8,32,256]{2,1,0:T(8,128)S(1)}, f32[8,32,256]{2,1,0:T(8,128)S(1)}, f32[8,32,256]{2,1,0:T(8,128)S(1)}) custom-call(s32[1]{0:T(128)} %bitcast.me_ref, f32[7,64,256]{2,1,0:T(8,128)S(1)} %bitcast.18, f32[7,32,256]{2,1,0:T(8,128)S(1)} %collective-permute-done.refs_0_.coef_below, ...), custom_call_target="tpu_custom_call" | custom-call | tf_op jit(solution)/shard_map/operator/pallas_call | solution.py:221
  138.1 4.7 %collective-permute-start.7 = (f32[4,8,32,256]{3,2,1,0:T(8,128)S(1)}, f32[4,8,32,256]{3,2,1,0:T(8,128)S(1)}, u32[]{:S(2)}, u32[]{:S(2)}) collective-permute-start(f32[4,8,32,256]{3,2,1,0:T(8,128)S(1)} %gather.7), channel_id=1, source_target_pairs={{4,0},{8,4},{12,8},{16,12},{20,16},{24,20},{28,24},{5,1},{9,5},{13... | collective-permute-start | bytes 3145736 | tf_op jit(solution)/shard_map/ppermute | solution.py:297
  145.9 3.3 %collective-permute-start.17 = (f32[8,32,256]{2,1,0:T(8,128)S(1)}, f32[8,32,256]{2,1,0:T(8,128)S(1)}, u32[]{:S(2)}, u32[]{:S(2)}) collective-permute-start(f32[8,32,256]{2,1,0:T(8,128)S(1)} %get-tuple-element.38), channel_id=1, source_target_pairs={{0,3},{1,0},{2,1},{3,2},{4,7},{5,4},{6,5},{7,6},{8,11},{9,8},{10,9... | collective-permute-start | bytes 786440 | tf_op jit(solution)/shard_map/ppermute | solution.py:294
  152.8 6.2 %operator.7 = (f32[8,32,256]{2,1,0:T(8,128)S(1)}, f32[8,32,256]{2,1,0:T(8,128)S(1)}, f32[8,32,256]{2,1,0:T(8,128)S(1)}, f32[8,32,256]{2,1,0:T(8,128)S(1)}) custom-call(s32[1]{0:T(128)} %bitcast.me_ref, f32[7,64,256]{2,1,0:T(8,128)S(1)} %bitcast.19, f32[7,32,256]{2,1,0:T(8,128)S(1)} %collective-permute-done.refs_0_.coef_below, ...), custom_call_target="tpu_custom_call" | custom-call | tf_op jit(solution)/shard_map/operator/pallas_call | solution.py:221
  159.0 4.4 %collective-permute-start.19 = (f32[8,32,256]{2,1,0:T(8,128)S(1)}, f32[8,32,256]{2,1,0:T(8,128)S(1)}, u32[]{:S(2)}, u32[]{:S(2)}) collective-permute-start(f32[8,32,256]{2,1,0:T(8,128)S(1)} %copy-done.9), channel_id=1, source_target_pairs={{0,1},{1,2},{2,3},{3,0},{4,5},{5,6},{6,7},{7,4},{8,9},{9,10},{10,1... | collective-permute-start | bytes 786440 | tf_op jit(solution)/shard_map/ppermute | solution.py:294
  163.5 4.9 %collective-permute-done.6.refs_0_ = f32[4,8,32,256]{3,2,1,0:T(8,128)S(1)} collective-permute-done((f32[4,8,32,256]{3,2,1,0:T(8,128)S(1)}, f32[4,8,32,256]{3,2,1,0:T(8,128)S(1)}, u32[]{:S(2)}, u32[]{:S(2)}) %collective-permute-start.6) | collective-permute-done | bytes 1048608 | tf_op jit(solution)/shard_map/ppermute | solution.py:297
  168.3 2.4 %collective-permute-start.21 = (f32[8,32,256]{2,1,0:T(8,128)S(1)}, f32[8,32,256]{2,1,0:T(8,128)S(1)}, u32[]{:S(2)}, u32[]{:S(2)}) collective-permute-start(f32[8,32,256]{2,1,0:T(8,128)S(1)} %get-tuple-element.42), channel_id=1, source_target_pairs={{0,2},{1,3},{2,0},{3,1},{4,6},{5,7},{6,4},{7,5},{8,10},{9,11},{10,... | collective-permute-start | bytes 786440 | tf_op jit(solution)/shard_map/ppermute | solution.py:294
  172.2 6.2 %operator.6 = (f32[8,32,256]{2,1,0:T(8,128)S(1)}, f32[8,32,256]{2,1,0:T(8,128)S(1)}, f32[8,32,256]{2,1,0:T(8,128)S(1)}, f32[8,32,256]{2,1,0:T(8,128)S(1)}) custom-call(s32[1]{0:T(128)} %bitcast.me_ref, f32[7,64,256]{2,1,0:T(8,128)S(1)} %bitcast.20, f32[7,32,256]{2,1,0:T(8,128)S(1)} %collective-permute-done.refs_0_.coef_below, ...), custom_call_target="tpu_custom_call" | custom-call | tf_op jit(solution)/shard_map/operator/pallas_call | solution.py:221
  178.4 10.3 %collective-permute-done.18.refs_3_ = f32[8,32,256]{2,1,0:T(8,128)S(1)} collective-permute-done((f32[8,32,256]{2,1,0:T(8,128)S(1)}, f32[8,32,256]{2,1,0:T(8,128)S(1)}, u32[]{:S(2)}, u32[]{:S(2)}) %collective-permute-start.18) | collective-permute-done | bytes 262176 | tf_op jit(solution)/shard_map/ppermute | solution.py:294
  188.8 3.8 %collective-permute-start.9 = (f32[8,32,256]{2,1,0:T(8,128)S(1)}, f32[8,32,256]{2,1,0:T(8,128)S(1)}, u32[]{:S(2)}, u32[]{:S(2)}) collective-permute-start(f32[8,32,256]{2,1,0:T(8,128)S(1)} %get-tuple-element.31), channel_id=1, source_target_pairs={{0,3},{1,0},{2,1},{3,2},{4,7},{5,4},{6,5},{7,6},{8,11},{9,8},{10,9... | collective-permute-start | bytes 786440 | tf_op jit(solution)/shard_map/ppermute | solution.py:294
  193.9 13.2 %collective-permute-done.21.refs_3_ = f32[8,32,256]{2,1,0:T(8,128)S(1)} collective-permute-done((f32[8,32,256]{2,1,0:T(8,128)S(1)}, f32[8,32,256]{2,1,0:T(8,128)S(1)}, u32[]{:S(2)}, u32[]{:S(2)}) %collective-permute-start.21) | collective-permute-done | bytes 262176 | tf_op jit(solution)/shard_map/ppermute | solution.py:294
  207.1 12.0 %collective-permute-start.15 = (f32[8,32,256]{2,1,0:T(8,128)S(1)}, f32[8,32,256]{2,1,0:T(8,128)S(1)}, u32[]{:S(2)}, u32[]{:S(2)}) collective-permute-start(f32[8,32,256]{2,1,0:T(8,128)S(1)} %get-tuple-element.36), channel_id=1, source_target_pairs={{0,2},{1,3},{2,0},{3,1},{4,6},{5,7},{6,4},{7,5},{8,10},{9,11},{10,... | collective-permute-start | bytes 786440 | tf_op jit(solution)/shard_map/ppermute | solution.py:294
  220.9 2.6 %finish.4 = (f32[32,64,256]{2,1,0:T(8,128)}, f32[32,64,256]{2,1,0:T(8,128)}) custom-call(s32[1]{0:T(128)} %bitcast.me_ref, f32[8,32,256]{2,1,0:T(8,128)} %copy-done.3, f32[8,32,256]{2,1,0:T(8,128)} %copy-done.21, f32[8,32,256]{2,1,0:T(8,128)} %copy-done.22, f32[8,32,256]{2,1,0:T(8,128)} %copy-done.23, f32[32,64,256]{2,1,0:T(8,128)} %bitcast.27, ...), custom_call_target="tpu_custom_call" | custom-call | tf_op jit(solution)/shard_map/finish/pallas_call | solution.py:266
  223.5 2.5 %finish.5 = (f32[32,64,256]{2,1,0:T(8,128)}, f32[32,64,256]{2,1,0:T(8,128)}) custom-call(s32[1]{0:T(128)} %bitcast.me_ref, f32[8,32,256]{2,1,0:T(8,128)} %copy-done.2, f32[8,32,256]{2,1,0:T(8,128)} %copy-done.12, f32[8,32,256]{2,1,0:T(8,128)} %copy-done.13, f32[8,32,256]{2,1,0:T(8,128)} %copy-done.14, ...), custom_call_target="tpu_custom_call", output_to_operand_aliasing={{0}: (7, {}), {1}: (8, {})} | custom-call | tf_op jit(solution)/shard_map/finish/pallas_call | solution.py:266
  226.1 8.9 %collective-permute-done.15.refs_3_ = f32[8,32,256]{2,1,0:T(8,128)S(1)} collective-permute-done((f32[8,32,256]{2,1,0:T(8,128)S(1)}, f32[8,32,256]{2,1,0:T(8,128)S(1)}, u32[]{:S(2)}, u32[]{:S(2)}) %collective-permute-start.15) | collective-permute-done | bytes 262176 | tf_op jit(solution)/shard_map/ppermute | solution.py:294
  235.6 2.5 %finish.6 = (f32[32,64,256]{2,1,0:T(8,128)}, f32[32,64,256]{2,1,0:T(8,128)}) custom-call(s32[1]{0:T(128)} %bitcast.me_ref, f32[8,32,256]{2,1,0:T(8,128)} %copy-done.4, f32[8,32,256]{2,1,0:T(8,128)} %copy-done.16, f32[8,32,256]{2,1,0:T(8,128)} %copy-done.19, f32[8,32,256]{2,1,0:T(8,128)} %copy-done.20, ...), custom_call_target="tpu_custom_call", output_to_operand_aliasing={{0}: (7, {}), {1}: (8, {})} | custom-call | tf_op jit(solution)/shard_map/finish/pallas_call | solution.py:266
  239.1 2.5 %finish.7 = (f32[32,64,256]{2,1,0:T(8,128)}, f32[32,64,256]{2,1,0:T(8,128)}) custom-call(s32[1]{0:T(128)} %bitcast.me_ref, f32[8,32,256]{2,1,0:T(8,128)} %copy-done.5, f32[8,32,256]{2,1,0:T(8,128)} %copy-done.15, f32[8,32,256]{2,1,0:T(8,128)} %copy-done.17, f32[8,32,256]{2,1,0:T(8,128)} %copy-done.18, ...), custom_call_target="tpu_custom_call", output_to_operand_aliasing={{0}: (7, {}), {1}: (8, {})} | custom-call | tf_op jit(solution)/shard_map/finish/pallas_call | solution.py:266
  (81 shorter events, 29.0 us)
Async XLA Ops:
  4.2 55.9 %all-to-all-start.1 = ((f32[4,17,32,256]{3,2,1,0:T(8,128)}), f32[4,17,32,256]{3,2,1,0:T(8,128)S(1)}, u32[]{:S(2)}, u32[]{:S(2)}) async-start(f32[4,17,32,256]{3,2,1,0:T(8,128)} %bitcast.41), calls=%async_computation.1 | async-start | bytes 4456448 | tf_op jit(solution)/shard_map/all_to_all | solution.py:308
  60.0 21.8 %copy-start = (f32[4,17,32,256]{3,2,1,0:T(8,128)}, f32[4,17,32,256]{3,2,1,0:T(8,128)S(1)}, u32[]{:S(2)}) copy-start(f32[4,17,32,256]{3,2,1,0:T(8,128)S(1)} %all-to-all-done.1.part_ref.refs_2_.refs_3_.refs_4_) | copy-start | bytes 6684676
  60.0 52.3 %all-to-all-start = ((f32[4,16,32,256]{3,2,1,0:T(8,128)}), f32[4,16,32,256]{3,2,1,0:T(8,128)}, u32[]{:S(2)}, u32[]{:S(2)}) async-start(f32[4,16,32,256]{3,2,1,0:T(8,128)} %bitcast.42), calls=%async_computation | async-start | bytes 4194304 | tf_op jit(solution)/shard_map/all_to_all | solution.py:308
  64.7 8.2 %collective-permute-start = (f32[7,32,256]{2,1,0:T(8,128)S(1)}, f32[7,32,256]{2,1,0:T(8,128)S(1)}, u32[]{:S(2)}, u32[]{:S(2)}) collective-permute-start(f32[7,32,256]{2,1,0:T(8,128)S(1)} %dynamic-slice_bitcast_fusion), channel_id=1, source_target_pairs={{0,4},{4,8},{8,12},{12,16},{16,20},{20,24},{24,28},{1,5},{5,9},{9,... | collective-permute-start | bytes 688136 | tf_op jit(solution)/shard_map/ppermute | solution.py:297
  66.6 8.1 %collective-permute-start.1 = (f32[7,32,256]{2,1,0:T(8,128)S(1)}, f32[7,32,256]{2,1,0:T(8,128)S(1)}, u32[]{:S(2)}, u32[]{:S(2)}) collective-permute-start(f32[7,32,256]{2,1,0:T(8,128)S(1)} %dynamic-slice_bitcast_fusion), channel_id=1, source_target_pairs={{4,0},{8,4},{12,8},{16,12},{20,16},{24,20},{28,24},{5,1},{9,5},{13... | collective-permute-start | bytes 688136 | tf_op jit(solution)/shard_map/ppermute | solution.py:297
  74.8 26.1 %collective-permute-start.2 = (f32[4,8,32,256]{3,2,1,0:T(8,128)S(1)}, f32[4,8,32,256]{3,2,1,0:T(8,128)S(1)}, u32[]{:S(2)}, u32[]{:S(2)}) collective-permute-start(f32[4,8,32,256]{3,2,1,0:T(8,128)S(1)} %gather.4.refs_0_), channel_id=1, source_target_pairs={{0,4},{4,8},{8,12},{12,16},{16,20},{20,24},{24,28},{1,5},{5,9},{9,... | collective-permute-start | bytes 3145736 | tf_op jit(solution)/shard_map/ppermute | solution.py:297
  78.0 27.5 %collective-permute-start.3 = (f32[4,8,32,256]{3,2,1,0:T(8,128)S(1)}, f32[4,8,32,256]{3,2,1,0:T(8,128)S(1)}, u32[]{:S(2)}, u32[]{:S(2)}) collective-permute-start(f32[4,8,32,256]{3,2,1,0:T(8,128)S(1)} %gather.4.refs_0_), channel_id=1, source_target_pairs={{4,0},{8,4},{12,8},{16,12},{20,16},{24,20},{28,24},{5,1},{9,5},{13... | collective-permute-start | bytes 3145736 | tf_op jit(solution)/shard_map/ppermute | solution.py:297
  82.9 40.6 %collective-permute-start.4 = (f32[4,8,32,256]{3,2,1,0:T(8,128)}, f32[4,8,32,256]{3,2,1,0:T(8,128)}, u32[]{:S(2)}, u32[]{:S(2)}) collective-permute-start(f32[4,8,32,256]{3,2,1,0:T(8,128)} %gather.5.refs_0_), channel_id=1, source_target_pairs={{0,4},{4,8},{8,12},{12,16},{16,20},{20,24},{24,28},{1,5},{5,9},{9,... | collective-permute-start | bytes 3145736 | tf_op jit(solution)/shard_map/ppermute | solution.py:297
  84.8 43.2 %collective-permute-start.5 = (f32[4,8,32,256]{3,2,1,0:T(8,128)}, f32[4,8,32,256]{3,2,1,0:T(8,128)}, u32[]{:S(2)}, u32[]{:S(2)}) collective-permute-start(f32[4,8,32,256]{3,2,1,0:T(8,128)} %gather.5.refs_0_), channel_id=1, source_target_pairs={{4,0},{8,4},{12,8},{16,12},{20,16},{24,20},{28,24},{5,1},{9,5},{13... | collective-permute-start | bytes 3145736 | tf_op jit(solution)/shard_map/ppermute | solution.py:297
  113.7 32.2 %collective-permute-start.11 = (f32[4,8,32,256]{3,2,1,0:T(8,128)S(1)}, f32[4,8,32,256]{3,2,1,0:T(8,128)S(1)}, u32[]{:S(2)}, u32[]{:S(2)}) collective-permute-start(f32[4,8,32,256]{3,2,1,0:T(8,128)S(1)} %gather.6.refs_0_), channel_id=1, source_target_pairs={{0,4},{4,8},{8,12},{12,16},{16,20},{20,24},{24,28},{1,5},{5,9},{9,... | collective-permute-start | bytes 3145736 | tf_op jit(solution)/shard_map/ppermute | solution.py:297
  115.6 34.7 %collective-permute-start.12 = (f32[4,8,32,256]{3,2,1,0:T(8,128)S(1)}, f32[4,8,32,256]{3,2,1,0:T(8,128)S(1)}, u32[]{:S(2)}, u32[]{:S(2)}) collective-permute-start(f32[4,8,32,256]{3,2,1,0:T(8,128)S(1)} %gather.6.refs_0_), channel_id=1, source_target_pairs={{4,0},{8,4},{12,8},{16,12},{20,16},{24,20},{28,24},{5,1},{9,5},{13... | collective-permute-start | bytes 3145736 | tf_op jit(solution)/shard_map/ppermute | solution.py:297
  136.2 32.1 %collective-permute-start.6 = (f32[4,8,32,256]{3,2,1,0:T(8,128)S(1)}, f32[4,8,32,256]{3,2,1,0:T(8,128)S(1)}, u32[]{:S(2)}, u32[]{:S(2)}) collective-permute-start(f32[4,8,32,256]{3,2,1,0:T(8,128)S(1)} %gather.7), channel_id=1, source_target_pairs={{0,4},{4,8},{8,12},{12,16},{16,20},{20,24},{24,28},{1,5},{5,9},{9,... | collective-permute-start | bytes 3145736 | tf_op jit(solution)/shard_map/ppermute | solution.py:297
  138.1 32.7 %collective-permute-start.7 = (f32[4,8,32,256]{3,2,1,0:T(8,128)S(1)}, f32[4,8,32,256]{3,2,1,0:T(8,128)S(1)}, u32[]{:S(2)}, u32[]{:S(2)}) collective-permute-start(f32[4,8,32,256]{3,2,1,0:T(8,128)S(1)} %gather.7), channel_id=1, source_target_pairs={{4,0},{8,4},{12,8},{16,12},{20,16},{24,20},{28,24},{5,1},{9,5},{13... | collective-permute-start | bytes 3145736 | tf_op jit(solution)/shard_map/ppermute | solution.py:297
  142.8 16.1 %collective-permute-start.16 = (f32[8,32,256]{2,1,0:T(8,128)S(1)}, f32[8,32,256]{2,1,0:T(8,128)S(1)}, u32[]{:S(2)}, u32[]{:S(2)}) collective-permute-start(f32[8,32,256]{2,1,0:T(8,128)S(1)} %get-tuple-element.37), channel_id=1, source_target_pairs={{0,1},{1,2},{2,3},{3,0},{4,5},{5,6},{6,7},{7,4},{8,9},{9,10},{10,1... | collective-permute-start | bytes 786440 | tf_op jit(solution)/shard_map/ppermute | solution.py:294
  145.9 17.6 %collective-permute-start.17 = (f32[8,32,256]{2,1,0:T(8,128)S(1)}, f32[8,32,256]{2,1,0:T(8,128)S(1)}, u32[]{:S(2)}, u32[]{:S(2)}) collective-permute-start(f32[8,32,256]{2,1,0:T(8,128)S(1)} %get-tuple-element.38), channel_id=1, source_target_pairs={{0,3},{1,0},{2,1},{3,2},{4,7},{5,4},{6,5},{7,6},{8,11},{9,8},{10,9... | collective-permute-start | bytes 786440 | tf_op jit(solution)/shard_map/ppermute | solution.py:294
  150.4 38.4 %collective-permute-start.18 = (f32[8,32,256]{2,1,0:T(8,128)S(1)}, f32[8,32,256]{2,1,0:T(8,128)S(1)}, u32[]{:S(2)}, u32[]{:S(2)}) collective-permute-start(f32[8,32,256]{2,1,0:T(8,128)S(1)} %get-tuple-element.39), channel_id=1, source_target_pairs={{0,2},{1,3},{2,0},{3,1},{4,6},{5,7},{6,4},{7,5},{8,10},{9,11},{10,... | collective-permute-start | bytes 786440 | tf_op jit(solution)/shard_map/ppermute | solution.py:294
  159.0 19.5 %copy-start.4 = (f32[8,32,256]{2,1,0:T(8,128)}, f32[8,32,256]{2,1,0:T(8,128)S(1)}, u32[]{:S(2)}) copy-start(f32[8,32,256]{2,1,0:T(8,128)S(1)} %get-tuple-element.33.refs_0_) | copy-start | bytes 786436
  159.0 29.8 %collective-permute-start.19 = (f32[8,32,256]{2,1,0:T(8,128)S(1)}, f32[8,32,256]{2,1,0:T(8,128)S(1)}, u32[]{:S(2)}, u32[]{:S(2)}) collective-permute-start(f32[8,32,256]{2,1,0:T(8,128)S(1)} %copy-done.9), channel_id=1, source_target_pairs={{0,1},{1,2},{2,3},{3,0},{4,5},{5,6},{6,7},{7,4},{8,9},{9,10},{10,1... | collective-permute-start | bytes 786440 | tf_op jit(solution)/shard_map/ppermute | solution.py:294
  163.5 29.2 %collective-permute-start.20 = (f32[8,32,256]{2,1,0:T(8,128)S(1)}, f32[8,32,256]{2,1,0:T(8,128)S(1)}, u32[]{:S(2)}, u32[]{:S(2)}) collective-permute-start(f32[8,32,256]{2,1,0:T(8,128)S(1)} %get-tuple-element.41), channel_id=1, source_target_pairs={{0,3},{1,0},{2,1},{3,2},{4,7},{5,4},{6,5},{7,6},{8,11},{9,8},{10,9... | collective-permute-start | bytes 786440 | tf_op jit(solution)/shard_map/ppermute | solution.py:294
  168.3 38.8 %collective-permute-start.21 = (f32[8,32,256]{2,1,0:T(8,128)S(1)}, f32[8,32,256]{2,1,0:T(8,128)S(1)}, u32[]{:S(2)}, u32[]{:S(2)}) collective-permute-start(f32[8,32,256]{2,1,0:T(8,128)S(1)} %get-tuple-element.42), channel_id=1, source_target_pairs={{0,2},{1,3},{2,0},{3,1},{4,6},{5,7},{6,4},{7,5},{8,10},{9,11},{10,... | collective-permute-start | bytes 786440 | tf_op jit(solution)/shard_map/ppermute | solution.py:294
  170.8 48.4 %copy-start.10 = (f32[32,1,64,256]{3,2,1,0:T(8,128)S(1)}, f32[32,1,64,256]{3,2,1,0:T(8,128)}, u32[]{:S(2)}) copy-start(f32[32,1,64,256]{3,2,1,0:T(8,128)} %param.8) | copy-start | bytes 6291460
  170.8 48.4 %copy-start.11 = (f32[32,1,64,256]{3,2,1,0:T(8,128)S(1)}, f32[32,1,64,256]{3,2,1,0:T(8,128)}, u32[]{:S(2)}) copy-start(f32[32,1,64,256]{3,2,1,0:T(8,128)} %param.7) | copy-start | bytes 6291460
  170.8 36.4 %collective-permute-start.13 = (f32[8,32,256]{2,1,0:T(8,128)S(1)}, f32[8,32,256]{2,1,0:T(8,128)S(1)}, u32[]{:S(2)}, u32[]{:S(2)}) collective-permute-start(f32[8,32,256]{2,1,0:T(8,128)S(1)} %get-tuple-element.34), channel_id=1, source_target_pairs={{0,1},{1,2},{2,3},{3,0},{4,5},{5,6},{6,7},{7,4},{8,9},{9,10},{10,1... | collective-permute-start | bytes 786440 | tf_op jit(solution)/shard_map/ppermute | solution.py:294
  178.4 42.5 %copy-start.5 = (f32[8,32,256]{2,1,0:T(8,128)}, f32[8,32,256]{2,1,0:T(8,128)S(1)}, u32[]{:S(2)}) copy-start(f32[8,32,256]{2,1,0:T(8,128)S(1)} %get-tuple-element.29.refs_0_) | copy-start | bytes 786436
  188.8 32.1 %copy-start.14 = (f32[8,32,256]{2,1,0:T(8,128)}, f32[8,32,256]{2,1,0:T(8,128)S(1)}, u32[]{:S(2)}) copy-start(f32[8,32,256]{2,1,0:T(8,128)S(1)} %collective-permute-done.18.refs_3_) | copy-start | bytes 786436
  188.8 49.4 %collective-permute-start.8 = (f32[8,32,256]{2,1,0:T(8,128)S(1)}, f32[8,32,256]{2,1,0:T(8,128)S(1)}, u32[]{:S(2)}, u32[]{:S(2)}) collective-permute-start(f32[8,32,256]{2,1,0:T(8,128)S(1)} %get-tuple-element.30), channel_id=1, source_target_pairs={{0,1},{1,2},{2,3},{3,0},{4,5},{5,6},{6,7},{7,4},{8,9},{9,10},{10,1... | collective-permute-start | bytes 786440 | tf_op jit(solution)/shard_map/ppermute | solution.py:294
  188.8 32.1 %copy-start.21 = (f32[8,32,256]{2,1,0:T(8,128)}, f32[8,32,256]{2,1,0:T(8,128)S(1)}, u32[]{:S(2)}) copy-start(f32[8,32,256]{2,1,0:T(8,128)S(1)} %collective-permute-done.19.refs_1_) | copy-start | bytes 786436
  188.8 49.4 %collective-permute-start.9 = (f32[8,32,256]{2,1,0:T(8,128)S(1)}, f32[8,32,256]{2,1,0:T(8,128)S(1)}, u32[]{:S(2)}, u32[]{:S(2)}) collective-permute-start(f32[8,32,256]{2,1,0:T(8,128)S(1)} %get-tuple-element.31), channel_id=1, source_target_pairs={{0,3},{1,0},{2,1},{3,2},{4,7},{5,4},{6,5},{7,6},{8,11},{9,8},{10,9... | collective-permute-start | bytes 786440 | tf_op jit(solution)/shard_map/ppermute | solution.py:294
  192.6 28.3 %copy-start.22 = (f32[8,32,256]{2,1,0:T(8,128)}, f32[8,32,256]{2,1,0:T(8,128)S(1)}, u32[]{:S(2)}) copy-start(f32[8,32,256]{2,1,0:T(8,128)S(1)} %collective-permute-done.20.refs_2_) | copy-start | bytes 786436
  192.6 45.6 %collective-permute-start.10 = (f32[8,32,256]{2,1,0:T(8,128)S(1)}, f32[8,32,256]{2,1,0:T(8,128)S(1)}, u32[]{:S(2)}, u32[]{:S(2)}) collective-permute-start(f32[8,32,256]{2,1,0:T(8,128)S(1)} %get-tuple-element.32), channel_id=1, source_target_pairs={{0,2},{1,3},{2,0},{3,1},{4,6},{5,7},{6,4},{7,5},{8,10},{9,11},{10,... | collective-permute-start | bytes 786440 | tf_op jit(solution)/shard_map/ppermute | solution.py:294
  207.1 18.9 %collective-permute-start.14 = (f32[8,32,256]{2,1,0:T(8,128)S(1)}, f32[8,32,256]{2,1,0:T(8,128)S(1)}, u32[]{:S(2)}, u32[]{:S(2)}) collective-permute-start(f32[8,32,256]{2,1,0:T(8,128)S(1)} %get-tuple-element.35), channel_id=1, source_target_pairs={{0,3},{1,0},{2,1},{3,2},{4,7},{5,4},{6,5},{7,6},{8,11},{9,8},{10,9... | collective-permute-start | bytes 786440 | tf_op jit(solution)/shard_map/ppermute | solution.py:294
  207.1 27.8 %collective-permute-start.15 = (f32[8,32,256]{2,1,0:T(8,128)S(1)}, f32[8,32,256]{2,1,0:T(8,128)S(1)}, u32[]{:S(2)}, u32[]{:S(2)}) collective-permute-start(f32[8,32,256]{2,1,0:T(8,128)S(1)} %get-tuple-element.36), channel_id=1, source_target_pairs={{0,2},{1,3},{2,0},{3,1},{4,6},{5,7},{6,4},{7,5},{8,10},{9,11},{10,... | collective-permute-start | bytes 786440 | tf_op jit(solution)/shard_map/ppermute | solution.py:294
  (16 other events, 120.0 us)

commit v7 on v6

v7 whole, which is shorter than its diff:
```python
import functools

import jax
import jax.numpy as jnp
from jax import lax
from jax.experimental import pallas as pl
from jax.experimental.pallas import tpu as pltpu
from jax.sharding import PartitionSpec as P

TILE = 8
ANYWHERE = pl.BlockSpec(memory_space=pl.ANY)
SCALARS = pl.BlockSpec(memory_space=pltpu.SMEM)


def whole(array):
    return pl.BlockSpec(array.shape, lambda *_: (0,) * array.ndim)


def cost(micros):
    return pl.CostEstimate(flops=0, bytes_accessed=int(micros * 3.5e6), transcendentals=0)


def params(mib=48):
    return pltpu.CompilerParams(vmem_limit_bytes=mib * 1024 * 1024)


def matrix_kernel(shifts, me_ref, pattern_ref, weights_ref, out_ref, coupling):
    terms, entries, modes = pattern_ref.shape
    owners = len(shifts) + 1
    block = modes // owners
    rows = lax.broadcasted_iota(jnp.int32, (modes, modes), 0)
    for term in range(terms):
        flipped = jnp.zeros((modes, modes), jnp.float32)
        for entry in range(entries):
            hits = pattern_ref[term, entry : entry + 1, :] == rows
            flipped = flipped + jnp.where(hits, weights_ref[term, entry : entry + 1, :], 0.0)
        coupling[term] = 0.5 * (flipped + flipped.T)
    for term in range(terms):
        picked = []
        for shift in [0] + shifts:
            source = lax.rem(me_ref[0] + owners - shift, owners)
            picked.append(coupling[term, pl.ds(pl.multiple_of(source * block, block), block), :])
        columns = jnp.concatenate(picked, 0).T
        high = columns.astype(jnp.bfloat16)
        at = slice(term * modes, (term + 1) * modes)
        out_ref[:modes, at] = high
        out_ref[modes:, at] = (columns - high.astype(jnp.float32)).astype(jnp.bfloat16)


def coupling_matrices(me, pattern, weights, shifts):
    terms, modes, _ = pattern.shape
    pattern, weights = jnp.swapaxes(pattern, 1, 2), jnp.swapaxes(weights, 1, 2)
    shape = (2 * modes, terms * modes)
    return pl.pallas_call(
        functools.partial(matrix_kernel, shifts),
        grid=(1,),
        in_specs=[SCALARS, whole(pattern), whole(weights)],
        out_specs=pl.BlockSpec(shape, lambda i: (0, 0)),
        out_shape=jax.ShapeDtypeStruct(shape, jnp.bfloat16),
        scratch_shapes=[pltpu.VMEM((terms, modes, modes), jnp.float32)],
        compiler_params=params(),
        cost_estimate=cost(2),
        name="coupling",
    )(me, pattern, weights)


def target(me_ref, shift, owners):
    block = lax.rem(me_ref[0] + shift, owners)
    return block // (owners // 2), lax.rem(block, owners // 2)


def edge_count(halves):
    return 1 if halves == 2 else 2


def head_rows(terms, halves):
    return -(-(terms + edge_count(halves)) // TILE) * TILE


def fetch(me_ref, state_ref, adjoint_ref, shift, owners, first, rows, target_ref, sem):
    field, half = target(me_ref, shift, owners)
    height = state_ref.shape[1]
    half_rows = height // (owners // 2)
    at = pl.ds(pl.multiple_of(jnp.clip(half * half_rows + first(half), 0, height - rows), TILE), rows)
    copies = [pltpu.make_async_copy(ref.at[:, at, :], target_ref, sem) for ref in (state_ref, adjoint_ref)]
    for which in range(2):
        pl.when(field == which)(copies[which].start)
    return copies[0].wait


def fetch_edges(me_ref, state_ref, adjoint_ref, shift, owners, target_ref, sems):
    halves = owners // 2
    half_rows = state_ref.shape[1] // halves
    if halves == 2:
        places = [lambda half: jnp.where(half == 1, -TILE, half_rows)]
    else:
        places = [lambda half: -TILE, lambda half: half_rows]
    return [
        fetch(me_ref, state_ref, adjoint_ref, shift, owners, place, TILE, target_ref.at[i], sems[i])
        for i, place in enumerate(places)
    ]


def write_edges(out_ref, at, half, halves, tiles_ref):
    tiles = [jnp.swapaxes(tiles_ref[i], 0, 1) for i in range(edge_count(halves))]
    if halves == 2:
        out_ref[at] = jnp.where(half == 1, tiles[0][TILE - 1], tiles[0][0])
    else:
        out_ref[at] = jnp.where(half > 0, tiles[0][TILE - 1], 0.0)
        out_ref[at + 1] = jnp.where(half < halves - 1, tiles[1][0], 0.0)


def pack_kernel(shifts, owners, rows, part, me_ref, state_ref, adjoint_ref, *refs):
    buffers, sems = refs[-2:]
    outs = refs[-2 - len(shifts) : -2]
    waits = [
        fetch(me_ref, state_ref, adjoint_ref, shift, owners, lambda half: part * rows, rows, buffers.at[i], sems.at[i])
        for i, shift in enumerate(shifts)
    ]
    for index, wait in enumerate(waits):
        wait()
        outs[index][...] = jnp.swapaxes(buffers[index], 0, 1)


def pack(me, state, adjoint, shifts, part, rows, owners, earlier):
    modes, _, width = state.shape
    shape = (rows, modes, width)
    return pl.pallas_call(
        functools.partial(pack_kernel, shifts, owners, rows, part),
        grid=(1,),
        in_specs=[SCALARS] + [ANYWHERE] * (2 + len(earlier)),
        out_specs=[pl.BlockSpec(shape, lambda i: (0, 0, 0))] * len(shifts),
        out_shape=[jax.ShapeDtypeStruct(shape, jnp.float32)] * len(shifts),
        scratch_shapes=[
            pltpu.VMEM((len(shifts), modes, rows, width), jnp.float32),
            pltpu.SemaphoreType.DMA((len(shifts),)),
        ],
        compiler_params=params(60),
        cost_estimate=cost(3),
        name="pack",
    )(me, state, adjoint, *earlier)


def pack_all_kernel(halves, state_ref, adjoint_ref, out_ref, buffers, sems):
    height = state_ref.shape[1]
    half_rows = height // halves
    rows = buffers.shape[3]
    copies = []
    for field, ref in enumerate((state_ref, adjoint_ref)):
        for half in range(halves):
            first = half * half_rows
            starts = [first, max(first - TILE, 0), min(first + half_rows, height - TILE)]
            if halves == 2:
                starts.pop(2 if half else 1)
            for i, start in enumerate(starts):
                at = (field * halves + half, i)
                copies.append(
                    (at, pltpu.make_async_copy(ref.at[:, pl.ds(start, rows), :], buffers.at[at], sems.at[at]))
                )
    for _, copy in copies:
        copy.start()
    for (block, i), copy in copies:
        copy.wait()
        half = block % halves
        values = jnp.swapaxes(buffers[block, i], 0, 1)
        if i == 0:
            out_ref[block, :rows] = values
        elif halves == 2:
            out_ref[block, rows] = values[TILE - 1 if half else 0]
        else:
            inside = half > 0 if i == 1 else half < halves - 1
            out_ref[block, rows + i - 1] = values[TILE - 1 if i == 1 else 0] if inside else jnp.zeros_like(values[0])


def pack_all(state, adjoint, halves):
    modes, _, width = state.shape
    edges = edge_count(halves)
    shape = (2 * halves, TILE + edges, modes, width)
    return pl.pallas_call(
        functools.partial(pack_all_kernel, halves),
        grid=(1,),
        in_specs=[ANYWHERE] * 2,
        out_specs=pl.BlockSpec(shape, lambda i: (0,) * 4),
        out_shape=jax.ShapeDtypeStruct(shape, jnp.float32),
        scratch_shapes=[
            pltpu.VMEM((2 * halves, 1 + edges, modes, TILE, width), jnp.float32),
            pltpu.SemaphoreType.DMA((2 * halves, 1 + edges)),
        ],
        compiler_params=params(60),
        cost_estimate=cost(3),
        name="pack_all",
    )(state, adjoint)


def pack_own_kernel(owners, me_ref, state_ref, adjoint_ref, coef_ref, *refs):
    out_ref, buffer, tiles, sems = refs[-4:]
    halves = owners // 2
    terms, height, _ = coef_ref.shape
    half_rows = height // halves
    head = head_rows(terms, halves)
    _, half = target(me_ref, 0, owners)
    place = (me_ref, state_ref, adjoint_ref, 0, owners)
    sem = [sems.at[i] for i in range(2 + edge_count(halves))]
    waits = [fetch(*place, lambda half: 0, half_rows, buffer, sem[0])]
    waits += fetch_edges(*place, tiles, sem[2:])
    at = pl.ds(pl.multiple_of(half * half_rows, TILE), half_rows)
    coef_copy = pltpu.make_async_copy(coef_ref.at[:, at, :], out_ref.at[:terms], sem[1])
    coef_copy.start()
    for wait in waits:
        wait()
    out_ref[head:] = jnp.swapaxes(buffer[...], 0, 1)
    write_edges(out_ref, terms, half, halves, tiles)
    coef_copy.wait()


def pack_own(me, state, adjoint, coef, owners, earlier):
    modes, height, width = state.shape
    halves = owners // 2
    half_rows = height // halves
    edges = edge_count(halves)
    terms = coef.shape[0]
    count = head_rows(terms, halves) + half_rows
    return pl.pallas_call(
        functools.partial(pack_own_kernel, owners),
        grid=(1,),
        in_specs=[SCALARS] + [ANYWHERE] * (3 + len(earlier)),
        out_specs=pl.BlockSpec((count, modes, width), lambda i: (0, 0, 0)),
        out_shape=jax.ShapeDtypeStruct((count, modes, width), jnp.float32),
        scratch_shapes=[
            pltpu.VMEM((modes, half_rows, width), jnp.float32),
            pltpu.VMEM((edges, modes, TILE, width), jnp.float32),
            pltpu.SemaphoreType.DMA((2 + edges,)),
        ],
        compiler_params=params(60),
        cost_estimate=cost(3),
        name="pack_own",
    )(me, state, adjoint, coef, *earlier)


def gather_kernel(count, *refs):
    rows = refs[0].shape[0]
    for index in range(count):
        refs[-1][index * rows : (index + 1) * rows] = refs[index][...]


def gather(pieces, rows, index, earlier):
    _, modes, width = pieces[0].shape
    shape = (len(pieces) * rows, modes, width)
    return pl.pallas_call(
        functools.partial(gather_kernel, len(pieces)),
        grid=(1,),
        in_specs=[pl.BlockSpec((rows, modes, width), lambda i: (index, 0, 0))] * len(pieces)
        + [ANYWHERE] * len(earlier),
        out_specs=pl.BlockSpec(shape, lambda i: (0, 0, 0)),
        out_shape=jax.ShapeDtypeStruct(shape, jnp.float32),
        compiler_params=params(),
        cost_estimate=cost(1),
        name="gather",
    )(*pieces, *earlier)


def operator_kernel(shifts, terms, part, parts, by_owner, me_ref, coef_ref, matrix_ref, *refs):
    owners = len(shifts) + 1
    heads, own_near, near, refs = refs[:3], refs[3:5], refs[5:7], refs[7:]
    pieces, before, after = (refs[i * owners : (i + 1) * owners] for i in range(3))
    outs = refs[-7:-6] if by_owner else refs[-owners - 6 : -6]
    slots, mixed, faces = ((refs[-6], refs[-5]), (refs[-4], refs[-3])), refs[-2], refs[-1]
    rows, block, width = pieces[0].shape
    modes = owners * block
    halves = owners // 2
    me = me_ref[0]
    half = lax.rem(me, halves)
    step = 16
    lanes = lax.broadcasted_iota(jnp.int32, (step, width), 1)
    last = rows - 1

    def with_sides(values, lane):
        left = jnp.where(lane == 0, 0.0, pltpu.roll(values, 1, 1))
        right = jnp.where(lane == width - 1, 0.0, pltpu.roll(values, width - 1, 1))
        return left, right

    first_row = (half * parts + part) * rows
    height = coef_ref.shape[1]
    face_lanes = lax.broadcasted_iota(jnp.int32, (rows, width), 1)
    face_rows = lax.broadcasted_iota(jnp.int32, (rows, width), 0)
    here = slice(part * rows, (part + 1) * rows)
    for term in range(terms):
        centre = coef_ref[term, pl.ds(pl.multiple_of(first_row, TILE), rows), :]
        row_before = coef_ref[term, pl.ds(jnp.maximum(first_row - 1, 0), 1), :]
        row_after = coef_ref[term, pl.ds(jnp.minimum(first_row + rows, height - 1), 1), :]
        row_before = jnp.where(first_row > 0, row_before, 0.0)
        row_after = jnp.where(first_row + rows < height, row_after, 0.0)
        up = jnp.where(face_rows == 0, row_before, pltpu.roll(centre, 1, 0))
        down = jnp.where(face_rows == last, row_after, pltpu.roll(centre, last, 0))
        left, right = with_sides(centre, face_lanes)
        others = (heads[1][term, here, :], heads[2][term, here, :], up, down, left, right)
        for side, other in enumerate(others):
            faces[6 * term + side] = 0.5 * (centre + other)

    def beyond(index, which, here):
        if part != (0, parts - 1)[which]:
            return (before, after)[which][index][0, here, :]
        ref, at = ((before, after)[which][index], 0) if index else (heads[0], terms)
        if halves == 2:
            return jnp.where(half == 1 - which, ref[at, here, :], 0.0)
        return ref[at + which, here, :]

    def stencil(row, slot):
        high, low = slots[slot]
        for index in range(owners):
            side_refs, side_row = (near, (index - 1) * rows + row) if index else (own_near, row)
            for start in range(0, block, step):
                here = pl.ds(start, step)
                centre = pieces[index][row, here, :]
                up = pieces[index][row - 1, here, :] if row > 0 else beyond(index, 0, here)
                down = pieces[index][row + 1, here, :] if row < last else beyond(index, 1, here)
                left, right = with_sides(centre, lanes)
                others = (side_refs[0][side_row, here, :], side_refs[1][side_row, here, :], up, down, left, right)
                slopes = [centre - other for other in others]
                for term in range(terms):
                    total = faces[6 * term, row : row + 1, :] * slopes[0]
                    for side in range(1, 6):
                        total = total + faces[6 * term + side, row : row + 1, :] * slopes[side]
                    rounded = total.astype(jnp.bfloat16)
                    at = pl.ds(term * modes + index * block + start, step)
                    high[at, :] = rounded
                    low[at, :] = (total - rounded.astype(jnp.float32)).astype(jnp.bfloat16)

    def mix(row, slot):
        high, low = slots[slot]
        both = jnp.dot(matrix_ref[...], high[...], preferred_element_type=jnp.float32)
        rest = jnp.dot(matrix_ref[:modes, :], low[...], preferred_element_type=jnp.float32)
        total = both[:modes] + both[modes:] + rest
        if by_owner:
            for owner in range(owners):
                outs[0][owner, row] = total[owner * block : (owner + 1) * block]
            return
        mixed[...] = total
        for index, shift in enumerate([0] + shifts):
            owner = lax.rem(me + shift, owners)
            outs[index][row] = mixed[pl.ds(pl.multiple_of(owner * block, block), block), :]

    stencil(0, 0)
    for row in range(rows):
        if row < last:
            stencil(row + 1, (row + 1) % 2)
        mix(row, row % 2)


def apply_operator(me, coef, matrix, own, own_near, groups, near, part, rows, shifts, by_owner):
    _, block, width = own.shape
    owners = len(shifts) + 1
    modes = owners * block
    terms, height, _ = coef.shape
    parts = height // (owners // 2) // rows
    edges = edge_count(owners // 2)
    head = head_rows(terms, owners // 2)

    def at(count, first):
        return pl.BlockSpec((count, block, width), lambda i: (first // count, 0, 0))

    def pieces_at(first, count):
        group, first_in = first // rows, first % rows
        return [own, *groups[group]], [at(count, head + first)] + [at(count, first_in)] * len(shifts)

    def edge_pieces():
        return [own, *groups[0]], [at(1, 0)] + [at(edges, rows)] * len(shifts)

    operands = [coef, matrix, own, *own_near, *own_near, *near]
    in_specs = [SCALARS, whole(coef), whole(matrix)] + [at(head, 0)] * 3
    in_specs += [at(rows, head + part * rows)] * 2 + [whole(array) for array in near]
    for arrays, specs in (
        pieces_at(part * rows, rows),
        pieces_at(part * rows - 1, 1) if part else edge_pieces(),
        pieces_at((part + 1) * rows, 1) if part < parts - 1 else edge_pieces(),
    ):
        operands += arrays
        in_specs += specs
    shape, count = ((owners, rows, block, width), 1) if by_owner else ((rows, block, width), owners)
    return pl.pallas_call(
        functools.partial(operator_kernel, shifts, terms, part, parts, by_owner),
        grid=(1,),
        in_specs=in_specs,
        out_specs=[pl.BlockSpec(shape, lambda i: (0,) * len(shape))] * count,
        out_shape=[jax.ShapeDtypeStruct(shape, jnp.float32)] * count,
        scratch_shapes=[pltpu.VMEM((terms * modes, width), jnp.bfloat16)] * 4
        + [pltpu.VMEM((modes, width), jnp.float32), pltpu.VMEM((6 * terms, rows, width), jnp.float32)],
        compiler_params=params(),
        cost_estimate=cost(6),
        name="operator",
    )(me, *operands)


def finish_kernel(shifts, by_owner, me_ref, *refs):
    owners = len(shifts) + 1
    halves = owners // 2
    mixed = refs[: 2 if by_owner else owners]
    state_ref, control_ref = refs[len(mixed) : len(mixed) + 2]
    state_out, adjoint_out = refs[-2:]
    half = pl.program_id(0)
    if by_owner:
        adjoint_out[...] = jnp.swapaxes(mixed[0][0], 0, 1) - control_ref[...]
        state_out[...] = state_ref[...] + jnp.swapaxes(mixed[1][0], 0, 1)
        return
    for index, shift in enumerate([0] + shifts):
        source = lax.rem(me_ref[0] + owners - shift, owners)

        @pl.when(source == half)
        def _(index=index):
            adjoint_out[...] = jnp.swapaxes(mixed[index][...], 0, 1) - control_ref[...]

        @pl.when(source == halves + half)
        def _(index=index):
            state_out[...] = state_ref[...] + jnp.swapaxes(mixed[index][...], 0, 1)


def finish(me, mixed, state, control, outputs, part, shifts):
    modes, _, width = state.shape
    halves = (len(shifts) + 1) // 2
    rows = mixed[0].shape[-3]
    parts = state.shape[1] // halves // rows
    block = pl.BlockSpec((modes, rows, width), lambda h: (0, h * parts + part, 0))
    by_owner = len(mixed) == 1
    if by_owner:
        sources = [
            pl.BlockSpec((1, rows, modes, width), lambda h, field=field: (field * halves + h, 0, 0, 0))
            for field in range(2)
        ]
        mixed = mixed * 2
    else:
        sources = [whole(m) for m in mixed]
    in_specs = [SCALARS] + sources + [block] * 2
    operands = [me, *mixed, state, control]
    aliases = {}
    if outputs is not None:
        aliases = {len(operands) + i: i for i in range(2)}
        in_specs += [ANYWHERE] * 2
        operands += list(outputs)
    return pl.pallas_call(
        functools.partial(finish_kernel, shifts, by_owner),
        grid=(halves,),
        in_specs=in_specs,
        out_specs=[block] * 2,
        out_shape=[jax.ShapeDtypeStruct(state.shape, jnp.float32)] * 2,
        input_output_aliases=aliases,
        compiler_params=params(60),
        cost_estimate=cost(2.5),
        name="finish",
    )(*operands)


def shards(state, control, adjoint, coefficient, pattern, weights):
    shape = state.shape
    modes, _, height, width = shape
    control_residual = 0.5 * control - adjoint
    state, control, adjoint = (a.reshape(modes, height, width) for a in (state, control, adjoint))
    coef = coefficient[:, 0]
    owners = lax.axis_size("mode")
    rows = TILE
    parts = height // (owners // 2) // rows
    planes = lax.axis_size("space")
    forward = [(i, i + 1) for i in range(planes - 1)]
    backward = [(i + 1, i) for i in range(planes - 1)]
    me = lax.axis_index("mode").astype(jnp.int32).reshape(1)
    shifts = sorted(range(1, owners), key=lambda s: min(s, owners - s))

    def move(array, shift):
        return lax.ppermute(array, "mode", [(i, (i + shift) % owners) for i in range(owners)])

    def beside(array):
        return lax.ppermute(array, "space", forward), lax.ppermute(array, "space", backward)

    matrix = coupling_matrices(me, pattern, weights, shifts)
    groups, bodies, nears, mixed = [], [], [], []

    def exchange(part):
        earlier = [own] if part == 1 else [mixed[part - 3][0]] if part > 2 else [bodies[0]]
        packed = pack(me, state, adjoint, shifts, part, rows, owners, earlier)
        groups.append([move(piece, shift) for piece, shift in zip(packed, shifts)])

    def halo(part):
        earlier = [mixed[part - 2][0]] if part > 1 else [] if part else own_near
        bodies.append(gather(groups[part], rows, 0, earlier))
        nears.append(beside(bodies[part]))

    def operate(part):
        mixed.append(
            apply_operator(me, coef, matrix, own, own_near, groups, nears[part], part, rows, shifts, part == 0)
        )

    packed = pack_all(state, adjoint, owners // 2)
    everyone = lax.all_to_all(packed, "mode", 0, 0, tiled=True)
    groups.append(
        [lax.dynamic_index_in_dim(everyone, lax.rem(me[0] + owners - s, owners), keepdims=False) for s in shifts]
    )
    own = pack_own(me, state, adjoint, coef, owners, [packed])
    own_near = list(beside(own))
    halo(0)
    exchange(1)
    halo(1)
    for part in range(parts):
        if part + 2 < parts:
            exchange(part + 2)
        operate(part)
        if part + 2 < parts:
            halo(part + 2)

    outputs = None
    for part in range(parts):
        if part == 0:
            returned = [lax.all_to_all(mixed[0][0], "mode", 0, 0, tiled=True)]
        else:
            returned = [mixed[part][0]] + [move(m, shift) for m, shift in zip(mixed[part][1:], shifts)]
        outputs = finish(me, returned, state, control, outputs, part, shifts)
    return outputs[0].reshape(shape), control_residual, outputs[1].reshape(shape)


def solution(mesh):
    split = P("mode", "space", None, None)
    in_specs = (split, split, split, P(None, "space", None, None), P(), P())
    return jax.shard_map(shards, mesh=mesh, in_specs=in_specs, out_specs=(split, split, split), check_vma=False)
```

time: 245 us -> 212 us (0.87)
  waiting for transfers between devices: 115 us -> 77.3 us
  starting transfers between devices: 76.1 us -> 66.1 us
  Pallas kernels: 45.8 us -> 54 us
  local copies, waits for them, and re-layouts: 2.4 us -> 8.89 us
    all_to_all x2, waiting for transfers between devices: 48.4 us -> 24.8 us  [the longest x1 24.8 us: shards(): everyone = lax.all_to_all(packed, 'mode', 0, 0, tiled=True)]
    ppermute x5, waiting for transfers between devices: 21.9 us -> 6.65 us  [beside(): lax.ppermute(array, 'space', forward)]
    ppermute x12 -> x18, starting transfers between devices: 32.9 us -> 24.3 us  [move(): lax.ppermute(array, 'mode', [(i, (i + shift) % owners) for i in range(own...]
    ppermute x12 -> x18, waiting for transfers between devices: 32.4 us -> 39.2 us  [move(): lax.ppermute(array, 'mode', [(i, (i + shift) % owners) for i in range(own...]
    pallas_call x11 -> x14, Pallas kernels: 20.5 us -> 27.2 us  [the longest x4 9.97 us: finish(): pl.pallas_call(functools.partial(finish_kernel, shifts, by_owner), grid=(...]
    unnamed x48 -> x46, local copies, waits for them, and re-layouts: 2.37 us -> 7.69 us
    ppermute x5, waiting for transfers between devices: 11.9 us -> 6.62 us  [beside(): lax.ppermute(array, 'space', backward)]
  transfers between devices with their start and end apart: 24 -> 30, of which waited for: 14 -> 13; matrix products, arithmetic and copies ran while one was open for 1% -> 2% of each run, Pallas kernels for 16% -> 23%
where the time goes in v7:
time: 212 us; the launch traced here: 211 us
  waiting for transfers between devices  77.3 us (36%)
  starting transfers between devices  66.1 us (31%)
  Pallas kernels  54 us (25%)
  local copies, waits for them, and re-layouts  8.89 us (4%)
  other arithmetic  3.21 us (2%)
    ppermute x18, waiting for transfers between devices, move(): lax.ppermute(array, 'mode', [(i, (i + shift) % owners) for i in range(own...  39.2 us
    pallas_call x4, Pallas kernels, apply_operator(): pl.pallas_call(functools.partial(operator_kernel, shifts, terms, part, pa...  26.9 us
    all_to_all x1, waiting for transfers between devices, shards(): everyone = lax.all_to_all(packed, 'mode', 0, 0, tiled=True)  24.8 us
    ppermute x18, starting transfers between devices, move(): lax.ppermute(array, 'mode', [(i, (i + shift) % owners) for i in range(own...  24.3 us
    ppermute x5, starting transfers between devices, beside(): lax.ppermute(array, 'space', backward)  22.7 us
    pallas_call x4, Pallas kernels, finish(): pl.pallas_call(functools.partial(finish_kernel, shifts, by_owner), grid=(...  9.97 us
    ppermute x5, starting transfers between devices, beside(): lax.ppermute(array, 'space', forward)  9.71 us
    unnamed x46, local copies, waits for them, and re-layouts  7.69 us
  transfers between devices with their start and end apart: 30, of which 13 were waited for; matrix products, arithmetic and copies ran while one was open for 2% of the time, Pallas kernels for 23%

profile of v7, /device:TPU:4, one launch (start us, length us, event | category | flops | bytes accessed | tf_op | source)
XLA Modules:
  0.0 210.6 jit_solution(3932263369131429175)
XLA Ops:
  0.6 2.6 %pack_all.1.refs_0_ = f32[4,9,32,256]{3,2,1,0:T(8,128)} custom-call(f32[32,64,256]{2,1,0:T(8,128)} %bitcast.26, f32[32,64,256]{2,1,0:T(8,128)} %bitcast.35), custom_call_target="tpu_custom_call" | custom-call | bytes 10500000 | tf_op jit(solution)/shard_map/pack_all/pallas_call | solution.py:179
  3.3 4.9 %all-to-all-start = ((f32[4,9,32,256]{3,2,1,0:T(8,128)}), f32[4,9,32,256]{3,2,1,0:T(8,128)}, u32[]{:S(2)}, u32[]{:S(2)}) async-start(f32[4,9,32,256]{3,2,1,0:T(8,128)} %pack_all.1.refs_0_), calls=%async_computation | async-start | bytes 2359296 | tf_op jit(solution)/shard_map/all_to_all | solution.py:492
  8.1 2.6 %pack_own.1.refs_0_.refs_7_.refs_11_.refs_15_ = f32[40,32,256]{2,1,0:T(8,128)} custom-call(s32[1]{0:T(128)} %bitcast.me_ref, f32[32,64,256]{2,1,0:T(8,128)} %bitcast.27, f32[32,64,256]{2,1,0:T(8,128)} %bitcast.36, f32[7,64,256]{2,1,0:T(8,128)} %bitcast.19, f32[4,9,32,256]{3,2,1,0:T(8,128)} %pack_all.1.refs_0_), custom_call_target="tpu_custom_call" | custom-call | bytes 10500000 | tf_op jit(solution)/shard_map/pack_own/pallas_call | solution.py:223
  12.6 4.5 %collective-permute-start.1 = (f32[40,32,256]{2,1,0:T(8,128)}, f32[40,32,256]{2,1,0:T(8,128)S(1)}, u32[]{:S(2)}, u32[]{:S(2)}) collective-permute-start(f32[40,32,256]{2,1,0:T(8,128)} %pack_own.1.refs_0_.refs_7_.refs_11_.refs_15_), channel_id=1, source_target_pairs={{4,0},{8,4},{12,8},{16,12},{20,16},{24,20},{28,24},{5,1},{9,5},{13... | collective-permute-start | bytes 3932168 | tf_op jit(solution)/shard_map/ppermute | solution.py:471
  24.3 24.8 %all-to-all-done = f32[4,9,32,256]{3,2,1,0:T(8,128)} async-done(((f32[4,9,32,256]{3,2,1,0:T(8,128)}), f32[4,9,32,256]{3,2,1,0:T(8,128)}, u32[]{:S(2)}, u32[]{:S(2)}) %all-to-all-start) | async-done | bytes 1179680 | tf_op jit(solution)/shard_map/all_to_all | solution.py:492
  54.0 4.5 %collective-permute-start.3 = (f32[24,32,256]{2,1,0:T(8,128)}, f32[24,32,256]{2,1,0:T(8,128)}, u32[]{:S(2)}, u32[]{:S(2)}) collective-permute-start(f32[24,32,256]{2,1,0:T(8,128)} %gather.4.refs_0_), channel_id=1, source_target_pairs={{4,0},{8,4},{12,8},{16,12},{20,16},{24,20},{28,24},{5,1},{9,5},{13... | collective-permute-start | bytes 2359304 | tf_op jit(solution)/shard_map/ppermute | solution.py:471
  63.4 4.5 %collective-permute-start.11 = (f32[24,32,256]{2,1,0:T(8,128)}, f32[24,32,256]{2,1,0:T(8,128)S(1)}, u32[]{:S(2)}, u32[]{:S(2)}) collective-permute-start(f32[24,32,256]{2,1,0:T(8,128)} %gather.5), channel_id=1, source_target_pairs={{4,0},{8,4},{12,8},{16,12},{20,16},{24,20},{28,24},{5,1},{9,5},{13... | collective-permute-start | bytes 2359304 | tf_op jit(solution)/shard_map/ppermute | solution.py:471
  67.9 2.1 pack.5
  72.2 2.3 %collective-permute-start.13 = (f32[8,32,256]{2,1,0:T(8,128)}, f32[8,32,256]{2,1,0:T(8,128)S(1)}, u32[]{:S(2)}, u32[]{:S(2)}) collective-permute-start(f32[8,32,256]{2,1,0:T(8,128)} %get-tuple-element.39), channel_id=1, source_target_pairs={{0,3},{1,0},{2,1},{3,2},{4,7},{5,4},{6,5},{7,6},{8,11},{9,8},{10,9... | collective-permute-start | bytes 786440 | tf_op jit(solution)/shard_map/ppermute | solution.py:468
  74.5 2.3 %collective-permute-done.3.refs_6_ = f32[24,32,256]{2,1,0:T(8,128)} collective-permute-done((f32[24,32,256]{2,1,0:T(8,128)}, f32[24,32,256]{2,1,0:T(8,128)}, u32[]{:S(2)}, u32[]{:S(2)}) %collective-permute-start.3) | collective-permute-done | bytes 786464 | tf_op jit(solution)/shard_map/ppermute | solution.py:471
  76.8 6.5 %operator.4.refs_0_.refs_3_ = f32[4,8,32,256]{3,2,1,0:T(8,128)S(1)} custom-call(s32[1]{0:T(128)} %bitcast.me_ref, f32[7,64,256]{2,1,0:T(8,128)S(1)} %bitcast.20, bf16[256,896]{1,0:T(8,128)(2,1)S(1)} %coupling.1.matrix_ref, f32[40,32,256]{2,1,0:T(8,128)} %pack_own.1.refs_0_.refs_7_.refs_11_.refs_15_, f32[40,32,256]{2,1,0:T(8,128)} %copy-done, ...), custom_call_target="tpu_custom_call" | custom-call | bytes 21000000 | tf_op jit(solution)/shard_map/operator/pallas_call | solution.py:380
  86.4 2.5 %collective-permute-done.10.refs_5_ = f32[24,32,256]{2,1,0:T(8,128)S(1)} collective-permute-done((f32[24,32,256]{2,1,0:T(8,128)}, f32[24,32,256]{2,1,0:T(8,128)S(1)}, u32[]{:S(2)}, u32[]{:S(2)}) %collective-permute-start.10) | collective-permute-done | bytes 786464 | tf_op jit(solution)/shard_map/ppermute | solution.py:471
  89.9 3.7 %collective-permute-start.8 = (f32[8,32,256]{2,1,0:T(8,128)}, f32[8,32,256]{2,1,0:T(8,128)}, u32[]{:S(2)}, u32[]{:S(2)}) collective-permute-start(f32[8,32,256]{2,1,0:T(8,128)} %get-tuple-element.36), channel_id=1, source_target_pairs={{0,3},{1,0},{2,1},{3,2},{4,7},{5,4},{6,5},{7,6},{8,11},{9,8},{10,9... | collective-permute-start | bytes 786440 | tf_op jit(solution)/shard_map/ppermute | solution.py:468
  93.6 4.5 %all-to-all-start.1 = ((f32[4,8,32,256]{3,2,1,0:T(8,128)}), f32[4,8,32,256]{3,2,1,0:T(8,128)}, u32[]{:S(2)}, u32[]{:S(2)}) async-start(f32[4,8,32,256]{3,2,1,0:T(8,128)} %copy-done.2), calls=%async_computation.1 | async-start | bytes 2097152 | tf_op jit(solution)/shard_map/all_to_all | solution.py:511
  98.1 6.3 %collective-permute-done.14.refs_18_.refs_14_.refs_2_.refs_10_ = f32[8,32,256]{2,1,0:T(8,128)} collective-permute-done((f32[8,32,256]{2,1,0:T(8,128)}, f32[8,32,256]{2,1,0:T(8,128)}, u32[]{:S(2)}, u32[]{:S(2)}) %collective-permute-start.14) | collective-permute-done | bytes 262176 | tf_op jit(solution)/shard_map/ppermute | solution.py:468
  106.7 6.5 %operator.5 = (f32[8,32,256]{2,1,0:T(8,128)S(1)}, f32[8,32,256]{2,1,0:T(8,128)S(1)}, f32[8,32,256]{2,1,0:T(8,128)S(1)}, f32[8,32,256]{2,1,0:T(8,128)S(1)}) custom-call(s32[1]{0:T(128)} %bitcast.me_ref, f32[7,64,256]{2,1,0:T(8,128)S(1)} %bitcast.21, bf16[256,896]{1,0:T(8,128)(2,1)S(1)} %coupling.1.matrix_ref, ...), custom_call_target="tpu_custom_call" | custom-call | bytes 21000000 | tf_op jit(solution)/shard_map/operator/pallas_call | solution.py:380
  116.2 4.5 %collective-permute-start.21 = (f32[24,32,256]{2,1,0:T(8,128)S(1)}, f32[24,32,256]{2,1,0:T(8,128)S(1)}, u32[]{:S(2)}, u32[]{:S(2)}) collective-permute-start(f32[24,32,256]{2,1,0:T(8,128)S(1)} %gather.7), channel_id=1, source_target_pairs={{4,0},{8,4},{12,8},{16,12},{20,16},{24,20},{28,24},{5,1},{9,5},{13... | collective-permute-start | bytes 2359304 | tf_op jit(solution)/shard_map/ppermute | solution.py:471
  120.8 9.3 %collective-permute-done.9.refs_2_.refs_10_.refs_18_ = f32[8,32,256]{2,1,0:T(8,128)} collective-permute-done((f32[8,32,256]{2,1,0:T(8,128)}, f32[8,32,256]{2,1,0:T(8,128)}, u32[]{:S(2)}, u32[]{:S(2)}) %collective-permute-start.9) | collective-permute-done | bytes 262176 | tf_op jit(solution)/shard_map/ppermute | solution.py:468
  133.2 4.5 %collective-permute-start.16 = (f32[24,32,256]{2,1,0:T(8,128)S(1)}, f32[24,32,256]{2,1,0:T(8,128)S(1)}, u32[]{:S(2)}, u32[]{:S(2)}) collective-permute-start(f32[24,32,256]{2,1,0:T(8,128)S(1)} %gather.6), channel_id=1, source_target_pairs={{4,0},{8,4},{12,8},{16,12},{20,16},{24,20},{28,24},{5,1},{9,5},{13... | collective-permute-start | bytes 2359304 | tf_op jit(solution)/shard_map/ppermute | solution.py:471
  137.9 3.8 %collective-permute-start.26 = (f32[8,32,256]{2,1,0:T(8,128)S(1)}, f32[8,32,256]{2,1,0:T(8,128)S(1)}, u32[]{:S(2)}, u32[]{:S(2)}) collective-permute-start(f32[8,32,256]{2,1,0:T(8,128)S(1)} %get-tuple-element.51), channel_id=1, source_target_pairs={{0,3},{1,0},{2,1},{3,2},{4,7},{5,4},{6,5},{7,6},{8,11},{9,8},{10,9... | collective-permute-start | bytes 786440 | tf_op jit(solution)/shard_map/ppermute | solution.py:468
  141.7 6.4 %operator.7 = (f32[8,32,256]{2,1,0:T(8,128)S(1)}, f32[8,32,256]{2,1,0:T(8,128)S(1)}, f32[8,32,256]{2,1,0:T(8,128)S(1)}, f32[8,32,256]{2,1,0:T(8,128)S(1)}) custom-call(s32[1]{0:T(128)} %bitcast.me_ref, f32[7,64,256]{2,1,0:T(8,128)S(1)} %bitcast.22, bf16[256,896]{1,0:T(8,128)(2,1)S(1)} %coupling.1.matrix_ref, ...), custom_call_target="tpu_custom_call" | custom-call | bytes 21000000 | tf_op jit(solution)/shard_map/operator/pallas_call | solution.py:380
  148.8 2.6 %collective-permute-done.15.refs_5_ = f32[24,32,256]{2,1,0:T(8,128)S(1)} collective-permute-done((f32[24,32,256]{2,1,0:T(8,128)S(1)}, f32[24,32,256]{2,1,0:T(8,128)S(1)}, u32[]{:S(2)}, u32[]{:S(2)}) %collective-permute-start.15) | collective-permute-done | bytes 786464 | tf_op jit(solution)/shard_map/ppermute | solution.py:471
  151.4 4.1 %collective-permute-done.16.refs_6_ = f32[24,32,256]{2,1,0:T(8,128)S(1)} collective-permute-done((f32[24,32,256]{2,1,0:T(8,128)S(1)}, f32[24,32,256]{2,1,0:T(8,128)S(1)}, u32[]{:S(2)}, u32[]{:S(2)}) %collective-permute-start.16) | collective-permute-done | bytes 786464 | tf_op jit(solution)/shard_map/ppermute | solution.py:471
  155.5 7.4 %operator.6 = (f32[8,32,256]{2,1,0:T(8,128)S(1)}, f32[8,32,256]{2,1,0:T(8,128)}, f32[8,32,256]{2,1,0:T(8,128)S(1)}, f32[8,32,256]{2,1,0:T(8,128)S(1)}) custom-call(s32[1]{0:T(128)} %bitcast.me_ref, f32[7,64,256]{2,1,0:T(8,128)S(1)} %bitcast.23, bf16[256,896]{1,0:T(8,128)(2,1)S(1)} %coupling.1.matrix_ref, ...), custom_call_target="tpu_custom_call" | custom-call | bytes 21000000 | tf_op jit(solution)/shard_map/operator/pallas_call | solution.py:380
  165.6 15.0 %collective-permute-done.27.refs_3_ = f32[8,32,256]{2,1,0:T(8,128)S(1)} collective-permute-done((f32[8,32,256]{2,1,0:T(8,128)S(1)}, f32[8,32,256]{2,1,0:T(8,128)S(1)}, u32[]{:S(2)}, u32[]{:S(2)}) %collective-permute-start.27) | collective-permute-done | bytes 262176 | tf_op jit(solution)/shard_map/ppermute | solution.py:468
  180.6 7.5 %collective-permute-start.19 = (f32[8,32,256]{2,1,0:T(8,128)S(1)}, f32[8,32,256]{2,1,0:T(8,128)S(1)}, u32[]{:S(2)}, u32[]{:S(2)}) collective-permute-start(f32[8,32,256]{2,1,0:T(8,128)S(1)} %get-tuple-element.45), channel_id=1, source_target_pairs={{0,2},{1,3},{2,0},{3,1},{4,6},{5,7},{6,4},{7,5},{8,10},{9,11},{10,... | collective-permute-start | bytes 786440 | tf_op jit(solution)/shard_map/ppermute | solution.py:468
  188.1 3.2 %multiply_subtract_fusion = f32[32,1,64,256]{3,2,1,0:T(8,128)} fusion(f32[32,1,64,256]{3,2,1,0:T(8,128)S(1)} %copy-done.14, f32[32,1,64,256]{3,2,1,0:T(8,128)} %param.7), kind=kLoop, calls=%fused_computation | loop fusion | flops 1048576 | bytes 6291456 | tf_op jit(solution)/shard_map/sub | solution.py:455
  191.3 2.4 %finish.4 = (f32[32,64,256]{2,1,0:T(8,128)}, f32[32,64,256]{2,1,0:T(8,128)}) custom-call(s32[1]{0:T(128)} %bitcast.me_ref, f32[4,8,32,256]{3,2,1,0:T(8,128)} %all-to-all-done.1.refs_0_.refs_1_, f32[4,8,32,256]{3,2,1,0:T(8,128)} %all-to-all-done.1.refs_0_.refs_1_, f32[32,64,256]{2,1,0:T(8,128)} %bitcast.31, f32[32,64,256]{2,1,0:T(8,128)} %bitcast.40), custom_call_target="tpu_custom_call" | custom-call | bytes 8750000 | tf_op jit(solution)/shard_map/finish/pallas_call | solution.py:439
  193.7 2.5 %finish.5 = (f32[32,64,256]{2,1,0:T(8,128)}, f32[32,64,256]{2,1,0:T(8,128)}) custom-call(s32[1]{0:T(128)} %bitcast.me_ref, f32[8,32,256]{2,1,0:T(8,128)} %copy-done.5, f32[8,32,256]{2,1,0:T(8,128)} %copy-done.15, f32[8,32,256]{2,1,0:T(8,128)} %copy-done.16, f32[8,32,256]{2,1,0:T(8,128)} %copy-done.17, ...), custom_call_target="tpu_custom_call", output_to_operand_aliasing={{0}: (7, {}), {1}: (8, {})} | custom-call | bytes 8750000 | tf_op jit(solution)/shard_map/finish/pallas_call | solution.py:439
  198.2 2.5 %finish.6 = (f32[32,64,256]{2,1,0:T(8,128)}, f32[32,64,256]{2,1,0:T(8,128)}) custom-call(s32[1]{0:T(128)} %bitcast.me_ref, f32[8,32,256]{2,1,0:T(8,128)} %copy-done.10, f32[8,32,256]{2,1,0:T(8,128)} %copy-done.18, f32[8,32,256]{2,1,0:T(8,128)} %collective-permute-done.23.refs_2_, ...), custom_call_target="tpu_custom_call", output_to_operand_aliasing={{0}: (7, {}), {1}: (8, {})} | custom-call | bytes 8750000 | tf_op jit(solution)/shard_map/finish/pallas_call | solution.py:439
  200.8 6.6 %collective-permute-done.19.refs_3_ = f32[8,32,256]{2,1,0:T(8,128)S(1)} collective-permute-done((f32[8,32,256]{2,1,0:T(8,128)S(1)}, f32[8,32,256]{2,1,0:T(8,128)S(1)}, u32[]{:S(2)}, u32[]{:S(2)}) %collective-permute-start.19) | collective-permute-done | bytes 262176 | tf_op jit(solution)/shard_map/ppermute | solution.py:468
  208.0 2.5 %finish.7 = (f32[32,64,256]{2,1,0:T(8,128)}, f32[32,64,256]{2,1,0:T(8,128)}) custom-call(s32[1]{0:T(128)} %bitcast.me_ref, f32[8,32,256]{2,1,0:T(8,128)} %copy-done.11, f32[8,32,256]{2,1,0:T(8,128)} %copy-done.19, f32[8,32,256]{2,1,0:T(8,128)} %copy-done.20, f32[8,32,256]{2,1,0:T(8,128)} %copy-done.22, ...), custom_call_target="tpu_custom_call", output_to_operand_aliasing={{0}: (7, {}), {1}: (8, {})} | custom-call | bytes 8750000 | tf_op jit(solution)/shard_map/finish/pallas_call | solution.py:439
  (94 shorter events, 39.3 us)
Async XLA Ops:
  3.3 45.8 %all-to-all-start = ((f32[4,9,32,256]{3,2,1,0:T(8,128)}), f32[4,9,32,256]{3,2,1,0:T(8,128)}, u32[]{:S(2)}, u32[]{:S(2)}) async-start(f32[4,9,32,256]{3,2,1,0:T(8,128)} %pack_all.1.refs_0_), calls=%async_computation | async-start | bytes 2359296 | tf_op jit(solution)/shard_map/all_to_all | solution.py:492
  10.7 39.6 %collective-permute-start = (f32[40,32,256]{2,1,0:T(8,128)}, f32[40,32,256]{2,1,0:T(8,128)S(1)}, u32[]{:S(2)}, u32[]{:S(2)}) collective-permute-start(f32[40,32,256]{2,1,0:T(8,128)} %pack_own.1.refs_0_.refs_7_.refs_11_.refs_15_), channel_id=1, source_target_pairs={{0,4},{4,8},{8,12},{12,16},{16,20},{20,24},{24,28},{1,5},{5,9},{9,... | collective-permute-start | bytes 3932168 | tf_op jit(solution)/shard_map/ppermute | solution.py:471
  12.6 37.7 %collective-permute-start.1 = (f32[40,32,256]{2,1,0:T(8,128)}, f32[40,32,256]{2,1,0:T(8,128)S(1)}, u32[]{:S(2)}, u32[]{:S(2)}) collective-permute-start(f32[40,32,256]{2,1,0:T(8,128)} %pack_own.1.refs_0_.refs_7_.refs_11_.refs_15_), channel_id=1, source_target_pairs={{4,0},{8,4},{12,8},{16,12},{20,16},{24,20},{28,24},{5,1},{9,5},{13... | collective-permute-start | bytes 3932168 | tf_op jit(solution)/shard_map/ppermute | solution.py:471
  19.3 39.3 %collective-permute-start.4 = (f32[8,32,256]{2,1,0:T(8,128)}, f32[8,32,256]{2,1,0:T(8,128)}, u32[]{:S(2)}, u32[]{:S(2)}) collective-permute-start(f32[8,32,256]{2,1,0:T(8,128)} %get-tuple-element.32), channel_id=1, source_target_pairs={{0,1},{1,2},{2,3},{3,0},{4,5},{5,6},{6,7},{7,4},{8,9},{9,10},{10,1... | collective-permute-start | bytes 786440 | tf_op jit(solution)/shard_map/ppermute | solution.py:468
  21.3 37.2 %collective-permute-start.5 = (f32[8,32,256]{2,1,0:T(8,128)}, f32[8,32,256]{2,1,0:T(8,128)}, u32[]{:S(2)}, u32[]{:S(2)}) collective-permute-start(f32[8,32,256]{2,1,0:T(8,128)} %get-tuple-element.33), channel_id=1, source_target_pairs={{0,3},{1,0},{2,1},{3,2},{4,7},{5,4},{6,5},{7,6},{8,11},{9,8},{10,9... | collective-permute-start | bytes 786440 | tf_op jit(solution)/shard_map/ppermute | solution.py:468
  23.2 36.1 %collective-permute-start.6 = (f32[8,32,256]{2,1,0:T(8,128)}, f32[8,32,256]{2,1,0:T(8,128)}, u32[]{:S(2)}, u32[]{:S(2)}) collective-permute-start(f32[8,32,256]{2,1,0:T(8,128)} %get-tuple-element.34), channel_id=1, source_target_pairs={{0,2},{1,3},{2,0},{3,1},{4,6},{5,7},{6,4},{7,5},{8,10},{9,11},{10,... | collective-permute-start | bytes 786440 | tf_op jit(solution)/shard_map/ppermute | solution.py:468
  52.0 20.1 %collective-permute-start.2 = (f32[24,32,256]{2,1,0:T(8,128)}, f32[24,32,256]{2,1,0:T(8,128)}, u32[]{:S(2)}, u32[]{:S(2)}) collective-permute-start(f32[24,32,256]{2,1,0:T(8,128)} %gather.4.refs_0_), channel_id=1, source_target_pairs={{0,4},{4,8},{8,12},{12,16},{16,20},{20,24},{24,28},{1,5},{5,9},{9,... | collective-permute-start | bytes 2359304 | tf_op jit(solution)/shard_map/ppermute | solution.py:471
  54.0 22.8 %collective-permute-start.3 = (f32[24,32,256]{2,1,0:T(8,128)}, f32[24,32,256]{2,1,0:T(8,128)}, u32[]{:S(2)}, u32[]{:S(2)}) collective-permute-start(f32[24,32,256]{2,1,0:T(8,128)} %gather.4.refs_0_), channel_id=1, source_target_pairs={{4,0},{8,4},{12,8},{16,12},{20,16},{24,20},{28,24},{5,1},{9,5},{13... | collective-permute-start | bytes 2359304 | tf_op jit(solution)/shard_map/ppermute | solution.py:471
  61.3 27.6 %collective-permute-start.10 = (f32[24,32,256]{2,1,0:T(8,128)}, f32[24,32,256]{2,1,0:T(8,128)S(1)}, u32[]{:S(2)}, u32[]{:S(2)}) collective-permute-start(f32[24,32,256]{2,1,0:T(8,128)} %gather.5), channel_id=1, source_target_pairs={{0,4},{4,8},{8,12},{12,16},{16,20},{20,24},{24,28},{1,5},{5,9},{9,... | collective-permute-start | bytes 2359304 | tf_op jit(solution)/shard_map/ppermute | solution.py:471
  63.4 26.6 %collective-permute-start.11 = (f32[24,32,256]{2,1,0:T(8,128)}, f32[24,32,256]{2,1,0:T(8,128)S(1)}, u32[]{:S(2)}, u32[]{:S(2)}) collective-permute-start(f32[24,32,256]{2,1,0:T(8,128)} %gather.5), channel_id=1, source_target_pairs={{4,0},{8,4},{12,8},{16,12},{20,16},{24,20},{28,24},{5,1},{9,5},{13... | collective-permute-start | bytes 2359304 | tf_op jit(solution)/shard_map/ppermute | solution.py:471
  70.0 23.6 %collective-permute-start.12 = (f32[8,32,256]{2,1,0:T(8,128)}, f32[8,32,256]{2,1,0:T(8,128)S(1)}, u32[]{:S(2)}, u32[]{:S(2)}) collective-permute-start(f32[8,32,256]{2,1,0:T(8,128)} %get-tuple-element.38), channel_id=1, source_target_pairs={{0,1},{1,2},{2,3},{3,0},{4,5},{5,6},{6,7},{7,4},{8,9},{9,10},{10,1... | collective-permute-start | bytes 786440 | tf_op jit(solution)/shard_map/ppermute | solution.py:468
  72.2 25.9 %collective-permute-start.13 = (f32[8,32,256]{2,1,0:T(8,128)}, f32[8,32,256]{2,1,0:T(8,128)S(1)}, u32[]{:S(2)}, u32[]{:S(2)}) collective-permute-start(f32[8,32,256]{2,1,0:T(8,128)} %get-tuple-element.39), channel_id=1, source_target_pairs={{0,3},{1,0},{2,1},{3,2},{4,7},{5,4},{6,5},{7,6},{8,11},{9,8},{10,9... | collective-permute-start | bytes 786440 | tf_op jit(solution)/shard_map/ppermute | solution.py:468
  76.8 27.6 %collective-permute-start.14 = (f32[8,32,256]{2,1,0:T(8,128)}, f32[8,32,256]{2,1,0:T(8,128)}, u32[]{:S(2)}, u32[]{:S(2)}) collective-permute-start(f32[8,32,256]{2,1,0:T(8,128)} %get-tuple-element.40), channel_id=1, source_target_pairs={{0,2},{1,3},{2,0},{3,1},{4,6},{5,7},{6,4},{7,5},{8,10},{9,11},{10,... | collective-permute-start | bytes 786440 | tf_op jit(solution)/shard_map/ppermute | solution.py:468
  89.8 31.0 %collective-permute-start.7 = (f32[8,32,256]{2,1,0:T(8,128)}, f32[8,32,256]{2,1,0:T(8,128)}, u32[]{:S(2)}, u32[]{:S(2)}) collective-permute-start(f32[8,32,256]{2,1,0:T(8,128)} %get-tuple-element.35), channel_id=1, source_target_pairs={{0,1},{1,2},{2,3},{3,0},{4,5},{5,6},{6,7},{7,4},{8,9},{9,10},{10,1... | collective-permute-start | bytes 786440 | tf_op jit(solution)/shard_map/ppermute | solution.py:468
  89.9 30.8 %collective-permute-start.8 = (f32[8,32,256]{2,1,0:T(8,128)}, f32[8,32,256]{2,1,0:T(8,128)}, u32[]{:S(2)}, u32[]{:S(2)}) collective-permute-start(f32[8,32,256]{2,1,0:T(8,128)} %get-tuple-element.36), channel_id=1, source_target_pairs={{0,3},{1,0},{2,1},{3,2},{4,7},{5,4},{6,5},{7,6},{8,11},{9,8},{10,9... | collective-permute-start | bytes 786440 | tf_op jit(solution)/shard_map/ppermute | solution.py:468
  93.6 36.5 %collective-permute-start.9 = (f32[8,32,256]{2,1,0:T(8,128)}, f32[8,32,256]{2,1,0:T(8,128)}, u32[]{:S(2)}, u32[]{:S(2)}) collective-permute-start(f32[8,32,256]{2,1,0:T(8,128)} %get-tuple-element.37), channel_id=1, source_target_pairs={{0,2},{1,3},{2,0},{3,1},{4,6},{5,7},{6,4},{7,5},{8,10},{9,11},{10,... | collective-permute-start | bytes 786440 | tf_op jit(solution)/shard_map/ppermute | solution.py:468
  93.6 97.7 %all-to-all-start.1 = ((f32[4,8,32,256]{3,2,1,0:T(8,128)}), f32[4,8,32,256]{3,2,1,0:T(8,128)}, u32[]{:S(2)}, u32[]{:S(2)}) async-start(f32[4,8,32,256]{3,2,1,0:T(8,128)} %copy-done.2), calls=%async_computation.1 | async-start | bytes 2097152 | tf_op jit(solution)/shard_map/all_to_all | solution.py:511
  114.3 23.6 %collective-permute-start.20 = (f32[24,32,256]{2,1,0:T(8,128)S(1)}, f32[24,32,256]{2,1,0:T(8,128)S(1)}, u32[]{:S(2)}, u32[]{:S(2)}) collective-permute-start(f32[24,32,256]{2,1,0:T(8,128)S(1)} %gather.7), channel_id=1, source_target_pairs={{0,4},{4,8},{8,12},{12,16},{16,20},{20,24},{24,28},{1,5},{5,9},{9,... | collective-permute-start | bytes 2359304 | tf_op jit(solution)/shard_map/ppermute | solution.py:471
  116.2 25.4 %collective-permute-start.21 = (f32[24,32,256]{2,1,0:T(8,128)S(1)}, f32[24,32,256]{2,1,0:T(8,128)S(1)}, u32[]{:S(2)}, u32[]{:S(2)}) collective-permute-start(f32[24,32,256]{2,1,0:T(8,128)S(1)} %gather.7), channel_id=1, source_target_pairs={{4,0},{8,4},{12,8},{16,12},{20,16},{24,20},{28,24},{5,1},{9,5},{13... | collective-permute-start | bytes 2359304 | tf_op jit(solution)/shard_map/ppermute | solution.py:471
  131.3 20.1 %collective-permute-start.15 = (f32[24,32,256]{2,1,0:T(8,128)S(1)}, f32[24,32,256]{2,1,0:T(8,128)S(1)}, u32[]{:S(2)}, u32[]{:S(2)}) collective-permute-start(f32[24,32,256]{2,1,0:T(8,128)S(1)} %gather.6), channel_id=1, source_target_pairs={{0,4},{4,8},{8,12},{12,16},{16,20},{20,24},{24,28},{1,5},{5,9},{9,... | collective-permute-start | bytes 2359304 | tf_op jit(solution)/shard_map/ppermute | solution.py:471
  133.2 22.3 %collective-permute-start.16 = (f32[24,32,256]{2,1,0:T(8,128)S(1)}, f32[24,32,256]{2,1,0:T(8,128)S(1)}, u32[]{:S(2)}, u32[]{:S(2)}) collective-permute-start(f32[24,32,256]{2,1,0:T(8,128)S(1)} %gather.6), channel_id=1, source_target_pairs={{4,0},{8,4},{12,8},{16,12},{20,16},{24,20},{28,24},{5,1},{9,5},{13... | collective-permute-start | bytes 2359304 | tf_op jit(solution)/shard_map/ppermute | solution.py:471
  137.8 25.9 %collective-permute-start.25 = (f32[8,32,256]{2,1,0:T(8,128)S(1)}, f32[8,32,256]{2,1,0:T(8,128)S(1)}, u32[]{:S(2)}, u32[]{:S(2)}) collective-permute-start(f32[8,32,256]{2,1,0:T(8,128)S(1)} %get-tuple-element.50), channel_id=1, source_target_pairs={{0,1},{1,2},{2,3},{3,0},{4,5},{5,6},{6,7},{7,4},{8,9},{9,10},{10,1... | collective-permute-start | bytes 786440 | tf_op jit(solution)/shard_map/ppermute | solution.py:468
  137.9 25.8 %collective-permute-start.26 = (f32[8,32,256]{2,1,0:T(8,128)S(1)}, f32[8,32,256]{2,1,0:T(8,128)S(1)}, u32[]{:S(2)}, u32[]{:S(2)}) collective-permute-start(f32[8,32,256]{2,1,0:T(8,128)S(1)} %get-tuple-element.51), channel_id=1, source_target_pairs={{0,3},{1,0},{2,1},{3,2},{4,7},{5,4},{6,5},{7,6},{8,11},{9,8},{10,9... | collective-permute-start | bytes 786440 | tf_op jit(solution)/shard_map/ppermute | solution.py:468
  141.7 38.9 %collective-permute-start.27 = (f32[8,32,256]{2,1,0:T(8,128)S(1)}, f32[8,32,256]{2,1,0:T(8,128)S(1)}, u32[]{:S(2)}, u32[]{:S(2)}) collective-permute-start(f32[8,32,256]{2,1,0:T(8,128)S(1)} %get-tuple-element.52), channel_id=1, source_target_pairs={{0,2},{1,3},{2,0},{3,1},{4,6},{5,7},{6,4},{7,5},{8,10},{9,11},{10,... | collective-permute-start | bytes 786440 | tf_op jit(solution)/shard_map/ppermute | solution.py:468
  151.4 29.2 %collective-permute-start.22 = (f32[8,32,256]{2,1,0:T(8,128)S(1)}, f32[8,32,256]{2,1,0:T(8,128)S(1)}, u32[]{:S(2)}, u32[]{:S(2)}) collective-permute-start(f32[8,32,256]{2,1,0:T(8,128)S(1)} %get-tuple-element.47), channel_id=1, source_target_pairs={{0,1},{1,2},{2,3},{3,0},{4,5},{5,6},{6,7},{7,4},{8,9},{9,10},{10,1... | collective-permute-start | bytes 786440 | tf_op jit(solution)/shard_map/ppermute | solution.py:468
  155.5 32.6 %copy-start.14 = (f32[32,1,64,256]{3,2,1,0:T(8,128)S(1)}, f32[32,1,64,256]{3,2,1,0:T(8,128)}, u32[]{:S(2)}) copy-start(f32[32,1,64,256]{3,2,1,0:T(8,128)} %param.8) | copy-start | bytes 6291460
  155.5 40.7 %collective-permute-start.23 = (f32[8,32,256]{2,1,0:T(8,128)S(1)}, f32[8,32,256]{2,1,0:T(8,128)}, u32[]{:S(2)}, u32[]{:S(2)}) collective-permute-start(f32[8,32,256]{2,1,0:T(8,128)S(1)} %get-tuple-element.48), channel_id=1, source_target_pairs={{0,3},{1,0},{2,1},{3,2},{4,7},{5,4},{6,5},{7,6},{8,11},{9,8},{10,9... | collective-permute-start | bytes 786440 | tf_op jit(solution)/shard_map/ppermute | solution.py:468
  163.6 24.5 %copy-start.15 = (f32[8,32,256]{2,1,0:T(8,128)}, f32[8,32,256]{2,1,0:T(8,128)S(1)}, u32[]{:S(2)}) copy-start(f32[8,32,256]{2,1,0:T(8,128)S(1)} %collective-permute-done.25.refs_1_) | copy-start | bytes 786436
  163.6 33.9 %collective-permute-start.24 = (f32[8,32,256]{2,1,0:T(8,128)S(1)}, f32[8,32,256]{2,1,0:T(8,128)S(1)}, u32[]{:S(2)}, u32[]{:S(2)}) collective-permute-start(f32[8,32,256]{2,1,0:T(8,128)S(1)} %get-tuple-element.49), channel_id=1, source_target_pairs={{0,2},{1,3},{2,0},{3,1},{4,6},{5,7},{6,4},{7,5},{8,10},{9,11},{10,... | collective-permute-start | bytes 786440 | tf_op jit(solution)/shard_map/ppermute | solution.py:468
  163.7 37.1 %collective-permute-start.17 = (f32[8,32,256]{2,1,0:T(8,128)}, f32[8,32,256]{2,1,0:T(8,128)S(1)}, u32[]{:S(2)}, u32[]{:S(2)}) collective-permute-start(f32[8,32,256]{2,1,0:T(8,128)} %get-tuple-element.43), channel_id=1, source_target_pairs={{0,1},{1,2},{2,3},{3,0},{4,5},{5,6},{6,7},{7,4},{8,9},{9,10},{10,1... | collective-permute-start | bytes 786440 | tf_op jit(solution)/shard_map/ppermute | solution.py:468
  180.6 20.1 %collective-permute-start.18 = (f32[8,32,256]{2,1,0:T(8,128)S(1)}, f32[8,32,256]{2,1,0:T(8,128)S(1)}, u32[]{:S(2)}, u32[]{:S(2)}) collective-permute-start(f32[8,32,256]{2,1,0:T(8,128)S(1)} %get-tuple-element.44), channel_id=1, source_target_pairs={{0,3},{1,0},{2,1},{3,2},{4,7},{5,4},{6,5},{7,6},{8,11},{9,8},{10,9... | collective-permute-start | bytes 786440 | tf_op jit(solution)/shard_map/ppermute | solution.py:468
  180.6 26.7 %collective-permute-start.19 = (f32[8,32,256]{2,1,0:T(8,128)S(1)}, f32[8,32,256]{2,1,0:T(8,128)S(1)}, u32[]{:S(2)}, u32[]{:S(2)}) collective-permute-start(f32[8,32,256]{2,1,0:T(8,128)S(1)} %get-tuple-element.45), channel_id=1, source_target_pairs={{0,2},{1,3},{2,0},{3,1},{4,6},{5,7},{6,4},{7,5},{8,10},{9,11},{10,... | collective-permute-start | bytes 786440 | tf_op jit(solution)/shard_map/ppermute | solution.py:468
  (21 other events, 132.6 us)

commit v8 on v7

--- a/solution.py
+++ b/solution.py
@@ -110,11 +110,11 @@
         out_ref[at + 1] = jnp.where(half < halves - 1, tiles[1][0], 0.0)
 
 
-def pack_kernel(shifts, owners, rows, part, me_ref, state_ref, adjoint_ref, *refs):
+def pack_kernel(shifts, owners, first, rows, me_ref, state_ref, adjoint_ref, *refs):
     buffers, sems = refs[-2:]
     outs = refs[-2 - len(shifts) : -2]
     waits = [
-        fetch(me_ref, state_ref, adjoint_ref, shift, owners, lambda half: part * rows, rows, buffers.at[i], sems.at[i])
+        fetch(me_ref, state_ref, adjoint_ref, shift, owners, lambda half: first, rows, buffers.at[i], sems.at[i])
         for i, shift in enumerate(shifts)
     ]
     for index, wait in enumerate(waits):
@@ -122,11 +122,11 @@
         outs[index][...] = jnp.swapaxes(buffers[index], 0, 1)
 
 
-def pack(me, state, adjoint, shifts, part, rows, owners, earlier):
+def pack(me, state, adjoint, shifts, first, rows, owners, earlier):
     modes, _, width = state.shape
     shape = (rows, modes, width)
     return pl.pallas_call(
-        functools.partial(pack_kernel, shifts, owners, rows, part),
+        functools.partial(pack_kernel, shifts, owners, first, rows),
         grid=(1,),
         in_specs=[SCALARS] + [ANYWHERE] * (2 + len(earlier)),
         out_specs=[pl.BlockSpec(shape, lambda i: (0, 0, 0))] * len(shifts),
@@ -141,7 +141,8 @@
     )(me, state, adjoint, *earlier)
 
 
-def pack_all_kernel(halves, state_ref, adjoint_ref, out_ref, buffers, sems):
+def pack_all_kernel(halves, part, state_ref, adjoint_ref, *refs):
+    out_ref, buffers, sems = refs[-3:]
     height = state_ref.shape[1]
     half_rows = height // halves
     rows = buffers.shape[3]
@@ -149,8 +150,10 @@
     for field, ref in enumerate((state_ref, adjoint_ref)):
         for half in range(halves):
             first = half * half_rows
-            starts = [first, max(first - TILE, 0), min(first + half_rows, height - TILE)]
-            if halves == 2:
+            starts = [first + part * rows, max(first - TILE, 0), min(first + half_rows, height - TILE)]
+            if part:
+                del starts[1:]
+            elif halves == 2:
                 starts.pop(2 if half else 1)
             for i, start in enumerate(starts):
                 at = (field * halves + half, i)
@@ -172,14 +175,14 @@
             out_ref[block, rows + i - 1] = values[TILE - 1 if i == 1 else 0] if inside else jnp.zeros_like(values[0])
 
 
-def pack_all(state, adjoint, halves):
+def pack_all(state, adjoint, halves, part, earlier):
     modes, _, width = state.shape
-    edges = edge_count(halves)
+    edges = 0 if part else edge_count(halves)
     shape = (2 * halves, TILE + edges, modes, width)
     return pl.pallas_call(
-        functools.partial(pack_all_kernel, halves),
+        functools.partial(pack_all_kernel, halves, part),
         grid=(1,),
-        in_specs=[ANYWHERE] * 2,
+        in_specs=[ANYWHERE] * (2 + len(earlier)),
         out_specs=pl.BlockSpec(shape, lambda i: (0,) * 4),
         out_shape=jax.ShapeDtypeStruct(shape, jnp.float32),
         scratch_shapes=[
@@ -189,7 +192,7 @@
         compiler_params=params(60),
         cost_estimate=cost(3),
         name="pack_all",
-    )(state, adjoint)
+    )(state, adjoint, *earlier)
 
 
 def pack_own_kernel(owners, me_ref, state_ref, adjoint_ref, coef_ref, *refs):
@@ -347,7 +350,7 @@
         mix(row, row % 2)
 
 
-def apply_operator(me, coef, matrix, own, own_near, groups, near, part, rows, shifts, by_owner):
+def apply_operator(me, coef, matrix, own, own_near, groups, group_of, near, part, rows, shifts, by_owner):
     _, block, width = own.shape
     owners = len(shifts) + 1
     modes = owners * block
@@ -360,7 +363,8 @@
         return pl.BlockSpec((count, block, width), lambda i: (first // count, 0, 0))
 
     def pieces_at(first, count):
-        group, first_in = first // rows, first % rows
+        group, skipped = group_of[first // rows]
+        first_in = first - skipped * rows
         return [own, *groups[group]], [at(count, head + first)] + [at(count, first_in)] * len(shifts)
 
     def edge_pieces():
@@ -471,39 +475,48 @@
         return lax.ppermute(array, "space", forward), lax.ppermute(array, "space", backward)
 
     matrix = coupling_matrices(me, pattern, weights, shifts)
+    halves = owners // 2
     groups, bodies, nears, mixed = [], [], [], []
-
-    def exchange(part):
-        earlier = [own] if part == 1 else [mixed[part - 3][0]] if part > 2 else [bodies[0]]
-        packed = pack(me, state, adjoint, shifts, part, rows, owners, earlier)
+    if parts > 2:
+        members = [[0], list(range(1, parts - 1)), [parts - 1]]
+    else:
+        members = [[part] for part in range(parts)]
+    group_of = {part: (index, group[0]) for index, group in enumerate(members) for part in group}
+
+    def exchange_all(part, earlier):
+        packed = pack_all(state, adjoint, halves, part, earlier)
+        arrived = lax.all_to_all(packed, "mode", 0, 0, tiled=True)
+        groups.append(
+            [lax.dynamic_index_in_dim(arrived, lax.rem(me[0] + owners - s, owners), keepdims=False) for s in shifts]
+        )
+        return packed
+
+    def exchange(group, earlier):
+        packed = pack(me, state, adjoint, shifts, group[0] * rows, len(group) * rows, owners, earlier)
         groups.append([move(piece, shift) for piece, shift in zip(packed, shifts)])
 
-    def halo(part):
-        earlier = [mixed[part - 2][0]] if part > 1 else [] if part else own_near
-        bodies.append(gather(groups[part], rows, 0, earlier))
+    def halo(part, earlier):
+        group, skipped = group_of[part]
+        bodies.append(gather(groups[group], rows, part - skipped, earlier))
         nears.append(beside(bodies[part]))
 
-    def operate(part):
-        mixed.append(
-            apply_operator(me, coef, matrix, own, own_near, groups, nears[part], part, rows, shifts, part == 0)
-        )
-
-    packed = pack_all(state, adjoint, owners // 2)
-    everyone = lax.all_to_all(packed, "mode", 0, 0, tiled=True)
-    groups.append(
-        [lax.dynamic_index_in_dim(everyone, lax.rem(me[0] + owners - s, owners), keepdims=False) for s in shifts]
-    )
+    packed = exchange_all(0, [])
     own = pack_own(me, state, adjoint, coef, owners, [packed])
     own_near = list(beside(own))
-    halo(0)
-    exchange(1)
-    halo(1)
+    halo(0, own_near)
+    for group in members[1:]:
+        if group[0] > 1:
+            exchange_all(group[0], [bodies[0]])
+        else:
+            exchange(group, [own])
     for part in range(parts):
-        if part + 2 < parts:
-            exchange(part + 2)
-        operate(part)
-        if part + 2 < parts:
-            halo(part + 2)
+        if part:
+            halo(part, [mixed[part - 2][0]] if part > 1 else list(nears[0]))
+        mixed.append(
+            apply_operator(
+                me, coef, matrix, own, own_near, groups, group_of, nears[part], part, rows, shifts, part == 0
+            )
+        )
 
     outputs = None
     for part in range(parts):

time: 212 us -> 249 us (1.17)
  starting transfers between devices: 66.1 us -> 87.5 us
  waiting for transfers between devices: 77.3 us -> 96.9 us
  Pallas kernels: 54 us -> 49.4 us
    ppermute x18 -> x12, waiting for transfers between devices: 39.2 us -> 69.7 us  [move(): lax.ppermute(array, 'mode', [(i, (i + shift) % owners) for i in range(own...]
    ppermute x18 -> x12, starting transfers between devices: 24.3 us -> 38.1 us  [move(): lax.ppermute(array, 'mode', [(i, (i + shift) % owners) for i in range(own...]
    ppermute x5, waiting for transfers between devices: 6.62 us -> 1.04 us  [beside(): lax.ppermute(array, 'space', backward)]
    all_to_all x1 -> x2, waiting for transfers between devices: 24.8 us -> 19.6 us  [exchange_all(): arrived = lax.all_to_all(packed, 'mode', 0, 0, tiled=True)]
    all_to_all x1 -> x2, starting transfers between devices: 4.88 us -> 9.99 us  [exchange_all(): arrived = lax.all_to_all(packed, 'mode', 0, 0, tiled=True)]
    pallas_call x4, Pallas kernels: 5.33 us -> 1.12 us  [gather(): pl.pallas_call(functools.partial(gather_kernel, len(pieces)), grid=(1,),...]
    ppermute x5, starting transfers between devices: 22.7 us -> 25.6 us  [beside(): lax.ppermute(array, 'space', backward)]
    pallas_call x4 -> x3, Pallas kernels: 8.79 us -> 7.46 us  [the longest x2 4.88 us: pack_all(): pl.pallas_call(functools.partial(pack_all_kernel, halves, part), grid=(1,...]
  transfers between devices with their start and end apart: 30 -> 25, of which waited for: 13 -> 10; matrix products, arithmetic and copies ran while one was open for 2% -> 2% of each run, Pallas kernels for 23% -> 17%
where the time goes in v8:
time: 249 us; the launch traced here: 247 us
  waiting for transfers between devices  96.9 us (39%)
  starting transfers between devices  87.5 us (35%)
  Pallas kernels  49.4 us (20%)
  local copies, waits for them, and re-layouts  10.1 us (4%)
    ppermute x12, waiting for transfers between devices, move(): lax.ppermute(array, 'mode', [(i, (i + shift) % owners) for i in range(own...  69.7 us
    ppermute x12, starting transfers between devices, move(): lax.ppermute(array, 'mode', [(i, (i + shift) % owners) for i in range(own...  38.1 us
    pallas_call x4, Pallas kernels, apply_operator(): pl.pallas_call(functools.partial(operator_kernel, shifts, terms, part, pa...  27.7 us
    ppermute x5, starting transfers between devices, beside(): lax.ppermute(array, 'space', backward)  25.6 us
    all_to_all x2, waiting for transfers between devices, exchange_all(): arrived = lax.all_to_all(packed, 'mode', 0, 0, tiled=True)  19.6 us
    all_to_all x2, starting transfers between devices, exchange_all(): arrived = lax.all_to_all(packed, 'mode', 0, 0, tiled=True)  9.99 us
    pallas_call x4, Pallas kernels, finish(): pl.pallas_call(functools.partial(finish_kernel, shifts, by_owner), grid=(...  9.97 us
    ppermute x5, starting transfers between devices, beside(): lax.ppermute(array, 'space', forward)  9.57 us
  transfers between devices with their start and end apart: 25, of which 10 were waited for; matrix products, arithmetic and copies ran while one was open for 2% of the time, Pallas kernels for 17%

profile of v8, /device:TPU:4, one launch (start us, length us, event | category | flops | bytes accessed | tf_op | source)
XLA Modules:
  0.0 246.6 jit_solution(14203045346215970207)
XLA Ops:
  0.6 2.6 %pack_all.2.refs_0_ = f32[4,9,32,256]{3,2,1,0:T(8,128)} custom-call(f32[32,64,256]{2,1,0:T(8,128)} %bitcast.32, f32[32,64,256]{2,1,0:T(8,128)} %bitcast.44), custom_call_target="tpu_custom_call" | custom-call | bytes 10500000 | tf_op jit(solution)/shard_map/pack_all/pallas_call | solution.py:182
  3.3 4.9 %all-to-all-start = ((f32[4,9,32,256]{3,2,1,0:T(8,128)}), f32[4,9,32,256]{3,2,1,0:T(8,128)}, u32[]{:S(2)}, u32[]{:S(2)}) async-start(f32[4,9,32,256]{3,2,1,0:T(8,128)} %pack_all.2.refs_0_), calls=%async_computation | async-start | bytes 2359296 | tf_op jit(solution)/shard_map/all_to_all | solution.py:488
  8.1 2.6 %pack_own.1.refs_0_.refs_7_.refs_11_.refs_15_ = f32[40,32,256]{2,1,0:T(8,128)} custom-call(s32[1]{0:T(128)} %bitcast.me_ref, f32[32,64,256]{2,1,0:T(8,128)} %bitcast.33, f32[32,64,256]{2,1,0:T(8,128)} %bitcast.45, f32[7,64,256]{2,1,0:T(8,128)} %bitcast.25, f32[4,9,32,256]{3,2,1,0:T(8,128)} %pack_all.2.refs_0_), custom_call_target="tpu_custom_call" | custom-call | bytes 10500000 | tf_op jit(solution)/shard_map/pack_own/pallas_call | solution.py:226
  12.6 4.5 %collective-permute-start.1 = (f32[40,32,256]{2,1,0:T(8,128)}, f32[40,32,256]{2,1,0:T(8,128)S(1)}, u32[]{:S(2)}, u32[]{:S(2)}) collective-permute-start(f32[40,32,256]{2,1,0:T(8,128)} %pack_own.1.refs_0_.refs_7_.refs_11_.refs_15_), channel_id=1, source_target_pairs={{4,0},{8,4},{12,8},{16,12},{20,16},{24,20},{28,24},{5,1},{9,5},{13... | collective-permute-start | bytes 3932168 | tf_op jit(solution)/shard_map/ppermute | solution.py:475
  17.2 19.6 %all-to-all-done = f32[4,9,32,256]{3,2,1,0:T(8,128)} async-done(((f32[4,9,32,256]{3,2,1,0:T(8,128)}), f32[4,9,32,256]{3,2,1,0:T(8,128)}, u32[]{:S(2)}, u32[]{:S(2)}) %all-to-all-start) | async-done | bytes 1179680 | tf_op jit(solution)/shard_map/all_to_all | solution.py:488
  38.0 4.0 %collective-permute-done.refs_3_.refs_1_ = f32[40,32,256]{2,1,0:T(8,128)S(1)} collective-permute-done((f32[40,32,256]{2,1,0:T(8,128)}, f32[40,32,256]{2,1,0:T(8,128)S(1)}, u32[]{:S(2)}, u32[]{:S(2)}) %collective-permute-start) | collective-permute-done | bytes 1310752 | tf_op jit(solution)/shard_map/ppermute | solution.py:475
  45.0 2.3 pack_all.3
  47.2 5.1 %all-to-all-start.1 = ((f32[4,8,32,256]{3,2,1,0:T(8,128)}), f32[4,8,32,256]{3,2,1,0:T(8,128)}, u32[]{:S(2)}, u32[]{:S(2)}) async-start(f32[4,8,32,256]{3,2,1,0:T(8,128)} %pack_all.3), calls=%async_computation.1 | async-start | bytes 2097152 | tf_op jit(solution)/shard_map/all_to_all | solution.py:488
  54.3 4.5 %collective-permute-start.6 = (f32[24,32,256]{2,1,0:T(8,128)}, f32[24,32,256]{2,1,0:T(8,128)}, u32[]{:S(2)}, u32[]{:S(2)}) collective-permute-start(f32[24,32,256]{2,1,0:T(8,128)} %copy-done.5), channel_id=1, source_target_pairs={{4,0},{8,4},{12,8},{16,12},{20,16},{24,20},{28,24},{5,1},{9,5},{13... | collective-permute-start | bytes 2359304 | tf_op jit(solution)/shard_map/ppermute | solution.py:475
  58.8 2.6 %pack.1 = (f32[16,32,256]{2,1,0:T(8,128)}, f32[16,32,256]{2,1,0:T(8,128)}, f32[16,32,256]{2,1,0:T(8,128)}) custom-call(s32[1]{0:T(128)} %bitcast.me_ref, f32[32,64,256]{2,1,0:T(8,128)} %bitcast.35, f32[32,64,256]{2,1,0:T(8,128)} %bitcast.47, f32[40,32,256]{2,1,0:T(8,128)} %pack_own.1.refs_0_.refs_7_.refs_11_.refs_15_), custom_call_target="tpu_custom_call" | custom-call | bytes 10500000 | tf_op jit(solution)/shard_map/pack/pallas_call | solution.py:128
  66.4 19.7 %collective-permute-done.2.refs_0_.refs_8_.refs_16_.refs_12_ = f32[16,32,256]{2,1,0:T(8,128)S(1)} collective-permute-done((f32[16,32,256]{2,1,0:T(8,128)}, f32[16,32,256]{2,1,0:T(8,128)S(1)}, u32[]{:S(2)}, u32[]{:S(2)}) %collective-permute-start.2) | collective-permute-done | bytes 524320 | tf_op jit(solution)/shard_map/ppermute | solution.py:472
  86.1 7.1 %collective-permute-done.3.refs_1_.refs_9_.refs_17_.refs_13_ = f32[16,32,256]{2,1,0:T(8,128)S(1)} collective-permute-done((f32[16,32,256]{2,1,0:T(8,128)}, f32[16,32,256]{2,1,0:T(8,128)S(1)}, u32[]{:S(2)}, u32[]{:S(2)}) %collective-permute-start.3) | collective-permute-done | bytes 524320 | tf_op jit(solution)/shard_map/ppermute | solution.py:472
  93.2 26.8 %collective-permute-done.4.refs_2_.refs_10_.refs_18_.refs_14_ = f32[16,32,256]{2,1,0:T(8,128)S(1)} collective-permute-done((f32[16,32,256]{2,1,0:T(8,128)}, f32[16,32,256]{2,1,0:T(8,128)S(1)}, u32[]{:S(2)}, u32[]{:S(2)}) %collective-permute-start.4) | collective-permute-done | bytes 524320 | tf_op jit(solution)/shard_map/ppermute | solution.py:472
  122.9 7.2 %collective-permute-start.8 = (f32[24,32,256]{2,1,0:T(8,128)}, f32[24,32,256]{2,1,0:T(8,128)}, u32[]{:S(2)}, u32[]{:S(2)}) collective-permute-start(f32[24,32,256]{2,1,0:T(8,128)} %gather.5), channel_id=1, source_target_pairs={{4,0},{8,4},{12,8},{16,12},{20,16},{24,20},{28,24},{5,1},{9,5},{13... | collective-permute-start | bytes 2359304 | tf_op jit(solution)/shard_map/ppermute | solution.py:475
  130.7 6.5 %operator.6.refs_3_ = f32[4,8,32,256]{3,2,1,0:T(8,128)S(1)} custom-call(s32[1]{0:T(128)} %bitcast.me_ref, f32[7,64,256]{2,1,0:T(8,128)S(1)} %bitcast.26, bf16[256,896]{1,0:T(8,128)(2,1)S(1)} %coupling.1.matrix_ref, f32[40,32,256]{2,1,0:T(8,128)} %pack_own.1.refs_0_.refs_7_.refs_11_.refs_15_, f32[40,32,256]{2,1,0:T(8,128)} %copy-done, ...), custom_call_target="tpu_custom_call" | custom-call | bytes 21000000 | tf_op jit(solution)/shard_map/operator/pallas_call | solution.py:384
  138.2 4.3 %all-to-all-start.2 = ((f32[4,8,32,256]{3,2,1,0:T(8,128)}), f32[4,8,32,256]{3,2,1,0:T(8,128)}, u32[]{:S(2)}, u32[]{:S(2)}) async-start(f32[4,8,32,256]{3,2,1,0:T(8,128)} %copy-done.3), calls=%async_computation.2 | async-start | bytes 2097152 | tf_op jit(solution)/shard_map/all_to_all | solution.py:524
  145.7 4.7 %collective-permute-start.15 = (f32[24,32,256]{2,1,0:T(8,128)S(1)}, f32[24,32,256]{2,1,0:T(8,128)S(1)}, u32[]{:S(2)}, u32[]{:S(2)}) collective-permute-start(f32[24,32,256]{2,1,0:T(8,128)S(1)} %gather.7), channel_id=1, source_target_pairs={{4,0},{8,4},{12,8},{16,12},{20,16},{24,20},{28,24},{5,1},{9,5},{13... | collective-permute-start | bytes 2359304 | tf_op jit(solution)/shard_map/ppermute | solution.py:475
  151.7 6.8 %operator.4 = (f32[8,32,256]{2,1,0:T(8,128)S(1)}, f32[8,32,256]{2,1,0:T(8,128)S(1)}, f32[8,32,256]{2,1,0:T(8,128)S(1)}, f32[8,32,256]{2,1,0:T(8,128)S(1)}) custom-call(s32[1]{0:T(128)} %bitcast.me_ref, f32[7,64,256]{2,1,0:T(8,128)S(1)} %bitcast.27, bf16[256,896]{1,0:T(8,128)(2,1)S(1)} %coupling.1.matrix_ref, ...), custom_call_target="tpu_custom_call" | custom-call | bytes 21000000 | tf_op jit(solution)/shard_map/operator/pallas_call | solution.py:384
  161.1 4.5 %collective-permute-start.10 = (f32[24,32,256]{2,1,0:T(8,128)S(1)}, f32[24,32,256]{2,1,0:T(8,128)S(1)}, u32[]{:S(2)}, u32[]{:S(2)}) collective-permute-start(f32[24,32,256]{2,1,0:T(8,128)S(1)} %gather.6), channel_id=1, source_target_pairs={{4,0},{8,4},{12,8},{16,12},{20,16},{24,20},{28,24},{5,1},{9,5},{13... | collective-permute-start | bytes 2359304 | tf_op jit(solution)/shard_map/ppermute | solution.py:475
  165.7 7.0 %operator.7 = (f32[8,32,256]{2,1,0:T(8,128)S(1)}, f32[8,32,256]{2,1,0:T(8,128)S(1)}, f32[8,32,256]{2,1,0:T(8,128)}, f32[8,32,256]{2,1,0:T(8,128)}) custom-call(s32[1]{0:T(128)} %bitcast.me_ref, f32[7,64,256]{2,1,0:T(8,128)S(1)} %bitcast.28, bf16[256,896]{1,0:T(8,128)(2,1)S(1)} %coupling.1.matrix_ref, ...), custom_call_target="tpu_custom_call" | custom-call | bytes 21000000 | tf_op jit(solution)/shard_map/operator/pallas_call | solution.py:384
  176.9 2.4 collective-permute-start.20
  179.3 2.6 %collective-permute-done.9.refs_5_ = f32[24,32,256]{2,1,0:T(8,128)S(1)} collective-permute-done((f32[24,32,256]{2,1,0:T(8,128)S(1)}, f32[24,32,256]{2,1,0:T(8,128)S(1)}, u32[]{:S(2)}, u32[]{:S(2)}) %collective-permute-start.9) | collective-permute-done | bytes 786464 | tf_op jit(solution)/shard_map/ppermute | solution.py:475
  181.9 2.9 %collective-permute-start.21 = (f32[8,32,256]{2,1,0:T(8,128)S(1)}, f32[8,32,256]{2,1,0:T(8,128)S(1)}, u32[]{:S(2)}, u32[]{:S(2)}) collective-permute-start(f32[8,32,256]{2,1,0:T(8,128)S(1)} %get-tuple-element.40), channel_id=1, source_target_pairs={{0,2},{1,3},{2,0},{3,1},{4,6},{5,7},{6,4},{7,5},{8,10},{9,11},{10,... | collective-permute-start | bytes 786440 | tf_op jit(solution)/shard_map/ppermute | solution.py:472
  186.5 7.4 %operator.5 = (f32[8,32,256]{2,1,0:T(8,128)S(1)}, f32[8,32,256]{2,1,0:T(8,128)}, f32[8,32,256]{2,1,0:T(8,128)}, f32[8,32,256]{2,1,0:T(8,128)}) custom-call(s32[1]{0:T(128)} %bitcast.me_ref, f32[7,64,256]{2,1,0:T(8,128)S(1)} %bitcast.29, bf16[256,896]{1,0:T(8,128)(2,1)S(1)} %coupling.1.matrix_ref, f32[40,32,256]{2,1,0:T(8,128)} %pack_own.1.refs_0_.refs_7_.refs_11_.refs_15_, ...), custom_call_target="tpu_custom_call" | custom-call | bytes 21000000 | tf_op jit(solution)/shard_map/operator/pallas_call | solution.py:384
  196.1 15.1 %collective-permute-start.11 = (f32[8,32,256]{2,1,0:T(8,128)}, f32[8,32,256]{2,1,0:T(8,128)S(1)}, u32[]{:S(2)}, u32[]{:S(2)}) collective-permute-start(f32[8,32,256]{2,1,0:T(8,128)} %get-tuple-element.31), channel_id=1, source_target_pairs={{0,1},{1,2},{2,3},{3,0},{4,5},{5,6},{6,7},{7,4},{8,9},{9,10},{10,1... | collective-permute-start | bytes 786440 | tf_op jit(solution)/shard_map/ppermute | solution.py:472
  212.5 6.1 %collective-permute-start.13 = (f32[8,32,256]{2,1,0:T(8,128)}, f32[8,32,256]{2,1,0:T(8,128)S(1)}, u32[]{:S(2)}, u32[]{:S(2)}) collective-permute-start(f32[8,32,256]{2,1,0:T(8,128)} %get-tuple-element.33), channel_id=1, source_target_pairs={{0,2},{1,3},{2,0},{3,1},{4,6},{5,7},{6,4},{7,5},{8,10},{9,11},{10,... | collective-permute-start | bytes 786440 | tf_op jit(solution)/shard_map/ppermute | solution.py:472
  220.4 2.4 finish.4
  222.8 2.5 %finish.5 = (f32[32,64,256]{2,1,0:T(8,128)}, f32[32,64,256]{2,1,0:T(8,128)}) custom-call(s32[1]{0:T(128)} %bitcast.me_ref, f32[8,32,256]{2,1,0:T(8,128)} %copy-done.6, f32[8,32,256]{2,1,0:T(8,128)} %copy-done.15, f32[8,32,256]{2,1,0:T(8,128)} %copy-done.16, f32[8,32,256]{2,1,0:T(8,128)} %copy-done.17, ...), custom_call_target="tpu_custom_call", output_to_operand_aliasing={{0}: (7, {}), {1}: (8, {})} | custom-call | bytes 8750000 | tf_op jit(solution)/shard_map/finish/pallas_call | solution.py:443
  225.4 4.1 %collective-permute-done.18.refs_3_ = f32[8,32,256]{2,1,0:T(8,128)S(1)} collective-permute-done((f32[8,32,256]{2,1,0:T(8,128)}, f32[8,32,256]{2,1,0:T(8,128)S(1)}, u32[]{:S(2)}, u32[]{:S(2)}) %collective-permute-start.18) | collective-permute-done | bytes 262176 | tf_op jit(solution)/shard_map/ppermute | solution.py:472
  230.2 2.5 %finish.6 = (f32[32,64,256]{2,1,0:T(8,128)}, f32[32,64,256]{2,1,0:T(8,128)}) custom-call(s32[1]{0:T(128)} %bitcast.me_ref, f32[8,32,256]{2,1,0:T(8,128)} %copy-done.7, f32[8,32,256]{2,1,0:T(8,128)} %copy-done.14, f32[8,32,256]{2,1,0:T(8,128)} %collective-permute-done.17.refs_2_, ...), custom_call_target="tpu_custom_call", output_to_operand_aliasing={{0}: (7, {}), {1}: (8, {})} | custom-call | bytes 8750000 | tf_op jit(solution)/shard_map/finish/pallas_call | solution.py:443
  232.7 10.7 %collective-permute-done.13.refs_3_ = f32[8,32,256]{2,1,0:T(8,128)S(1)} collective-permute-done((f32[8,32,256]{2,1,0:T(8,128)}, f32[8,32,256]{2,1,0:T(8,128)S(1)}, u32[]{:S(2)}, u32[]{:S(2)}) %collective-permute-start.13) | collective-permute-done | bytes 262176 | tf_op jit(solution)/shard_map/ppermute | solution.py:472
  244.1 2.5 %finish.7 = (f32[32,64,256]{2,1,0:T(8,128)}, f32[32,64,256]{2,1,0:T(8,128)}) custom-call(s32[1]{0:T(128)} %bitcast.me_ref, f32[8,32,256]{2,1,0:T(8,128)} %copy-done.8, f32[8,32,256]{2,1,0:T(8,128)} %copy-done.18, f32[8,32,256]{2,1,0:T(8,128)} %copy-done.19, f32[8,32,256]{2,1,0:T(8,128)} %copy-done.21, ...), custom_call_target="tpu_custom_call", output_to_operand_aliasing={{0}: (7, {}), {1}: (8, {})} | custom-call | bytes 8750000 | tf_op jit(solution)/shard_map/finish/pallas_call | solution.py:443
  (82 shorter events, 37.1 us)
Async XLA Ops:
  3.3 33.5 %all-to-all-start = ((f32[4,9,32,256]{3,2,1,0:T(8,128)}), f32[4,9,32,256]{3,2,1,0:T(8,128)}, u32[]{:S(2)}, u32[]{:S(2)}) async-start(f32[4,9,32,256]{3,2,1,0:T(8,128)} %pack_all.2.refs_0_), calls=%async_computation | async-start | bytes 2359296 | tf_op jit(solution)/shard_map/all_to_all | solution.py:488
  10.7 31.3 %collective-permute-start = (f32[40,32,256]{2,1,0:T(8,128)}, f32[40,32,256]{2,1,0:T(8,128)S(1)}, u32[]{:S(2)}, u32[]{:S(2)}) collective-permute-start(f32[40,32,256]{2,1,0:T(8,128)} %pack_own.1.refs_0_.refs_7_.refs_11_.refs_15_), channel_id=1, source_target_pairs={{0,4},{4,8},{8,12},{12,16},{16,20},{20,24},{24,28},{1,5},{5,9},{9,... | collective-permute-start | bytes 3932168 | tf_op jit(solution)/shard_map/ppermute | solution.py:475
  12.6 30.4 %collective-permute-start.1 = (f32[40,32,256]{2,1,0:T(8,128)}, f32[40,32,256]{2,1,0:T(8,128)S(1)}, u32[]{:S(2)}, u32[]{:S(2)}) collective-permute-start(f32[40,32,256]{2,1,0:T(8,128)} %pack_own.1.refs_0_.refs_7_.refs_11_.refs_15_), channel_id=1, source_target_pairs={{4,0},{8,4},{12,8},{16,12},{20,16},{24,20},{28,24},{5,1},{9,5},{13... | collective-permute-start | bytes 3932168 | tf_op jit(solution)/shard_map/ppermute | solution.py:475
  47.2 91.0 %all-to-all-start.1 = ((f32[4,8,32,256]{3,2,1,0:T(8,128)}), f32[4,8,32,256]{3,2,1,0:T(8,128)}, u32[]{:S(2)}, u32[]{:S(2)}) async-start(f32[4,8,32,256]{3,2,1,0:T(8,128)} %pack_all.3), calls=%async_computation.1 | async-start | bytes 2097152 | tf_op jit(solution)/shard_map/all_to_all | solution.py:488
  52.3 67.7 %collective-permute-start.5 = (f32[24,32,256]{2,1,0:T(8,128)}, f32[24,32,256]{2,1,0:T(8,128)}, u32[]{:S(2)}, u32[]{:S(2)}) collective-permute-start(f32[24,32,256]{2,1,0:T(8,128)} %copy-done.5), channel_id=1, source_target_pairs={{0,4},{4,8},{8,12},{12,16},{16,20},{20,24},{24,28},{1,5},{5,9},{9,... | collective-permute-start | bytes 2359304 | tf_op jit(solution)/shard_map/ppermute | solution.py:475
  54.3 65.8 %collective-permute-start.6 = (f32[24,32,256]{2,1,0:T(8,128)}, f32[24,32,256]{2,1,0:T(8,128)}, u32[]{:S(2)}, u32[]{:S(2)}) collective-permute-start(f32[24,32,256]{2,1,0:T(8,128)} %copy-done.5), channel_id=1, source_target_pairs={{4,0},{8,4},{12,8},{16,12},{20,16},{24,20},{28,24},{5,1},{9,5},{13... | collective-permute-start | bytes 2359304 | tf_op jit(solution)/shard_map/ppermute | solution.py:475
  61.4 68.7 %copy-start.9 = (s32[7,128,4]{1,2,0:T(4,128)S(1)}, s32[7,128,4]{1,2,0:T(4,128)}, u32[]{:S(2)}) copy-start(s32[7,128,4]{1,2,0:T(4,128)} %param.10) | copy-start | bytes 43012
  61.4 68.7 %copy-start.10 = (f32[7,128,4]{1,2,0:T(4,128)S(1)}, f32[7,128,4]{1,2,0:T(4,128)}, u32[]{:S(2)}) copy-start(f32[7,128,4]{1,2,0:T(4,128)} %param.11) | copy-start | bytes 43012
  61.4 24.7 %collective-permute-start.2 = (f32[16,32,256]{2,1,0:T(8,128)}, f32[16,32,256]{2,1,0:T(8,128)S(1)}, u32[]{:S(2)}, u32[]{:S(2)}) collective-permute-start(f32[16,32,256]{2,1,0:T(8,128)} %get-tuple-element.26), channel_id=1, source_target_pairs={{0,1},{1,2},{2,3},{3,0},{4,5},{5,6},{6,7},{7,4},{8,9},{9,10},{10,1... | collective-permute-start | bytes 1572872 | tf_op jit(solution)/shard_map/ppermute | solution.py:472
  63.5 29.7 %collective-permute-start.3 = (f32[16,32,256]{2,1,0:T(8,128)}, f32[16,32,256]{2,1,0:T(8,128)S(1)}, u32[]{:S(2)}, u32[]{:S(2)}) collective-permute-start(f32[16,32,256]{2,1,0:T(8,128)} %get-tuple-element.27), channel_id=1, source_target_pairs={{0,3},{1,0},{2,1},{3,2},{4,7},{5,4},{6,5},{7,6},{8,11},{9,8},{10,9... | collective-permute-start | bytes 1572872 | tf_op jit(solution)/shard_map/ppermute | solution.py:472
  65.4 65.3 %copy-start.2 = (f32[7,1,64,256]{3,2,1,0:T(8,128)S(1)}, f32[7,1,64,256]{3,2,1,0:T(8,128)}, u32[]{:S(2)}) copy-start(f32[7,1,64,256]{3,2,1,0:T(8,128)} %param.9) | copy-start | bytes 1376260
  65.4 54.6 %collective-permute-start.4 = (f32[16,32,256]{2,1,0:T(8,128)}, f32[16,32,256]{2,1,0:T(8,128)S(1)}, u32[]{:S(2)}, u32[]{:S(2)}) collective-permute-start(f32[16,32,256]{2,1,0:T(8,128)} %get-tuple-element.28), channel_id=1, source_target_pairs={{0,2},{1,3},{2,0},{3,1},{4,6},{5,7},{6,4},{7,5},{8,10},{9,11},{10,... | collective-permute-start | bytes 1572872 | tf_op jit(solution)/shard_map/ppermute | solution.py:472
  121.0 30.7 %collective-permute-start.7 = (f32[24,32,256]{2,1,0:T(8,128)}, f32[24,32,256]{2,1,0:T(8,128)}, u32[]{:S(2)}, u32[]{:S(2)}) collective-permute-start(f32[24,32,256]{2,1,0:T(8,128)} %gather.5), channel_id=1, source_target_pairs={{0,4},{4,8},{8,12},{12,16},{16,20},{20,24},{24,28},{1,5},{5,9},{9,... | collective-permute-start | bytes 2359304 | tf_op jit(solution)/shard_map/ppermute | solution.py:475
  122.9 28.8 %collective-permute-start.8 = (f32[24,32,256]{2,1,0:T(8,128)}, f32[24,32,256]{2,1,0:T(8,128)}, u32[]{:S(2)}, u32[]{:S(2)}) collective-permute-start(f32[24,32,256]{2,1,0:T(8,128)} %gather.5), channel_id=1, source_target_pairs={{4,0},{8,4},{12,8},{16,12},{20,16},{24,20},{28,24},{5,1},{9,5},{13... | collective-permute-start | bytes 2359304 | tf_op jit(solution)/shard_map/ppermute | solution.py:475
  138.2 82.2 %all-to-all-start.2 = ((f32[4,8,32,256]{3,2,1,0:T(8,128)}), f32[4,8,32,256]{3,2,1,0:T(8,128)}, u32[]{:S(2)}, u32[]{:S(2)}) async-start(f32[4,8,32,256]{3,2,1,0:T(8,128)} %copy-done.3), calls=%async_computation.2 | async-start | bytes 2097152 | tf_op jit(solution)/shard_map/all_to_all | solution.py:524
  143.8 21.9 %collective-permute-start.14 = (f32[24,32,256]{2,1,0:T(8,128)S(1)}, f32[24,32,256]{2,1,0:T(8,128)S(1)}, u32[]{:S(2)}, u32[]{:S(2)}) collective-permute-start(f32[24,32,256]{2,1,0:T(8,128)S(1)} %gather.7), channel_id=1, source_target_pairs={{0,4},{4,8},{8,12},{12,16},{16,20},{20,24},{24,28},{1,5},{5,9},{9,... | collective-permute-start | bytes 2359304 | tf_op jit(solution)/shard_map/ppermute | solution.py:475
  145.7 20.0 %collective-permute-start.15 = (f32[24,32,256]{2,1,0:T(8,128)S(1)}, f32[24,32,256]{2,1,0:T(8,128)S(1)}, u32[]{:S(2)}, u32[]{:S(2)}) collective-permute-start(f32[24,32,256]{2,1,0:T(8,128)S(1)} %gather.7), channel_id=1, source_target_pairs={{4,0},{8,4},{12,8},{16,12},{20,16},{24,20},{28,24},{5,1},{9,5},{13... | collective-permute-start | bytes 2359304 | tf_op jit(solution)/shard_map/ppermute | solution.py:475
  159.2 22.7 %collective-permute-start.9 = (f32[24,32,256]{2,1,0:T(8,128)S(1)}, f32[24,32,256]{2,1,0:T(8,128)S(1)}, u32[]{:S(2)}, u32[]{:S(2)}) collective-permute-start(f32[24,32,256]{2,1,0:T(8,128)S(1)} %gather.6), channel_id=1, source_target_pairs={{0,4},{4,8},{8,12},{12,16},{16,20},{20,24},{24,28},{1,5},{5,9},{9,... | collective-permute-start | bytes 2359304 | tf_op jit(solution)/shard_map/ppermute | solution.py:475
  161.1 23.7 %collective-permute-start.10 = (f32[24,32,256]{2,1,0:T(8,128)S(1)}, f32[24,32,256]{2,1,0:T(8,128)S(1)}, u32[]{:S(2)}, u32[]{:S(2)}) collective-permute-start(f32[24,32,256]{2,1,0:T(8,128)S(1)} %gather.6), channel_id=1, source_target_pairs={{4,0},{8,4},{12,8},{16,12},{20,16},{24,20},{28,24},{5,1},{9,5},{13... | collective-permute-start | bytes 2359304 | tf_op jit(solution)/shard_map/ppermute | solution.py:475
  173.5 21.2 %collective-permute-start.16 = (f32[8,32,256]{2,1,0:T(8,128)S(1)}, f32[8,32,256]{2,1,0:T(8,128)S(1)}, u32[]{:S(2)}, u32[]{:S(2)}) collective-permute-start(f32[8,32,256]{2,1,0:T(8,128)S(1)} %get-tuple-element.35), channel_id=1, source_target_pairs={{0,1},{1,2},{2,3},{3,0},{4,5},{5,6},{6,7},{7,4},{8,9},{9,10},{10,1... | collective-permute-start | bytes 786440 | tf_op jit(solution)/shard_map/ppermute | solution.py:472
  175.4 20.7 %collective-permute-start.19 = (f32[8,32,256]{2,1,0:T(8,128)S(1)}, f32[8,32,256]{2,1,0:T(8,128)S(1)}, u32[]{:S(2)}, u32[]{:S(2)}) collective-permute-start(f32[8,32,256]{2,1,0:T(8,128)S(1)} %get-tuple-element.38), channel_id=1, source_target_pairs={{0,1},{1,2},{2,3},{3,0},{4,5},{5,6},{6,7},{7,4},{8,9},{9,10},{10,1... | collective-permute-start | bytes 786440 | tf_op jit(solution)/shard_map/ppermute | solution.py:472
  176.9 34.3 %collective-permute-start.20 = (f32[8,32,256]{2,1,0:T(8,128)S(1)}, f32[8,32,256]{2,1,0:T(8,128)S(1)}, u32[]{:S(2)}, u32[]{:S(2)}) collective-permute-start(f32[8,32,256]{2,1,0:T(8,128)S(1)} %get-tuple-element.39), channel_id=1, source_target_pairs={{0,3},{1,0},{2,1},{3,2},{4,7},{5,4},{6,5},{7,6},{8,11},{9,8},{10,9... | collective-permute-start | bytes 786440 | tf_op jit(solution)/shard_map/ppermute | solution.py:472
  181.9 30.6 %collective-permute-start.21 = (f32[8,32,256]{2,1,0:T(8,128)S(1)}, f32[8,32,256]{2,1,0:T(8,128)S(1)}, u32[]{:S(2)}, u32[]{:S(2)}) collective-permute-start(f32[8,32,256]{2,1,0:T(8,128)S(1)} %get-tuple-element.40), channel_id=1, source_target_pairs={{0,2},{1,3},{2,0},{3,1},{4,6},{5,7},{6,4},{7,5},{8,10},{9,11},{10,... | collective-permute-start | bytes 786440 | tf_op jit(solution)/shard_map/ppermute | solution.py:472
  184.8 33.9 %copy-start.11 = (f32[32,1,64,256]{3,2,1,0:T(8,128)S(1)}, f32[32,1,64,256]{3,2,1,0:T(8,128)}, u32[]{:S(2)}) copy-start(f32[32,1,64,256]{3,2,1,0:T(8,128)} %param.7) | copy-start | bytes 6291460
  184.8 33.9 %copy-start.12 = (f32[32,1,64,256]{3,2,1,0:T(8,128)S(1)}, f32[32,1,64,256]{3,2,1,0:T(8,128)}, u32[]{:S(2)}) copy-start(f32[32,1,64,256]{3,2,1,0:T(8,128)} %param.8) | copy-start | bytes 6291460
  184.8 40.5 %collective-permute-start.17 = (f32[8,32,256]{2,1,0:T(8,128)}, f32[8,32,256]{2,1,0:T(8,128)}, u32[]{:S(2)}, u32[]{:S(2)}) collective-permute-start(f32[8,32,256]{2,1,0:T(8,128)} %get-tuple-element.36), channel_id=1, source_target_pairs={{0,3},{1,0},{2,1},{3,2},{4,7},{5,4},{6,5},{7,6},{8,11},{9,8},{10,9... | collective-permute-start | bytes 786440 | tf_op jit(solution)/shard_map/ppermute | solution.py:472
  194.7 17.9 %copy-start.14 = (f32[8,32,256]{2,1,0:T(8,128)}, f32[8,32,256]{2,1,0:T(8,128)S(1)}, u32[]{:S(2)}) copy-start(f32[8,32,256]{2,1,0:T(8,128)S(1)} %collective-permute-done.16.refs_1_) | copy-start | bytes 786436
  194.7 34.8 %collective-permute-start.18 = (f32[8,32,256]{2,1,0:T(8,128)}, f32[8,32,256]{2,1,0:T(8,128)S(1)}, u32[]{:S(2)}, u32[]{:S(2)}) collective-permute-start(f32[8,32,256]{2,1,0:T(8,128)} %get-tuple-element.37), channel_id=1, source_target_pairs={{0,2},{1,3},{2,0},{3,1},{4,6},{5,7},{6,4},{7,5},{8,10},{9,11},{10,... | collective-permute-start | bytes 786440 | tf_op jit(solution)/shard_map/ppermute | solution.py:472
  196.1 16.4 %copy-start.15 = (f32[8,32,256]{2,1,0:T(8,128)}, f32[8,32,256]{2,1,0:T(8,128)S(1)}, u32[]{:S(2)}) copy-start(f32[8,32,256]{2,1,0:T(8,128)S(1)} %collective-permute-done.19.refs_1_) | copy-start | bytes 786436
  196.1 36.6 %collective-permute-start.11 = (f32[8,32,256]{2,1,0:T(8,128)}, f32[8,32,256]{2,1,0:T(8,128)S(1)}, u32[]{:S(2)}, u32[]{:S(2)}) collective-permute-start(f32[8,32,256]{2,1,0:T(8,128)} %get-tuple-element.31), channel_id=1, source_target_pairs={{0,1},{1,2},{2,3},{3,0},{4,5},{5,6},{6,7},{7,4},{8,9},{9,10},{10,1... | collective-permute-start | bytes 786440 | tf_op jit(solution)/shard_map/ppermute | solution.py:472
  211.2 21.5 %collective-permute-start.12 = (f32[8,32,256]{2,1,0:T(8,128)}, f32[8,32,256]{2,1,0:T(8,128)S(1)}, u32[]{:S(2)}, u32[]{:S(2)}) collective-permute-start(f32[8,32,256]{2,1,0:T(8,128)} %get-tuple-element.32), channel_id=1, source_target_pairs={{0,3},{1,0},{2,1},{3,2},{4,7},{5,4},{6,5},{7,6},{8,11},{9,8},{10,9... | collective-permute-start | bytes 786440 | tf_op jit(solution)/shard_map/ppermute | solution.py:472
  212.5 30.8 %collective-permute-start.13 = (f32[8,32,256]{2,1,0:T(8,128)}, f32[8,32,256]{2,1,0:T(8,128)S(1)}, u32[]{:S(2)}, u32[]{:S(2)}) collective-permute-start(f32[8,32,256]{2,1,0:T(8,128)} %get-tuple-element.33), channel_id=1, source_target_pairs={{0,2},{1,3},{2,0},{3,1},{4,6},{5,7},{6,4},{7,5},{8,10},{9,11},{10,... | collective-permute-start | bytes 786440 | tf_op jit(solution)/shard_map/ppermute | solution.py:472
  (15 other events, 45.6 us)

commit v9 on v8

--- a/solution.py
+++ b/solution.py
@@ -477,10 +477,7 @@
     matrix = coupling_matrices(me, pattern, weights, shifts)
     halves = owners // 2
     groups, bodies, nears, mixed = [], [], [], []
-    if parts > 2:
-        members = [[0], list(range(1, parts - 1)), [parts - 1]]
-    else:
-        members = [[part] for part in range(parts)]
+    members = [[part] for part in range(parts)]
     group_of = {part: (index, group[0]) for index, group in enumerate(members) for part in group}
 
     def exchange_all(part, earlier):
@@ -504,14 +501,15 @@
     own = pack_own(me, state, adjoint, coef, owners, [packed])
     own_near = list(beside(own))
     halo(0, own_near)
-    for group in members[1:]:
-        if group[0] > 1:
-            exchange_all(group[0], [bodies[0]])
+    for part in range(1, parts):
+        earlier = [own] if part == 1 else [bodies[0]]
+        if 1 < part == parts - 1:
+            exchange_all(part, earlier)
         else:
-            exchange(group, [own])
+            exchange([part], earlier)
     for part in range(parts):
         if part:
-            halo(part, [mixed[part - 2][0]] if part > 1 else list(nears[0]))
+            halo(part, [mixed[part - 2][0]] if part > 1 else [])
         mixed.append(
             apply_operator(
                 me, coef, matrix, own, own_near, groups, group_of, nears[part], part, rows, shifts, part == 0

time: 249 us -> 241 us (0.968)
  starting transfers between devices: 87.5 us -> 72.5 us
  waiting for transfers between devices: 96.9 us -> 105 us
  local copies, waits for them, and re-layouts: 10.1 us -> 6.44 us
    ppermute x12 -> x15, starting transfers between devices: 38.1 us -> 23 us  [move(): lax.ppermute(array, 'mode', [(i, (i + shift) % owners) for i in range(own...]
    ppermute x5, waiting for transfers between devices: 6.64 us -> 17 us  [beside(): lax.ppermute(array, 'space', forward)]
    ppermute x12 -> x15, waiting for transfers between devices: 69.7 us -> 64.5 us  [move(): lax.ppermute(array, 'mode', [(i, (i + shift) % owners) for i in range(own...]
    unnamed x44 -> x40, local copies, waits for them, and re-layouts: 7.75 us -> 4.06 us
    ppermute x5, waiting for transfers between devices: 1.04 us -> 4.22 us  [beside(): lax.ppermute(array, 'space', backward)]
  transfers between devices with their start and end apart: 25 -> 28, of which waited for: 10 -> 13; matrix products, arithmetic and copies ran while one was open for 2% -> 2% of each run, Pallas kernels for 17% -> 18%
where the time goes in v9:
time: 241 us; the launch traced here: 238 us
  waiting for transfers between devices  105 us (44%)
  starting transfers between devices  72.5 us (30%)
  Pallas kernels  51 us (21%)
  local copies, waits for them, and re-layouts  6.44 us (3%)
    ppermute x15, waiting for transfers between devices, move(): lax.ppermute(array, 'mode', [(i, (i + shift) % owners) for i in range(own...  64.5 us
    pallas_call x4, Pallas kernels, apply_operator(): pl.pallas_call(functools.partial(operator_kernel, shifts, terms, part, pa...  27.7 us
    ppermute x5, starting transfers between devices, beside(): lax.ppermute(array, 'space', backward)  25.4 us
    ppermute x15, starting transfers between devices, move(): lax.ppermute(array, 'mode', [(i, (i + shift) % owners) for i in range(own...  23 us
    all_to_all x2, waiting for transfers between devices, exchange_all(): arrived = lax.all_to_all(packed, 'mode', 0, 0, tiled=True)  19.6 us
    ppermute x5, waiting for transfers between devices, beside(): lax.ppermute(array, 'space', forward)  17 us
    all_to_all x2, starting transfers between devices, exchange_all(): arrived = lax.all_to_all(packed, 'mode', 0, 0, tiled=True)  9.99 us
    pallas_call x4, Pallas kernels, finish(): pl.pallas_call(functools.partial(finish_kernel, shifts, by_owner), grid=(...  9.97 us
  transfers between devices with their start and end apart: 28, of which 13 were waited for; matrix products, arithmetic and copies ran while one was open for 2% of the time, Pallas kernels for 18%

profile of v9, /device:TPU:4, one launch (start us, length us, event | category | flops | bytes accessed | tf_op | source)
XLA Modules:
  0.0 238.0 jit_solution(16134393577811931083)
XLA Ops:
  0.6 2.6 %pack_all.2.refs_0_ = f32[4,9,32,256]{3,2,1,0:T(8,128)} custom-call(f32[32,64,256]{2,1,0:T(8,128)} %bitcast.32, f32[32,64,256]{2,1,0:T(8,128)} %bitcast.41), custom_call_target="tpu_custom_call" | custom-call | bytes 10500000 | tf_op jit(solution)/shard_map/pack_all/pallas_call | solution.py:182
  3.3 4.9 %all-to-all-start = ((f32[4,9,32,256]{3,2,1,0:T(8,128)}), f32[4,9,32,256]{3,2,1,0:T(8,128)}, u32[]{:S(2)}, u32[]{:S(2)}) async-start(f32[4,9,32,256]{3,2,1,0:T(8,128)} %pack_all.2.refs_0_), calls=%async_computation | async-start | bytes 2359296 | tf_op jit(solution)/shard_map/all_to_all | solution.py:485
  8.1 2.6 %pack_own.1.refs_0_.refs_7_.refs_11_.refs_15_ = f32[40,32,256]{2,1,0:T(8,128)} custom-call(s32[1]{0:T(128)} %bitcast.me_ref, f32[32,64,256]{2,1,0:T(8,128)} %bitcast.33, f32[32,64,256]{2,1,0:T(8,128)} %bitcast.42, f32[7,64,256]{2,1,0:T(8,128)} %bitcast.25, f32[4,9,32,256]{3,2,1,0:T(8,128)} %pack_all.2.refs_0_), custom_call_target="tpu_custom_call" | custom-call | bytes 10500000 | tf_op jit(solution)/shard_map/pack_own/pallas_call | solution.py:226
  12.6 4.5 %collective-permute-start.1 = (f32[40,32,256]{2,1,0:T(8,128)}, f32[40,32,256]{2,1,0:T(8,128)S(1)}, u32[]{:S(2)}, u32[]{:S(2)}) collective-permute-start(f32[40,32,256]{2,1,0:T(8,128)} %pack_own.1.refs_0_.refs_7_.refs_11_.refs_15_), channel_id=1, source_target_pairs={{4,0},{8,4},{12,8},{16,12},{20,16},{24,20},{28,24},{5,1},{9,5},{13... | collective-permute-start | bytes 3932168 | tf_op jit(solution)/shard_map/ppermute | solution.py:475
  17.2 19.6 %all-to-all-done = f32[4,9,32,256]{3,2,1,0:T(8,128)} async-done(((f32[4,9,32,256]{3,2,1,0:T(8,128)}), f32[4,9,32,256]{3,2,1,0:T(8,128)}, u32[]{:S(2)}, u32[]{:S(2)}) %all-to-all-start) | async-done | bytes 1179680 | tf_op jit(solution)/shard_map/all_to_all | solution.py:485
  38.0 4.0 %collective-permute-done.refs_3_.refs_1_ = f32[40,32,256]{2,1,0:T(8,128)S(1)} collective-permute-done((f32[40,32,256]{2,1,0:T(8,128)}, f32[40,32,256]{2,1,0:T(8,128)S(1)}, u32[]{:S(2)}, u32[]{:S(2)}) %collective-permute-start) | collective-permute-done | bytes 1310752 | tf_op jit(solution)/shard_map/ppermute | solution.py:475
  47.2 5.1 %all-to-all-start.1 = ((f32[4,8,32,256]{3,2,1,0:T(8,128)}), f32[4,8,32,256]{3,2,1,0:T(8,128)}, u32[]{:S(2)}, u32[]{:S(2)}) async-start(f32[4,8,32,256]{3,2,1,0:T(8,128)} %pack_all.3), calls=%async_computation.1 | async-start | bytes 2097152 | tf_op jit(solution)/shard_map/all_to_all | solution.py:485
  61.4 4.5 %collective-permute-start.16 = (f32[24,32,256]{2,1,0:T(8,128)S(1)}, f32[24,32,256]{2,1,0:T(8,128)}, u32[]{:S(2)}, u32[]{:S(2)}) collective-permute-start(f32[24,32,256]{2,1,0:T(8,128)S(1)} %copy-done.4), channel_id=1, source_target_pairs={{4,0},{8,4},{12,8},{16,12},{20,16},{24,20},{28,24},{5,1},{9,5},{13... | collective-permute-start | bytes 2359304 | tf_op jit(solution)/shard_map/ppermute | solution.py:475
  65.9 14.5 %collective-permute-done.2.refs_0_.refs_8_.refs_16_.refs_12_ = f32[8,32,256]{2,1,0:T(8,128)S(1)} collective-permute-done((f32[8,32,256]{2,1,0:T(8,128)}, f32[8,32,256]{2,1,0:T(8,128)S(1)}, u32[]{:S(2)}, u32[]{:S(2)}) %collective-permute-start.2) | collective-permute-done | bytes 262176 | tf_op jit(solution)/shard_map/ppermute | solution.py:472
  80.5 17.0 %collective-permute-done.4.refs_2_.refs_10_.refs_18_.refs_14_ = f32[8,32,256]{2,1,0:T(8,128)S(1)} collective-permute-done((f32[8,32,256]{2,1,0:T(8,128)}, f32[8,32,256]{2,1,0:T(8,128)S(1)}, u32[]{:S(2)}, u32[]{:S(2)}) %collective-permute-start.4) | collective-permute-done | bytes 262176 | tf_op jit(solution)/shard_map/ppermute | solution.py:472
  100.5 7.2 %collective-permute-start.6 = (f32[24,32,256]{2,1,0:T(8,128)}, f32[24,32,256]{2,1,0:T(8,128)}, u32[]{:S(2)}, u32[]{:S(2)}) collective-permute-start(f32[24,32,256]{2,1,0:T(8,128)} %gather.5), channel_id=1, source_target_pairs={{4,0},{8,4},{12,8},{16,12},{20,16},{24,20},{28,24},{5,1},{9,5},{13... | collective-permute-start | bytes 2359304 | tf_op jit(solution)/shard_map/ppermute | solution.py:475
  109.9 3.8 %collective-permute-start.8 = (f32[8,32,256]{2,1,0:T(8,128)}, f32[8,32,256]{2,1,0:T(8,128)S(1)}, u32[]{:S(2)}, u32[]{:S(2)}) collective-permute-start(f32[8,32,256]{2,1,0:T(8,128)} %get-tuple-element.33), channel_id=1, source_target_pairs={{0,3},{1,0},{2,1},{3,2},{4,7},{5,4},{6,5},{7,6},{8,11},{9,8},{10,9... | collective-permute-start | bytes 786440 | tf_op jit(solution)/shard_map/ppermute | solution.py:472
  114.3 7.6 %operator.6.refs_3_ = f32[4,8,32,256]{3,2,1,0:T(8,128)} custom-call(s32[1]{0:T(128)} %bitcast.me_ref, f32[7,64,256]{2,1,0:T(8,128)S(1)} %bitcast.26, bf16[256,896]{1,0:T(8,128)(2,1)S(1)} %coupling.1.matrix_ref, f32[40,32,256]{2,1,0:T(8,128)} %pack_own.1.refs_0_.refs_7_.refs_11_.refs_15_, f32[40,32,256]{2,1,0:T(8,128)} %copy-done, f32[40,32,256]{2,1,0:T(8,128)} %copy-done.1, ...), custom_call_target="tpu_custom_call" | custom-call | bytes 21000000 | tf_op jit(solution)/shard_map/operator/pallas_call | solution.py:384
  121.9 4.4 %all-to-all-start.2 = ((f32[4,8,32,256]{3,2,1,0:T(8,128)}), f32[4,8,32,256]{3,2,1,0:T(8,128)}, u32[]{:S(2)}, u32[]{:S(2)}) async-start(f32[4,8,32,256]{3,2,1,0:T(8,128)} %operator.6.refs_3_), calls=%async_computation.2 | async-start | bytes 2097152 | tf_op jit(solution)/shard_map/all_to_all | solution.py:522
  126.4 18.2 %collective-permute-done.9.refs_18_.refs_14_.refs_2_.refs_10_ = f32[8,32,256]{2,1,0:T(8,128)S(1)} collective-permute-done((f32[8,32,256]{2,1,0:T(8,128)}, f32[8,32,256]{2,1,0:T(8,128)S(1)}, u32[]{:S(2)}, u32[]{:S(2)}) %collective-permute-start.9) | collective-permute-done | bytes 262176 | tf_op jit(solution)/shard_map/ppermute | solution.py:472
  144.7 6.8 %operator.4 = (f32[8,32,256]{2,1,0:T(8,128)S(1)}, f32[8,32,256]{2,1,0:T(8,128)S(1)}, f32[8,32,256]{2,1,0:T(8,128)S(1)}, f32[8,32,256]{2,1,0:T(8,128)S(1)}) custom-call(s32[1]{0:T(128)} %bitcast.me_ref, f32[7,64,256]{2,1,0:T(8,128)S(1)} %bitcast.27, bf16[256,896]{1,0:T(8,128)(2,1)S(1)} %coupling.1.matrix_ref, ...), custom_call_target="tpu_custom_call" | custom-call | bytes 21000000 | tf_op jit(solution)/shard_map/operator/pallas_call | solution.py:384
  153.4 4.5 %collective-permute-start.18 = (f32[24,32,256]{2,1,0:T(8,128)S(1)}, f32[24,32,256]{2,1,0:T(8,128)S(1)}, u32[]{:S(2)}, u32[]{:S(2)}) collective-permute-start(f32[24,32,256]{2,1,0:T(8,128)S(1)} %gather.7), channel_id=1, source_target_pairs={{4,0},{8,4},{12,8},{16,12},{20,16},{24,20},{28,24},{5,1},{9,5},{13... | collective-permute-start | bytes 2359304 | tf_op jit(solution)/shard_map/ppermute | solution.py:475
  161.2 4.5 %collective-permute-start.11 = (f32[24,32,256]{2,1,0:T(8,128)S(1)}, f32[24,32,256]{2,1,0:T(8,128)S(1)}, u32[]{:S(2)}, u32[]{:S(2)}) collective-permute-start(f32[24,32,256]{2,1,0:T(8,128)S(1)} %gather.6), channel_id=1, source_target_pairs={{4,0},{8,4},{12,8},{16,12},{20,16},{24,20},{28,24},{5,1},{9,5},{13... | collective-permute-start | bytes 2359304 | tf_op jit(solution)/shard_map/ppermute | solution.py:475
  165.8 6.5 %collective-permute-done.17.refs_5_ = f32[24,32,256]{2,1,0:T(8,128)S(1)} collective-permute-done((f32[24,32,256]{2,1,0:T(8,128)S(1)}, f32[24,32,256]{2,1,0:T(8,128)S(1)}, u32[]{:S(2)}, u32[]{:S(2)}) %collective-permute-start.17) | collective-permute-done | bytes 786464 | tf_op jit(solution)/shard_map/ppermute | solution.py:475
  172.4 3.2 %collective-permute-done.18.refs_6_ = f32[24,32,256]{2,1,0:T(8,128)S(1)} collective-permute-done((f32[24,32,256]{2,1,0:T(8,128)S(1)}, f32[24,32,256]{2,1,0:T(8,128)S(1)}, u32[]{:S(2)}, u32[]{:S(2)}) %collective-permute-start.18) | collective-permute-done | bytes 786464 | tf_op jit(solution)/shard_map/ppermute | solution.py:475
  175.6 7.0 %operator.7 = (f32[8,32,256]{2,1,0:T(8,128)S(1)}, f32[8,32,256]{2,1,0:T(8,128)S(1)}, f32[8,32,256]{2,1,0:T(8,128)}, f32[8,32,256]{2,1,0:T(8,128)}) custom-call(s32[1]{0:T(128)} %bitcast.me_ref, f32[7,64,256]{2,1,0:T(8,128)S(1)} %bitcast.28, bf16[256,896]{1,0:T(8,128)(2,1)S(1)} %coupling.1.matrix_ref, ...), custom_call_target="tpu_custom_call" | custom-call | bytes 21000000 | tf_op jit(solution)/shard_map/operator/pallas_call | solution.py:384
  182.6 6.5 %collective-permute-done.10.refs_5_ = f32[24,32,256]{2,1,0:T(8,128)S(1)} collective-permute-done((f32[24,32,256]{2,1,0:T(8,128)S(1)}, f32[24,32,256]{2,1,0:T(8,128)S(1)}, u32[]{:S(2)}, u32[]{:S(2)}) %collective-permute-start.10) | collective-permute-done | bytes 786464 | tf_op jit(solution)/shard_map/ppermute | solution.py:475
  189.2 3.8 %collective-permute-start.20 = (f32[8,32,256]{2,1,0:T(8,128)}, f32[8,32,256]{2,1,0:T(8,128)}, u32[]{:S(2)}, u32[]{:S(2)}) collective-permute-start(f32[8,32,256]{2,1,0:T(8,128)} %get-tuple-element.42), channel_id=1, source_target_pairs={{0,3},{1,0},{2,1},{3,2},{4,7},{5,4},{6,5},{7,6},{8,11},{9,8},{10,9... | collective-permute-start | bytes 786440 | tf_op jit(solution)/shard_map/ppermute | solution.py:472
  193.0 6.3 %operator.5 = (f32[8,32,256]{2,1,0:T(8,128)S(1)}, f32[8,32,256]{2,1,0:T(8,128)S(1)}, f32[8,32,256]{2,1,0:T(8,128)S(1)}, f32[8,32,256]{2,1,0:T(8,128)S(1)}) custom-call(s32[1]{0:T(128)} %bitcast.me_ref, f32[7,64,256]{2,1,0:T(8,128)S(1)} %bitcast.29, bf16[256,896]{1,0:T(8,128)(2,1)S(1)} %coupling.1.matrix_ref, ...), custom_call_target="tpu_custom_call" | custom-call | bytes 21000000 | tf_op jit(solution)/shard_map/operator/pallas_call | solution.py:384
  200.7 2.9 %collective-permute-done.24.refs_3_ = f32[8,32,256]{2,1,0:T(8,128)S(1)} collective-permute-done((f32[8,32,256]{2,1,0:T(8,128)S(1)}, f32[8,32,256]{2,1,0:T(8,128)S(1)}, u32[]{:S(2)}, u32[]{:S(2)}) %collective-permute-start.24) | collective-permute-done | bytes 262176 | tf_op jit(solution)/shard_map/ppermute | solution.py:472
  203.9 9.2 %collective-permute-start.14 = (f32[8,32,256]{2,1,0:T(8,128)S(1)}, f32[8,32,256]{2,1,0:T(8,128)S(1)}, u32[]{:S(2)}, u32[]{:S(2)}) collective-permute-start(f32[8,32,256]{2,1,0:T(8,128)S(1)} %get-tuple-element.39), channel_id=1, source_target_pairs={{0,2},{1,3},{2,0},{3,1},{4,6},{5,7},{6,4},{7,5},{8,10},{9,11},{10,... | collective-permute-start | bytes 786440 | tf_op jit(solution)/shard_map/ppermute | solution.py:472
  214.8 2.4 %finish.4 = (f32[32,64,256]{2,1,0:T(8,128)}, f32[32,64,256]{2,1,0:T(8,128)}) custom-call(s32[1]{0:T(128)} %bitcast.me_ref, f32[4,8,32,256]{3,2,1,0:T(8,128)} %all-to-all-done.2.refs_0_.refs_1_, f32[4,8,32,256]{3,2,1,0:T(8,128)} %all-to-all-done.2.refs_0_.refs_1_, f32[32,64,256]{2,1,0:T(8,128)} %bitcast.37, f32[32,64,256]{2,1,0:T(8,128)} %bitcast.46), custom_call_target="tpu_custom_call" | custom-call | bytes 8750000 | tf_op jit(solution)/shard_map/finish/pallas_call | solution.py:443
  217.2 2.5 %finish.5 = (f32[32,64,256]{2,1,0:T(8,128)}, f32[32,64,256]{2,1,0:T(8,128)}) custom-call(s32[1]{0:T(128)} %bitcast.me_ref, f32[8,32,256]{2,1,0:T(8,128)} %copy-done.5, f32[8,32,256]{2,1,0:T(8,128)} %copy-done.12, f32[8,32,256]{2,1,0:T(8,128)} %copy-done.13, f32[8,32,256]{2,1,0:T(8,128)} %copy-done.14, ...), custom_call_target="tpu_custom_call", output_to_operand_aliasing={{0}: (7, {}), {1}: (8, {})} | custom-call | bytes 8750000 | tf_op jit(solution)/shard_map/finish/pallas_call | solution.py:443
  219.8 6.3 %collective-permute-done.21.refs_3_ = f32[8,32,256]{2,1,0:T(8,128)S(1)} collective-permute-done((f32[8,32,256]{2,1,0:T(8,128)}, f32[8,32,256]{2,1,0:T(8,128)S(1)}, u32[]{:S(2)}, u32[]{:S(2)}) %collective-permute-start.21) | collective-permute-done | bytes 262176 | tf_op jit(solution)/shard_map/ppermute | solution.py:472
  226.8 2.5 %finish.6 = (f32[32,64,256]{2,1,0:T(8,128)}, f32[32,64,256]{2,1,0:T(8,128)}) custom-call(s32[1]{0:T(128)} %bitcast.me_ref, f32[8,32,256]{2,1,0:T(8,128)} %copy-done.6, f32[8,32,256]{2,1,0:T(8,128)} %copy-done.15, f32[8,32,256]{2,1,0:T(8,128)} %collective-permute-done.20.refs_2_, ...), custom_call_target="tpu_custom_call", output_to_operand_aliasing={{0}: (7, {}), {1}: (8, {})} | custom-call | bytes 8750000 | tf_op jit(solution)/shard_map/finish/pallas_call | solution.py:443
  229.3 5.4 %collective-permute-done.14.refs_3_ = f32[8,32,256]{2,1,0:T(8,128)S(1)} collective-permute-done((f32[8,32,256]{2,1,0:T(8,128)S(1)}, f32[8,32,256]{2,1,0:T(8,128)S(1)}, u32[]{:S(2)}, u32[]{:S(2)}) %collective-permute-start.14) | collective-permute-done | bytes 262176 | tf_op jit(solution)/shard_map/ppermute | solution.py:472
  235.5 2.5 %finish.7 = (f32[32,64,256]{2,1,0:T(8,128)}, f32[32,64,256]{2,1,0:T(8,128)}) custom-call(s32[1]{0:T(128)} %bitcast.me_ref, f32[8,32,256]{2,1,0:T(8,128)} %copy-done.7, f32[8,32,256]{2,1,0:T(8,128)} %copy-done.16, f32[8,32,256]{2,1,0:T(8,128)} %copy-done.17, f32[8,32,256]{2,1,0:T(8,128)} %copy-done.19, ...), custom_call_target="tpu_custom_call", output_to_operand_aliasing={{0}: (7, {}), {1}: (8, {})} | custom-call | bytes 8750000 | tf_op jit(solution)/shard_map/finish/pallas_call | solution.py:443
  (85 shorter events, 33.3 us)
Async XLA Ops:
  3.3 33.5 %all-to-all-start = ((f32[4,9,32,256]{3,2,1,0:T(8,128)}), f32[4,9,32,256]{3,2,1,0:T(8,128)}, u32[]{:S(2)}, u32[]{:S(2)}) async-start(f32[4,9,32,256]{3,2,1,0:T(8,128)} %pack_all.2.refs_0_), calls=%async_computation | async-start | bytes 2359296 | tf_op jit(solution)/shard_map/all_to_all | solution.py:485
  10.7 31.3 %collective-permute-start = (f32[40,32,256]{2,1,0:T(8,128)}, f32[40,32,256]{2,1,0:T(8,128)S(1)}, u32[]{:S(2)}, u32[]{:S(2)}) collective-permute-start(f32[40,32,256]{2,1,0:T(8,128)} %pack_own.1.refs_0_.refs_7_.refs_11_.refs_15_), channel_id=1, source_target_pairs={{0,4},{4,8},{8,12},{12,16},{16,20},{20,24},{24,28},{1,5},{5,9},{9,... | collective-permute-start | bytes 3932168 | tf_op jit(solution)/shard_map/ppermute | solution.py:475
  12.6 30.4 %collective-permute-start.1 = (f32[40,32,256]{2,1,0:T(8,128)}, f32[40,32,256]{2,1,0:T(8,128)S(1)}, u32[]{:S(2)}, u32[]{:S(2)}) collective-permute-start(f32[40,32,256]{2,1,0:T(8,128)} %pack_own.1.refs_0_.refs_7_.refs_11_.refs_15_), channel_id=1, source_target_pairs={{4,0},{8,4},{12,8},{16,12},{20,16},{24,20},{28,24},{5,1},{9,5},{13... | collective-permute-start | bytes 3932168 | tf_op jit(solution)/shard_map/ppermute | solution.py:475
  47.2 74.7 %all-to-all-start.1 = ((f32[4,8,32,256]{3,2,1,0:T(8,128)}), f32[4,8,32,256]{3,2,1,0:T(8,128)}, u32[]{:S(2)}, u32[]{:S(2)}) async-start(f32[4,8,32,256]{3,2,1,0:T(8,128)} %pack_all.3), calls=%async_computation.1 | async-start | bytes 2097152 | tf_op jit(solution)/shard_map/all_to_all | solution.py:485
  54.5 26.0 %collective-permute-start.2 = (f32[8,32,256]{2,1,0:T(8,128)}, f32[8,32,256]{2,1,0:T(8,128)S(1)}, u32[]{:S(2)}, u32[]{:S(2)}) collective-permute-start(f32[8,32,256]{2,1,0:T(8,128)} %get-tuple-element.29), channel_id=1, source_target_pairs={{0,1},{1,2},{2,3},{3,0},{4,5},{5,6},{6,7},{7,4},{8,9},{9,10},{10,1... | collective-permute-start | bytes 786440 | tf_op jit(solution)/shard_map/ppermute | solution.py:472
  56.5 24.0 %collective-permute-start.3 = (f32[8,32,256]{2,1,0:T(8,128)}, f32[8,32,256]{2,1,0:T(8,128)S(1)}, u32[]{:S(2)}, u32[]{:S(2)}) collective-permute-start(f32[8,32,256]{2,1,0:T(8,128)} %get-tuple-element.30), channel_id=1, source_target_pairs={{0,3},{1,0},{2,1},{3,2},{4,7},{5,4},{6,5},{7,6},{8,11},{9,8},{10,9... | collective-permute-start | bytes 786440 | tf_op jit(solution)/shard_map/ppermute | solution.py:472
  58.4 39.1 %collective-permute-start.4 = (f32[8,32,256]{2,1,0:T(8,128)}, f32[8,32,256]{2,1,0:T(8,128)S(1)}, u32[]{:S(2)}, u32[]{:S(2)}) collective-permute-start(f32[8,32,256]{2,1,0:T(8,128)} %get-tuple-element.31), channel_id=1, source_target_pairs={{0,2},{1,3},{2,0},{3,1},{4,6},{5,7},{6,4},{7,5},{8,10},{9,11},{10,... | collective-permute-start | bytes 786440 | tf_op jit(solution)/shard_map/ppermute | solution.py:472
  59.5 50.5 %collective-permute-start.15 = (f32[24,32,256]{2,1,0:T(8,128)S(1)}, f32[24,32,256]{2,1,0:T(8,128)}, u32[]{:S(2)}, u32[]{:S(2)}) collective-permute-start(f32[24,32,256]{2,1,0:T(8,128)S(1)} %copy-done.4), channel_id=1, source_target_pairs={{0,4},{4,8},{8,12},{12,16},{16,20},{20,24},{24,28},{1,5},{5,9},{9,... | collective-permute-start | bytes 2359304 | tf_op jit(solution)/shard_map/ppermute | solution.py:475
  61.4 52.4 %collective-permute-start.16 = (f32[24,32,256]{2,1,0:T(8,128)S(1)}, f32[24,32,256]{2,1,0:T(8,128)}, u32[]{:S(2)}, u32[]{:S(2)}) collective-permute-start(f32[24,32,256]{2,1,0:T(8,128)S(1)} %copy-done.4), channel_id=1, source_target_pairs={{4,0},{8,4},{12,8},{16,12},{20,16},{24,20},{28,24},{5,1},{9,5},{13... | collective-permute-start | bytes 2359304 | tf_op jit(solution)/shard_map/ppermute | solution.py:475
  98.5 15.8 %copy-start.2 = (f32[7,1,64,256]{3,2,1,0:T(8,128)S(1)}, f32[7,1,64,256]{3,2,1,0:T(8,128)}, u32[]{:S(2)}) copy-start(f32[7,1,64,256]{3,2,1,0:T(8,128)} %param.9) | copy-start | bytes 1376260
  98.5 27.9 %collective-permute-start.5 = (f32[24,32,256]{2,1,0:T(8,128)}, f32[24,32,256]{2,1,0:T(8,128)}, u32[]{:S(2)}, u32[]{:S(2)}) collective-permute-start(f32[24,32,256]{2,1,0:T(8,128)} %gather.5), channel_id=1, source_target_pairs={{0,4},{4,8},{8,12},{12,16},{16,20},{20,24},{24,28},{1,5},{5,9},{9,... | collective-permute-start | bytes 2359304 | tf_op jit(solution)/shard_map/ppermute | solution.py:475
  100.5 25.9 %collective-permute-start.6 = (f32[24,32,256]{2,1,0:T(8,128)}, f32[24,32,256]{2,1,0:T(8,128)}, u32[]{:S(2)}, u32[]{:S(2)}) collective-permute-start(f32[24,32,256]{2,1,0:T(8,128)} %gather.5), channel_id=1, source_target_pairs={{4,0},{8,4},{12,8},{16,12},{20,16},{24,20},{28,24},{5,1},{9,5},{13... | collective-permute-start | bytes 2359304 | tf_op jit(solution)/shard_map/ppermute | solution.py:475
  109.9 16.5 %collective-permute-start.7 = (f32[8,32,256]{2,1,0:T(8,128)}, f32[8,32,256]{2,1,0:T(8,128)S(1)}, u32[]{:S(2)}, u32[]{:S(2)}) collective-permute-start(f32[8,32,256]{2,1,0:T(8,128)} %get-tuple-element.32), channel_id=1, source_target_pairs={{0,1},{1,2},{2,3},{3,0},{4,5},{5,6},{6,7},{7,4},{8,9},{9,10},{10,1... | collective-permute-start | bytes 786440 | tf_op jit(solution)/shard_map/ppermute | solution.py:472
  109.9 16.5 %collective-permute-start.8 = (f32[8,32,256]{2,1,0:T(8,128)}, f32[8,32,256]{2,1,0:T(8,128)S(1)}, u32[]{:S(2)}, u32[]{:S(2)}) collective-permute-start(f32[8,32,256]{2,1,0:T(8,128)} %get-tuple-element.33), channel_id=1, source_target_pairs={{0,3},{1,0},{2,1},{3,2},{4,7},{5,4},{6,5},{7,6},{8,11},{9,8},{10,9... | collective-permute-start | bytes 786440 | tf_op jit(solution)/shard_map/ppermute | solution.py:472
  113.7 30.9 %collective-permute-start.9 = (f32[8,32,256]{2,1,0:T(8,128)}, f32[8,32,256]{2,1,0:T(8,128)S(1)}, u32[]{:S(2)}, u32[]{:S(2)}) collective-permute-start(f32[8,32,256]{2,1,0:T(8,128)} %get-tuple-element.34), channel_id=1, source_target_pairs={{0,2},{1,3},{2,0},{3,1},{4,6},{5,7},{6,4},{7,5},{8,10},{9,11},{10,... | collective-permute-start | bytes 786440 | tf_op jit(solution)/shard_map/ppermute | solution.py:472
  121.9 92.9 %all-to-all-start.2 = ((f32[4,8,32,256]{3,2,1,0:T(8,128)}), f32[4,8,32,256]{3,2,1,0:T(8,128)}, u32[]{:S(2)}, u32[]{:S(2)}) async-start(f32[4,8,32,256]{3,2,1,0:T(8,128)} %operator.6.refs_3_), calls=%async_computation.2 | async-start | bytes 2097152 | tf_op jit(solution)/shard_map/all_to_all | solution.py:522
  151.5 20.8 %collective-permute-start.17 = (f32[24,32,256]{2,1,0:T(8,128)S(1)}, f32[24,32,256]{2,1,0:T(8,128)S(1)}, u32[]{:S(2)}, u32[]{:S(2)}) collective-permute-start(f32[24,32,256]{2,1,0:T(8,128)S(1)} %gather.7), channel_id=1, source_target_pairs={{0,4},{4,8},{8,12},{12,16},{16,20},{20,24},{24,28},{1,5},{5,9},{9,... | collective-permute-start | bytes 2359304 | tf_op jit(solution)/shard_map/ppermute | solution.py:475
  153.4 22.2 %collective-permute-start.18 = (f32[24,32,256]{2,1,0:T(8,128)S(1)}, f32[24,32,256]{2,1,0:T(8,128)S(1)}, u32[]{:S(2)}, u32[]{:S(2)}) collective-permute-start(f32[24,32,256]{2,1,0:T(8,128)S(1)} %gather.7), channel_id=1, source_target_pairs={{4,0},{8,4},{12,8},{16,12},{20,16},{24,20},{28,24},{5,1},{9,5},{13... | collective-permute-start | bytes 2359304 | tf_op jit(solution)/shard_map/ppermute | solution.py:475
  159.2 29.9 %collective-permute-start.10 = (f32[24,32,256]{2,1,0:T(8,128)S(1)}, f32[24,32,256]{2,1,0:T(8,128)S(1)}, u32[]{:S(2)}, u32[]{:S(2)}) collective-permute-start(f32[24,32,256]{2,1,0:T(8,128)S(1)} %gather.6), channel_id=1, source_target_pairs={{0,4},{4,8},{8,12},{12,16},{16,20},{20,24},{24,28},{1,5},{5,9},{9,... | collective-permute-start | bytes 2359304 | tf_op jit(solution)/shard_map/ppermute | solution.py:475
  161.2 28.0 %collective-permute-start.11 = (f32[24,32,256]{2,1,0:T(8,128)S(1)}, f32[24,32,256]{2,1,0:T(8,128)S(1)}, u32[]{:S(2)}, u32[]{:S(2)}) collective-permute-start(f32[24,32,256]{2,1,0:T(8,128)S(1)} %gather.6), channel_id=1, source_target_pairs={{4,0},{8,4},{12,8},{16,12},{20,16},{24,20},{28,24},{5,1},{9,5},{13... | collective-permute-start | bytes 2359304 | tf_op jit(solution)/shard_map/ppermute | solution.py:475
  165.7 34.3 %collective-permute-start.22 = (f32[8,32,256]{2,1,0:T(8,128)S(1)}, f32[8,32,256]{2,1,0:T(8,128)S(1)}, u32[]{:S(2)}, u32[]{:S(2)}) collective-permute-start(f32[8,32,256]{2,1,0:T(8,128)S(1)} %get-tuple-element.44), channel_id=1, source_target_pairs={{0,1},{1,2},{2,3},{3,0},{4,5},{5,6},{6,7},{7,4},{8,9},{9,10},{10,1... | collective-permute-start | bytes 786440 | tf_op jit(solution)/shard_map/ppermute | solution.py:472
  172.3 27.7 %collective-permute-start.23 = (f32[8,32,256]{2,1,0:T(8,128)S(1)}, f32[8,32,256]{2,1,0:T(8,128)S(1)}, u32[]{:S(2)}, u32[]{:S(2)}) collective-permute-start(f32[8,32,256]{2,1,0:T(8,128)S(1)} %get-tuple-element.45), channel_id=1, source_target_pairs={{0,3},{1,0},{2,1},{3,2},{4,7},{5,4},{6,5},{7,6},{8,11},{9,8},{10,9... | collective-permute-start | bytes 786440 | tf_op jit(solution)/shard_map/ppermute | solution.py:472
  175.6 28.0 %collective-permute-start.24 = (f32[8,32,256]{2,1,0:T(8,128)S(1)}, f32[8,32,256]{2,1,0:T(8,128)S(1)}, u32[]{:S(2)}, u32[]{:S(2)}) collective-permute-start(f32[8,32,256]{2,1,0:T(8,128)S(1)} %get-tuple-element.46), channel_id=1, source_target_pairs={{0,2},{1,3},{2,0},{3,1},{4,6},{5,7},{6,4},{7,5},{8,10},{9,11},{10,... | collective-permute-start | bytes 786440 | tf_op jit(solution)/shard_map/ppermute | solution.py:472
  182.6 16.6 %copy-start.6 = (f32[8,32,256]{2,1,0:T(8,128)}, f32[8,32,256]{2,1,0:T(8,128)S(1)}, u32[]{:S(2)}) copy-start(f32[8,32,256]{2,1,0:T(8,128)S(1)} %get-tuple-element.40.refs_0_) | copy-start | bytes 786436
  189.1 14.7 %collective-permute-start.19 = (f32[8,32,256]{2,1,0:T(8,128)S(1)}, f32[8,32,256]{2,1,0:T(8,128)S(1)}, u32[]{:S(2)}, u32[]{:S(2)}) collective-permute-start(f32[8,32,256]{2,1,0:T(8,128)S(1)} %get-tuple-element.41), channel_id=1, source_target_pairs={{0,1},{1,2},{2,3},{3,0},{4,5},{5,6},{6,7},{7,4},{8,9},{9,10},{10,1... | collective-permute-start | bytes 786440 | tf_op jit(solution)/shard_map/ppermute | solution.py:472
  189.2 23.9 %copy-start.10 = (f32[32,1,64,256]{3,2,1,0:T(8,128)S(1)}, f32[32,1,64,256]{3,2,1,0:T(8,128)}, u32[]{:S(2)}) copy-start(f32[32,1,64,256]{3,2,1,0:T(8,128)} %param.8) | copy-start | bytes 6291460
  189.2 23.9 %copy-start.11 = (f32[32,1,64,256]{3,2,1,0:T(8,128)S(1)}, f32[32,1,64,256]{3,2,1,0:T(8,128)}, u32[]{:S(2)}) copy-start(f32[32,1,64,256]{3,2,1,0:T(8,128)} %param.7) | copy-start | bytes 6291460
  189.2 30.6 %collective-permute-start.20 = (f32[8,32,256]{2,1,0:T(8,128)}, f32[8,32,256]{2,1,0:T(8,128)}, u32[]{:S(2)}, u32[]{:S(2)}) collective-permute-start(f32[8,32,256]{2,1,0:T(8,128)} %get-tuple-element.42), channel_id=1, source_target_pairs={{0,3},{1,0},{2,1},{3,2},{4,7},{5,4},{6,5},{7,6},{8,11},{9,8},{10,9... | collective-permute-start | bytes 786440 | tf_op jit(solution)/shard_map/ppermute | solution.py:472
  200.0 26.1 %collective-permute-start.21 = (f32[8,32,256]{2,1,0:T(8,128)}, f32[8,32,256]{2,1,0:T(8,128)S(1)}, u32[]{:S(2)}, u32[]{:S(2)}) collective-permute-start(f32[8,32,256]{2,1,0:T(8,128)} %get-tuple-element.43), channel_id=1, source_target_pairs={{0,2},{1,3},{2,0},{3,1},{4,6},{5,7},{6,4},{7,5},{8,10},{9,11},{10,... | collective-permute-start | bytes 786440 | tf_op jit(solution)/shard_map/ppermute | solution.py:472
  200.0 29.3 %collective-permute-start.12 = (f32[8,32,256]{2,1,0:T(8,128)S(1)}, f32[8,32,256]{2,1,0:T(8,128)S(1)}, u32[]{:S(2)}, u32[]{:S(2)}) collective-permute-start(f32[8,32,256]{2,1,0:T(8,128)S(1)} %get-tuple-element.37), channel_id=1, source_target_pairs={{0,1},{1,2},{2,3},{3,0},{4,5},{5,6},{6,7},{7,4},{8,9},{9,10},{10,1... | collective-permute-start | bytes 786440 | tf_op jit(solution)/shard_map/ppermute | solution.py:472
  203.6 25.7 %collective-permute-start.13 = (f32[8,32,256]{2,1,0:T(8,128)S(1)}, f32[8,32,256]{2,1,0:T(8,128)S(1)}, u32[]{:S(2)}, u32[]{:S(2)}) collective-permute-start(f32[8,32,256]{2,1,0:T(8,128)S(1)} %get-tuple-element.38), channel_id=1, source_target_pairs={{0,3},{1,0},{2,1},{3,2},{4,7},{5,4},{6,5},{7,6},{8,11},{9,8},{10,9... | collective-permute-start | bytes 786440 | tf_op jit(solution)/shard_map/ppermute | solution.py:472
  203.9 30.9 %collective-permute-start.14 = (f32[8,32,256]{2,1,0:T(8,128)S(1)}, f32[8,32,256]{2,1,0:T(8,128)S(1)}, u32[]{:S(2)}, u32[]{:S(2)}) collective-permute-start(f32[8,32,256]{2,1,0:T(8,128)S(1)} %get-tuple-element.39), channel_id=1, source_target_pairs={{0,2},{1,3},{2,0},{3,1},{4,6},{5,7},{6,4},{7,5},{8,10},{9,11},{10,... | collective-permute-start | bytes 786440 | tf_op jit(solution)/shard_map/ppermute | solution.py:472
  (16 other events, 106.4 us)

commit v10 on v7

--- a/solution.py
+++ b/solution.py
@@ -141,7 +141,8 @@
     )(me, state, adjoint, *earlier)
 
 
-def pack_all_kernel(halves, state_ref, adjoint_ref, out_ref, buffers, sems):
+def pack_all_kernel(halves, part, state_ref, adjoint_ref, *refs):
+    out_ref, buffers, sems = refs[-3:]
     height = state_ref.shape[1]
     half_rows = height // halves
     rows = buffers.shape[3]
@@ -149,8 +150,10 @@
     for field, ref in enumerate((state_ref, adjoint_ref)):
         for half in range(halves):
             first = half * half_rows
-            starts = [first, max(first - TILE, 0), min(first + half_rows, height - TILE)]
-            if halves == 2:
+            starts = [first + part * rows, max(first - TILE, 0), min(first + half_rows, height - TILE)]
+            if part:
+                del starts[1:]
+            elif halves == 2:
                 starts.pop(2 if half else 1)
             for i, start in enumerate(starts):
                 at = (field * halves + half, i)
@@ -172,14 +175,14 @@
             out_ref[block, rows + i - 1] = values[TILE - 1 if i == 1 else 0] if inside else jnp.zeros_like(values[0])
 
 
-def pack_all(state, adjoint, halves):
+def pack_all(state, adjoint, halves, part, earlier):
     modes, _, width = state.shape
-    edges = edge_count(halves)
+    edges = 0 if part else edge_count(halves)
     shape = (2 * halves, TILE + edges, modes, width)
     return pl.pallas_call(
-        functools.partial(pack_all_kernel, halves),
+        functools.partial(pack_all_kernel, halves, part),
         grid=(1,),
-        in_specs=[ANYWHERE] * 2,
+        in_specs=[ANYWHERE] * (2 + len(earlier)),
         out_specs=pl.BlockSpec(shape, lambda i: (0,) * 4),
         out_shape=jax.ShapeDtypeStruct(shape, jnp.float32),
         scratch_shapes=[
@@ -189,7 +192,7 @@
         compiler_params=params(60),
         cost_estimate=cost(3),
         name="pack_all",
-    )(state, adjoint)
+    )(state, adjoint, *earlier)
 
 
 def pack_own_kernel(owners, me_ref, state_ref, adjoint_ref, coef_ref, *refs):
@@ -263,7 +266,8 @@
     owners = len(shifts) + 1
     heads, own_near, near, refs = refs[:3], refs[3:5], refs[5:7], refs[7:]
     pieces, before, after = (refs[i * owners : (i + 1) * owners] for i in range(3))
-    outs = refs[-7:-6] if by_owner else refs[-owners - 6 : -6]
+    outs = refs[-8:-7] if by_owner else refs[-owners - 7 : -7]
+    refs[-7][...] = jnp.zeros_like(refs[-7])
     slots, mixed, faces = ((refs[-6], refs[-5]), (refs[-4], refs[-3])), refs[-2], refs[-1]
     rows, block, width = pieces[0].shape
     modes = owners * block
@@ -347,7 +351,7 @@
         mix(row, row % 2)
 
 
-def apply_operator(me, coef, matrix, own, own_near, groups, near, part, rows, shifts, by_owner):
+def apply_operator(me, coef, matrix, own, own_near, groups, near, part, rows, shifts, by_owner, filled, after):
     _, block, width = own.shape
     owners = len(shifts) + 1
     modes = owners * block
@@ -376,13 +380,27 @@
     ):
         operands += arrays
         in_specs += specs
-    shape, count = ((owners, rows, block, width), 1) if by_owner else ((rows, block, width), owners)
+    aliases = {}
+    operands += after
+    in_specs += [ANYWHERE] * len(after)
+    if filled is not None:
+        aliases = {len(operands) + 1: 0}
+        operands.append(filled)
+        in_specs.append(ANYWHERE)
+    if by_owner:
+        out_specs = [pl.BlockSpec((owners, rows, block, width), lambda i: (0, part, 0, 0))]
+        shapes = [(owners, by_owner * rows, block, width)]
+    else:
+        out_specs = [pl.BlockSpec((rows, block, width), lambda i: (0, 0, 0))] * owners
+        shapes = [(rows, block, width)] * owners
+    note = (TILE, width)
     return pl.pallas_call(
         functools.partial(operator_kernel, shifts, terms, part, parts, by_owner),
         grid=(1,),
         in_specs=in_specs,
-        out_specs=[pl.BlockSpec(shape, lambda i: (0,) * len(shape))] * count,
-        out_shape=[jax.ShapeDtypeStruct(shape, jnp.float32)] * count,
+        out_specs=out_specs + [pl.BlockSpec(note, lambda i: (0, 0))],
+        out_shape=[jax.ShapeDtypeStruct(shape, jnp.float32) for shape in shapes + [note]],
+        input_output_aliases=aliases,
         scratch_shapes=[pltpu.VMEM((terms * modes, width), jnp.bfloat16)] * 4
         + [pltpu.VMEM((modes, width), jnp.float32), pltpu.VMEM((6 * terms, rows, width), jnp.float32)],
         compiler_params=params(),
@@ -414,16 +432,15 @@
             state_out[...] = state_ref[...] + jnp.swapaxes(mixed[index][...], 0, 1)
 
 
-def finish(me, mixed, state, control, outputs, part, shifts):
+def finish(me, mixed, state, control, outputs, part, rows, shifts):
     modes, _, width = state.shape
     halves = (len(shifts) + 1) // 2
-    rows = mixed[0].shape[-3]
     parts = state.shape[1] // halves // rows
     block = pl.BlockSpec((modes, rows, width), lambda h: (0, h * parts + part, 0))
     by_owner = len(mixed) == 1
     if by_owner:
         sources = [
-            pl.BlockSpec((1, rows, modes, width), lambda h, field=field: (field * halves + h, 0, 0, 0))
+            pl.BlockSpec((1, rows, modes, width), lambda h, field=field: (field * halves + h, part, 0, 0))
             for field in range(2)
         ]
         mixed = mixed * 2
@@ -472,23 +489,37 @@
 
     matrix = coupling_matrices(me, pattern, weights, shifts)
     groups, bodies, nears, mixed = [], [], [], []
+    together = min(parts, 2)
+    packs = {}
+
+    def relative(arrived):
+        return [lax.dynamic_index_in_dim(arrived, lax.rem(me[0] + owners - s, owners), keepdims=False) for s in shifts]
 
     def exchange(part):
-        earlier = [own] if part == 1 else [mixed[part - 3][0]] if part > 2 else [bodies[0]]
-        packed = pack(me, state, adjoint, shifts, part, rows, owners, earlier)
-        groups.append([move(piece, shift) for piece, shift in zip(packed, shifts)])
+        earlier = [own] if part == 1 else [mixed[part - 3][-1]] if part > 2 else [bodies[0]]
+        if part > 2:
+            packs[part] = [pack_all(state, adjoint, owners // 2, part, earlier)]
+            groups.append(relative(lax.all_to_all(packs[part][0], "mode", 0, 0, tiled=True)))
+        else:
+            packed = pack(me, state, adjoint, shifts, part, rows, owners, earlier)
+            groups.append([move(piece, shift) for piece, shift in zip(packed, shifts)])
 
     def halo(part):
-        earlier = [mixed[part - 2][0]] if part > 1 else [] if part else own_near
+        earlier = [mixed[min(1, len(mixed) - 1)][-1]] if part > 1 else [] if part else own_near
         bodies.append(gather(groups[part], rows, 0, earlier))
         nears.append(beside(bodies[part]))
 
     def operate(part):
+        by_owner = together if part < together else 0
+        filled = mixed[part - 1][0] if 0 < part < together else None
+        after = [packs[3][0]] if part == 1 and parts > 3 else []
         mixed.append(
-            apply_operator(me, coef, matrix, own, own_near, groups, nears[part], part, rows, shifts, part == 0)
+            apply_operator(
+                me, coef, matrix, own, own_near, groups, nears[part], part, rows, shifts, by_owner, filled, after
+            )
         )
 
-    packed = pack_all(state, adjoint, owners // 2)
+    packed = pack_all(state, adjoint, owners // 2, 0, [])
     everyone = lax.all_to_all(packed, "mode", 0, 0, tiled=True)
     groups.append(
         [lax.dynamic_index_in_dim(everyone, lax.rem(me[0] + owners - s, owners), keepdims=False) for s in shifts]
@@ -498,20 +529,24 @@
     halo(0)
     exchange(1)
     halo(1)
+    if parts > 2:
+        exchange(2)
     for part in range(parts):
-        if part + 2 < parts:
-            exchange(part + 2)
         operate(part)
-        if part + 2 < parts:
-            halo(part + 2)
+        if part + 3 < parts:
+            exchange(part + 3)
+        if part == 1 or parts < 4 and part + 2 < parts:
+            for later in range(part + 1, parts):
+                halo(later)
 
     outputs = None
+    first_parts = lax.all_to_all(mixed[together - 1][0], "mode", 0, 0, tiled=True)
     for part in range(parts):
-        if part == 0:
-            returned = [lax.all_to_all(mixed[0][0], "mode", 0, 0, tiled=True)]
+        if part < together:
+            returned = [first_parts]
         else:
-            returned = [mixed[part][0]] + [move(m, shift) for m, shift in zip(mixed[part][1:], shifts)]
-        outputs = finish(me, returned, state, control, outputs, part, shifts)
+            returned = [mixed[part][0]] + [move(m, shift) for m, shift in zip(mixed[part][1:-1], shifts)]
+        outputs = finish(me, returned, state, control, outputs, part, rows, shifts)
     return outputs[0].reshape(shape), control_residual, outputs[1].reshape(shape)
 
 

time: 212 us -> 258 us (1.22)
  the two profiles are of different devices: /device:TPU:4 before, /device:TPU:0 now
where the time goes in v10:
time: 258 us; the launch traced here: 257 us
  waiting for transfers between devices  103 us (40%)
  starting transfers between devices  89 us (34%)
  Pallas kernels  53.4 us (21%)
  local copies, waits for them, and re-layouts  9.34 us (4%)
    ppermute x12, waiting for transfers between devices, move(): lax.ppermute(array, 'mode', [(i, (i + shift) % owners) for i in range(own...  79.7 us
    ppermute x12, starting transfers between devices, move(): lax.ppermute(array, 'mode', [(i, (i + shift) % owners) for i in range(own...  47.7 us
    pallas_call x4, Pallas kernels, apply_operator(): pl.pallas_call(functools.partial(operator_kernel, shifts, terms, part, pa...  29.4 us
    all_to_all x1, waiting for transfers between devices, shards(): everyone = lax.all_to_all(packed, 'mode', 0, 0, tiled=True)  23.2 us
    ppermute x5, starting transfers between devices, beside(): lax.ppermute(array, 'space', forward)  19.4 us
    pallas_call x4, Pallas kernels, finish(): pl.pallas_call(functools.partial(finish_kernel, shifts, by_owner), grid=(...  9.82 us
    unnamed x66, local copies, waits for them, and re-layouts  6.95 us
    ppermute x5, starting transfers between devices, beside(): lax.ppermute(array, 'space', backward)  6.57 us
  transfers between devices with their start and end apart: 25, of which 10 were waited for; matrix products, arithmetic and copies ran while one was open for 2% of the time, Pallas kernels for 15%

profile of v10, /device:TPU:0, one launch (start us, length us, event | category | flops | bytes accessed | tf_op | source)
XLA Modules:
  0.0 257.5 jit_solution(4128024928758436079)
XLA Ops:
  0.6 2.6 %pack_all.2.refs_0_ = f32[4,9,32,256]{3,2,1,0:T(8,128)} custom-call(f32[32,64,256]{2,1,0:T(8,128)} %bitcast.32, f32[32,64,256]{2,1,0:T(8,128)} %bitcast.41), custom_call_target="tpu_custom_call" | custom-call | bytes 10500000 | tf_op jit(solution)/shard_map/pack_all/pallas_call | solution.py:182
  3.3 6.3 %all-to-all-start = ((f32[4,9,32,256]{3,2,1,0:T(8,128)}), f32[4,9,32,256]{3,2,1,0:T(8,128)}, u32[]{:S(2)}, u32[]{:S(2)}) async-start(f32[4,9,32,256]{3,2,1,0:T(8,128)} %pack_all.2.refs_0_), calls=%async_computation | async-start | bytes 2359296 | tf_op jit(solution)/shard_map/all_to_all | solution.py:523
  9.6 2.6 pack_own.1.refs_0_.refs_7_.refs_11_.refs_15_
  15.0 23.2 %all-to-all-done = f32[4,9,32,256]{3,2,1,0:T(8,128)} async-done(((f32[4,9,32,256]{3,2,1,0:T(8,128)}), f32[4,9,32,256]{3,2,1,0:T(8,128)}, u32[]{:S(2)}, u32[]{:S(2)}) %all-to-all-start) | async-done | bytes 1179680 | tf_op jit(solution)/shard_map/all_to_all | solution.py:523
  42.6 9.2 %collective-permute-start.2 = (f32[24,32,256]{2,1,0:T(8,128)}, f32[24,32,256]{2,1,0:T(8,128)}, u32[]{:S(2)}, u32[]{:S(2)}) collective-permute-start(f32[24,32,256]{2,1,0:T(8,128)} %gather.4.refs_0_), channel_id=1, source_target_pairs={{0,4},{4,8},{8,12},{12,16},{16,20},{20,24},{24,28},{1,5},{5,9},{9,... | collective-permute-start | bytes 2359304 | tf_op jit(solution)/shard_map/ppermute | solution.py:488
  53.2 2.1 pack.2
  55.3 2.1 collective-permute-start.4
  60.8 5.5 %collective-permute-done.4.refs_16_.refs_0_.refs_8_.refs_12_ = f32[8,32,256]{2,1,0:T(8,128)S(1)} collective-permute-done((f32[8,32,256]{2,1,0:T(8,128)}, f32[8,32,256]{2,1,0:T(8,128)S(1)}, u32[]{:S(2)}, u32[]{:S(2)}) %collective-permute-start.4) | collective-permute-done | bytes 262176 | tf_op jit(solution)/shard_map/ppermute | solution.py:485
  66.4 5.8 %collective-permute-done.5.refs_17_.refs_1_.refs_9_.refs_13_ = f32[8,32,256]{2,1,0:T(8,128)S(1)} collective-permute-done((f32[8,32,256]{2,1,0:T(8,128)}, f32[8,32,256]{2,1,0:T(8,128)S(1)}, u32[]{:S(2)}, u32[]{:S(2)}) %collective-permute-start.5) | collective-permute-done | bytes 262176 | tf_op jit(solution)/shard_map/ppermute | solution.py:485
  72.2 11.2 %collective-permute-done.6.refs_18_.refs_2_.refs_10_.refs_14_ = f32[8,32,256]{2,1,0:T(8,128)S(1)} collective-permute-done((f32[8,32,256]{2,1,0:T(8,128)}, f32[8,32,256]{2,1,0:T(8,128)S(1)}, u32[]{:S(2)}, u32[]{:S(2)}) %collective-permute-start.6) | collective-permute-done | bytes 262176 | tf_op jit(solution)/shard_map/ppermute | solution.py:485
  83.5 7.5 %operator.4 = (f32[4,16,32,256]{3,2,1,0:T(8,128)}, f32[8,256]{1,0:T(8,128)S(1)}) custom-call(s32[1]{0:T(128)} %bitcast.me_ref, f32[7,64,256]{2,1,0:T(8,128)S(1)} %bitcast.26, bf16[256,896]{1,0:T(8,128)(2,1)S(1)} %coupling.1.matrix_ref, f32[40,32,256]{2,1,0:T(8,128)S(1)} %copy-done, f32[40,32,256]{2,1,0:T(8,128)} %copy-done.1, f32[40,32,256]{2,1,0:T(8,128)} %copy-done.2, ...), custom_call_target="tpu_custom_call" | custom-call | bytes 21000000 | tf_op jit(solution)/shard_map/operator/pallas_call | solution.py:397
  91.6 2.3 pack_all.3.refs_19_
  93.9 4.4 %all-to-all-start.1 = ((f32[4,8,32,256]{3,2,1,0:T(8,128)}), f32[4,8,32,256]{3,2,1,0:T(8,128)}, u32[]{:S(2)}, u32[]{:S(2)}) async-start(f32[4,8,32,256]{3,2,1,0:T(8,128)} %pack_all.3.refs_19_), calls=%async_computation.1 | async-start | bytes 2097152 | tf_op jit(solution)/shard_map/all_to_all | solution.py:502
  99.3 3.0 %collective-permute-start.7 = (f32[24,32,256]{2,1,0:T(8,128)}, f32[24,32,256]{2,1,0:T(8,128)}, u32[]{:S(2)}, u32[]{:S(2)}) collective-permute-start(f32[24,32,256]{2,1,0:T(8,128)} %gather.5), channel_id=1, source_target_pairs={{0,4},{4,8},{8,12},{12,16},{16,20},{20,24},{24,28},{1,5},{5,9},{9,... | collective-permute-start | bytes 2359304 | tf_op jit(solution)/shard_map/ppermute | solution.py:488
  103.6 2.1 pack.3
  107.4 2.1 collective-permute-start.10
  110.3 16.0 %collective-permute-done.9.refs_16_.refs_12_.refs_0_.refs_8_ = f32[8,32,256]{2,1,0:T(8,128)S(1)} collective-permute-done((f32[8,32,256]{2,1,0:T(8,128)}, f32[8,32,256]{2,1,0:T(8,128)S(1)}, u32[]{:S(2)}, u32[]{:S(2)}) %collective-permute-start.9) | collective-permute-done | bytes 262176 | tf_op jit(solution)/shard_map/ppermute | solution.py:485
  127.8 19.2 %collective-permute-done.11.refs_18_.refs_14_.refs_2_.refs_10_ = f32[8,32,256]{2,1,0:T(8,128)S(1)} collective-permute-done((f32[8,32,256]{2,1,0:T(8,128)}, f32[8,32,256]{2,1,0:T(8,128)S(1)}, u32[]{:S(2)}, u32[]{:S(2)}) %collective-permute-start.11) | collective-permute-done | bytes 262176 | tf_op jit(solution)/shard_map/ppermute | solution.py:485
  147.0 7.7 %operator.5 = (f32[4,16,32,256]{3,2,1,0:T(8,128)}, f32[8,256]{1,0:T(8,128)S(1)}) custom-call(s32[1]{0:T(128)} %bitcast.me_ref, f32[7,64,256]{2,1,0:T(8,128)S(1)} %bitcast.27, bf16[256,896]{1,0:T(8,128)(2,1)S(1)} %coupling.1.matrix_ref, f32[40,32,256]{2,1,0:T(8,128)} %pack_own.1.refs_0_.refs_7_.refs_11_.refs_15_, ...), custom_call_target="tpu_custom_call", output_to_operand_aliasing={{0}: (23, {})} | custom-call | bytes 21000000 | tf_op jit(solution)/shard_map/operator/pallas_call | solution.py:397
  156.8 4.6 %all-to-all-start.2 = ((f32[4,16,32,256]{3,2,1,0:T(8,128)}), f32[4,16,32,256]{3,2,1,0:T(8,128)}, u32[]{:S(2)}, u32[]{:S(2)}) async-start(f32[4,16,32,256]{3,2,1,0:T(8,128)} %get-tuple-element.46), calls=%async_computation.2 | async-start | bytes 4194304 | tf_op jit(solution)/shard_map/all_to_all | solution.py:543
  165.4 4.2 %collective-permute-start.12 = (f32[24,32,256]{2,1,0:T(8,128)S(1)}, f32[24,32,256]{2,1,0:T(8,128)S(1)}, u32[]{:S(2)}, u32[]{:S(2)}) collective-permute-start(f32[24,32,256]{2,1,0:T(8,128)S(1)} %gather.6), channel_id=1, source_target_pairs={{0,4},{4,8},{8,12},{12,16},{16,20},{20,24},{24,28},{1,5},{5,9},{9,... | collective-permute-start | bytes 2359304 | tf_op jit(solution)/shard_map/ppermute | solution.py:488
  171.0 7.1 %operator.7 = (f32[8,32,256]{2,1,0:T(8,128)S(1)}, f32[8,32,256]{2,1,0:T(8,128)S(1)}, f32[8,32,256]{2,1,0:T(8,128)}, f32[8,32,256]{2,1,0:T(8,128)}, f32[8,256]{1,0:T(8,128)}) custom-call(s32[1]{0:T(128)} %bitcast.me_ref, f32[7,64,256]{2,1,0:T(8,128)S(1)} %bitcast.28, bf16[256,896]{1,0:T(8,128)(2,1)S(1)} %coupling.1.matrix_ref, ...), custom_call_target="tpu_custom_call" | custom-call | bytes 21000000 | tf_op jit(solution)/shard_map/operator/pallas_call | solution.py:397
  183.7 7.1 %operator.6 = (f32[8,32,256]{2,1,0:T(8,128)S(1)}, f32[8,32,256]{2,1,0:T(8,128)}, f32[8,32,256]{2,1,0:T(8,128)S(1)}, f32[8,32,256]{2,1,0:T(8,128)S(1)}, f32[8,256]{1,0:T(8,128)}) custom-call(s32[1]{0:T(128)} %bitcast.me_ref, f32[7,64,256]{2,1,0:T(8,128)S(1)} %bitcast.29, bf16[256,896]{1,0:T(8,128)(2,1)S(1)} %coupling.1.matrix_ref, ...), custom_call_target="tpu_custom_call" | custom-call | bytes 21000000 | tf_op jit(solution)/shard_map/operator/pallas_call | solution.py:397
  192.8 2.5 collective-permute-start.15
  195.3 9.4 %collective-permute-done.19.refs_1_ = f32[8,32,256]{2,1,0:T(8,128)S(1)} collective-permute-done((f32[8,32,256]{2,1,0:T(8,128)S(1)}, f32[8,32,256]{2,1,0:T(8,128)S(1)}, u32[]{:S(2)}, u32[]{:S(2)}) %collective-permute-start.19) | collective-permute-done | bytes 262176 | tf_op jit(solution)/shard_map/ppermute | solution.py:485
  204.8 29.4 %collective-permute-start.16 = (f32[8,32,256]{2,1,0:T(8,128)S(1)}, f32[8,32,256]{2,1,0:T(8,128)S(1)}, u32[]{:S(2)}, u32[]{:S(2)}) collective-permute-start(f32[8,32,256]{2,1,0:T(8,128)S(1)} %get-tuple-element.41), channel_id=1, source_target_pairs={{0,2},{1,3},{2,0},{3,1},{4,6},{5,7},{6,4},{7,5},{8,10},{9,11},{10,... | collective-permute-start | bytes 786440 | tf_op jit(solution)/shard_map/ppermute | solution.py:485
  235.9 2.4 finish.4
  238.2 2.4 finish.5
  240.6 3.6 %collective-permute-done.21.refs_3_ = f32[8,32,256]{2,1,0:T(8,128)} collective-permute-done((f32[8,32,256]{2,1,0:T(8,128)}, f32[8,32,256]{2,1,0:T(8,128)}, u32[]{:S(2)}, u32[]{:S(2)}) %collective-permute-start.21) | collective-permute-done | bytes 262176 | tf_op jit(solution)/shard_map/ppermute | solution.py:485
  244.2 2.5 finish.6
  246.7 7.5 %collective-permute-done.16.refs_3_ = f32[8,32,256]{2,1,0:T(8,128)S(1)} collective-permute-done((f32[8,32,256]{2,1,0:T(8,128)S(1)}, f32[8,32,256]{2,1,0:T(8,128)S(1)}, u32[]{:S(2)}, u32[]{:S(2)}) %collective-permute-start.16) | collective-permute-done | bytes 262176 | tf_op jit(solution)/shard_map/ppermute | solution.py:485
  254.9 2.5 finish.7
  (105 shorter events, 36.1 us)
Async XLA Ops:
  3.3 35.0 %all-to-all-start = ((f32[4,9,32,256]{3,2,1,0:T(8,128)}), f32[4,9,32,256]{3,2,1,0:T(8,128)}, u32[]{:S(2)}, u32[]{:S(2)}) async-start(f32[4,9,32,256]{3,2,1,0:T(8,128)} %pack_all.2.refs_0_), calls=%async_computation | async-start | bytes 2359296 | tf_op jit(solution)/shard_map/all_to_all | solution.py:523
  12.2 27.3 %collective-permute-start = (f32[40,32,256]{2,1,0:T(8,128)}, f32[40,32,256]{2,1,0:T(8,128)S(1)}, u32[]{:S(2)}, u32[]{:S(2)}) collective-permute-start(f32[40,32,256]{2,1,0:T(8,128)} %pack_own.1.refs_0_.refs_7_.refs_11_.refs_15_), channel_id=1, source_target_pairs={{0,4},{4,8},{8,12},{12,16},{16,20},{20,24},{24,28},{1,5},{5,9},{9,... | collective-permute-start | bytes 3932168 | tf_op jit(solution)/shard_map/ppermute | solution.py:488
  13.7 25.8 %collective-permute-start.1 = (f32[40,32,256]{2,1,0:T(8,128)}, f32[40,32,256]{2,1,0:T(8,128)S(1)}, u32[]{:S(2)}, u32[]{:S(2)}) collective-permute-start(f32[40,32,256]{2,1,0:T(8,128)} %pack_own.1.refs_0_.refs_7_.refs_11_.refs_15_), channel_id=1, source_target_pairs={{4,0},{8,4},{12,8},{16,12},{20,16},{24,20},{28,24},{5,1},{9,5},{13... | collective-permute-start | bytes 3932168 | tf_op jit(solution)/shard_map/ppermute | solution.py:488
  39.4 44.0 %copy-start.4 = (f32[9,32,256]{2,1,0:T(8,128)}, f32[9,32,256]{2,1,0:T(8,128)S(1)}, u32[]{:S(2)}) copy-start(f32[9,32,256]{2,1,0:T(8,128)S(1)} %get-tuple-element.59.refs_1_.refs_9_.refs_13_.refs_17_) | copy-start | bytes 884740
  42.6 40.9 %copy-start.3 = (f32[7,1,64,256]{3,2,1,0:T(8,128)S(1)}, f32[7,1,64,256]{3,2,1,0:T(8,128)}, u32[]{:S(2)}) copy-start(f32[7,1,64,256]{3,2,1,0:T(8,128)} %param.9) | copy-start | bytes 1376260
  42.6 40.8 %collective-permute-start.2 = (f32[24,32,256]{2,1,0:T(8,128)}, f32[24,32,256]{2,1,0:T(8,128)}, u32[]{:S(2)}, u32[]{:S(2)}) collective-permute-start(f32[24,32,256]{2,1,0:T(8,128)} %gather.4.refs_0_), channel_id=1, source_target_pairs={{0,4},{4,8},{8,12},{12,16},{16,20},{20,24},{24,28},{1,5},{5,9},{9,... | collective-permute-start | bytes 2359304 | tf_op jit(solution)/shard_map/ppermute | solution.py:488
  51.8 31.6 %collective-permute-start.3 = (f32[24,32,256]{2,1,0:T(8,128)}, f32[24,32,256]{2,1,0:T(8,128)}, u32[]{:S(2)}, u32[]{:S(2)}) collective-permute-start(f32[24,32,256]{2,1,0:T(8,128)} %gather.4.refs_0_), channel_id=1, source_target_pairs={{4,0},{8,4},{12,8},{16,12},{20,16},{24,20},{28,24},{5,1},{9,5},{13... | collective-permute-start | bytes 2359304 | tf_op jit(solution)/shard_map/ppermute | solution.py:488
  55.3 11.0 %collective-permute-start.4 = (f32[8,32,256]{2,1,0:T(8,128)}, f32[8,32,256]{2,1,0:T(8,128)S(1)}, u32[]{:S(2)}, u32[]{:S(2)}) collective-permute-start(f32[8,32,256]{2,1,0:T(8,128)} %get-tuple-element.29), channel_id=1, source_target_pairs={{0,1},{1,2},{2,3},{3,0},{4,5},{5,6},{6,7},{7,4},{8,9},{9,10},{10,1... | collective-permute-start | bytes 786440 | tf_op jit(solution)/shard_map/ppermute | solution.py:485
  57.4 14.8 %collective-permute-start.5 = (f32[8,32,256]{2,1,0:T(8,128)}, f32[8,32,256]{2,1,0:T(8,128)S(1)}, u32[]{:S(2)}, u32[]{:S(2)}) collective-permute-start(f32[8,32,256]{2,1,0:T(8,128)} %get-tuple-element.30), channel_id=1, source_target_pairs={{0,3},{1,0},{2,1},{3,2},{4,7},{5,4},{6,5},{7,6},{8,11},{9,8},{10,9... | collective-permute-start | bytes 786440 | tf_op jit(solution)/shard_map/ppermute | solution.py:485
  59.3 24.2 %collective-permute-start.6 = (f32[8,32,256]{2,1,0:T(8,128)}, f32[8,32,256]{2,1,0:T(8,128)S(1)}, u32[]{:S(2)}, u32[]{:S(2)}) collective-permute-start(f32[8,32,256]{2,1,0:T(8,128)} %get-tuple-element.31), channel_id=1, source_target_pairs={{0,2},{1,3},{2,0},{3,1},{4,6},{5,7},{6,4},{7,5},{8,10},{9,11},{10,... | collective-permute-start | bytes 786440 | tf_op jit(solution)/shard_map/ppermute | solution.py:485
  93.9 62.9 %all-to-all-start.1 = ((f32[4,8,32,256]{3,2,1,0:T(8,128)}), f32[4,8,32,256]{3,2,1,0:T(8,128)}, u32[]{:S(2)}, u32[]{:S(2)}) async-start(f32[4,8,32,256]{3,2,1,0:T(8,128)} %pack_all.3.refs_19_), calls=%async_computation.1 | async-start | bytes 2097152 | tf_op jit(solution)/shard_map/all_to_all | solution.py:502
  99.3 47.7 %copy-start.5 = (f32[9,32,256]{2,1,0:T(8,128)S(1)}, f32[9,32,256]{2,1,0:T(8,128)}, u32[]{:S(2)}) copy-start(f32[9,32,256]{2,1,0:T(8,128)} %copy-done.4) | copy-start | bytes 884740
  99.3 47.7 %copy-start.8 = (f32[4,8,32,256]{3,2,1,0:T(8,128)S(1)}, f32[4,8,32,256]{3,2,1,0:T(8,128)}, u32[]{:S(2)}) copy-start(f32[4,8,32,256]{3,2,1,0:T(8,128)} %pack_all.3.refs_19_) | copy-start | bytes 3145732
  99.3 47.7 %copy-start.14 = (f32[8,32,256]{2,1,0:T(8,128)S(1)}, f32[8,32,256]{2,1,0:T(8,128)}, u32[]{:S(2)}) copy-start(f32[8,32,256]{2,1,0:T(8,128)} %copy-done.13) | copy-start | bytes 786436
  99.3 11.1 %collective-permute-start.7 = (f32[24,32,256]{2,1,0:T(8,128)}, f32[24,32,256]{2,1,0:T(8,128)}, u32[]{:S(2)}, u32[]{:S(2)}) collective-permute-start(f32[24,32,256]{2,1,0:T(8,128)} %gather.5), channel_id=1, source_target_pairs={{0,4},{4,8},{8,12},{12,16},{16,20},{20,24},{24,28},{1,5},{5,9},{9,... | collective-permute-start | bytes 2359304 | tf_op jit(solution)/shard_map/ppermute | solution.py:488
  102.3 8.0 %collective-permute-start.8 = (f32[24,32,256]{2,1,0:T(8,128)}, f32[24,32,256]{2,1,0:T(8,128)}, u32[]{:S(2)}, u32[]{:S(2)}) collective-permute-start(f32[24,32,256]{2,1,0:T(8,128)} %gather.5), channel_id=1, source_target_pairs={{4,0},{8,4},{12,8},{16,12},{20,16},{24,20},{28,24},{5,1},{9,5},{13... | collective-permute-start | bytes 2359304 | tf_op jit(solution)/shard_map/ppermute | solution.py:488
  105.7 20.7 %collective-permute-start.9 = (f32[8,32,256]{2,1,0:T(8,128)}, f32[8,32,256]{2,1,0:T(8,128)S(1)}, u32[]{:S(2)}, u32[]{:S(2)}) collective-permute-start(f32[8,32,256]{2,1,0:T(8,128)} %get-tuple-element.33), channel_id=1, source_target_pairs={{0,1},{1,2},{2,3},{3,0},{4,5},{5,6},{6,7},{7,4},{8,9},{9,10},{10,1... | collective-permute-start | bytes 786440 | tf_op jit(solution)/shard_map/ppermute | solution.py:485
  107.4 20.4 %collective-permute-start.10 = (f32[8,32,256]{2,1,0:T(8,128)}, f32[8,32,256]{2,1,0:T(8,128)S(1)}, u32[]{:S(2)}, u32[]{:S(2)}) collective-permute-start(f32[8,32,256]{2,1,0:T(8,128)} %get-tuple-element.34), channel_id=1, source_target_pairs={{0,3},{1,0},{2,1},{3,2},{4,7},{5,4},{6,5},{7,6},{8,11},{9,8},{10,9... | collective-permute-start | bytes 786440 | tf_op jit(solution)/shard_map/ppermute | solution.py:485
  109.6 37.5 %collective-permute-start.11 = (f32[8,32,256]{2,1,0:T(8,128)}, f32[8,32,256]{2,1,0:T(8,128)S(1)}, u32[]{:S(2)}, u32[]{:S(2)}) collective-permute-start(f32[8,32,256]{2,1,0:T(8,128)} %get-tuple-element.35), channel_id=1, source_target_pairs={{0,2},{1,3},{2,0},{3,1},{4,6},{5,7},{6,4},{7,5},{8,10},{9,11},{10,... | collective-permute-start | bytes 786440 | tf_op jit(solution)/shard_map/ppermute | solution.py:485
  156.8 79.1 %all-to-all-start.2 = ((f32[4,16,32,256]{3,2,1,0:T(8,128)}), f32[4,16,32,256]{3,2,1,0:T(8,128)}, u32[]{:S(2)}, u32[]{:S(2)}) async-start(f32[4,16,32,256]{3,2,1,0:T(8,128)} %get-tuple-element.46), calls=%async_computation.2 | async-start | bytes 4194304 | tf_op jit(solution)/shard_map/all_to_all | solution.py:543
  161.5 9.4 %collective-permute-start.17 = (f32[24,32,256]{2,1,0:T(8,128)S(1)}, f32[24,32,256]{2,1,0:T(8,128)S(1)}, u32[]{:S(2)}, u32[]{:S(2)}) collective-permute-start(f32[24,32,256]{2,1,0:T(8,128)S(1)} %gather.7), channel_id=1, source_target_pairs={{0,4},{4,8},{8,12},{12,16},{16,20},{20,24},{24,28},{1,5},{5,9},{9,... | collective-permute-start | bytes 2359304 | tf_op jit(solution)/shard_map/ppermute | solution.py:488
  162.9 8.1 %collective-permute-start.18 = (f32[24,32,256]{2,1,0:T(8,128)S(1)}, f32[24,32,256]{2,1,0:T(8,128)S(1)}, u32[]{:S(2)}, u32[]{:S(2)}) collective-permute-start(f32[24,32,256]{2,1,0:T(8,128)S(1)} %gather.7), channel_id=1, source_target_pairs={{4,0},{8,4},{12,8},{16,12},{20,16},{24,20},{28,24},{5,1},{9,5},{13... | collective-permute-start | bytes 2359304 | tf_op jit(solution)/shard_map/ppermute | solution.py:488
  165.4 18.3 %collective-permute-start.12 = (f32[24,32,256]{2,1,0:T(8,128)S(1)}, f32[24,32,256]{2,1,0:T(8,128)S(1)}, u32[]{:S(2)}, u32[]{:S(2)}) collective-permute-start(f32[24,32,256]{2,1,0:T(8,128)S(1)} %gather.6), channel_id=1, source_target_pairs={{0,4},{4,8},{8,12},{12,16},{16,20},{20,24},{24,28},{1,5},{5,9},{9,... | collective-permute-start | bytes 2359304 | tf_op jit(solution)/shard_map/ppermute | solution.py:488
  169.6 14.0 %collective-permute-start.13 = (f32[24,32,256]{2,1,0:T(8,128)S(1)}, f32[24,32,256]{2,1,0:T(8,128)S(1)}, u32[]{:S(2)}, u32[]{:S(2)}) collective-permute-start(f32[24,32,256]{2,1,0:T(8,128)S(1)} %gather.6), channel_id=1, source_target_pairs={{4,0},{8,4},{12,8},{16,12},{20,16},{24,20},{28,24},{5,1},{9,5},{13... | collective-permute-start | bytes 2359304 | tf_op jit(solution)/shard_map/ppermute | solution.py:488
  178.8 26.0 %collective-permute-start.19 = (f32[8,32,256]{2,1,0:T(8,128)S(1)}, f32[8,32,256]{2,1,0:T(8,128)S(1)}, u32[]{:S(2)}, u32[]{:S(2)}) collective-permute-start(f32[8,32,256]{2,1,0:T(8,128)S(1)} %get-tuple-element.43), channel_id=1, source_target_pairs={{0,1},{1,2},{2,3},{3,0},{4,5},{5,6},{6,7},{7,4},{8,9},{9,10},{10,1... | collective-permute-start | bytes 786440 | tf_op jit(solution)/shard_map/ppermute | solution.py:485
  180.7 59.9 %collective-permute-start.20 = (f32[8,32,256]{2,1,0:T(8,128)}, f32[8,32,256]{2,1,0:T(8,128)}, u32[]{:S(2)}, u32[]{:S(2)}) collective-permute-start(f32[8,32,256]{2,1,0:T(8,128)} %get-tuple-element.44), channel_id=1, source_target_pairs={{0,3},{1,0},{2,1},{3,2},{4,7},{5,4},{6,5},{7,6},{8,11},{9,8},{10,9... | collective-permute-start | bytes 786440 | tf_op jit(solution)/shard_map/ppermute | solution.py:485
  182.6 51.5 %copy-start.27 = (f32[32,1,64,256]{3,2,1,0:T(8,128)S(1)}, f32[32,1,64,256]{3,2,1,0:T(8,128)}, u32[]{:S(2)}) copy-start(f32[32,1,64,256]{3,2,1,0:T(8,128)} %param.8) | copy-start | bytes 6291460
  182.6 51.5 %copy-start.28 = (f32[32,1,64,256]{3,2,1,0:T(8,128)S(1)}, f32[32,1,64,256]{3,2,1,0:T(8,128)}, u32[]{:S(2)}) copy-start(f32[32,1,64,256]{3,2,1,0:T(8,128)} %param.7) | copy-start | bytes 6291460
  182.6 61.6 %collective-permute-start.21 = (f32[8,32,256]{2,1,0:T(8,128)}, f32[8,32,256]{2,1,0:T(8,128)}, u32[]{:S(2)}, u32[]{:S(2)}) collective-permute-start(f32[8,32,256]{2,1,0:T(8,128)} %get-tuple-element.45), channel_id=1, source_target_pairs={{0,2},{1,3},{2,0},{3,1},{4,6},{5,7},{6,4},{7,5},{8,10},{9,11},{10,... | collective-permute-start | bytes 786440 | tf_op jit(solution)/shard_map/ppermute | solution.py:485
  191.5 55.2 %collective-permute-start.14 = (f32[8,32,256]{2,1,0:T(8,128)}, f32[8,32,256]{2,1,0:T(8,128)S(1)}, u32[]{:S(2)}, u32[]{:S(2)}) collective-permute-start(f32[8,32,256]{2,1,0:T(8,128)} %get-tuple-element.39), channel_id=1, source_target_pairs={{0,1},{1,2},{2,3},{3,0},{4,5},{5,6},{6,7},{7,4},{8,9},{9,10},{10,1... | collective-permute-start | bytes 786440 | tf_op jit(solution)/shard_map/ppermute | solution.py:485
  192.8 53.9 %collective-permute-start.15 = (f32[8,32,256]{2,1,0:T(8,128)S(1)}, f32[8,32,256]{2,1,0:T(8,128)S(1)}, u32[]{:S(2)}, u32[]{:S(2)}) collective-permute-start(f32[8,32,256]{2,1,0:T(8,128)S(1)} %get-tuple-element.40), channel_id=1, source_target_pairs={{0,3},{1,0},{2,1},{3,2},{4,7},{5,4},{6,5},{7,6},{8,11},{9,8},{10,9... | collective-permute-start | bytes 786440 | tf_op jit(solution)/shard_map/ppermute | solution.py:485
  204.8 49.5 %collective-permute-start.16 = (f32[8,32,256]{2,1,0:T(8,128)S(1)}, f32[8,32,256]{2,1,0:T(8,128)S(1)}, u32[]{:S(2)}, u32[]{:S(2)}) collective-permute-start(f32[8,32,256]{2,1,0:T(8,128)S(1)} %get-tuple-element.41), channel_id=1, source_target_pairs={{0,2},{1,3},{2,0},{3,1},{4,6},{5,7},{6,4},{7,5},{8,10},{9,11},{10,... | collective-permute-start | bytes 786440 | tf_op jit(solution)/shard_map/ppermute | solution.py:485
  (26 other events, 252.7 us)

commit v11 on v8

--- a/solution.py
+++ b/solution.py
@@ -504,19 +504,18 @@
     own = pack_own(me, state, adjoint, coef, owners, [packed])
     own_near = list(beside(own))
     halo(0, own_near)
-    for group in members[1:]:
-        if group[0] > 1:
-            exchange_all(group[0], [bodies[0]])
-        else:
-            exchange(group, [own])
+    if len(members) > 1:
+        exchange(members[1], [own])
     for part in range(parts):
         if part:
-            halo(part, [mixed[part - 2][0]] if part > 1 else list(nears[0]))
+            halo(part, [mixed[part - 2][0]] if part > 1 else [bodies[0]])
         mixed.append(
             apply_operator(
                 me, coef, matrix, own, own_near, groups, group_of, nears[part], part, rows, shifts, part == 0
             )
         )
+        if part == 0 and len(members) > 2:
+            exchange(members[2], [bodies[0]])
 
     outputs = None
     for part in range(parts):

time: 249 us -> 214 us (0.86)
  waiting for transfers between devices: 96.9 us -> 72.9 us
  starting transfers between devices: 87.5 us -> 78.6 us
  local copies, waits for them, and re-layouts: 10.1 us -> 5.17 us
  Pallas kernels: 49.4 us -> 53.8 us
    ppermute x12 -> x15, waiting for transfers between devices: 69.7 us -> 44 us  [move(): lax.ppermute(array, 'mode', [(i, (i + shift) % owners) for i in range(own...]
    all_to_all x2 -> x1, starting transfers between devices: 9.99 us -> 4.88 us  [exchange_all(): arrived = lax.all_to_all(packed, 'mode', 0, 0, tiled=True)]
    all_to_all x2 -> x1, waiting for transfers between devices: 19.6 us -> 24.3 us  [exchange_all(): arrived = lax.all_to_all(packed, 'mode', 0, 0, tiled=True)]
    unnamed x44 -> x48, local copies, waits for them, and re-layouts: 7.75 us -> 3.96 us
    pallas_call x4, Pallas kernels: 1.12 us -> 4.24 us  [gather(): pl.pallas_call(functools.partial(gather_kernel, len(pieces)), grid=(1,),...]
    ppermute x5, starting transfers between devices: 25.6 us -> 22.9 us  [beside(): lax.ppermute(array, 'space', backward)]
    ppermute x12 -> x15, starting transfers between devices: 38.1 us -> 36.9 us  [move(): lax.ppermute(array, 'mode', [(i, (i + shift) % owners) for i in range(own...]
  transfers between devices with their start and end apart: 25 -> 27, of which waited for: 10 -> 6; matrix products, arithmetic and copies ran while one was open for 2% -> 1% of each run, Pallas kernels for 17% -> 23%
where the time goes in v11:
time: 214 us; the launch traced here: 213 us
  starting transfers between devices  78.6 us (37%)
  waiting for transfers between devices  72.9 us (34%)
  Pallas kernels  53.8 us (25%)
  local copies, waits for them, and re-layouts  5.17 us (2%)
    ppermute x15, waiting for transfers between devices, move(): lax.ppermute(array, 'mode', [(i, (i + shift) % owners) for i in range(own...  44 us
    ppermute x15, starting transfers between devices, move(): lax.ppermute(array, 'mode', [(i, (i + shift) % owners) for i in range(own...  36.9 us
    pallas_call x4, Pallas kernels, apply_operator(): pl.pallas_call(functools.partial(operator_kernel, shifts, terms, part, pa...  29.3 us
    all_to_all x1, waiting for transfers between devices, exchange_all(): arrived = lax.all_to_all(packed, 'mode', 0, 0, tiled=True)  24.3 us
    ppermute x5, starting transfers between devices, beside(): lax.ppermute(array, 'space', backward)  22.9 us
    pallas_call x4, Pallas kernels, finish(): pl.pallas_call(functools.partial(finish_kernel, shifts, by_owner), grid=(...  9.98 us
    ppermute x5, starting transfers between devices, beside(): lax.ppermute(array, 'space', forward)  9.72 us
    all_to_all x1, starting transfers between devices, exchange_all(): arrived = lax.all_to_all(packed, 'mode', 0, 0, tiled=True)  4.88 us
  transfers between devices with their start and end apart: 27, of which 6 were waited for; matrix products, arithmetic and copies ran while one was open for 1% of the time, Pallas kernels for 23%

profile of v11, /device:TPU:4, one launch (start us, length us, event | category | flops | bytes accessed | tf_op | source)
XLA Modules:
  0.0 213.4 jit_solution(9841950941902641336)
XLA Ops:
  0.6 2.6 %pack_all.1.refs_0_ = f32[4,9,32,256]{3,2,1,0:T(8,128)} custom-call(f32[32,64,256]{2,1,0:T(8,128)} %bitcast.26, f32[32,64,256]{2,1,0:T(8,128)} %bitcast.38), custom_call_target="tpu_custom_call" | custom-call | bytes 10500000 | tf_op jit(solution)/shard_map/pack_all/pallas_call | solution.py:182
  3.3 4.9 %all-to-all-start = ((f32[4,9,32,256]{3,2,1,0:T(8,128)}), f32[4,9,32,256]{3,2,1,0:T(8,128)}, u32[]{:S(2)}, u32[]{:S(2)}) async-start(f32[4,9,32,256]{3,2,1,0:T(8,128)} %pack_all.1.refs_0_), calls=%async_computation | async-start | bytes 2359296 | tf_op jit(solution)/shard_map/all_to_all | solution.py:488
  8.1 2.6 %pack_own.1.refs_0_.refs_7_.refs_11_.refs_15_ = f32[40,32,256]{2,1,0:T(8,128)} custom-call(s32[1]{0:T(128)} %bitcast.me_ref, f32[32,64,256]{2,1,0:T(8,128)} %bitcast.27, f32[32,64,256]{2,1,0:T(8,128)} %bitcast.39, f32[7,64,256]{2,1,0:T(8,128)} %bitcast.19, f32[4,9,32,256]{3,2,1,0:T(8,128)} %pack_all.1.refs_0_), custom_call_target="tpu_custom_call" | custom-call | bytes 10500000 | tf_op jit(solution)/shard_map/pack_own/pallas_call | solution.py:226
  12.6 4.5 %collective-permute-start.1 = (f32[40,32,256]{2,1,0:T(8,128)}, f32[40,32,256]{2,1,0:T(8,128)S(1)}, u32[]{:S(2)}, u32[]{:S(2)}) collective-permute-start(f32[40,32,256]{2,1,0:T(8,128)} %pack_own.1.refs_0_.refs_7_.refs_11_.refs_15_), channel_id=1, source_target_pairs={{4,0},{8,4},{12,8},{16,12},{20,16},{24,20},{28,24},{5,1},{9,5},{13... | collective-permute-start | bytes 3932168 | tf_op jit(solution)/shard_map/ppermute | solution.py:475
  17.2 2.6 %pack.3 = (f32[16,32,256]{2,1,0:T(8,128)}, f32[16,32,256]{2,1,0:T(8,128)}, f32[16,32,256]{2,1,0:T(8,128)}) custom-call(s32[1]{0:T(128)} %bitcast.me_ref, f32[32,64,256]{2,1,0:T(8,128)} %bitcast.28, f32[32,64,256]{2,1,0:T(8,128)} %bitcast.40, f32[40,32,256]{2,1,0:T(8,128)} %pack_own.1.refs_0_.refs_7_.refs_11_.refs_15_), custom_call_target="tpu_custom_call" | custom-call | bytes 10500000 | tf_op jit(solution)/shard_map/pack/pallas_call | solution.py:128
  19.8 2.1 collective-permute-start.5
  24.8 24.3 %all-to-all-done = f32[4,9,32,256]{3,2,1,0:T(8,128)} async-done(((f32[4,9,32,256]{3,2,1,0:T(8,128)}), f32[4,9,32,256]{3,2,1,0:T(8,128)}, u32[]{:S(2)}, u32[]{:S(2)}) %all-to-all-start) | async-done | bytes 1179680 | tf_op jit(solution)/shard_map/all_to_all | solution.py:488
  54.1 4.5 %collective-permute-start.16 = (f32[24,32,256]{2,1,0:T(8,128)}, f32[24,32,256]{2,1,0:T(8,128)}, u32[]{:S(2)}, u32[]{:S(2)}) collective-permute-start(f32[24,32,256]{2,1,0:T(8,128)} %gather.4.refs_0_.refs_3_), channel_id=1, source_target_pairs={{4,0},{8,4},{12,8},{16,12},{20,16},{24,20},{28,24},{5,1},{9,5},{13... | collective-permute-start | bytes 2359304 | tf_op jit(solution)/shard_map/ppermute | solution.py:475
  58.6 23.1 %collective-permute-done.7.refs_2_.refs_10_.refs_18_.refs_14_ = f32[16,32,256]{2,1,0:T(8,128)} collective-permute-done((f32[16,32,256]{2,1,0:T(8,128)}, f32[16,32,256]{2,1,0:T(8,128)}, u32[]{:S(2)}, u32[]{:S(2)}) %collective-permute-start.7) | collective-permute-done | bytes 524320 | tf_op jit(solution)/shard_map/ppermute | solution.py:472
  83.8 2.1 collective-permute-start.8
  85.8 4.5 %collective-permute-start.9 = (f32[24,32,256]{2,1,0:T(8,128)}, f32[24,32,256]{2,1,0:T(8,128)}, u32[]{:S(2)}, u32[]{:S(2)}) collective-permute-start(f32[24,32,256]{2,1,0:T(8,128)} %gather.5), channel_id=1, source_target_pairs={{4,0},{8,4},{12,8},{16,12},{20,16},{24,20},{28,24},{5,1},{9,5},{13... | collective-permute-start | bytes 2359304 | tf_op jit(solution)/shard_map/ppermute | solution.py:475
  90.4 2.1 pack.2
  92.5 3.8 %collective-permute-start.3 = (f32[8,32,256]{2,1,0:T(8,128)}, f32[8,32,256]{2,1,0:T(8,128)S(1)}, u32[]{:S(2)}, u32[]{:S(2)}) collective-permute-start(f32[8,32,256]{2,1,0:T(8,128)} %get-tuple-element.30), channel_id=1, source_target_pairs={{0,3},{1,0},{2,1},{3,2},{4,7},{5,4},{6,5},{7,6},{8,11},{9,8},{10,9... | collective-permute-start | bytes 786440 | tf_op jit(solution)/shard_map/ppermute | solution.py:472
  96.9 7.7 %operator.6.refs_3_ = f32[4,8,32,256]{3,2,1,0:T(8,128)} custom-call(s32[1]{0:T(128)} %bitcast.me_ref, f32[7,64,256]{2,1,0:T(8,128)S(1)} %bitcast.20, bf16[256,896]{1,0:T(8,128)(2,1)S(1)} %coupling.1.matrix_ref, f32[40,32,256]{2,1,0:T(8,128)} %pack_own.1.refs_0_.refs_7_.refs_11_.refs_15_, f32[40,32,256]{2,1,0:T(8,128)} %copy-done, f32[40,32,256]{2,1,0:T(8,128)} %copy-done.1, ...), custom_call_target="tpu_custom_call" | custom-call | bytes 21000000 | tf_op jit(solution)/shard_map/operator/pallas_call | solution.py:384
  104.6 4.3 %all-to-all-start.1 = ((f32[4,8,32,256]{3,2,1,0:T(8,128)}), f32[4,8,32,256]{3,2,1,0:T(8,128)}, u32[]{:S(2)}, u32[]{:S(2)}) async-start(f32[4,8,32,256]{3,2,1,0:T(8,128)} %operator.6.refs_3_), calls=%async_computation.1 | async-start | bytes 2097152 | tf_op jit(solution)/shard_map/all_to_all | solution.py:523
  112.0 4.7 %collective-permute-start.18 = (f32[24,32,256]{2,1,0:T(8,128)S(1)}, f32[24,32,256]{2,1,0:T(8,128)S(1)}, u32[]{:S(2)}, u32[]{:S(2)}) collective-permute-start(f32[24,32,256]{2,1,0:T(8,128)S(1)} %gather.7), channel_id=1, source_target_pairs={{4,0},{8,4},{12,8},{16,12},{20,16},{24,20},{28,24},{5,1},{9,5},{13... | collective-permute-start | bytes 2359304 | tf_op jit(solution)/shard_map/ppermute | solution.py:475
  116.7 6.9 %operator.4 = (f32[8,32,256]{2,1,0:T(8,128)S(1)}, f32[8,32,256]{2,1,0:T(8,128)S(1)}, f32[8,32,256]{2,1,0:T(8,128)S(1)}, f32[8,32,256]{2,1,0:T(8,128)S(1)}) custom-call(s32[1]{0:T(128)} %bitcast.me_ref, f32[7,64,256]{2,1,0:T(8,128)S(1)} %bitcast.21, bf16[256,896]{1,0:T(8,128)(2,1)S(1)} %coupling.1.matrix_ref, ...), custom_call_target="tpu_custom_call" | custom-call | bytes 21000000 | tf_op jit(solution)/shard_map/operator/pallas_call | solution.py:384
  123.7 2.2 %collective-permute-done.4.refs_2_.refs_10_.refs_18_ = f32[8,32,256]{2,1,0:T(8,128)S(1)} collective-permute-done((f32[8,32,256]{2,1,0:T(8,128)}, f32[8,32,256]{2,1,0:T(8,128)S(1)}, u32[]{:S(2)}, u32[]{:S(2)}) %collective-permute-start.4) | collective-permute-done | bytes 262176 | tf_op jit(solution)/shard_map/ppermute | solution.py:472
  127.8 4.5 %collective-permute-start.11 = (f32[24,32,256]{2,1,0:T(8,128)S(1)}, f32[24,32,256]{2,1,0:T(8,128)S(1)}, u32[]{:S(2)}, u32[]{:S(2)}) collective-permute-start(f32[24,32,256]{2,1,0:T(8,128)S(1)} %gather.6), channel_id=1, source_target_pairs={{4,0},{8,4},{12,8},{16,12},{20,16},{24,20},{28,24},{5,1},{9,5},{13... | collective-permute-start | bytes 2359304 | tf_op jit(solution)/shard_map/ppermute | solution.py:475
  132.4 3.8 %collective-permute-start.23 = (f32[8,32,256]{2,1,0:T(8,128)S(1)}, f32[8,32,256]{2,1,0:T(8,128)S(1)}, u32[]{:S(2)}, u32[]{:S(2)}) collective-permute-start(f32[8,32,256]{2,1,0:T(8,128)S(1)} %get-tuple-element.45), channel_id=1, source_target_pairs={{0,3},{1,0},{2,1},{3,2},{4,7},{5,4},{6,5},{7,6},{8,11},{9,8},{10,9... | collective-permute-start | bytes 786440 | tf_op jit(solution)/shard_map/ppermute | solution.py:472
  136.7 7.2 %operator.7 = (f32[8,32,256]{2,1,0:T(8,128)S(1)}, f32[8,32,256]{2,1,0:T(8,128)S(1)}, f32[8,32,256]{2,1,0:T(8,128)}, f32[8,32,256]{2,1,0:T(8,128)}) custom-call(s32[1]{0:T(128)} %bitcast.me_ref, f32[7,64,256]{2,1,0:T(8,128)S(1)} %bitcast.22, bf16[256,896]{1,0:T(8,128)(2,1)S(1)} %coupling.1.matrix_ref, ...), custom_call_target="tpu_custom_call" | custom-call | bytes 21000000 | tf_op jit(solution)/shard_map/operator/pallas_call | solution.py:384
  143.9 4.6 %collective-permute-done.10.refs_5_ = f32[24,32,256]{2,1,0:T(8,128)S(1)} collective-permute-done((f32[24,32,256]{2,1,0:T(8,128)S(1)}, f32[24,32,256]{2,1,0:T(8,128)S(1)}, u32[]{:S(2)}, u32[]{:S(2)}) %collective-permute-start.10) | collective-permute-done | bytes 786464 | tf_op jit(solution)/shard_map/ppermute | solution.py:475
  150.5 7.4 %operator.5 = (f32[8,32,256]{2,1,0:T(8,128)S(1)}, f32[8,32,256]{2,1,0:T(8,128)}, f32[8,32,256]{2,1,0:T(8,128)}, f32[8,32,256]{2,1,0:T(8,128)}) custom-call(s32[1]{0:T(128)} %bitcast.me_ref, f32[7,64,256]{2,1,0:T(8,128)S(1)} %bitcast.23, bf16[256,896]{1,0:T(8,128)(2,1)S(1)} %coupling.1.matrix_ref, f32[40,32,256]{2,1,0:T(8,128)} %pack_own.1.refs_0_.refs_7_.refs_11_.refs_15_, ...), custom_call_target="tpu_custom_call" | custom-call | bytes 21000000 | tf_op jit(solution)/shard_map/operator/pallas_call | solution.py:384
  159.4 2.4 %collective-permute-start.13 = (f32[8,32,256]{2,1,0:T(8,128)}, f32[8,32,256]{2,1,0:T(8,128)S(1)}, u32[]{:S(2)}, u32[]{:S(2)}) collective-permute-start(f32[8,32,256]{2,1,0:T(8,128)} %get-tuple-element.38), channel_id=1, source_target_pairs={{0,3},{1,0},{2,1},{3,2},{4,7},{5,4},{6,5},{7,6},{8,11},{9,8},{10,9... | collective-permute-start | bytes 786440 | tf_op jit(solution)/shard_map/ppermute | solution.py:472
  161.8 9.4 %collective-permute-start.14 = (f32[8,32,256]{2,1,0:T(8,128)}, f32[8,32,256]{2,1,0:T(8,128)S(1)}, u32[]{:S(2)}, u32[]{:S(2)}) collective-permute-start(f32[8,32,256]{2,1,0:T(8,128)} %get-tuple-element.39), channel_id=1, source_target_pairs={{0,2},{1,3},{2,0},{3,1},{4,6},{5,7},{6,4},{7,5},{8,10},{9,11},{10,... | collective-permute-start | bytes 786440 | tf_op jit(solution)/shard_map/ppermute | solution.py:472
  171.2 7.5 %collective-permute-done.24.refs_3_ = f32[8,32,256]{2,1,0:T(8,128)S(1)} collective-permute-done((f32[8,32,256]{2,1,0:T(8,128)S(1)}, f32[8,32,256]{2,1,0:T(8,128)S(1)}, u32[]{:S(2)}, u32[]{:S(2)}) %collective-permute-start.24) | collective-permute-done | bytes 262176 | tf_op jit(solution)/shard_map/ppermute | solution.py:472
  179.4 9.4 %collective-permute-start.21 = (f32[8,32,256]{2,1,0:T(8,128)}, f32[8,32,256]{2,1,0:T(8,128)S(1)}, u32[]{:S(2)}, u32[]{:S(2)}) collective-permute-start(f32[8,32,256]{2,1,0:T(8,128)} %get-tuple-element.43), channel_id=1, source_target_pairs={{0,2},{1,3},{2,0},{3,1},{4,6},{5,7},{6,4},{7,5},{8,10},{9,11},{10,... | collective-permute-start | bytes 786440 | tf_op jit(solution)/shard_map/ppermute | solution.py:472
  190.6 2.4 %finish.4 = (f32[32,64,256]{2,1,0:T(8,128)}, f32[32,64,256]{2,1,0:T(8,128)}) custom-call(s32[1]{0:T(128)} %bitcast.me_ref, f32[4,8,32,256]{3,2,1,0:T(8,128)} %all-to-all-done.1.refs_0_.refs_1_, f32[4,8,32,256]{3,2,1,0:T(8,128)} %all-to-all-done.1.refs_0_.refs_1_, f32[32,64,256]{2,1,0:T(8,128)} %bitcast.30, f32[32,64,256]{2,1,0:T(8,128)} %bitcast.34), custom_call_target="tpu_custom_call" | custom-call | bytes 8750000 | tf_op jit(solution)/shard_map/finish/pallas_call | solution.py:443
  193.0 2.5 %finish.5 = (f32[32,64,256]{2,1,0:T(8,128)}, f32[32,64,256]{2,1,0:T(8,128)}) custom-call(s32[1]{0:T(128)} %bitcast.me_ref, f32[8,32,256]{2,1,0:T(8,128)} %copy-done.7, f32[8,32,256]{2,1,0:T(8,128)} %copy-done.15, f32[8,32,256]{2,1,0:T(8,128)} %copy-done.16, f32[8,32,256]{2,1,0:T(8,128)} %copy-done.18, ...), custom_call_target="tpu_custom_call", output_to_operand_aliasing={{0}: (7, {}), {1}: (8, {})} | custom-call | bytes 8750000 | tf_op jit(solution)/shard_map/finish/pallas_call | solution.py:443
  195.5 11.2 %collective-permute-done.21.refs_3_ = f32[8,32,256]{2,1,0:T(8,128)S(1)} collective-permute-done((f32[8,32,256]{2,1,0:T(8,128)}, f32[8,32,256]{2,1,0:T(8,128)S(1)}, u32[]{:S(2)}, u32[]{:S(2)}) %collective-permute-start.21) | collective-permute-done | bytes 262176 | tf_op jit(solution)/shard_map/ppermute | solution.py:472
  207.4 2.5 %finish.6 = (f32[32,64,256]{2,1,0:T(8,128)}, f32[32,64,256]{2,1,0:T(8,128)}) custom-call(s32[1]{0:T(128)} %bitcast.me_ref, f32[8,32,256]{2,1,0:T(8,128)} %copy-done.9, f32[8,32,256]{2,1,0:T(8,128)} %copy-done.17, f32[8,32,256]{2,1,0:T(8,128)} %copy-done.22, f32[8,32,256]{2,1,0:T(8,128)} %copy-done.23, ...), custom_call_target="tpu_custom_call", output_to_operand_aliasing={{0}: (7, {}), {1}: (8, {})} | custom-call | bytes 8750000 | tf_op jit(solution)/shard_map/finish/pallas_call | solution.py:443
  210.9 2.5 %finish.7 = (f32[32,64,256]{2,1,0:T(8,128)}, f32[32,64,256]{2,1,0:T(8,128)}) custom-call(s32[1]{0:T(128)} %bitcast.me_ref, f32[8,32,256]{2,1,0:T(8,128)} %copy-done.8, f32[8,32,256]{2,1,0:T(8,128)} %copy-done.19, f32[8,32,256]{2,1,0:T(8,128)} %copy-done.20, f32[8,32,256]{2,1,0:T(8,128)} %copy-done.21, ...), custom_call_target="tpu_custom_call", output_to_operand_aliasing={{0}: (7, {}), {1}: (8, {})} | custom-call | bytes 8750000 | tf_op jit(solution)/shard_map/finish/pallas_call | solution.py:443
  (89 shorter events, 25.4 us)
Async XLA Ops:
  3.3 45.8 %all-to-all-start = ((f32[4,9,32,256]{3,2,1,0:T(8,128)}), f32[4,9,32,256]{3,2,1,0:T(8,128)}, u32[]{:S(2)}, u32[]{:S(2)}) async-start(f32[4,9,32,256]{3,2,1,0:T(8,128)} %pack_all.1.refs_0_), calls=%async_computation | async-start | bytes 2359296 | tf_op jit(solution)/shard_map/all_to_all | solution.py:488
  10.7 39.6 %collective-permute-start = (f32[40,32,256]{2,1,0:T(8,128)}, f32[40,32,256]{2,1,0:T(8,128)S(1)}, u32[]{:S(2)}, u32[]{:S(2)}) collective-permute-start(f32[40,32,256]{2,1,0:T(8,128)} %pack_own.1.refs_0_.refs_7_.refs_11_.refs_15_), channel_id=1, source_target_pairs={{0,4},{4,8},{8,12},{12,16},{16,20},{20,24},{24,28},{1,5},{5,9},{9,... | collective-permute-start | bytes 3932168 | tf_op jit(solution)/shard_map/ppermute | solution.py:475
  12.6 37.7 %collective-permute-start.1 = (f32[40,32,256]{2,1,0:T(8,128)}, f32[40,32,256]{2,1,0:T(8,128)S(1)}, u32[]{:S(2)}, u32[]{:S(2)}) collective-permute-start(f32[40,32,256]{2,1,0:T(8,128)} %pack_own.1.refs_0_.refs_7_.refs_11_.refs_15_), channel_id=1, source_target_pairs={{4,0},{8,4},{12,8},{16,12},{20,16},{24,20},{28,24},{5,1},{9,5},{13... | collective-permute-start | bytes 3932168 | tf_op jit(solution)/shard_map/ppermute | solution.py:475
  19.8 38.8 %collective-permute-start.5 = (f32[16,32,256]{2,1,0:T(8,128)}, f32[16,32,256]{2,1,0:T(8,128)S(1)}, u32[]{:S(2)}, u32[]{:S(2)}) collective-permute-start(f32[16,32,256]{2,1,0:T(8,128)} %get-tuple-element.32), channel_id=1, source_target_pairs={{0,1},{1,2},{2,3},{3,0},{4,5},{5,6},{6,7},{7,4},{8,9},{9,10},{10,1... | collective-permute-start | bytes 1572872 | tf_op jit(solution)/shard_map/ppermute | solution.py:472
  21.9 36.8 %collective-permute-start.6 = (f32[16,32,256]{2,1,0:T(8,128)}, f32[16,32,256]{2,1,0:T(8,128)}, u32[]{:S(2)}, u32[]{:S(2)}) collective-permute-start(f32[16,32,256]{2,1,0:T(8,128)} %get-tuple-element.33), channel_id=1, source_target_pairs={{0,3},{1,0},{2,1},{3,2},{4,7},{5,4},{6,5},{7,6},{8,11},{9,8},{10,9... | collective-permute-start | bytes 1572872 | tf_op jit(solution)/shard_map/ppermute | solution.py:472
  23.7 58.0 %collective-permute-start.7 = (f32[16,32,256]{2,1,0:T(8,128)}, f32[16,32,256]{2,1,0:T(8,128)}, u32[]{:S(2)}, u32[]{:S(2)}) collective-permute-start(f32[16,32,256]{2,1,0:T(8,128)} %get-tuple-element.34), channel_id=1, source_target_pairs={{0,2},{1,3},{2,0},{3,1},{4,6},{5,7},{6,4},{7,5},{8,10},{9,11},{10,... | collective-permute-start | bytes 1572872 | tf_op jit(solution)/shard_map/ppermute | solution.py:472
  50.3 46.5 %copy-start.3 = (f32[9,32,256]{2,1,0:T(8,128)}, f32[9,32,256]{2,1,0:T(8,128)S(1)}, u32[]{:S(2)}) copy-start(f32[9,32,256]{2,1,0:T(8,128)S(1)} %get-tuple-element.59.refs_1_.refs_13_.refs_17_.refs_9_) | copy-start | bytes 884740
  52.1 40.4 %collective-permute-start.15 = (f32[24,32,256]{2,1,0:T(8,128)}, f32[24,32,256]{2,1,0:T(8,128)}, u32[]{:S(2)}, u32[]{:S(2)}) collective-permute-start(f32[24,32,256]{2,1,0:T(8,128)} %gather.4.refs_0_.refs_3_), channel_id=1, source_target_pairs={{0,4},{4,8},{8,12},{12,16},{16,20},{20,24},{24,28},{1,5},{5,9},{9,... | collective-permute-start | bytes 2359304 | tf_op jit(solution)/shard_map/ppermute | solution.py:475
  54.1 42.3 %collective-permute-start.16 = (f32[24,32,256]{2,1,0:T(8,128)}, f32[24,32,256]{2,1,0:T(8,128)}, u32[]{:S(2)}, u32[]{:S(2)}) collective-permute-start(f32[24,32,256]{2,1,0:T(8,128)} %gather.4.refs_0_.refs_3_), channel_id=1, source_target_pairs={{4,0},{8,4},{12,8},{16,12},{20,16},{24,20},{28,24},{5,1},{9,5},{13... | collective-permute-start | bytes 2359304 | tf_op jit(solution)/shard_map/ppermute | solution.py:475
  83.8 26.2 %collective-permute-start.8 = (f32[24,32,256]{2,1,0:T(8,128)}, f32[24,32,256]{2,1,0:T(8,128)}, u32[]{:S(2)}, u32[]{:S(2)}) collective-permute-start(f32[24,32,256]{2,1,0:T(8,128)} %gather.5), channel_id=1, source_target_pairs={{0,4},{4,8},{8,12},{12,16},{16,20},{20,24},{24,28},{1,5},{5,9},{9,... | collective-permute-start | bytes 2359304 | tf_op jit(solution)/shard_map/ppermute | solution.py:475
  85.8 26.1 %collective-permute-start.9 = (f32[24,32,256]{2,1,0:T(8,128)}, f32[24,32,256]{2,1,0:T(8,128)}, u32[]{:S(2)}, u32[]{:S(2)}) collective-permute-start(f32[24,32,256]{2,1,0:T(8,128)} %gather.5), channel_id=1, source_target_pairs={{4,0},{8,4},{12,8},{16,12},{20,16},{24,20},{28,24},{5,1},{9,5},{13... | collective-permute-start | bytes 2359304 | tf_op jit(solution)/shard_map/ppermute | solution.py:475
  92.5 31.2 %collective-permute-start.2 = (f32[8,32,256]{2,1,0:T(8,128)}, f32[8,32,256]{2,1,0:T(8,128)S(1)}, u32[]{:S(2)}, u32[]{:S(2)}) collective-permute-start(f32[8,32,256]{2,1,0:T(8,128)} %get-tuple-element.29), channel_id=1, source_target_pairs={{0,1},{1,2},{2,3},{3,0},{4,5},{5,6},{6,7},{7,4},{8,9},{9,10},{10,1... | collective-permute-start | bytes 786440 | tf_op jit(solution)/shard_map/ppermute | solution.py:472
  92.5 31.1 %collective-permute-start.3 = (f32[8,32,256]{2,1,0:T(8,128)}, f32[8,32,256]{2,1,0:T(8,128)S(1)}, u32[]{:S(2)}, u32[]{:S(2)}) collective-permute-start(f32[8,32,256]{2,1,0:T(8,128)} %get-tuple-element.30), channel_id=1, source_target_pairs={{0,3},{1,0},{2,1},{3,2},{4,7},{5,4},{6,5},{7,6},{8,11},{9,8},{10,9... | collective-permute-start | bytes 786440 | tf_op jit(solution)/shard_map/ppermute | solution.py:472
  96.3 29.5 %collective-permute-start.4 = (f32[8,32,256]{2,1,0:T(8,128)}, f32[8,32,256]{2,1,0:T(8,128)S(1)}, u32[]{:S(2)}, u32[]{:S(2)}) collective-permute-start(f32[8,32,256]{2,1,0:T(8,128)} %get-tuple-element.31), channel_id=1, source_target_pairs={{0,2},{1,3},{2,0},{3,1},{4,6},{5,7},{6,4},{7,5},{8,10},{9,11},{10,... | collective-permute-start | bytes 786440 | tf_op jit(solution)/shard_map/ppermute | solution.py:472
  104.6 86.0 %all-to-all-start.1 = ((f32[4,8,32,256]{3,2,1,0:T(8,128)}), f32[4,8,32,256]{3,2,1,0:T(8,128)}, u32[]{:S(2)}, u32[]{:S(2)}) async-start(f32[4,8,32,256]{3,2,1,0:T(8,128)} %operator.6.refs_3_), calls=%async_computation.1 | async-start | bytes 2097152 | tf_op jit(solution)/shard_map/all_to_all | solution.py:523
  110.0 22.4 %collective-permute-start.17 = (f32[24,32,256]{2,1,0:T(8,128)S(1)}, f32[24,32,256]{2,1,0:T(8,128)S(1)}, u32[]{:S(2)}, u32[]{:S(2)}) collective-permute-start(f32[24,32,256]{2,1,0:T(8,128)S(1)} %gather.7), channel_id=1, source_target_pairs={{0,4},{4,8},{8,12},{12,16},{16,20},{20,24},{24,28},{1,5},{5,9},{9,... | collective-permute-start | bytes 2359304 | tf_op jit(solution)/shard_map/ppermute | solution.py:475
  112.0 24.3 %collective-permute-start.18 = (f32[24,32,256]{2,1,0:T(8,128)S(1)}, f32[24,32,256]{2,1,0:T(8,128)S(1)}, u32[]{:S(2)}, u32[]{:S(2)}) collective-permute-start(f32[24,32,256]{2,1,0:T(8,128)S(1)} %gather.7), channel_id=1, source_target_pairs={{4,0},{8,4},{12,8},{16,12},{20,16},{24,20},{28,24},{5,1},{9,5},{13... | collective-permute-start | bytes 2359304 | tf_op jit(solution)/shard_map/ppermute | solution.py:475
  125.9 22.7 %collective-permute-start.10 = (f32[24,32,256]{2,1,0:T(8,128)S(1)}, f32[24,32,256]{2,1,0:T(8,128)S(1)}, u32[]{:S(2)}, u32[]{:S(2)}) collective-permute-start(f32[24,32,256]{2,1,0:T(8,128)S(1)} %gather.6), channel_id=1, source_target_pairs={{0,4},{4,8},{8,12},{12,16},{16,20},{20,24},{24,28},{1,5},{5,9},{9,... | collective-permute-start | bytes 2359304 | tf_op jit(solution)/shard_map/ppermute | solution.py:475
  127.8 21.8 %collective-permute-start.11 = (f32[24,32,256]{2,1,0:T(8,128)S(1)}, f32[24,32,256]{2,1,0:T(8,128)S(1)}, u32[]{:S(2)}, u32[]{:S(2)}) collective-permute-start(f32[24,32,256]{2,1,0:T(8,128)S(1)} %gather.6), channel_id=1, source_target_pairs={{4,0},{8,4},{12,8},{16,12},{20,16},{24,20},{28,24},{5,1},{9,5},{13... | collective-permute-start | bytes 2359304 | tf_op jit(solution)/shard_map/ppermute | solution.py:475
  132.4 27.0 %collective-permute-start.22 = (f32[8,32,256]{2,1,0:T(8,128)S(1)}, f32[8,32,256]{2,1,0:T(8,128)S(1)}, u32[]{:S(2)}, u32[]{:S(2)}) collective-permute-start(f32[8,32,256]{2,1,0:T(8,128)S(1)} %get-tuple-element.44), channel_id=1, source_target_pairs={{0,1},{1,2},{2,3},{3,0},{4,5},{5,6},{6,7},{7,4},{8,9},{9,10},{10,1... | collective-permute-start | bytes 786440 | tf_op jit(solution)/shard_map/ppermute | solution.py:472
  132.4 29.3 %collective-permute-start.23 = (f32[8,32,256]{2,1,0:T(8,128)S(1)}, f32[8,32,256]{2,1,0:T(8,128)S(1)}, u32[]{:S(2)}, u32[]{:S(2)}) collective-permute-start(f32[8,32,256]{2,1,0:T(8,128)S(1)} %get-tuple-element.45), channel_id=1, source_target_pairs={{0,3},{1,0},{2,1},{3,2},{4,7},{5,4},{6,5},{7,6},{8,11},{9,8},{10,9... | collective-permute-start | bytes 786440 | tf_op jit(solution)/shard_map/ppermute | solution.py:472
  136.2 42.4 %collective-permute-start.24 = (f32[8,32,256]{2,1,0:T(8,128)S(1)}, f32[8,32,256]{2,1,0:T(8,128)S(1)}, u32[]{:S(2)}, u32[]{:S(2)}) collective-permute-start(f32[8,32,256]{2,1,0:T(8,128)S(1)} %get-tuple-element.46), channel_id=1, source_target_pairs={{0,2},{1,3},{2,0},{3,1},{4,6},{5,7},{6,4},{7,5},{8,10},{9,11},{10,... | collective-permute-start | bytes 786440 | tf_op jit(solution)/shard_map/ppermute | solution.py:472
  148.6 40.3 %copy-start.12 = (f32[32,1,64,256]{3,2,1,0:T(8,128)S(1)}, f32[32,1,64,256]{3,2,1,0:T(8,128)}, u32[]{:S(2)}) copy-start(f32[32,1,64,256]{3,2,1,0:T(8,128)} %param.7) | copy-start | bytes 6291460
  148.6 40.3 %copy-start.13 = (f32[32,1,64,256]{3,2,1,0:T(8,128)S(1)}, f32[32,1,64,256]{3,2,1,0:T(8,128)}, u32[]{:S(2)}) copy-start(f32[32,1,64,256]{3,2,1,0:T(8,128)} %param.8) | copy-start | bytes 6291460
  148.6 30.1 %collective-permute-start.19 = (f32[8,32,256]{2,1,0:T(8,128)S(1)}, f32[8,32,256]{2,1,0:T(8,128)S(1)}, u32[]{:S(2)}, u32[]{:S(2)}) collective-permute-start(f32[8,32,256]{2,1,0:T(8,128)S(1)} %get-tuple-element.41), channel_id=1, source_target_pairs={{0,1},{1,2},{2,3},{3,0},{4,5},{5,6},{6,7},{7,4},{8,9},{9,10},{10,1... | collective-permute-start | bytes 786440 | tf_op jit(solution)/shard_map/ppermute | solution.py:472
  157.9 32.7 %copy-start.8 = (f32[8,32,256]{2,1,0:T(8,128)}, f32[8,32,256]{2,1,0:T(8,128)S(1)}, u32[]{:S(2)}) copy-start(f32[8,32,256]{2,1,0:T(8,128)S(1)} %get-tuple-element.36.refs_0_) | copy-start | bytes 786436
  157.9 52.1 %collective-permute-start.12 = (f32[8,32,256]{2,1,0:T(8,128)}, f32[8,32,256]{2,1,0:T(8,128)S(1)}, u32[]{:S(2)}, u32[]{:S(2)}) collective-permute-start(f32[8,32,256]{2,1,0:T(8,128)} %get-tuple-element.37), channel_id=1, source_target_pairs={{0,1},{1,2},{2,3},{3,0},{4,5},{5,6},{6,7},{7,4},{8,9},{9,10},{10,1... | collective-permute-start | bytes 786440 | tf_op jit(solution)/shard_map/ppermute | solution.py:472
  159.4 31.2 %copy-start.15 = (f32[8,32,256]{2,1,0:T(8,128)}, f32[8,32,256]{2,1,0:T(8,128)S(1)}, u32[]{:S(2)}) copy-start(f32[8,32,256]{2,1,0:T(8,128)S(1)} %collective-permute-done.22.refs_1_) | copy-start | bytes 786436
  159.4 50.6 %collective-permute-start.13 = (f32[8,32,256]{2,1,0:T(8,128)}, f32[8,32,256]{2,1,0:T(8,128)S(1)}, u32[]{:S(2)}, u32[]{:S(2)}) collective-permute-start(f32[8,32,256]{2,1,0:T(8,128)} %get-tuple-element.38), channel_id=1, source_target_pairs={{0,3},{1,0},{2,1},{3,2},{4,7},{5,4},{6,5},{7,6},{8,11},{9,8},{10,9... | collective-permute-start | bytes 786440 | tf_op jit(solution)/shard_map/ppermute | solution.py:472
  161.8 48.2 %collective-permute-start.14 = (f32[8,32,256]{2,1,0:T(8,128)}, f32[8,32,256]{2,1,0:T(8,128)S(1)}, u32[]{:S(2)}, u32[]{:S(2)}) collective-permute-start(f32[8,32,256]{2,1,0:T(8,128)} %get-tuple-element.39), channel_id=1, source_target_pairs={{0,2},{1,3},{2,0},{3,1},{4,6},{5,7},{6,4},{7,5},{8,10},{9,11},{10,... | collective-permute-start | bytes 786440 | tf_op jit(solution)/shard_map/ppermute | solution.py:472
  178.7 16.8 %collective-permute-start.20 = (f32[8,32,256]{2,1,0:T(8,128)}, f32[8,32,256]{2,1,0:T(8,128)S(1)}, u32[]{:S(2)}, u32[]{:S(2)}) collective-permute-start(f32[8,32,256]{2,1,0:T(8,128)} %get-tuple-element.42), channel_id=1, source_target_pairs={{0,3},{1,0},{2,1},{3,2},{4,7},{5,4},{6,5},{7,6},{8,11},{9,8},{10,9... | collective-permute-start | bytes 786440 | tf_op jit(solution)/shard_map/ppermute | solution.py:472
  179.4 27.3 %collective-permute-start.21 = (f32[8,32,256]{2,1,0:T(8,128)}, f32[8,32,256]{2,1,0:T(8,128)S(1)}, u32[]{:S(2)}, u32[]{:S(2)}) collective-permute-start(f32[8,32,256]{2,1,0:T(8,128)} %get-tuple-element.43), channel_id=1, source_target_pairs={{0,2},{1,3},{2,0},{3,1},{4,6},{5,7},{6,4},{7,5},{8,10},{9,11},{10,... | collective-permute-start | bytes 786440 | tf_op jit(solution)/shard_map/ppermute | solution.py:472
  (19 other events, 141.7 us)

commit v12 on v7

--- a/solution.py
+++ b/solution.py
@@ -462,7 +462,7 @@
     forward = [(i, i + 1) for i in range(planes - 1)]
     backward = [(i + 1, i) for i in range(planes - 1)]
     me = lax.axis_index("mode").astype(jnp.int32).reshape(1)
-    shifts = sorted(range(1, owners), key=lambda s: min(s, owners - s))
+    shifts = sorted(range(1, owners), key=lambda s: -min(s, owners - s))
 
     def move(array, shift):
         return lax.ppermute(array, "mode", [(i, (i + shift) % owners) for i in range(owners)])

time: 212 us -> 210 us (level)
  waiting for transfers between devices: 77.3 us -> 40.4 us
  starting transfers between devices: 66.1 us -> 98.2 us
    ppermute x18, starting transfers between devices: 24.3 us -> 56.4 us  [move(): lax.ppermute(array, 'mode', [(i, (i + shift) % owners) for i in range(own...]
    ppermute x18, waiting for transfers between devices: 39.2 us -> 11.2 us  [move(): lax.ppermute(array, 'mode', [(i, (i + shift) % owners) for i in range(own...]
    ppermute x5, waiting for transfers between devices: 6.65 us -> 1.63 us  [beside(): lax.ppermute(array, 'space', forward)]
  transfers between devices with their start and end apart: 30 -> 30, of which waited for: 13 -> 7; matrix products, arithmetic and copies ran while one was open for 2% -> 2% of each run, Pallas kernels for 23% -> 24%
where the time goes in v12:
time: 210 us; the launch traced here: 207 us
  starting transfers between devices  98.2 us (47%)
  Pallas kernels  53.9 us (26%)
  waiting for transfers between devices  40.4 us (19%)
  local copies, waits for them, and re-layouts  9.8 us (5%)
  other arithmetic  3.21 us (2%)
    ppermute x18, starting transfers between devices, move(): lax.ppermute(array, 'mode', [(i, (i + shift) % owners) for i in range(own...  56.4 us
    pallas_call x4, Pallas kernels, apply_operator(): pl.pallas_call(functools.partial(operator_kernel, shifts, terms, part, pa...  26.7 us
    all_to_all x1, waiting for transfers between devices, shards(): everyone = lax.all_to_all(packed, 'mode', 0, 0, tiled=True)  23 us
    ppermute x5, starting transfers between devices, beside(): lax.ppermute(array, 'space', backward)  22.7 us
    ppermute x18, waiting for transfers between devices, move(): lax.ppermute(array, 'mode', [(i, (i + shift) % owners) for i in range(own...  11.2 us
    pallas_call x4, Pallas kernels, finish(): pl.pallas_call(functools.partial(finish_kernel, shifts, by_owner), grid=(...  9.97 us
    ppermute x5, starting transfers between devices, beside(): lax.ppermute(array, 'space', forward)  9.71 us
    unnamed x46, local copies, waits for them, and re-layouts  8.6 us
  transfers between devices with their start and end apart: 30, of which 7 were waited for; matrix products, arithmetic and copies ran while one was open for 2% of the time, Pallas kernels for 24%

profile of v12, /device:TPU:4, one launch (start us, length us, event | category | flops | bytes accessed | tf_op | source)
XLA Modules:
  0.0 206.5 jit_solution(9763855143873047047)
XLA Ops:
  0.6 2.6 %pack_all.1.refs_0_ = f32[4,9,32,256]{3,2,1,0:T(8,128)} custom-call(f32[32,64,256]{2,1,0:T(8,128)} %bitcast.26, f32[32,64,256]{2,1,0:T(8,128)} %bitcast.35), custom_call_target="tpu_custom_call" | custom-call | bytes 10500000 | tf_op jit(solution)/shard_map/pack_all/pallas_call | solution.py:179
  3.3 4.9 %all-to-all-start = ((f32[4,9,32,256]{3,2,1,0:T(8,128)}), f32[4,9,32,256]{3,2,1,0:T(8,128)}, u32[]{:S(2)}, u32[]{:S(2)}) async-start(f32[4,9,32,256]{3,2,1,0:T(8,128)} %pack_all.1.refs_0_), calls=%async_computation | async-start | bytes 2359296 | tf_op jit(solution)/shard_map/all_to_all | solution.py:492
  8.1 2.6 %pack_own.1.refs_0_.refs_7_.refs_11_.refs_15_ = f32[40,32,256]{2,1,0:T(8,128)} custom-call(s32[1]{0:T(128)} %bitcast.me_ref, f32[32,64,256]{2,1,0:T(8,128)} %bitcast.27, f32[32,64,256]{2,1,0:T(8,128)} %bitcast.36, f32[7,64,256]{2,1,0:T(8,128)} %bitcast.19, f32[4,9,32,256]{3,2,1,0:T(8,128)} %pack_all.1.refs_0_), custom_call_target="tpu_custom_call" | custom-call | bytes 10500000 | tf_op jit(solution)/shard_map/pack_own/pallas_call | solution.py:223
  12.6 4.5 %collective-permute-start.1 = (f32[40,32,256]{2,1,0:T(8,128)}, f32[40,32,256]{2,1,0:T(8,128)S(1)}, u32[]{:S(2)}, u32[]{:S(2)}) collective-permute-start(f32[40,32,256]{2,1,0:T(8,128)} %pack_own.1.refs_0_.refs_7_.refs_11_.refs_15_), channel_id=1, source_target_pairs={{4,0},{8,4},{12,8},{16,12},{20,16},{24,20},{28,24},{5,1},{9,5},{13... | collective-permute-start | bytes 3932168 | tf_op jit(solution)/shard_map/ppermute | solution.py:471
  19.3 3.0 %collective-permute-start.4 = (f32[8,32,256]{2,1,0:T(8,128)}, f32[8,32,256]{2,1,0:T(8,128)}, u32[]{:S(2)}, u32[]{:S(2)}) collective-permute-start(f32[8,32,256]{2,1,0:T(8,128)} %get-tuple-element.32), channel_id=1, source_target_pairs={{0,2},{1,3},{2,0},{3,1},{4,6},{5,7},{6,4},{7,5},{8,10},{9,11},{10,... | collective-permute-start | bytes 786440 | tf_op jit(solution)/shard_map/ppermute | solution.py:468
  23.7 2.4 %collective-permute-start.6 = (f32[8,32,256]{2,1,0:T(8,128)}, f32[8,32,256]{2,1,0:T(8,128)}, u32[]{:S(2)}, u32[]{:S(2)}) collective-permute-start(f32[8,32,256]{2,1,0:T(8,128)} %get-tuple-element.34), channel_id=1, source_target_pairs={{0,3},{1,0},{2,1},{3,2},{4,7},{5,4},{6,5},{7,6},{8,11},{9,8},{10,9... | collective-permute-start | bytes 786440 | tf_op jit(solution)/shard_map/ppermute | solution.py:468
  26.1 23.0 %all-to-all-done = f32[4,9,32,256]{3,2,1,0:T(8,128)} async-done(((f32[4,9,32,256]{3,2,1,0:T(8,128)}), f32[4,9,32,256]{3,2,1,0:T(8,128)}, u32[]{:S(2)}, u32[]{:S(2)}) %all-to-all-start) | async-done | bytes 1179680 | tf_op jit(solution)/shard_map/all_to_all | solution.py:492
  54.0 4.5 %collective-permute-start.3 = (f32[24,32,256]{2,1,0:T(8,128)}, f32[24,32,256]{2,1,0:T(8,128)}, u32[]{:S(2)}, u32[]{:S(2)}) collective-permute-start(f32[24,32,256]{2,1,0:T(8,128)} %gather.4.refs_0_), channel_id=1, source_target_pairs={{4,0},{8,4},{12,8},{16,12},{20,16},{24,20},{28,24},{5,1},{9,5},{13... | collective-permute-start | bytes 2359304 | tf_op jit(solution)/shard_map/ppermute | solution.py:471
  62.7 4.5 %collective-permute-start.11 = (f32[24,32,256]{2,1,0:T(8,128)}, f32[24,32,256]{2,1,0:T(8,128)S(1)}, u32[]{:S(2)}, u32[]{:S(2)}) collective-permute-start(f32[24,32,256]{2,1,0:T(8,128)} %gather.5), channel_id=1, source_target_pairs={{4,0},{8,4},{12,8},{16,12},{20,16},{24,20},{28,24},{5,1},{9,5},{13... | collective-permute-start | bytes 2359304 | tf_op jit(solution)/shard_map/ppermute | solution.py:471
  67.2 2.1 %pack.5 = (f32[8,32,256]{2,1,0:T(8,128)}, f32[8,32,256]{2,1,0:T(8,128)}, f32[8,32,256]{2,1,0:T(8,128)}) custom-call(s32[1]{0:T(128)} %bitcast.me_ref, f32[32,64,256]{2,1,0:T(8,128)} %bitcast.29, f32[32,64,256]{2,1,0:T(8,128)} %bitcast.38, f32[24,32,256]{2,1,0:T(8,128)} %gather.4.refs_0_), custom_call_target="tpu_custom_call" | custom-call | bytes 10500000 | tf_op jit(solution)/shard_map/pack/pallas_call | solution.py:128
  72.4 4.4 %collective-permute-done.3.refs_6_ = f32[24,32,256]{2,1,0:T(8,128)} collective-permute-done((f32[24,32,256]{2,1,0:T(8,128)}, f32[24,32,256]{2,1,0:T(8,128)}, u32[]{:S(2)}, u32[]{:S(2)}) %collective-permute-start.3) | collective-permute-done | bytes 786464 | tf_op jit(solution)/shard_map/ppermute | solution.py:471
  78.7 6.5 %operator.4.refs_0_.refs_3_ = f32[4,8,32,256]{3,2,1,0:T(8,128)S(1)} custom-call(s32[1]{0:T(128)} %bitcast.me_ref, f32[7,64,256]{2,1,0:T(8,128)S(1)} %bitcast.20, bf16[256,896]{1,0:T(8,128)(2,1)S(1)} %coupling.1.matrix_ref, f32[40,32,256]{2,1,0:T(8,128)} %pack_own.1.refs_0_.refs_7_.refs_11_.refs_15_, f32[40,32,256]{2,1,0:T(8,128)} %copy-done, ...), custom_call_target="tpu_custom_call" | custom-call | bytes 21000000 | tf_op jit(solution)/shard_map/operator/pallas_call | solution.py:380
  89.9 2.3 %collective-permute-start.8 = (f32[8,32,256]{2,1,0:T(8,128)}, f32[8,32,256]{2,1,0:T(8,128)}, u32[]{:S(2)}, u32[]{:S(2)}) collective-permute-start(f32[8,32,256]{2,1,0:T(8,128)} %get-tuple-element.36), channel_id=1, source_target_pairs={{0,1},{1,2},{2,3},{3,0},{4,5},{5,6},{6,7},{7,4},{8,9},{9,10},{10,1... | collective-permute-start | bytes 786440 | tf_op jit(solution)/shard_map/ppermute | solution.py:468
  93.8 4.5 %all-to-all-start.1 = ((f32[4,8,32,256]{3,2,1,0:T(8,128)}), f32[4,8,32,256]{3,2,1,0:T(8,128)}, u32[]{:S(2)}, u32[]{:S(2)}) async-start(f32[4,8,32,256]{3,2,1,0:T(8,128)} %copy-done.2), calls=%async_computation.1 | async-start | bytes 2097152 | tf_op jit(solution)/shard_map/all_to_all | solution.py:511
  100.6 6.5 %operator.5 = (f32[8,32,256]{2,1,0:T(8,128)S(1)}, f32[8,32,256]{2,1,0:T(8,128)S(1)}, f32[8,32,256]{2,1,0:T(8,128)S(1)}, f32[8,32,256]{2,1,0:T(8,128)S(1)}) custom-call(s32[1]{0:T(128)} %bitcast.me_ref, f32[7,64,256]{2,1,0:T(8,128)S(1)} %bitcast.21, bf16[256,896]{1,0:T(8,128)(2,1)S(1)} %coupling.1.matrix_ref, ...), custom_call_target="tpu_custom_call" | custom-call | bytes 21000000 | tf_op jit(solution)/shard_map/operator/pallas_call | solution.py:380
  110.2 4.5 %collective-permute-start.21 = (f32[24,32,256]{2,1,0:T(8,128)S(1)}, f32[24,32,256]{2,1,0:T(8,128)S(1)}, u32[]{:S(2)}, u32[]{:S(2)}) collective-permute-start(f32[24,32,256]{2,1,0:T(8,128)S(1)} %gather.7), channel_id=1, source_target_pairs={{4,0},{8,4},{12,8},{16,12},{20,16},{24,20},{28,24},{5,1},{9,5},{13... | collective-permute-start | bytes 2359304 | tf_op jit(solution)/shard_map/ppermute | solution.py:471
  114.7 6.1 %collective-permute-done.7.refs_0_.refs_8_.refs_16_ = f32[8,32,256]{2,1,0:T(8,128)} collective-permute-done((f32[8,32,256]{2,1,0:T(8,128)}, f32[8,32,256]{2,1,0:T(8,128)}, u32[]{:S(2)}, u32[]{:S(2)}) %collective-permute-start.7) | collective-permute-done | bytes 262176 | tf_op jit(solution)/shard_map/ppermute | solution.py:468
  123.9 4.5 %collective-permute-start.16 = (f32[24,32,256]{2,1,0:T(8,128)S(1)}, f32[24,32,256]{2,1,0:T(8,128)S(1)}, u32[]{:S(2)}, u32[]{:S(2)}) collective-permute-start(f32[24,32,256]{2,1,0:T(8,128)S(1)} %gather.6), channel_id=1, source_target_pairs={{4,0},{8,4},{12,8},{16,12},{20,16},{24,20},{28,24},{5,1},{9,5},{13... | collective-permute-start | bytes 2359304 | tf_op jit(solution)/shard_map/ppermute | solution.py:471
  128.5 9.1 %collective-permute-start.25 = (f32[8,32,256]{2,1,0:T(8,128)S(1)}, f32[8,32,256]{2,1,0:T(8,128)S(1)}, u32[]{:S(2)}, u32[]{:S(2)}) collective-permute-start(f32[8,32,256]{2,1,0:T(8,128)S(1)} %get-tuple-element.50), channel_id=1, source_target_pairs={{0,2},{1,3},{2,0},{3,1},{4,6},{5,7},{6,4},{7,5},{8,10},{9,11},{10,... | collective-permute-start | bytes 786440 | tf_op jit(solution)/shard_map/ppermute | solution.py:468
  137.5 5.1 %collective-permute-start.26 = (f32[8,32,256]{2,1,0:T(8,128)S(1)}, f32[8,32,256]{2,1,0:T(8,128)S(1)}, u32[]{:S(2)}, u32[]{:S(2)}) collective-permute-start(f32[8,32,256]{2,1,0:T(8,128)S(1)} %get-tuple-element.51), channel_id=1, source_target_pairs={{0,1},{1,2},{2,3},{3,0},{4,5},{5,6},{6,7},{7,4},{8,9},{9,10},{10,1... | collective-permute-start | bytes 786440 | tf_op jit(solution)/shard_map/ppermute | solution.py:468
  142.6 6.4 %operator.7 = (f32[8,32,256]{2,1,0:T(8,128)S(1)}, f32[8,32,256]{2,1,0:T(8,128)S(1)}, f32[8,32,256]{2,1,0:T(8,128)S(1)}, f32[8,32,256]{2,1,0:T(8,128)S(1)}) custom-call(s32[1]{0:T(128)} %bitcast.me_ref, f32[7,64,256]{2,1,0:T(8,128)S(1)} %bitcast.22, bf16[256,896]{1,0:T(8,128)(2,1)S(1)} %coupling.1.matrix_ref, ...), custom_call_target="tpu_custom_call" | custom-call | bytes 21000000 | tf_op jit(solution)/shard_map/operator/pallas_call | solution.py:380
  149.8 8.2 %collective-permute-start.22 = (f32[8,32,256]{2,1,0:T(8,128)S(1)}, f32[8,32,256]{2,1,0:T(8,128)S(1)}, u32[]{:S(2)}, u32[]{:S(2)}) collective-permute-start(f32[8,32,256]{2,1,0:T(8,128)S(1)} %get-tuple-element.47), channel_id=1, source_target_pairs={{0,2},{1,3},{2,0},{3,1},{4,6},{5,7},{6,4},{7,5},{8,10},{9,11},{10,... | collective-permute-start | bytes 786440 | tf_op jit(solution)/shard_map/ppermute | solution.py:468
  159.1 7.2 %operator.6 = (f32[8,32,256]{2,1,0:T(8,128)S(1)}, f32[8,32,256]{2,1,0:T(8,128)}, f32[8,32,256]{2,1,0:T(8,128)S(1)}, f32[8,32,256]{2,1,0:T(8,128)S(1)}) custom-call(s32[1]{0:T(128)} %bitcast.me_ref, f32[7,64,256]{2,1,0:T(8,128)S(1)} %bitcast.23, bf16[256,896]{1,0:T(8,128)(2,1)S(1)} %coupling.1.matrix_ref, ...), custom_call_target="tpu_custom_call" | custom-call | bytes 21000000 | tf_op jit(solution)/shard_map/operator/pallas_call | solution.py:380
  167.0 2.7 %collective-permute-start.24 = (f32[8,32,256]{2,1,0:T(8,128)S(1)}, f32[8,32,256]{2,1,0:T(8,128)S(1)}, u32[]{:S(2)}, u32[]{:S(2)}) collective-permute-start(f32[8,32,256]{2,1,0:T(8,128)S(1)} %get-tuple-element.49), channel_id=1, source_target_pairs={{0,3},{1,0},{2,1},{3,2},{4,7},{5,4},{6,5},{7,6},{8,11},{9,8},{10,9... | collective-permute-start | bytes 786440 | tf_op jit(solution)/shard_map/ppermute | solution.py:468
  169.8 5.2 %collective-permute-start.17 = (f32[8,32,256]{2,1,0:T(8,128)}, f32[8,32,256]{2,1,0:T(8,128)S(1)}, u32[]{:S(2)}, u32[]{:S(2)}) collective-permute-start(f32[8,32,256]{2,1,0:T(8,128)} %get-tuple-element.43), channel_id=1, source_target_pairs={{0,2},{1,3},{2,0},{3,1},{4,6},{5,7},{6,4},{7,5},{8,10},{9,11},{10,... | collective-permute-start | bytes 786440 | tf_op jit(solution)/shard_map/ppermute | solution.py:468
  175.0 10.9 %collective-permute-start.18 = (f32[8,32,256]{2,1,0:T(8,128)S(1)}, f32[8,32,256]{2,1,0:T(8,128)S(1)}, u32[]{:S(2)}, u32[]{:S(2)}) collective-permute-start(f32[8,32,256]{2,1,0:T(8,128)S(1)} %get-tuple-element.44), channel_id=1, source_target_pairs={{0,1},{1,2},{2,3},{3,0},{4,5},{5,6},{6,7},{7,4},{8,9},{9,10},{10,1... | collective-permute-start | bytes 786440 | tf_op jit(solution)/shard_map/ppermute | solution.py:468
  185.9 5.1 %collective-permute-done.22.refs_1_ = f32[8,32,256]{2,1,0:T(8,128)S(1)} collective-permute-done((f32[8,32,256]{2,1,0:T(8,128)S(1)}, f32[8,32,256]{2,1,0:T(8,128)S(1)}, u32[]{:S(2)}, u32[]{:S(2)}) %collective-permute-start.22) | collective-permute-done | bytes 262176 | tf_op jit(solution)/shard_map/ppermute | solution.py:468
  191.7 3.2 %multiply_subtract_fusion = f32[32,1,64,256]{3,2,1,0:T(8,128)} fusion(f32[32,1,64,256]{3,2,1,0:T(8,128)S(1)} %copy-done.14, f32[32,1,64,256]{3,2,1,0:T(8,128)} %param.7), kind=kLoop, calls=%fused_computation | loop fusion | flops 1048576 | bytes 6291456 | tf_op jit(solution)/shard_map/sub | solution.py:455
  194.9 2.4 %finish.4 = (f32[32,64,256]{2,1,0:T(8,128)}, f32[32,64,256]{2,1,0:T(8,128)}) custom-call(s32[1]{0:T(128)} %bitcast.me_ref, f32[4,8,32,256]{3,2,1,0:T(8,128)} %all-to-all-done.1.refs_0_.refs_1_, f32[4,8,32,256]{3,2,1,0:T(8,128)} %all-to-all-done.1.refs_0_.refs_1_, f32[32,64,256]{2,1,0:T(8,128)} %bitcast.31, f32[32,64,256]{2,1,0:T(8,128)} %bitcast.40), custom_call_target="tpu_custom_call" | custom-call | bytes 8750000 | tf_op jit(solution)/shard_map/finish/pallas_call | solution.py:439
  197.3 2.5 %finish.5 = (f32[32,64,256]{2,1,0:T(8,128)}, f32[32,64,256]{2,1,0:T(8,128)}) custom-call(s32[1]{0:T(128)} %bitcast.me_ref, f32[8,32,256]{2,1,0:T(8,128)} %copy-done.5, f32[8,32,256]{2,1,0:T(8,128)} %copy-done.15, f32[8,32,256]{2,1,0:T(8,128)} %copy-done.16, f32[8,32,256]{2,1,0:T(8,128)} %copy-done.17, ...), custom_call_target="tpu_custom_call", output_to_operand_aliasing={{0}: (7, {}), {1}: (8, {})} | custom-call | bytes 8750000 | tf_op jit(solution)/shard_map/finish/pallas_call | solution.py:439
  200.5 2.5 %finish.6 = (f32[32,64,256]{2,1,0:T(8,128)}, f32[32,64,256]{2,1,0:T(8,128)}) custom-call(s32[1]{0:T(128)} %bitcast.me_ref, f32[8,32,256]{2,1,0:T(8,128)} %copy-done.10, f32[8,32,256]{2,1,0:T(8,128)} %copy-done.18, f32[8,32,256]{2,1,0:T(8,128)} %collective-permute-done.23.refs_2_, ...), custom_call_target="tpu_custom_call", output_to_operand_aliasing={{0}: (7, {}), {1}: (8, {})} | custom-call | bytes 8750000 | tf_op jit(solution)/shard_map/finish/pallas_call | solution.py:439
  204.0 2.5 %finish.7 = (f32[32,64,256]{2,1,0:T(8,128)}, f32[32,64,256]{2,1,0:T(8,128)}) custom-call(s32[1]{0:T(128)} %bitcast.me_ref, f32[8,32,256]{2,1,0:T(8,128)} %copy-done.11, f32[8,32,256]{2,1,0:T(8,128)} %copy-done.19, f32[8,32,256]{2,1,0:T(8,128)} %copy-done.20, f32[8,32,256]{2,1,0:T(8,128)} %copy-done.22, ...), custom_call_target="tpu_custom_call", output_to_operand_aliasing={{0}: (7, {}), {1}: (8, {})} | custom-call | bytes 8750000 | tf_op jit(solution)/shard_map/finish/pallas_call | solution.py:439
  (94 shorter events, 38.8 us)
Async XLA Ops:
  3.3 45.8 %all-to-all-start = ((f32[4,9,32,256]{3,2,1,0:T(8,128)}), f32[4,9,32,256]{3,2,1,0:T(8,128)}, u32[]{:S(2)}, u32[]{:S(2)}) async-start(f32[4,9,32,256]{3,2,1,0:T(8,128)} %pack_all.1.refs_0_), calls=%async_computation | async-start | bytes 2359296 | tf_op jit(solution)/shard_map/all_to_all | solution.py:492
  10.7 39.6 %collective-permute-start = (f32[40,32,256]{2,1,0:T(8,128)}, f32[40,32,256]{2,1,0:T(8,128)S(1)}, u32[]{:S(2)}, u32[]{:S(2)}) collective-permute-start(f32[40,32,256]{2,1,0:T(8,128)} %pack_own.1.refs_0_.refs_7_.refs_11_.refs_15_), channel_id=1, source_target_pairs={{0,4},{4,8},{8,12},{12,16},{16,20},{20,24},{24,28},{1,5},{5,9},{9,... | collective-permute-start | bytes 3932168 | tf_op jit(solution)/shard_map/ppermute | solution.py:471
  12.6 37.7 %collective-permute-start.1 = (f32[40,32,256]{2,1,0:T(8,128)}, f32[40,32,256]{2,1,0:T(8,128)S(1)}, u32[]{:S(2)}, u32[]{:S(2)}) collective-permute-start(f32[40,32,256]{2,1,0:T(8,128)} %pack_own.1.refs_0_.refs_7_.refs_11_.refs_15_), channel_id=1, source_target_pairs={{4,0},{8,4},{12,8},{16,12},{20,16},{24,20},{28,24},{5,1},{9,5},{13... | collective-permute-start | bytes 3932168 | tf_op jit(solution)/shard_map/ppermute | solution.py:471
  19.3 39.3 %collective-permute-start.4 = (f32[8,32,256]{2,1,0:T(8,128)}, f32[8,32,256]{2,1,0:T(8,128)}, u32[]{:S(2)}, u32[]{:S(2)}) collective-permute-start(f32[8,32,256]{2,1,0:T(8,128)} %get-tuple-element.32), channel_id=1, source_target_pairs={{0,2},{1,3},{2,0},{3,1},{4,6},{5,7},{6,4},{7,5},{8,10},{9,11},{10,... | collective-permute-start | bytes 786440 | tf_op jit(solution)/shard_map/ppermute | solution.py:468
  22.2 36.3 %collective-permute-start.5 = (f32[8,32,256]{2,1,0:T(8,128)}, f32[8,32,256]{2,1,0:T(8,128)}, u32[]{:S(2)}, u32[]{:S(2)}) collective-permute-start(f32[8,32,256]{2,1,0:T(8,128)} %get-tuple-element.33), channel_id=1, source_target_pairs={{0,1},{1,2},{2,3},{3,0},{4,5},{5,6},{6,7},{7,4},{8,9},{9,10},{10,1... | collective-permute-start | bytes 786440 | tf_op jit(solution)/shard_map/ppermute | solution.py:468
  23.7 34.8 %collective-permute-start.6 = (f32[8,32,256]{2,1,0:T(8,128)}, f32[8,32,256]{2,1,0:T(8,128)}, u32[]{:S(2)}, u32[]{:S(2)}) collective-permute-start(f32[8,32,256]{2,1,0:T(8,128)} %get-tuple-element.34), channel_id=1, source_target_pairs={{0,3},{1,0},{2,1},{3,2},{4,7},{5,4},{6,5},{7,6},{8,11},{9,8},{10,9... | collective-permute-start | bytes 786440 | tf_op jit(solution)/shard_map/ppermute | solution.py:468
  52.0 20.1 %collective-permute-start.2 = (f32[24,32,256]{2,1,0:T(8,128)}, f32[24,32,256]{2,1,0:T(8,128)}, u32[]{:S(2)}, u32[]{:S(2)}) collective-permute-start(f32[24,32,256]{2,1,0:T(8,128)} %gather.4.refs_0_), channel_id=1, source_target_pairs={{0,4},{4,8},{8,12},{12,16},{16,20},{20,24},{24,28},{1,5},{5,9},{9,... | collective-permute-start | bytes 2359304 | tf_op jit(solution)/shard_map/ppermute | solution.py:471
  54.0 22.8 %collective-permute-start.3 = (f32[24,32,256]{2,1,0:T(8,128)}, f32[24,32,256]{2,1,0:T(8,128)}, u32[]{:S(2)}, u32[]{:S(2)}) collective-permute-start(f32[24,32,256]{2,1,0:T(8,128)} %gather.4.refs_0_), channel_id=1, source_target_pairs={{4,0},{8,4},{12,8},{16,12},{20,16},{24,20},{28,24},{5,1},{9,5},{13... | collective-permute-start | bytes 2359304 | tf_op jit(solution)/shard_map/ppermute | solution.py:471
  60.6 28.3 %collective-permute-start.10 = (f32[24,32,256]{2,1,0:T(8,128)}, f32[24,32,256]{2,1,0:T(8,128)S(1)}, u32[]{:S(2)}, u32[]{:S(2)}) collective-permute-start(f32[24,32,256]{2,1,0:T(8,128)} %gather.5), channel_id=1, source_target_pairs={{0,4},{4,8},{8,12},{12,16},{16,20},{20,24},{24,28},{1,5},{5,9},{9,... | collective-permute-start | bytes 2359304 | tf_op jit(solution)/shard_map/ppermute | solution.py:471
  62.7 27.3 %collective-permute-start.11 = (f32[24,32,256]{2,1,0:T(8,128)}, f32[24,32,256]{2,1,0:T(8,128)S(1)}, u32[]{:S(2)}, u32[]{:S(2)}) collective-permute-start(f32[24,32,256]{2,1,0:T(8,128)} %gather.5), channel_id=1, source_target_pairs={{4,0},{8,4},{12,8},{16,12},{20,16},{24,20},{28,24},{5,1},{9,5},{13... | collective-permute-start | bytes 2359304 | tf_op jit(solution)/shard_map/ppermute | solution.py:471
  69.3 22.9 %collective-permute-start.12 = (f32[8,32,256]{2,1,0:T(8,128)}, f32[8,32,256]{2,1,0:T(8,128)S(1)}, u32[]{:S(2)}, u32[]{:S(2)}) collective-permute-start(f32[8,32,256]{2,1,0:T(8,128)} %get-tuple-element.38), channel_id=1, source_target_pairs={{0,2},{1,3},{2,0},{3,1},{4,6},{5,7},{6,4},{7,5},{8,10},{9,11},{10,... | collective-permute-start | bytes 786440 | tf_op jit(solution)/shard_map/ppermute | solution.py:468
  72.2 26.1 %collective-permute-start.13 = (f32[8,32,256]{2,1,0:T(8,128)}, f32[8,32,256]{2,1,0:T(8,128)S(1)}, u32[]{:S(2)}, u32[]{:S(2)}) collective-permute-start(f32[8,32,256]{2,1,0:T(8,128)} %get-tuple-element.39), channel_id=1, source_target_pairs={{0,1},{1,2},{2,3},{3,0},{4,5},{5,6},{6,7},{7,4},{8,9},{9,10},{10,1... | collective-permute-start | bytes 786440 | tf_op jit(solution)/shard_map/ppermute | solution.py:468
  76.8 21.5 %collective-permute-start.14 = (f32[8,32,256]{2,1,0:T(8,128)}, f32[8,32,256]{2,1,0:T(8,128)}, u32[]{:S(2)}, u32[]{:S(2)}) collective-permute-start(f32[8,32,256]{2,1,0:T(8,128)} %get-tuple-element.40), channel_id=1, source_target_pairs={{0,3},{1,0},{2,1},{3,2},{4,7},{5,4},{6,5},{7,6},{8,11},{9,8},{10,9... | collective-permute-start | bytes 786440 | tf_op jit(solution)/shard_map/ppermute | solution.py:468
  89.8 31.0 %collective-permute-start.7 = (f32[8,32,256]{2,1,0:T(8,128)}, f32[8,32,256]{2,1,0:T(8,128)}, u32[]{:S(2)}, u32[]{:S(2)}) collective-permute-start(f32[8,32,256]{2,1,0:T(8,128)} %get-tuple-element.35), channel_id=1, source_target_pairs={{0,2},{1,3},{2,0},{3,1},{4,6},{5,7},{6,4},{7,5},{8,10},{9,11},{10,... | collective-permute-start | bytes 786440 | tf_op jit(solution)/shard_map/ppermute | solution.py:468
  89.9 30.9 %collective-permute-start.8 = (f32[8,32,256]{2,1,0:T(8,128)}, f32[8,32,256]{2,1,0:T(8,128)}, u32[]{:S(2)}, u32[]{:S(2)}) collective-permute-start(f32[8,32,256]{2,1,0:T(8,128)} %get-tuple-element.36), channel_id=1, source_target_pairs={{0,1},{1,2},{2,3},{3,0},{4,5},{5,6},{6,7},{7,4},{8,9},{9,10},{10,1... | collective-permute-start | bytes 786440 | tf_op jit(solution)/shard_map/ppermute | solution.py:468
  92.2 28.6 %collective-permute-start.9 = (f32[8,32,256]{2,1,0:T(8,128)}, f32[8,32,256]{2,1,0:T(8,128)}, u32[]{:S(2)}, u32[]{:S(2)}) collective-permute-start(f32[8,32,256]{2,1,0:T(8,128)} %get-tuple-element.37), channel_id=1, source_target_pairs={{0,3},{1,0},{2,1},{3,2},{4,7},{5,4},{6,5},{7,6},{8,11},{9,8},{10,9... | collective-permute-start | bytes 786440 | tf_op jit(solution)/shard_map/ppermute | solution.py:468
  93.8 101.1 %all-to-all-start.1 = ((f32[4,8,32,256]{3,2,1,0:T(8,128)}), f32[4,8,32,256]{3,2,1,0:T(8,128)}, u32[]{:S(2)}, u32[]{:S(2)}) async-start(f32[4,8,32,256]{3,2,1,0:T(8,128)} %copy-done.2), calls=%async_computation.1 | async-start | bytes 2097152 | tf_op jit(solution)/shard_map/all_to_all | solution.py:511
  108.2 29.3 %collective-permute-start.20 = (f32[24,32,256]{2,1,0:T(8,128)S(1)}, f32[24,32,256]{2,1,0:T(8,128)S(1)}, u32[]{:S(2)}, u32[]{:S(2)}) collective-permute-start(f32[24,32,256]{2,1,0:T(8,128)S(1)} %gather.7), channel_id=1, source_target_pairs={{0,4},{4,8},{8,12},{12,16},{16,20},{20,24},{24,28},{1,5},{5,9},{9,... | collective-permute-start | bytes 2359304 | tf_op jit(solution)/shard_map/ppermute | solution.py:471
  110.2 32.5 %collective-permute-start.21 = (f32[24,32,256]{2,1,0:T(8,128)S(1)}, f32[24,32,256]{2,1,0:T(8,128)S(1)}, u32[]{:S(2)}, u32[]{:S(2)}) collective-permute-start(f32[24,32,256]{2,1,0:T(8,128)S(1)} %gather.7), channel_id=1, source_target_pairs={{4,0},{8,4},{12,8},{16,12},{20,16},{24,20},{28,24},{5,1},{9,5},{13... | collective-permute-start | bytes 2359304 | tf_op jit(solution)/shard_map/ppermute | solution.py:471
  122.0 27.8 %collective-permute-start.15 = (f32[24,32,256]{2,1,0:T(8,128)S(1)}, f32[24,32,256]{2,1,0:T(8,128)S(1)}, u32[]{:S(2)}, u32[]{:S(2)}) collective-permute-start(f32[24,32,256]{2,1,0:T(8,128)S(1)} %gather.6), channel_id=1, source_target_pairs={{0,4},{4,8},{8,12},{12,16},{16,20},{20,24},{24,28},{1,5},{5,9},{9,... | collective-permute-start | bytes 2359304 | tf_op jit(solution)/shard_map/ppermute | solution.py:471
  123.9 34.0 %collective-permute-start.16 = (f32[24,32,256]{2,1,0:T(8,128)S(1)}, f32[24,32,256]{2,1,0:T(8,128)S(1)}, u32[]{:S(2)}, u32[]{:S(2)}) collective-permute-start(f32[24,32,256]{2,1,0:T(8,128)S(1)} %gather.6), channel_id=1, source_target_pairs={{4,0},{8,4},{12,8},{16,12},{20,16},{24,20},{28,24},{5,1},{9,5},{13... | collective-permute-start | bytes 2359304 | tf_op jit(solution)/shard_map/ppermute | solution.py:471
  128.5 38.5 %collective-permute-start.25 = (f32[8,32,256]{2,1,0:T(8,128)S(1)}, f32[8,32,256]{2,1,0:T(8,128)S(1)}, u32[]{:S(2)}, u32[]{:S(2)}) collective-permute-start(f32[8,32,256]{2,1,0:T(8,128)S(1)} %get-tuple-element.50), channel_id=1, source_target_pairs={{0,2},{1,3},{2,0},{3,1},{4,6},{5,7},{6,4},{7,5},{8,10},{9,11},{10,... | collective-permute-start | bytes 786440 | tf_op jit(solution)/shard_map/ppermute | solution.py:468
  137.5 32.2 %collective-permute-start.26 = (f32[8,32,256]{2,1,0:T(8,128)S(1)}, f32[8,32,256]{2,1,0:T(8,128)S(1)}, u32[]{:S(2)}, u32[]{:S(2)}) collective-permute-start(f32[8,32,256]{2,1,0:T(8,128)S(1)} %get-tuple-element.51), channel_id=1, source_target_pairs={{0,1},{1,2},{2,3},{3,0},{4,5},{5,6},{6,7},{7,4},{8,9},{9,10},{10,1... | collective-permute-start | bytes 786440 | tf_op jit(solution)/shard_map/ppermute | solution.py:468
  142.6 32.4 %collective-permute-start.27 = (f32[8,32,256]{2,1,0:T(8,128)S(1)}, f32[8,32,256]{2,1,0:T(8,128)S(1)}, u32[]{:S(2)}, u32[]{:S(2)}) collective-permute-start(f32[8,32,256]{2,1,0:T(8,128)S(1)} %get-tuple-element.52), channel_id=1, source_target_pairs={{0,3},{1,0},{2,1},{3,2},{4,7},{5,4},{6,5},{7,6},{8,11},{9,8},{10,9... | collective-permute-start | bytes 786440 | tf_op jit(solution)/shard_map/ppermute | solution.py:468
  149.8 41.2 %collective-permute-start.22 = (f32[8,32,256]{2,1,0:T(8,128)S(1)}, f32[8,32,256]{2,1,0:T(8,128)S(1)}, u32[]{:S(2)}, u32[]{:S(2)}) collective-permute-start(f32[8,32,256]{2,1,0:T(8,128)S(1)} %get-tuple-element.47), channel_id=1, source_target_pairs={{0,2},{1,3},{2,0},{3,1},{4,6},{5,7},{6,4},{7,5},{8,10},{9,11},{10,... | collective-permute-start | bytes 786440 | tf_op jit(solution)/shard_map/ppermute | solution.py:468
  158.0 33.7 %copy-start.14 = (f32[32,1,64,256]{3,2,1,0:T(8,128)S(1)}, f32[32,1,64,256]{3,2,1,0:T(8,128)}, u32[]{:S(2)}) copy-start(f32[32,1,64,256]{3,2,1,0:T(8,128)} %param.8) | copy-start | bytes 6291460
  158.0 41.9 %collective-permute-start.23 = (f32[8,32,256]{2,1,0:T(8,128)S(1)}, f32[8,32,256]{2,1,0:T(8,128)}, u32[]{:S(2)}, u32[]{:S(2)}) collective-permute-start(f32[8,32,256]{2,1,0:T(8,128)S(1)} %get-tuple-element.48), channel_id=1, source_target_pairs={{0,1},{1,2},{2,3},{3,0},{4,5},{5,6},{6,7},{7,4},{8,9},{9,10},{10,1... | collective-permute-start | bytes 786440 | tf_op jit(solution)/shard_map/ppermute | solution.py:468
  167.0 24.0 %copy-start.15 = (f32[8,32,256]{2,1,0:T(8,128)}, f32[8,32,256]{2,1,0:T(8,128)S(1)}, u32[]{:S(2)}) copy-start(f32[8,32,256]{2,1,0:T(8,128)S(1)} %collective-permute-done.25.refs_1_) | copy-start | bytes 786436
  167.0 32.8 %collective-permute-start.24 = (f32[8,32,256]{2,1,0:T(8,128)S(1)}, f32[8,32,256]{2,1,0:T(8,128)S(1)}, u32[]{:S(2)}, u32[]{:S(2)}) collective-permute-start(f32[8,32,256]{2,1,0:T(8,128)S(1)} %get-tuple-element.49), channel_id=1, source_target_pairs={{0,3},{1,0},{2,1},{3,2},{4,7},{5,4},{6,5},{7,6},{8,11},{9,8},{10,9... | collective-permute-start | bytes 786440 | tf_op jit(solution)/shard_map/ppermute | solution.py:468
  169.8 33.3 %collective-permute-start.17 = (f32[8,32,256]{2,1,0:T(8,128)}, f32[8,32,256]{2,1,0:T(8,128)S(1)}, u32[]{:S(2)}, u32[]{:S(2)}) collective-permute-start(f32[8,32,256]{2,1,0:T(8,128)} %get-tuple-element.43), channel_id=1, source_target_pairs={{0,2},{1,3},{2,0},{3,1},{4,6},{5,7},{6,4},{7,5},{8,10},{9,11},{10,... | collective-permute-start | bytes 786440 | tf_op jit(solution)/shard_map/ppermute | solution.py:468
  175.0 28.1 %collective-permute-start.18 = (f32[8,32,256]{2,1,0:T(8,128)S(1)}, f32[8,32,256]{2,1,0:T(8,128)S(1)}, u32[]{:S(2)}, u32[]{:S(2)}) collective-permute-start(f32[8,32,256]{2,1,0:T(8,128)S(1)} %get-tuple-element.44), channel_id=1, source_target_pairs={{0,1},{1,2},{2,3},{3,0},{4,5},{5,6},{6,7},{7,4},{8,9},{9,10},{10,1... | collective-permute-start | bytes 786440 | tf_op jit(solution)/shard_map/ppermute | solution.py:468
  191.0 12.1 %collective-permute-start.19 = (f32[8,32,256]{2,1,0:T(8,128)S(1)}, f32[8,32,256]{2,1,0:T(8,128)S(1)}, u32[]{:S(2)}, u32[]{:S(2)}) collective-permute-start(f32[8,32,256]{2,1,0:T(8,128)S(1)} %get-tuple-element.45), channel_id=1, source_target_pairs={{0,3},{1,0},{2,1},{3,2},{4,7},{5,4},{6,5},{7,6},{8,11},{9,8},{10,9... | collective-permute-start | bytes 786440 | tf_op jit(solution)/shard_map/ppermute | solution.py:468
  (21 other events, 115.4 us)
